TPU v7x, 256 devices: a whole 4x4x8 slice. The times are simulated.
256 devices in a mesh: blk: 32 (over z, y_hi, core), bulk: 8 (over x, y_lo).
Axes of the slice: x: 4, y: 4 (y_hi: 2, y_lo: 2; y = y_hi * 2 + y_lo), z: 8, core: 2. Of those that a mesh axis runs over, the one named last changes fastest.
Arguments:
- footage_embeds: bfloat16 [32768, 768], P(('blk', 'bulk')), may hold values from -0.21582031 to 0.21582031
- caption_embeds: bfloat16 [32768, 768], P(('blk', 'bulk')), may hold values from -0.21582031 to 0.21582031
- score_scale: float32 [1], replicated, may hold values from 4 to 16
- score_offset: float32 [1], replicated, may hold values from -4 to -2
Outputs:
- video_grad: float32 [32768, 768], P(('blk', 'bulk'))
- text_grad: float32 [32768, 768], P(('blk', 'bulk'))
All inputs are finite; a program needn't handle non-finite values.
Results may differ from a plain program's by a relative error of at most 0.007.
Values may be sent and summed in bfloat16 or wider, within the bound.
No kernel may reach another device: no remote copies, remote signals or barrier semaphores. Data moves between devices by JAX's collectives and lax.ppermute only.
A program may use at most 64 MiB of HBM per device.

v0:
```python
import jax
import jax.numpy as jnp
from jax import lax
from jax.sharding import PartitionSpec as P

EPSILON = 1e-06


def from_behind(x, axis, by):
    count = lax.axis_size(axis)
    return lax.ppermute(x, axis, [(i, (i + by) % count) for i in range(count)])


def unit_rows(embedding):
    values = embedding.astype(jnp.float32)
    inverse = lax.rsqrt(jnp.sum(values * values, axis=1, keepdims=True) + EPSILON)
    return (values * inverse, inverse)


def back_rows(unit, inverse, grad_unit):
    return (grad_unit - unit * jnp.sum(unit * grad_unit, axis=1, keepdims=True)) * inverse


def move_text(block, offset):
    return from_behind(block, "blk", offset)


def move_grads(carried, offset):
    return from_behind(carried, "blk", offset)


def local(footage_embeds, caption_embeds, score_scale, score_offset):
    clip_rows = footage_embeds.shape[0]
    feature_dim = footage_embeds.shape[1]
    cycle_size = lax.axis_size("blk")
    cycle_index = lax.axis_index("blk")
    bulk_size = lax.axis_size("bulk")
    bulk_index = lax.axis_index("bulk")
    reach = cycle_size // 4
    band = 2 * reach + 1
    smoothing_coefficient = score_scale[0]
    shifted_bias = score_offset[0]
    video_unit, video_inverse = unit_rows(footage_embeds)
    text_unit, text_inverse = unit_rows(caption_embeds)
    text_low = text_unit.astype(jnp.bfloat16)
    group = lax.all_gather(video_unit.astype(jnp.bfloat16), "bulk", axis=0, tiled=True)
    group_rows = group.shape[0]
    row_ids = cycle_index * group_rows + jnp.arange(group_rows, dtype=jnp.int32)
    column_base = jnp.arange(clip_rows, dtype=jnp.int32)

    def visit(block, owner, slot, pair_weights, tile_sequence):
        logit_matrix = (
            smoothing_coefficient
            * lax.dot_general(
                group, block, (((1,), (1,)), ((), ())), preferred_element_type=jnp.float32
            )
            + shifted_bias
        )
        col_ids = (owner * bulk_size + bulk_index) * clip_rows + column_base
        label = (row_ids[:, None] == col_ids[None, :]).astype(jnp.float32)
        pair_weight = (jax.nn.sigmoid(logit_matrix) - label).astype(jnp.bfloat16)
        place = jnp.asarray(slot * clip_rows, jnp.int32)
        pair_weights = lax.dynamic_update_slice(pair_weights, pair_weight, (jnp.int32(0), place))
        tile_sequence = lax.dynamic_update_slice(tile_sequence, block, (place, jnp.int32(0)))
        return (pair_weights, tile_sequence, pair_weight)

    def contribution(pair_weight):
        return smoothing_coefficient * lax.dot_general(
            pair_weight, group, (((0,), (0,)), ((), ())), preferred_element_type=jnp.float32
        )

    def step_forward(block, carried, owner, slot, offset, pair_weights, tile_sequence):
        block = move_text(block, offset)
        pair_weights, tile_sequence, pair_weight = visit(
            block, owner, slot, pair_weights, tile_sequence
        )
        carried = move_grads(carried, offset) + contribution(pair_weight)
        return (block, carried, pair_weights, tile_sequence)

    pair_weights = jnp.zeros((group_rows, band * clip_rows), jnp.bfloat16)
    tile_sequence = jnp.zeros((band * clip_rows, feature_dim), jnp.bfloat16)
    first = move_text(text_low, -reach)
    pair_weights, tile_sequence, pair_weight = visit(
        first, (cycle_index + reach) % cycle_size, 0, pair_weights, tile_sequence
    )
    forward = contribution(pair_weight)

    def one_turn(turn, carry):
        block, carried, pair_weights, tile_sequence = carry
        owner = (cycle_index + reach - turn) % cycle_size
        return step_forward(block, carried, owner, turn, 1, pair_weights, tile_sequence)

    block, forward, pair_weights, tile_sequence = lax.fori_loop(
        1, band, one_turn, (first, forward, pair_weights, tile_sequence)
    )
    caption_derivative_normed = move_grads(forward, -reach)
    video_grad_unit = lax.psum_scatter(
        smoothing_coefficient
        * jnp.dot(pair_weights, tile_sequence, preferred_element_type=jnp.float32),
        "bulk",
        scatter_dimension=0,
        tiled=True,
    )
    video_grad = back_rows(video_unit, video_inverse, video_grad_unit)
    text_grad = back_rows(text_unit, text_inverse, caption_derivative_normed)
    return (video_grad, text_grad)


def solution(mesh):
    return jax.shard_map(
        local,
        mesh=mesh,
        in_specs=(P(("blk", "bulk"), None), P(("blk", "bulk"), None), P(), P()),
        out_specs=(P(("blk", "bulk"), None), P(("blk", "bulk"), None)),
        check_vma=False,
    )
```

profile of v0, /device:TPU:2, one launch (start us, length us, event | category | flops | bytes accessed | tf_op | source)
XLA Modules:
  0.0 380.2 jit_solution(9388595258893967713)
XLA Ops:
  12.1 6.4 %collective-permute-start.2 = (bf16[128,768]{1,0:T(8,128)(2,1)S(1)}, bf16[128,768]{1,0:T(8,128)(2,1)S(1)}, u32[]{:S(2)}, u32[]{:S(2)}) collective-permute-start(bf16[128,768]{1,0:T(8,128)(2,1)S(1)} %fusion.24), channel_id=1, source_target_pairs={{0,192},{8,200},{16,208},{24,216},{32,224},{40,232},{48,240},{56,2... | collective-permute-start | bytes 589832 | tf_op jit(solution)/shard_map/ppermute | solution.py:11
  19.8 7.1 %collective-permute-done.2 = bf16[128,768]{1,0:T(8,128)(2,1)S(1)} collective-permute-done((bf16[128,768]{1,0:T(8,128)(2,1)S(1)}, bf16[128,768]{1,0:T(8,128)(2,1)S(1)}, u32[]{:S(2)}, u32[]{:S(2)}) %collective-permute-start.2) | collective-permute-done | bytes 196640 | tf_op jit(solution)/shard_map/ppermute | solution.py:11
  28.9 29.5 %all-gather.2.cloned.1.call-done = bf16[1024,768]{1,0:T(8,128)(2,1)} async-done(((bf16[128,768]{1,0:T(8,128)(2,1)}), bf16[1024,768]{1,0:T(8,128)(2,1)}) %all-gather.2.cloned.1.call-update) | async-done | bytes 1572880 | tf_op jit(solution)/shard_map/all_gather | solution.py:46
  63.1 225.2 %while.22 = (s32[]{:T(128)}, bf16[128,768]{1,0:T(8,128)(2,1)S(1)}, f32[128,768]{1,0:T(8,128)S(1)}, bf16[1024,2176]{1,0:T(8,128)(2,1)}, bf16[2176,768]{1,0:T(8,12...) while((s32[]{:T(128)}, bf16[128,768]{1,0:T(8,128)(2,1)S(1)}, ...), condition=%wide.region_3.4_spmd.clone, body=%wide.region_2.3_spmd.clone.sunk | while | flops 404030592 | bytes 8071636 | solution.py:93
  63.2 2.9 collective-permute-start.1
  66.2 5.8 %collective-permute-done = bf16[128,768]{1,0:T(8,128)(2,1)S(1)} collective-permute-done((bf16[128,768]{1,0:T(8,128)(2,1)S(1)}, bf16[128,768]{1,0:T(8,128)(2,1)S(1)}, u32[]{:S(2)}, u32[]{:S(2)}) %collective-permute-start) | collective-permute-done | bytes 196640 | tf_op jit(solution)/shard_map/while/body/eval_jaxpr/ppermute | solution.py:11
  78.1 7.9 %collective-permute-done = bf16[128,768]{1,0:T(8,128)(2,1)S(1)} collective-permute-done((bf16[128,768]{1,0:T(8,128)(2,1)S(1)}, bf16[128,768]{1,0:T(8,128)(2,1)S(1)}, u32[]{:S(2)}, u32[]{:S(2)}) %collective-permute-start) | collective-permute-done | bytes 196640 | tf_op jit(solution)/shard_map/while/body/eval_jaxpr/ppermute | solution.py:11
  86.7 2.6 constant_dynamic-update-slice_fusion.4
  91.5 8.6 %collective-permute-done = bf16[128,768]{1,0:T(8,128)(2,1)S(1)} collective-permute-done((bf16[128,768]{1,0:T(8,128)(2,1)S(1)}, bf16[128,768]{1,0:T(8,128)(2,1)S(1)}, u32[]{:S(2)}, u32[]{:S(2)}) %collective-permute-start) | collective-permute-done | bytes 196640 | tf_op jit(solution)/shard_map/while/body/eval_jaxpr/ppermute | solution.py:11
  105.6 8.6 %collective-permute-done = bf16[128,768]{1,0:T(8,128)(2,1)S(1)} collective-permute-done((bf16[128,768]{1,0:T(8,128)(2,1)S(1)}, bf16[128,768]{1,0:T(8,128)(2,1)S(1)}, u32[]{:S(2)}, u32[]{:S(2)}) %collective-permute-start) | collective-permute-done | bytes 196640 | tf_op jit(solution)/shard_map/while/body/eval_jaxpr/ppermute | solution.py:11
  119.7 8.6 %collective-permute-done = bf16[128,768]{1,0:T(8,128)(2,1)S(1)} collective-permute-done((bf16[128,768]{1,0:T(8,128)(2,1)S(1)}, bf16[128,768]{1,0:T(8,128)(2,1)S(1)}, u32[]{:S(2)}, u32[]{:S(2)}) %collective-permute-start) | collective-permute-done | bytes 196640 | tf_op jit(solution)/shard_map/while/body/eval_jaxpr/ppermute | solution.py:11
  129.0 2.6 constant_dynamic-update-slice_fusion.4
  133.7 8.6 %collective-permute-done = bf16[128,768]{1,0:T(8,128)(2,1)S(1)} collective-permute-done((bf16[128,768]{1,0:T(8,128)(2,1)S(1)}, bf16[128,768]{1,0:T(8,128)(2,1)S(1)}, u32[]{:S(2)}, u32[]{:S(2)}) %collective-permute-start) | collective-permute-done | bytes 196640 | tf_op jit(solution)/shard_map/while/body/eval_jaxpr/ppermute | solution.py:11
  143.0 2.6 constant_dynamic-update-slice_fusion.4
  147.8 8.6 %collective-permute-done = bf16[128,768]{1,0:T(8,128)(2,1)S(1)} collective-permute-done((bf16[128,768]{1,0:T(8,128)(2,1)S(1)}, bf16[128,768]{1,0:T(8,128)(2,1)S(1)}, u32[]{:S(2)}, u32[]{:S(2)}) %collective-permute-start) | collective-permute-done | bytes 196640 | tf_op jit(solution)/shard_map/while/body/eval_jaxpr/ppermute | solution.py:11
  161.9 8.6 %collective-permute-done = bf16[128,768]{1,0:T(8,128)(2,1)S(1)} collective-permute-done((bf16[128,768]{1,0:T(8,128)(2,1)S(1)}, bf16[128,768]{1,0:T(8,128)(2,1)S(1)}, u32[]{:S(2)}, u32[]{:S(2)}) %collective-permute-start) | collective-permute-done | bytes 196640 | tf_op jit(solution)/shard_map/while/body/eval_jaxpr/ppermute | solution.py:11
  176.0 8.6 %collective-permute-done = bf16[128,768]{1,0:T(8,128)(2,1)S(1)} collective-permute-done((bf16[128,768]{1,0:T(8,128)(2,1)S(1)}, bf16[128,768]{1,0:T(8,128)(2,1)S(1)}, u32[]{:S(2)}, u32[]{:S(2)}) %collective-permute-start) | collective-permute-done | bytes 196640 | tf_op jit(solution)/shard_map/while/body/eval_jaxpr/ppermute | solution.py:11
  190.0 8.6 %collective-permute-done = bf16[128,768]{1,0:T(8,128)(2,1)S(1)} collective-permute-done((bf16[128,768]{1,0:T(8,128)(2,1)S(1)}, bf16[128,768]{1,0:T(8,128)(2,1)S(1)}, u32[]{:S(2)}, u32[]{:S(2)}) %collective-permute-start) | collective-permute-done | bytes 196640 | tf_op jit(solution)/shard_map/while/body/eval_jaxpr/ppermute | solution.py:11
  199.3 2.7 constant_dynamic-update-slice_fusion.4
  204.1 8.6 %collective-permute-done = bf16[128,768]{1,0:T(8,128)(2,1)S(1)} collective-permute-done((bf16[128,768]{1,0:T(8,128)(2,1)S(1)}, bf16[128,768]{1,0:T(8,128)(2,1)S(1)}, u32[]{:S(2)}, u32[]{:S(2)}) %collective-permute-start) | collective-permute-done | bytes 196640 | tf_op jit(solution)/shard_map/while/body/eval_jaxpr/ppermute | solution.py:11
  218.2 8.6 %collective-permute-done = bf16[128,768]{1,0:T(8,128)(2,1)S(1)} collective-permute-done((bf16[128,768]{1,0:T(8,128)(2,1)S(1)}, bf16[128,768]{1,0:T(8,128)(2,1)S(1)}, u32[]{:S(2)}, u32[]{:S(2)}) %collective-permute-start) | collective-permute-done | bytes 196640 | tf_op jit(solution)/shard_map/while/body/eval_jaxpr/ppermute | solution.py:11
  227.5 2.6 constant_dynamic-update-slice_fusion.4
  232.3 8.6 %collective-permute-done = bf16[128,768]{1,0:T(8,128)(2,1)S(1)} collective-permute-done((bf16[128,768]{1,0:T(8,128)(2,1)S(1)}, bf16[128,768]{1,0:T(8,128)(2,1)S(1)}, u32[]{:S(2)}, u32[]{:S(2)}) %collective-permute-start) | collective-permute-done | bytes 196640 | tf_op jit(solution)/shard_map/while/body/eval_jaxpr/ppermute | solution.py:11
  246.3 8.6 %collective-permute-done = bf16[128,768]{1,0:T(8,128)(2,1)S(1)} collective-permute-done((bf16[128,768]{1,0:T(8,128)(2,1)S(1)}, bf16[128,768]{1,0:T(8,128)(2,1)S(1)}, u32[]{:S(2)}, u32[]{:S(2)}) %collective-permute-start) | collective-permute-done | bytes 196640 | tf_op jit(solution)/shard_map/while/body/eval_jaxpr/ppermute | solution.py:11
  255.6 2.7 constant_dynamic-update-slice_fusion.4
  260.4 8.6 %collective-permute-done = bf16[128,768]{1,0:T(8,128)(2,1)S(1)} collective-permute-done((bf16[128,768]{1,0:T(8,128)(2,1)S(1)}, bf16[128,768]{1,0:T(8,128)(2,1)S(1)}, u32[]{:S(2)}, u32[]{:S(2)}) %collective-permute-start) | collective-permute-done | bytes 196640 | tf_op jit(solution)/shard_map/while/body/eval_jaxpr/ppermute | solution.py:11
  269.7 2.6 constant_dynamic-update-slice_fusion.4
  274.5 8.6 %collective-permute-done = bf16[128,768]{1,0:T(8,128)(2,1)S(1)} collective-permute-done((bf16[128,768]{1,0:T(8,128)(2,1)S(1)}, bf16[128,768]{1,0:T(8,128)(2,1)S(1)}, u32[]{:S(2)}, u32[]{:S(2)}) %collective-permute-start) | collective-permute-done | bytes 196640 | tf_op jit(solution)/shard_map/while/body/eval_jaxpr/ppermute | solution.py:11
  283.7 2.6 constant_dynamic-update-slice_fusion.4
  288.3 8.9 %convolution_multiply_fusion.2 = f32[1024,768]{1,0:T(8,128)} fusion(bf16[1024,2176]{1,0:T(8,128)(2,1)} %get-tuple-element.293, bf16[2176,768]{1,0:T(8,128)(2,1)} %get-tuple-element.294, f32[]{:T(128)} %bitcast.20), kind=kOutput, calls=%fused_computation.16 | convolution fusion | flops 3423338496 | bytes 10944516 | tf_op jit(solution)/shard_map/dot_general | solution.py:99
  297.3 10.4 %collective-permute-done.3 = f32[128,768]{1,0:T(8,128)S(1)} collective-permute-done((f32[128,768]{1,0:T(8,128)S(1)}, f32[128,768]{1,0:T(8,128)S(1)}, u32[]{:S(2)}, u32[]{:S(2)}) %collective-permute-start.3) | collective-permute-done | bytes 393248 | tf_op jit(solution)/shard_map/ppermute | solution.py:11
  308.8 61.4 %reduce-scatter.2.cloned.1.call-done = f32[128,768]{1,0:T(8,128)} async-done(((f32[1024,768]{1,0:T(8,128)}), f32[128,768]{1,0:T(8,128)}) %reduce-scatter.2.cloned.1.call-update) | async-done | bytes 393232 | tf_op jit(solution)/shard_map/reduce_scatter | solution.py:97
  (162 shorter events, 82.5 us)
Async XLA Ops:
  7.2 51.2 %all-gather.2.cloned.1.call-start = ((), (), s32[]{:S(2)}) async-start(), calls=%async_computation.1 | async-start | bytes 1769472 | tf_op jit(solution)/shard_map/all_gather | solution.py:46
  10.0 360.2 %reduce-scatter.2.cloned.1.call-start = ((), (), s32[]{:S(2)}) async-start(), calls=%async_computation.2 | async-start | bytes 3538944 | tf_op jit(solution)/shard_map/reduce_scatter | solution.py:97
  12.1 14.8 %collective-permute-start.2 = (bf16[128,768]{1,0:T(8,128)(2,1)S(1)}, bf16[128,768]{1,0:T(8,128)(2,1)S(1)}, u32[]{:S(2)}, u32[]{:S(2)}) collective-permute-start(bf16[128,768]{1,0:T(8,128)(2,1)S(1)} %fusion.24), channel_id=1, source_target_pairs={{0,192},{8,200},{16,208},{24,216},{32,224},{40,232},{48,240},{56,2... | collective-permute-start | bytes 589832 | tf_op jit(solution)/shard_map/ppermute | solution.py:11
  63.2 8.8 %collective-permute-start = (bf16[128,768]{1,0:T(8,128)(2,1)S(1)}, bf16[128,768]{1,0:T(8,128)(2,1)S(1)}, u32[]{:S(2)}, u32[]{:S(2)}) collective-permute-start(bf16[128,768]{1,0:T(8,128)(2,1)S(1)} %get-tuple-element.436), channel_id=1, source_target_pairs={{0,8},{8,16},{16,24},{24,32},{32,40},{40,48},{48,56},{56,64},{64,7... | collective-permute-start | bytes 589832 | tf_op jit(solution)/shard_map/while/body/eval_jaxpr/ppermute | solution.py:11
  63.2 12.9 %collective-permute-start.1 = (f32[128,768]{1,0:T(8,128)S(1)}, f32[128,768]{1,0:T(8,128)S(1)}, u32[]{:S(2)}, u32[]{:S(2)}) collective-permute-start(f32[128,768]{1,0:T(8,128)S(1)} %get-tuple-element.437), channel_id=1, source_target_pairs={{0,8},{8,16},{16,24},{24,32},{32,40},{40,48},{48,56},{56,64},{64,7... | collective-permute-start | bytes 1179656 | tf_op jit(solution)/shard_map/while/body/eval_jaxpr/ppermute | solution.py:11
  77.3 12.9 %collective-permute-start.1 = (f32[128,768]{1,0:T(8,128)S(1)}, f32[128,768]{1,0:T(8,128)S(1)}, u32[]{:S(2)}, u32[]{:S(2)}) collective-permute-start(f32[128,768]{1,0:T(8,128)S(1)} %get-tuple-element.437), channel_id=1, source_target_pairs={{0,8},{8,16},{16,24},{24,32},{32,40},{40,48},{48,56},{56,64},{64,7... | collective-permute-start | bytes 1179656 | tf_op jit(solution)/shard_map/while/body/eval_jaxpr/ppermute | solution.py:11
  91.3 8.8 %collective-permute-start = (bf16[128,768]{1,0:T(8,128)(2,1)S(1)}, bf16[128,768]{1,0:T(8,128)(2,1)S(1)}, u32[]{:S(2)}, u32[]{:S(2)}) collective-permute-start(bf16[128,768]{1,0:T(8,128)(2,1)S(1)} %get-tuple-element.436), channel_id=1, source_target_pairs={{0,8},{8,16},{16,24},{24,32},{32,40},{40,48},{48,56},{56,64},{64,7... | collective-permute-start | bytes 589832 | tf_op jit(solution)/shard_map/while/body/eval_jaxpr/ppermute | solution.py:11
  91.4 12.9 %collective-permute-start.1 = (f32[128,768]{1,0:T(8,128)S(1)}, f32[128,768]{1,0:T(8,128)S(1)}, u32[]{:S(2)}, u32[]{:S(2)}) collective-permute-start(f32[128,768]{1,0:T(8,128)S(1)} %get-tuple-element.437), channel_id=1, source_target_pairs={{0,8},{8,16},{16,24},{24,32},{32,40},{40,48},{48,56},{56,64},{64,7... | collective-permute-start | bytes 1179656 | tf_op jit(solution)/shard_map/while/body/eval_jaxpr/ppermute | solution.py:11
  105.4 8.8 %collective-permute-start = (bf16[128,768]{1,0:T(8,128)(2,1)S(1)}, bf16[128,768]{1,0:T(8,128)(2,1)S(1)}, u32[]{:S(2)}, u32[]{:S(2)}) collective-permute-start(bf16[128,768]{1,0:T(8,128)(2,1)S(1)} %get-tuple-element.436), channel_id=1, source_target_pairs={{0,8},{8,16},{16,24},{24,32},{32,40},{40,48},{48,56},{56,64},{64,7... | collective-permute-start | bytes 589832 | tf_op jit(solution)/shard_map/while/body/eval_jaxpr/ppermute | solution.py:11
  105.5 12.9 %collective-permute-start.1 = (f32[128,768]{1,0:T(8,128)S(1)}, f32[128,768]{1,0:T(8,128)S(1)}, u32[]{:S(2)}, u32[]{:S(2)}) collective-permute-start(f32[128,768]{1,0:T(8,128)S(1)} %get-tuple-element.437), channel_id=1, source_target_pairs={{0,8},{8,16},{16,24},{24,32},{32,40},{40,48},{48,56},{56,64},{64,7... | collective-permute-start | bytes 1179656 | tf_op jit(solution)/shard_map/while/body/eval_jaxpr/ppermute | solution.py:11
  119.4 8.8 %collective-permute-start = (bf16[128,768]{1,0:T(8,128)(2,1)S(1)}, bf16[128,768]{1,0:T(8,128)(2,1)S(1)}, u32[]{:S(2)}, u32[]{:S(2)}) collective-permute-start(bf16[128,768]{1,0:T(8,128)(2,1)S(1)} %get-tuple-element.436), channel_id=1, source_target_pairs={{0,8},{8,16},{16,24},{24,32},{32,40},{40,48},{48,56},{56,64},{64,7... | collective-permute-start | bytes 589832 | tf_op jit(solution)/shard_map/while/body/eval_jaxpr/ppermute | solution.py:11
  119.5 12.9 %collective-permute-start.1 = (f32[128,768]{1,0:T(8,128)S(1)}, f32[128,768]{1,0:T(8,128)S(1)}, u32[]{:S(2)}, u32[]{:S(2)}) collective-permute-start(f32[128,768]{1,0:T(8,128)S(1)} %get-tuple-element.437), channel_id=1, source_target_pairs={{0,8},{8,16},{16,24},{24,32},{32,40},{40,48},{48,56},{56,64},{64,7... | collective-permute-start | bytes 1179656 | tf_op jit(solution)/shard_map/while/body/eval_jaxpr/ppermute | solution.py:11
  133.5 8.8 %collective-permute-start = (bf16[128,768]{1,0:T(8,128)(2,1)S(1)}, bf16[128,768]{1,0:T(8,128)(2,1)S(1)}, u32[]{:S(2)}, u32[]{:S(2)}) collective-permute-start(bf16[128,768]{1,0:T(8,128)(2,1)S(1)} %get-tuple-element.436), channel_id=1, source_target_pairs={{0,8},{8,16},{16,24},{24,32},{32,40},{40,48},{48,56},{56,64},{64,7... | collective-permute-start | bytes 589832 | tf_op jit(solution)/shard_map/while/body/eval_jaxpr/ppermute | solution.py:11
  133.6 12.9 %collective-permute-start.1 = (f32[128,768]{1,0:T(8,128)S(1)}, f32[128,768]{1,0:T(8,128)S(1)}, u32[]{:S(2)}, u32[]{:S(2)}) collective-permute-start(f32[128,768]{1,0:T(8,128)S(1)} %get-tuple-element.437), channel_id=1, source_target_pairs={{0,8},{8,16},{16,24},{24,32},{32,40},{40,48},{48,56},{56,64},{64,7... | collective-permute-start | bytes 1179656 | tf_op jit(solution)/shard_map/while/body/eval_jaxpr/ppermute | solution.py:11
  147.6 8.8 %collective-permute-start = (bf16[128,768]{1,0:T(8,128)(2,1)S(1)}, bf16[128,768]{1,0:T(8,128)(2,1)S(1)}, u32[]{:S(2)}, u32[]{:S(2)}) collective-permute-start(bf16[128,768]{1,0:T(8,128)(2,1)S(1)} %get-tuple-element.436), channel_id=1, source_target_pairs={{0,8},{8,16},{16,24},{24,32},{32,40},{40,48},{48,56},{56,64},{64,7... | collective-permute-start | bytes 589832 | tf_op jit(solution)/shard_map/while/body/eval_jaxpr/ppermute | solution.py:11
  147.7 12.9 %collective-permute-start.1 = (f32[128,768]{1,0:T(8,128)S(1)}, f32[128,768]{1,0:T(8,128)S(1)}, u32[]{:S(2)}, u32[]{:S(2)}) collective-permute-start(f32[128,768]{1,0:T(8,128)S(1)} %get-tuple-element.437), channel_id=1, source_target_pairs={{0,8},{8,16},{16,24},{24,32},{32,40},{40,48},{48,56},{56,64},{64,7... | collective-permute-start | bytes 1179656 | tf_op jit(solution)/shard_map/while/body/eval_jaxpr/ppermute | solution.py:11
  161.7 8.8 %collective-permute-start = (bf16[128,768]{1,0:T(8,128)(2,1)S(1)}, bf16[128,768]{1,0:T(8,128)(2,1)S(1)}, u32[]{:S(2)}, u32[]{:S(2)}) collective-permute-start(bf16[128,768]{1,0:T(8,128)(2,1)S(1)} %get-tuple-element.436), channel_id=1, source_target_pairs={{0,8},{8,16},{16,24},{24,32},{32,40},{40,48},{48,56},{56,64},{64,7... | collective-permute-start | bytes 589832 | tf_op jit(solution)/shard_map/while/body/eval_jaxpr/ppermute | solution.py:11
  161.8 12.9 %collective-permute-start.1 = (f32[128,768]{1,0:T(8,128)S(1)}, f32[128,768]{1,0:T(8,128)S(1)}, u32[]{:S(2)}, u32[]{:S(2)}) collective-permute-start(f32[128,768]{1,0:T(8,128)S(1)} %get-tuple-element.437), channel_id=1, source_target_pairs={{0,8},{8,16},{16,24},{24,32},{32,40},{40,48},{48,56},{56,64},{64,7... | collective-permute-start | bytes 1179656 | tf_op jit(solution)/shard_map/while/body/eval_jaxpr/ppermute | solution.py:11
  175.8 12.9 %collective-permute-start.1 = (f32[128,768]{1,0:T(8,128)S(1)}, f32[128,768]{1,0:T(8,128)S(1)}, u32[]{:S(2)}, u32[]{:S(2)}) collective-permute-start(f32[128,768]{1,0:T(8,128)S(1)} %get-tuple-element.437), channel_id=1, source_target_pairs={{0,8},{8,16},{16,24},{24,32},{32,40},{40,48},{48,56},{56,64},{64,7... | collective-permute-start | bytes 1179656 | tf_op jit(solution)/shard_map/while/body/eval_jaxpr/ppermute | solution.py:11
  189.8 8.8 %collective-permute-start = (bf16[128,768]{1,0:T(8,128)(2,1)S(1)}, bf16[128,768]{1,0:T(8,128)(2,1)S(1)}, u32[]{:S(2)}, u32[]{:S(2)}) collective-permute-start(bf16[128,768]{1,0:T(8,128)(2,1)S(1)} %get-tuple-element.436), channel_id=1, source_target_pairs={{0,8},{8,16},{16,24},{24,32},{32,40},{40,48},{48,56},{56,64},{64,7... | collective-permute-start | bytes 589832 | tf_op jit(solution)/shard_map/while/body/eval_jaxpr/ppermute | solution.py:11
  189.9 12.9 %collective-permute-start.1 = (f32[128,768]{1,0:T(8,128)S(1)}, f32[128,768]{1,0:T(8,128)S(1)}, u32[]{:S(2)}, u32[]{:S(2)}) collective-permute-start(f32[128,768]{1,0:T(8,128)S(1)} %get-tuple-element.437), channel_id=1, source_target_pairs={{0,8},{8,16},{16,24},{24,32},{32,40},{40,48},{48,56},{56,64},{64,7... | collective-permute-start | bytes 1179656 | tf_op jit(solution)/shard_map/while/body/eval_jaxpr/ppermute | solution.py:11
  203.9 8.8 %collective-permute-start = (bf16[128,768]{1,0:T(8,128)(2,1)S(1)}, bf16[128,768]{1,0:T(8,128)(2,1)S(1)}, u32[]{:S(2)}, u32[]{:S(2)}) collective-permute-start(bf16[128,768]{1,0:T(8,128)(2,1)S(1)} %get-tuple-element.436), channel_id=1, source_target_pairs={{0,8},{8,16},{16,24},{24,32},{32,40},{40,48},{48,56},{56,64},{64,7... | collective-permute-start | bytes 589832 | tf_op jit(solution)/shard_map/while/body/eval_jaxpr/ppermute | solution.py:11
  204.0 12.9 %collective-permute-start.1 = (f32[128,768]{1,0:T(8,128)S(1)}, f32[128,768]{1,0:T(8,128)S(1)}, u32[]{:S(2)}, u32[]{:S(2)}) collective-permute-start(f32[128,768]{1,0:T(8,128)S(1)} %get-tuple-element.437), channel_id=1, source_target_pairs={{0,8},{8,16},{16,24},{24,32},{32,40},{40,48},{48,56},{56,64},{64,7... | collective-permute-start | bytes 1179656 | tf_op jit(solution)/shard_map/while/body/eval_jaxpr/ppermute | solution.py:11
  218.0 8.8 %collective-permute-start = (bf16[128,768]{1,0:T(8,128)(2,1)S(1)}, bf16[128,768]{1,0:T(8,128)(2,1)S(1)}, u32[]{:S(2)}, u32[]{:S(2)}) collective-permute-start(bf16[128,768]{1,0:T(8,128)(2,1)S(1)} %get-tuple-element.436), channel_id=1, source_target_pairs={{0,8},{8,16},{16,24},{24,32},{32,40},{40,48},{48,56},{56,64},{64,7... | collective-permute-start | bytes 589832 | tf_op jit(solution)/shard_map/while/body/eval_jaxpr/ppermute | solution.py:11
  218.0 12.9 %collective-permute-start.1 = (f32[128,768]{1,0:T(8,128)S(1)}, f32[128,768]{1,0:T(8,128)S(1)}, u32[]{:S(2)}, u32[]{:S(2)}) collective-permute-start(f32[128,768]{1,0:T(8,128)S(1)} %get-tuple-element.437), channel_id=1, source_target_pairs={{0,8},{8,16},{16,24},{24,32},{32,40},{40,48},{48,56},{56,64},{64,7... | collective-permute-start | bytes 1179656 | tf_op jit(solution)/shard_map/while/body/eval_jaxpr/ppermute | solution.py:11
  232.0 8.8 %collective-permute-start = (bf16[128,768]{1,0:T(8,128)(2,1)S(1)}, bf16[128,768]{1,0:T(8,128)(2,1)S(1)}, u32[]{:S(2)}, u32[]{:S(2)}) collective-permute-start(bf16[128,768]{1,0:T(8,128)(2,1)S(1)} %get-tuple-element.436), channel_id=1, source_target_pairs={{0,8},{8,16},{16,24},{24,32},{32,40},{40,48},{48,56},{56,64},{64,7... | collective-permute-start | bytes 589832 | tf_op jit(solution)/shard_map/while/body/eval_jaxpr/ppermute | solution.py:11
  232.1 12.9 %collective-permute-start.1 = (f32[128,768]{1,0:T(8,128)S(1)}, f32[128,768]{1,0:T(8,128)S(1)}, u32[]{:S(2)}, u32[]{:S(2)}) collective-permute-start(f32[128,768]{1,0:T(8,128)S(1)} %get-tuple-element.437), channel_id=1, source_target_pairs={{0,8},{8,16},{16,24},{24,32},{32,40},{40,48},{48,56},{56,64},{64,7... | collective-permute-start | bytes 1179656 | tf_op jit(solution)/shard_map/while/body/eval_jaxpr/ppermute | solution.py:11
  246.1 8.8 %collective-permute-start = (bf16[128,768]{1,0:T(8,128)(2,1)S(1)}, bf16[128,768]{1,0:T(8,128)(2,1)S(1)}, u32[]{:S(2)}, u32[]{:S(2)}) collective-permute-start(bf16[128,768]{1,0:T(8,128)(2,1)S(1)} %get-tuple-element.436), channel_id=1, source_target_pairs={{0,8},{8,16},{16,24},{24,32},{32,40},{40,48},{48,56},{56,64},{64,7... | collective-permute-start | bytes 589832 | tf_op jit(solution)/shard_map/while/body/eval_jaxpr/ppermute | solution.py:11
  246.2 12.9 %collective-permute-start.1 = (f32[128,768]{1,0:T(8,128)S(1)}, f32[128,768]{1,0:T(8,128)S(1)}, u32[]{:S(2)}, u32[]{:S(2)}) collective-permute-start(f32[128,768]{1,0:T(8,128)S(1)} %get-tuple-element.437), channel_id=1, source_target_pairs={{0,8},{8,16},{16,24},{24,32},{32,40},{40,48},{48,56},{56,64},{64,7... | collective-permute-start | bytes 1179656 | tf_op jit(solution)/shard_map/while/body/eval_jaxpr/ppermute | solution.py:11
  260.3 12.9 %collective-permute-start.1 = (f32[128,768]{1,0:T(8,128)S(1)}, f32[128,768]{1,0:T(8,128)S(1)}, u32[]{:S(2)}, u32[]{:S(2)}) collective-permute-start(f32[128,768]{1,0:T(8,128)S(1)} %get-tuple-element.437), channel_id=1, source_target_pairs={{0,8},{8,16},{16,24},{24,32},{32,40},{40,48},{48,56},{56,64},{64,7... | collective-permute-start | bytes 1179656 | tf_op jit(solution)/shard_map/while/body/eval_jaxpr/ppermute | solution.py:11
  274.3 12.9 %collective-permute-start.1 = (f32[128,768]{1,0:T(8,128)S(1)}, f32[128,768]{1,0:T(8,128)S(1)}, u32[]{:S(2)}, u32[]{:S(2)}) collective-permute-start(f32[128,768]{1,0:T(8,128)S(1)} %get-tuple-element.437), channel_id=1, source_target_pairs={{0,8},{8,16},{16,24},{24,32},{32,40},{40,48},{48,56},{56,64},{64,7... | collective-permute-start | bytes 1179656 | tf_op jit(solution)/shard_map/while/body/eval_jaxpr/ppermute | solution.py:11
  297.2 10.4 %collective-permute-start.3 = (f32[128,768]{1,0:T(8,128)S(1)}, f32[128,768]{1,0:T(8,128)S(1)}, u32[]{:S(2)}, u32[]{:S(2)}) collective-permute-start(f32[128,768]{1,0:T(8,128)S(1)} %get-tuple-element.295), channel_id=1, source_target_pairs={{0,192},{8,200},{16,208},{24,216},{32,224},{40,232},{48,240},{56,2... | collective-permute-start | bytes 1179656 | tf_op jit(solution)/shard_map/ppermute | solution.py:11
  (7 other events, 129.9 us)
Sparse Core Ops, SparseCore 0:
  10.4 47.9 all-gather.1
  297.4 72.8 reduce-scatter.1
where the time goes:
time: 381 us; the launch traced here: 380 us
  waiting for transfers between devices  256 us (67%)
  matrix products  70.2 us (18%)
  local copies, waits for them, and re-layouts  15.8 us (4%)
  between operations  15.4 us (4%)
  starting transfers between devices  12.8 us (3%)
  other arithmetic  9.21 us (2%)
    ppermute x34, waiting for transfers between devices, from_behind(): return lax.ppermute(x, axis, [(i, (i + by) % count) for i in range(count)])  165 us
    reduce_scatter x1, waiting for transfers between devices, local(): lax.psum_scatter(smoothing_coefficient * jnp.dot(pair_weights, tile_seque...  61.4 us
    dot_general x17, matrix products, visit(): lax.dot_general(group, block, (((1,), (1,)), ((), ())), preferred_element...  44 us
    all_gather x1, waiting for transfers between devices, local(): lax.all_gather(video_unit.astype(jnp.bfloat16), 'bulk', axis=0, tiled=True)  29.5 us
    dot_general x17, matrix products, contribution(): lax.dot_general(pair_weight, group, (((0,), (0,)), ((), ())), preferred_e...  17.3 us
    dynamic_update_slice x17, local copies, waits for them, and re-layouts, visit(): lax.dynamic_update_slice(tile_sequence, block, (place, jnp.int32(0)))  13.2 us
    ppermute x34, starting transfers between devices, from_behind(): return lax.ppermute(x, axis, [(i, (i + by) % count) for i in range(count)])  12.7 us
    dot_general x1, matrix products, local(): jnp.dot(pair_weights, tile_sequence, preferred_element_type=jnp.float32)  8.9 us
  transfers between devices with their start and end apart: 36, of which 36 were waited for; matrix products, arithmetic and copies ran while one was open for 15% of the time, Pallas kernels for 0%

commit v1 on v0

v1 whole, which is shorter than its diff:
```python
import jax
import jax.numpy as jnp
from jax import lax
from jax.experimental import pallas as pl
from jax.experimental.pallas import tpu as pltpu
from jax.sharding import PartitionSpec as P

EPSILON = 1e-06
NZ, NX = 8, 4
AXES = ("blk", "bulk")
ANY = pl.BlockSpec(memory_space=pl.ANY)
SMEM = pl.BlockSpec(memory_space=pltpu.SMEM)


def move(block, x=0, z=0, y_lo=0, y_hi=0, core=0):
    pairs = []
    for blk in range(4 * NZ):
        for bulk in range(2 * NX):
            to_z = (blk // 4 + z) % NZ
            to_x = (bulk // 2 + x) % NX
            to_blk = to_z * 4 + (((blk // 2) % 2) ^ y_hi) * 2 + ((blk % 2) ^ core)
            to_bulk = to_x * 2 + ((bulk % 2) ^ y_lo)
            pairs.append((blk * 2 * NX + bulk, to_blk * 2 * NX + to_bulk))
    return lax.ppermute(block, AXES, pairs)


def add(*parts):
    total = parts[0].astype(jnp.float32)
    for part in parts[1:]:
        total = total + part.astype(jnp.float32)
    return total.astype(jnp.bfloat16)


def unit_rows(embedding):
    values = embedding.astype(jnp.float32)
    inverse = lax.rsqrt(jnp.sum(values * values, axis=1, keepdims=True) + EPSILON)
    return values * inverse, inverse


def unit_kernel(video_ref, text_ref, video_out, text_out):
    text_out[...] = unit_rows(text_ref[...])[0].astype(jnp.bfloat16)
    video_out[...] = unit_rows(video_ref[...])[0].astype(jnp.bfloat16)


def unit_low(video, text):
    shape = jax.ShapeDtypeStruct(video.shape, jnp.bfloat16)
    return pl.pallas_call(unit_kernel, out_shape=(shape, shape), name="unit_low")(video, text)


def back_kernel(scale_ref, embedding_ref, *refs):
    *parts, out = refs
    rows = out.shape[0]
    total = parts[0][:rows, :].astype(jnp.float32)
    for part in parts[1:]:
        total = total + part[:rows, :].astype(jnp.float32)
    grad_unit = scale_ref[0] * total
    unit, inverse = unit_rows(embedding_ref[...])
    along = jnp.sum(unit * grad_unit, axis=1, keepdims=True)
    out[...] = (grad_unit - unit * along) * inverse


def back_rows(scale, embedding, parts):
    vmem = pl.BlockSpec(memory_space=pltpu.VMEM)
    return pl.pallas_call(
        back_kernel,
        out_shape=jax.ShapeDtypeStruct(embedding.shape, jnp.float32),
        in_specs=[SMEM] + [vmem] * (1 + len(parts)),
        out_specs=vmem,
        name="back_rows",
    )(scale, embedding, *parts)


PAIR, D = 256, 768
N_TEXT, N_VIDEO = 5, 8
LOG2_E = 1.4426950408889634


def weight_kernel(scale_ref, offset_ref, place_ref, *refs):
    texts, videos = refs[:N_TEXT], refs[N_TEXT : N_TEXT + N_VIDEO]
    refs = refs[N_TEXT + N_VIDEO :]
    weights, video_outs, (text, video, grads) = refs[0], refs[1 : 1 + N_VIDEO], refs[1 + N_VIDEO :]
    core, y_hi = place_ref[0], place_ref[1]
    factor = -LOG2_E * scale_ref[0]
    shift = -LOG2_E * offset_ref[0]
    for i, block in enumerate(texts):
        text[pl.ds(i * PAIR, PAIR), :] = block[...]
    for i, block in enumerate(videos):
        video[pl.ds(i * PAIR, PAIR), :] = block[...]
    tile = 2 * PAIR
    steps = N_VIDEO // 2
    row = lax.broadcasted_iota(jnp.int32, (tile, PAIR), 0)
    column = lax.broadcasted_iota(jnp.int32, (tile, PAIR), 1)
    same = (row == column) & (row < PAIR // 2)
    half = lax.broadcasted_iota(jnp.int32, (1, PAIR), 1) < PAIR // 2

    @pl.loop(0, steps)
    def _(step):
        rows = pl.ds(pl.multiple_of(step * tile, tile), tile)
        video_tile = video[rows, :]
        own = step < steps // 2
        below = jnp.where(half, jnp.where(own | (core == 1), 1.0, 0.0), jnp.where(y_hi == 0, 1.0, 0.0))
        above = jnp.where(half, jnp.where(own | (core == 0), 1.0, 0.0), jnp.where(y_hi == 1, 1.0, 0.0))
        for i in range(N_TEXT):
            products = lax.dot_general(
                video_tile,
                text[pl.ds(i * PAIR, PAIR), :],
                (((1,), (1,)), ((), ())),
                preferred_element_type=jnp.float32,
            )
            weight = pl.reciprocal(1.0 + jnp.exp2(products * factor + shift), approx=True)
            if i == 0:
                weight = weight - jnp.where(same, jnp.where(step == 0, 1.0, 0.0), 0.0)
            elif i == 3:
                weight = weight * below
            elif i == 4:
                weight = weight * above
            weights[rows, pl.ds(i * PAIR, PAIR)] = weight.astype(jnp.bfloat16)
        grads[rows, :] = jnp.dot(
            weights[rows, :], text[...], preferred_element_type=jnp.float32
        ).astype(jnp.bfloat16)

    for i, block in enumerate(video_outs):
        block[...] = grads[pl.ds(i * PAIR, PAIR), :]


def text_kernel(weights, *refs):
    videos, outs, video = refs[:N_VIDEO], refs[N_VIDEO : N_VIDEO + N_TEXT], refs[N_VIDEO + N_TEXT]
    for i, block in enumerate(videos):
        video[pl.ds(i * PAIR, PAIR), :] = block[...]
    for i, block in enumerate(outs):
        block[...] = lax.dot_general(
            weights[:, pl.ds(i * PAIR, PAIR)],
            video[...],
            (((0,), (0,)), ((), ())),
            preferred_element_type=jnp.float32,
        ).astype(jnp.bfloat16)


VMEM = pl.BlockSpec(memory_space=pltpu.VMEM)
MIB = 1024 * 1024
FLOPS = 2 * N_VIDEO * N_TEXT * PAIR * PAIR * D
pair_shape = jax.ShapeDtypeStruct((PAIR, D), jnp.bfloat16)


def weights_and_video_grads(scale, offset, place, texts, videos):
    weights, *grads = pl.pallas_call(
        weight_kernel,
        out_shape=[jax.ShapeDtypeStruct((N_VIDEO * PAIR, N_TEXT * PAIR), jnp.bfloat16)]
        + [pair_shape] * N_VIDEO,
        in_specs=[SMEM] * 3 + [VMEM] * (N_TEXT + N_VIDEO),
        out_specs=[VMEM] * (1 + N_VIDEO),
        scratch_shapes=[
            pltpu.VMEM((N_TEXT * PAIR, D), jnp.bfloat16),
            pltpu.VMEM((N_VIDEO * PAIR, D), jnp.bfloat16),
            pltpu.VMEM((N_VIDEO * PAIR, D), jnp.bfloat16),
        ],
        compiler_params=pltpu.CompilerParams(vmem_limit_bytes=28 * MIB),
        cost_estimate=pl.CostEstimate(
            flops=2 * FLOPS, bytes_accessed=0, transcendentals=2 * N_VIDEO * N_TEXT * PAIR * PAIR
        ),
        name="weights_and_video_grads",
    )(scale, offset, place, *texts, *videos)
    return weights, grads


def text_grads(weights, videos):
    return pl.pallas_call(
        text_kernel,
        out_shape=[pair_shape] * N_TEXT,
        in_specs=[VMEM] * (1 + N_VIDEO),
        out_specs=[VMEM] * N_TEXT,
        scratch_shapes=[pltpu.VMEM((N_VIDEO * PAIR, D), jnp.bfloat16)],
        compiler_params=pltpu.CompilerParams(vmem_limit_bytes=20 * MIB),
        cost_estimate=pl.CostEstimate(flops=FLOPS, bytes_accessed=0, transcendentals=0),
        name="text_grads",
    )(weights, *videos)


def local(footage_embeds, caption_embeds, score_scale, score_offset):
    blk = lax.axis_index("blk")
    place = jnp.stack([blk % 2, (blk // 2) % 2]).astype(jnp.int32)
    rows = footage_embeds.shape[0]
    v0, t0 = unit_low(footage_embeds, caption_embeds)

    tp, v1 = move(t0, y_hi=1), move(v0, y_lo=1)
    a1m, a1p = move(t0, z=1), move(t0, z=-1)
    v01 = jnp.concatenate([v0, v1])
    vm, vp = move(v01, x=1), move(v01, x=-1)
    b1m, b1p = move(tp, z=1), move(tp, z=-1)
    t01 = jnp.concatenate([t0, tp])
    tm, tq = jnp.concatenate([a1m, b1m]), jnp.concatenate([a1p, b1p])
    tmm, tqq = move(tm, z=1), move(tq, z=-1)
    v2 = jnp.concatenate([move(vm[:rows], x=1), move(vp[rows:], x=-1)])
    own = [v01, vm, vp, v2]
    videos = own + [move(block, core=1) for block in own]
    texts = [t01, tm, tq, tmm, tqq]

    weights, vg = weights_and_video_grads(score_scale, score_offset, place, texts, videos)
    tg = text_grads(weights, videos)

    g01, gm, gp, g2 = vg[:4]
    r01, rm, rp, r2 = [move(block, core=1) for block in vg[4:]]
    to_m = move(add(g2[:rows], r2[:rows]), x=-1)
    to_p = move(add(g2[rows:], r2[rows:]), x=1)
    none = jnp.zeros_like(to_m)
    gm = add(gm, rm, jnp.concatenate([to_m, none]))
    gp = add(gp, rp, jnp.concatenate([none, to_p]))
    from_p, from_m = move(gp, x=1), move(gm, x=-1)
    last = move(add(g01[rows:], r01[rows:], from_p[rows:], from_m[rows:]), y_lo=1)
    video_parts = [g01, r01, from_p, from_m, last]

    h01, hm, hq, hmm, hqq = tg
    hq = add(hq, move(hqq, z=1))
    hm = add(hm, move(hmm, z=-1))
    up, down = move(hq, z=1), move(hm, z=-1)
    last = move(add(h01[rows:], up[rows:], down[rows:]), y_hi=1)
    text_parts = [h01, up, down, last]

    video_grad = back_rows(score_scale, footage_embeds, video_parts)
    text_grad = back_rows(score_scale, caption_embeds, text_parts)
    return (video_grad, text_grad)


def solution(mesh):
    assert mesh.shape["blk"] == 4 * NZ and mesh.shape["bulk"] == 2 * NX
    return jax.shard_map(
        local,
        mesh=mesh,
        in_specs=(P(AXES, None), P(AXES, None), P(), P()),
        out_specs=(P(AXES, None), P(AXES, None)),
        check_vma=False,
    )
```

time: 381 us -> 107 us (0.28)
  the two profiles are of different devices: /device:TPU:2 before, /device:TPU:16 now
where the time goes in v1:
time: 107 us; the launch traced here: 106 us
  starting transfers between devices  38.6 us (36%)
  waiting for transfers between devices  36 us (34%)
  Pallas kernels  23.5 us (22%)
  local copies, waits for them, and re-layouts  4.18 us (4%)
  between operations  2.21 us (2%)
  other arithmetic  1.81 us (2%)
    ppermute x30, starting transfers between devices, move(): return lax.ppermute(block, AXES, pairs)  38.6 us
    ppermute x30, waiting for transfers between devices, move(): return lax.ppermute(block, AXES, pairs)  36 us
    pallas_call x1, Pallas kernels, weights_and_video_grads(): pl.pallas_call(weight_kernel, out_shape=[jax.ShapeDtypeStruct((N_VIDEO *...  11.3 us
    pallas_call x1, Pallas kernels, text_grads(): pl.pallas_call(text_kernel, out_shape=[pair_shape] * N_TEXT, in_specs=[VM...  5.44 us
    pallas_call x2, Pallas kernels, back_rows(): pl.pallas_call(back_kernel, out_shape=jax.ShapeDtypeStruct(embedding.shap...  4.84 us
    unnamed x28, local copies, waits for them, and re-layouts  4.09 us
  transfers between devices with their start and end apart: 30, of which 12 were waited for; matrix products, arithmetic and copies ran while one was open for 3% of the time, Pallas kernels for 7%

profile of v1, /device:TPU:16, one launch (start us, length us, event | category | flops | bytes accessed | tf_op | source)
XLA Modules:
  0.0 106.2 jit_solution(6358087356238664020)
XLA Ops:
  0.6 1.9 %unit_low.1 = (bf16[128,768]{1,0:T(8,128)(2,1)}, bf16[128,768]{1,0:T(8,128)(2,1)}) custom-call(bf16[128,768]{1,0:T(8,128)(2,1)} %embedding_ref.2, bf16[128,768]{1,0:T(8,128)(2,1)} %embedding_ref.3), custom_call_target="tpu_custom_call" | custom-call | tf_op jit(solution)/shard_map/unit_low/pallas_call | solution.py:47
  2.5 1.3 %collective-permute-start.7 = (bf16[128,768]{1,0:T(8,128)(2,1)}, bf16[128,768]{1,0:T(8,128)(2,1)S(1)}, u32[]{:S(2)}, u32[]{:S(2)}) collective-permute-start(bf16[128,768]{1,0:T(8,128)(2,1)} %get-tuple-element.19), channel_id=1, source_target_pairs={{0,1},{1,0},{2,3},{3,2},{4,5},{5,4},{6,7},{7,6},{8,9},{9,8},{10,11... | collective-permute-start | bytes 589832 | tf_op jit(solution)/shard_map/ppermute | solution.py:24
  3.8 5.9 %collective-permute-start.3 = (bf16[128,768]{1,0:T(8,128)(2,1)}, bf16[128,768]{1,0:T(8,128)(2,1)S(1)}, u32[]{:S(2)}, u32[]{:S(2)}) collective-permute-start(bf16[128,768]{1,0:T(8,128)(2,1)} %get-tuple-element.18), channel_id=1, source_target_pairs={{0,224},{1,225},{2,226},{3,227},{4,228},{5,229},{6,230},{7,231},{8... | collective-permute-start | bytes 589832 | tf_op jit(solution)/shard_map/ppermute | solution.py:24
  10.3 0.9 constant_dynamic-update-slice_fusion.5
  11.3 1.6 %collective-permute-start.8 = (bf16[256,768]{1,0:T(8,128)(2,1)S(1)}, bf16[256,768]{1,0:T(8,128)(2,1)S(1)}, u32[]{:S(2)}, u32[]{:S(2)}) collective-permute-start(bf16[256,768]{1,0:T(8,128)(2,1)S(1)} %constant_dynamic-update-slice_fusion.4.refs_5_.refs_0_), channel_id=1, source_target_pairs={{0,2},{1,3},{2,4},{3,5},{4,6},{5,7},{6,0},{7,1},{8,10},{9,11},{10,... | collective-permute-start | bytes 1179656 | tf_op jit(solution)/shard_map/ppermute | solution.py:24
  12.8 1.2 %collective-permute-start.1 = (bf16[128,768]{1,0:T(8,128)(2,1)}, bf16[128,768]{1,0:T(8,128)(2,1)S(1)}, u32[]{:S(2)}, u32[]{:S(2)}) collective-permute-start(bf16[128,768]{1,0:T(8,128)(2,1)} %get-tuple-element.18), channel_id=1, source_target_pairs={{0,32},{1,33},{2,34},{3,35},{4,36},{5,37},{6,38},{7,39},{8,40},{9,... | collective-permute-start | bytes 589832 | tf_op jit(solution)/shard_map/ppermute | solution.py:24
  14.0 1.7 %collective-permute-start.9 = (bf16[256,768]{1,0:T(8,128)(2,1)S(1)}, bf16[256,768]{1,0:T(8,128)(2,1)S(1)}, u32[]{:S(2)}, u32[]{:S(2)}) collective-permute-start(bf16[256,768]{1,0:T(8,128)(2,1)S(1)} %constant_dynamic-update-slice_fusion.4.refs_5_.refs_0_), channel_id=1, source_target_pairs={{0,6},{1,7},{2,0},{3,1},{4,2},{5,3},{6,4},{7,5},{8,14},{9,15},{10,... | collective-permute-start | bytes 1179656 | tf_op jit(solution)/shard_map/ppermute | solution.py:24
  15.8 1.7 %collective-permute-done = bf16[128,768]{1,0:T(8,128)(2,1)S(1)} collective-permute-done((bf16[128,768]{1,0:T(8,128)(2,1)}, bf16[128,768]{1,0:T(8,128)(2,1)S(1)}, u32[]{:S(2)}, u32[]{:S(2)}) %collective-permute-start) | collective-permute-done | bytes 196640 | tf_op jit(solution)/shard_map/ppermute | solution.py:24
  17.8 4.7 %collective-permute-done.1 = bf16[128,768]{1,0:T(8,128)(2,1)S(1)} collective-permute-done((bf16[128,768]{1,0:T(8,128)(2,1)}, bf16[128,768]{1,0:T(8,128)(2,1)S(1)}, u32[]{:S(2)}, u32[]{:S(2)}) %collective-permute-start.1) | collective-permute-done | bytes 196640 | tf_op jit(solution)/shard_map/ppermute | solution.py:24
  22.5 2.0 %collective-permute-start.4 = (bf16[128,768]{1,0:T(8,128)(2,1)S(1)}, bf16[128,768]{1,0:T(8,128)(2,1)S(1)}, u32[]{:S(2)}, u32[]{:S(2)}) collective-permute-start(bf16[128,768]{1,0:T(8,128)(2,1)S(1)} %collective-permute-done), channel_id=1, source_target_pairs={{0,224},{1,225},{2,226},{3,227},{4,228},{5,229},{6,230},{7,231},{8... | collective-permute-start | bytes 589832 | tf_op jit(solution)/shard_map/ppermute | solution.py:24
  24.6 2.8 %collective-permute-start.10 = (bf16[128,768]{1,0:T(8,128)(2,1)S(1)}, bf16[128,768]{1,0:T(8,128)(2,1)S(1)}, u32[]{:S(2)}, u32[]{:S(2)}) collective-permute-start(bf16[128,768]{1,0:T(8,128)(2,1)S(1)} %slice.52), channel_id=1, source_target_pairs={{0,2},{1,3},{2,4},{3,5},{4,6},{5,7},{6,0},{7,1},{8,10},{9,11},{10,... | collective-permute-start | bytes 589832 | tf_op jit(solution)/shard_map/ppermute | solution.py:24
  28.2 3.3 %collective-permute-start.6 = (bf16[256,768]{1,0:T(8,128)(2,1)S(1)}, bf16[256,768]{1,0:T(8,128)(2,1)}, u32[]{:S(2)}, u32[]{:S(2)}) collective-permute-start(bf16[256,768]{1,0:T(8,128)(2,1)S(1)} %constant_dynamic-update-slice_fusion.2.refs_2_), channel_id=1, source_target_pairs={{0,224},{1,225},{2,226},{3,227},{4,228},{5,229},{6,230},{7,231},{8... | collective-permute-start | bytes 1179656 | tf_op jit(solution)/shard_map/ppermute | solution.py:24
  31.6 1.7 %collective-permute-done.11 = bf16[128,768]{1,0:T(8,128)(2,1)S(1)} collective-permute-done((bf16[128,768]{1,0:T(8,128)(2,1)S(1)}, bf16[128,768]{1,0:T(8,128)(2,1)S(1)}, u32[]{:S(2)}, u32[]{:S(2)}) %collective-permute-start.11) | collective-permute-done | bytes 196640 | tf_op jit(solution)/shard_map/ppermute | solution.py:24
  33.3 0.8 collective-permute-start.15
  35.5 1.0 pad_maximum_fusion.refs_0_
  36.5 1.2 %collective-permute-done.5.refs_3_ = bf16[256,768]{1,0:T(8,128)(2,1)S(1)} collective-permute-done((bf16[256,768]{1,0:T(8,128)(2,1)S(1)}, bf16[256,768]{1,0:T(8,128)(2,1)S(1)}, u32[]{:S(2)}, u32[]{:S(2)}) %collective-permute-start.5) | collective-permute-done | bytes 393248 | tf_op jit(solution)/shard_map/ppermute | solution.py:24
  38.7 1.0 copy-done.3
  39.7 11.3 %weights_and_video_grads.1 = (bf16[2048,1280]{1,0:T(8,128)(2,1)S(1)}, bf16[256,768]{1,0:T(8,128)(2,1)S(1)}, bf16[256,768]{1,0:T(8,128)(2,1)S(1)}, bf16[256,768]{...) custom-call(f32[1]{0:T(128)S(6)} %copy.10.scale_ref, ...), custom_call_target="tpu_custom_call" | custom-call | flops 8053063680 | tf_op jit(solution)/shard_map/weights_and_video_grads/pallas_call | solution.py:146
  51.1 5.4 %text_grads.1 = (bf16[256,768]{1,0:T(8,128)(2,1)S(1)}, bf16[256,768]{1,0:T(8,128)(2,1)S(1)}, bf16[256,768]{1,0:T(8,128)(2,1)S(1)}, bf16[256,768]{1,0:T(8,128)(2,1)S(1)}, bf16[256,768]{1,0:T(8,128)(2,1)S(1)}) custom-call(bf16[2048,1280]{1,0:T(8,128)(2,1)S(1)} %get-tuple-element.28.weights, ...), custom_call_target="tpu_custom_call" | custom-call | flops 4026531840 | tf_op jit(solution)/shard_map/text_grads/pallas_call | solution.py:167
  56.5 2.6 %collective-permute-start.25 = (bf16[256,768]{1,0:T(8,128)(2,1)S(1)}, bf16[256,768]{1,0:T(8,128)(2,1)S(1)}, u32[]{:S(2)}, u32[]{:S(2)}) collective-permute-start(bf16[256,768]{1,0:T(8,128)(2,1)S(1)} %get-tuple-element.31), channel_id=1, source_target_pairs={{0,32},{1,33},{2,34},{3,35},{4,36},{5,37},{6,38},{7,39},{8,40},{9,... | collective-permute-start | bytes 1179656 | tf_op jit(solution)/shard_map/ppermute | solution.py:24
  59.8 1.7 %collective-permute-start.27 = (bf16[256,768]{1,0:T(8,128)(2,1)S(1)}, bf16[256,768]{1,0:T(8,128)(2,1)S(1)}, u32[]{:S(2)}, u32[]{:S(2)}) collective-permute-start(bf16[256,768]{1,0:T(8,128)(2,1)S(1)} %get-tuple-element.33), channel_id=1, source_target_pairs={{0,224},{1,225},{2,226},{3,227},{4,228},{5,229},{6,230},{7,231},{8... | collective-permute-start | bytes 1179656 | tf_op jit(solution)/shard_map/ppermute | solution.py:24
  61.6 8.6 %collective-permute-done.25 = bf16[256,768]{1,0:T(8,128)(2,1)S(1)} collective-permute-done((bf16[256,768]{1,0:T(8,128)(2,1)S(1)}, bf16[256,768]{1,0:T(8,128)(2,1)S(1)}, u32[]{:S(2)}, u32[]{:S(2)}) %collective-permute-start.25) | collective-permute-done | bytes 393248 | tf_op jit(solution)/shard_map/ppermute | solution.py:24
  70.2 1.3 %collective-permute-start.22 = (bf16[128,768]{1,0:T(8,128)(2,1)S(1)}, bf16[128,768]{1,0:T(8,128)(2,1)S(1)}, u32[]{:S(2)}, u32[]{:S(2)}) collective-permute-start(bf16[128,768]{1,0:T(8,128)(2,1)S(1)} %get-tuple-element.34), channel_id=1, source_target_pairs={{0,6},{1,7},{2,0},{3,1},{4,2},{5,3},{6,4},{7,5},{8,14},{9,15},{10,... | collective-permute-start | bytes 589832 | tf_op jit(solution)/shard_map/ppermute | solution.py:24
  72.5 3.0 %collective-permute-start.26 = (bf16[256,768]{1,0:T(8,128)(2,1)S(1)}, bf16[256,768]{1,0:T(8,128)(2,1)S(1)}, u32[]{:S(2)}, u32[]{:S(2)}) collective-permute-start(bf16[256,768]{1,0:T(8,128)(2,1)S(1)} %add_convert_fusion.1), channel_id=1, source_target_pairs={{0,32},{1,33},{2,34},{3,35},{4,36},{5,37},{6,38},{7,39},{8,40},{9,... | collective-permute-start | bytes 1179656 | tf_op jit(solution)/shard_map/ppermute | solution.py:24
  75.5 4.4 %collective-permute-done.19 = bf16[128,768]{1,0:T(8,128)(2,1)S(1)} collective-permute-done((bf16[128,768]{1,0:T(8,128)(2,1)S(1)}, bf16[128,768]{1,0:T(8,128)(2,1)S(1)}, u32[]{:S(2)}, u32[]{:S(2)}) %collective-permute-start.19) | collective-permute-done | bytes 196640 | tf_op jit(solution)/shard_map/ppermute | solution.py:24
  79.9 1.2 %collective-permute-start.28 = (bf16[256,768]{1,0:T(8,128)(2,1)S(1)}, bf16[256,768]{1,0:T(8,128)(2,1)S(1)}, u32[]{:S(2)}, u32[]{:S(2)}) collective-permute-start(bf16[256,768]{1,0:T(8,128)(2,1)S(1)} %add_convert_fusion), channel_id=1, source_target_pairs={{0,224},{1,225},{2,226},{3,227},{4,228},{5,229},{6,230},{7,231},{8... | collective-permute-start | bytes 1179656 | tf_op jit(solution)/shard_map/ppermute | solution.py:24
  81.9 2.9 %collective-permute-start.23 = (bf16[256,768]{1,0:T(8,128)(2,1)S(1)}, bf16[256,768]{1,0:T(8,128)(2,1)S(1)}, u32[]{:S(2)}, u32[]{:S(2)}) collective-permute-start(bf16[256,768]{1,0:T(8,128)(2,1)S(1)} %add_convert_fusion.2), channel_id=1, source_target_pairs={{0,6},{1,7},{2,0},{3,1},{4,2},{5,3},{6,4},{7,5},{8,14},{9,15},{10,... | collective-permute-start | bytes 1179656 | tf_op jit(solution)/shard_map/ppermute | solution.py:24
  84.8 6.3 %collective-permute-done.28.refs_2_ = bf16[256,768]{1,0:T(8,128)(2,1)S(1)} collective-permute-done((bf16[256,768]{1,0:T(8,128)(2,1)S(1)}, bf16[256,768]{1,0:T(8,128)(2,1)S(1)}, u32[]{:S(2)}, u32[]{:S(2)}) %collective-permute-start.28) | collective-permute-done | bytes 393248 | tf_op jit(solution)/shard_map/ppermute | solution.py:24
  91.7 1.9 %collective-permute-start.24 = (bf16[128,768]{1,0:T(8,128)(2,1)S(1)}, bf16[128,768]{1,0:T(8,128)(2,1)S(1)}, u32[]{:S(2)}, u32[]{:S(2)}) collective-permute-start(bf16[128,768]{1,0:T(8,128)(2,1)S(1)} %add_convert_fusion.5), channel_id=1, source_target_pairs={{0,1},{1,0},{2,3},{3,2},{4,5},{5,4},{6,7},{7,6},{8,9},{9,8},{10,11... | collective-permute-start | bytes 589832 | tf_op jit(solution)/shard_map/ppermute | solution.py:24
  93.7 6.3 %collective-permute-done.29.refs_3_ = bf16[128,768]{1,0:T(8,128)(2,1)S(1)} collective-permute-done((bf16[128,768]{1,0:T(8,128)(2,1)S(1)}, bf16[128,768]{1,0:T(8,128)(2,1)S(1)}, u32[]{:S(2)}, u32[]{:S(2)}) %collective-permute-start.29) | collective-permute-done | bytes 196640 | tf_op jit(solution)/shard_map/ppermute | solution.py:24
  100.7 2.4 %back_rows.3 = f32[128,768]{1,0:T(8,128)} custom-call(f32[1]{0:T(128)S(6)} %copy.10.scale_ref, bf16[128,768]{1,0:T(8,128)(2,1)} %embedding_ref.3, bf16[256,768]{1,0:T(8,128)(2,1)} %copy-done.1, bf16[256,768]{1,0:T(8,128)(2,1)} %copy-done.7, bf16[256,768]{1,0:T(8,128)(2,1)} %copy-done.8, bf16[128,768]{1,0:T(8,128)(2,1)} %copy-done.9), custom_call_target="tpu_custom_call" | custom-call | tf_op jit(solution)/shard_map/back_rows/pallas_call | solution.py:64
  103.7 2.5 %back_rows.2 = f32[128,768]{1,0:T(8,128)} custom-call(f32[1]{0:T(128)S(6)} %copy.10.scale_ref, bf16[128,768]{1,0:T(8,128)(2,1)} %embedding_ref.2, bf16[256,768]{1,0:T(8,128)(2,1)} %copy-done, bf16[256,768]{1,0:T(8,128)(2,1)} %copy-done.4, bf16[256,768]{1,0:T(8,128)(2,1)} %copy-done.5, bf16[256,768]{1,0:T(8,128)(2,1)} %copy-done.6, bf16[128,768]{1,0:T(8,128)(2,1)} %copy-done.10), custom_call_target="tpu_custom_call" | custom-call | tf_op jit(solution)/shard_map/back_rows/pallas_call | solution.py:64
  (76 shorter events, 7.4 us)
Async XLA Ops:
  2.5 8.7 %collective-permute-start.7 = (bf16[128,768]{1,0:T(8,128)(2,1)}, bf16[128,768]{1,0:T(8,128)(2,1)S(1)}, u32[]{:S(2)}, u32[]{:S(2)}) collective-permute-start(bf16[128,768]{1,0:T(8,128)(2,1)} %get-tuple-element.19), channel_id=1, source_target_pairs={{0,1},{1,0},{2,3},{3,2},{4,5},{5,4},{6,7},{7,6},{8,9},{9,8},{10,11... | collective-permute-start | bytes 589832 | tf_op jit(solution)/shard_map/ppermute | solution.py:24
  3.8 12.0 %collective-permute-start.3 = (bf16[128,768]{1,0:T(8,128)(2,1)}, bf16[128,768]{1,0:T(8,128)(2,1)S(1)}, u32[]{:S(2)}, u32[]{:S(2)}) collective-permute-start(bf16[128,768]{1,0:T(8,128)(2,1)} %get-tuple-element.18), channel_id=1, source_target_pairs={{0,224},{1,225},{2,226},{3,227},{4,228},{5,229},{6,230},{7,231},{8... | collective-permute-start | bytes 589832 | tf_op jit(solution)/shard_map/ppermute | solution.py:24
  9.7 7.8 %collective-permute-start = (bf16[128,768]{1,0:T(8,128)(2,1)}, bf16[128,768]{1,0:T(8,128)(2,1)S(1)}, u32[]{:S(2)}, u32[]{:S(2)}) collective-permute-start(bf16[128,768]{1,0:T(8,128)(2,1)} %get-tuple-element.18), channel_id=1, source_target_pairs={{0,16},{1,17},{2,18},{3,19},{4,20},{5,21},{6,22},{7,23},{8,24},{9,... | collective-permute-start | bytes 589832 | tf_op jit(solution)/shard_map/ppermute | solution.py:24
  11.3 13.3 %collective-permute-start.8 = (bf16[256,768]{1,0:T(8,128)(2,1)S(1)}, bf16[256,768]{1,0:T(8,128)(2,1)S(1)}, u32[]{:S(2)}, u32[]{:S(2)}) collective-permute-start(bf16[256,768]{1,0:T(8,128)(2,1)S(1)} %constant_dynamic-update-slice_fusion.4.refs_5_.refs_0_), channel_id=1, source_target_pairs={{0,2},{1,3},{2,4},{3,5},{4,6},{5,7},{6,0},{7,1},{8,10},{9,11},{10,... | collective-permute-start | bytes 1179656 | tf_op jit(solution)/shard_map/ppermute | solution.py:24
  12.8 9.7 %collective-permute-start.1 = (bf16[128,768]{1,0:T(8,128)(2,1)}, bf16[128,768]{1,0:T(8,128)(2,1)S(1)}, u32[]{:S(2)}, u32[]{:S(2)}) collective-permute-start(bf16[128,768]{1,0:T(8,128)(2,1)} %get-tuple-element.18), channel_id=1, source_target_pairs={{0,32},{1,33},{2,34},{3,35},{4,36},{5,37},{6,38},{7,39},{8,40},{9,... | collective-permute-start | bytes 589832 | tf_op jit(solution)/shard_map/ppermute | solution.py:24
  14.0 13.5 %collective-permute-start.9 = (bf16[256,768]{1,0:T(8,128)(2,1)S(1)}, bf16[256,768]{1,0:T(8,128)(2,1)S(1)}, u32[]{:S(2)}, u32[]{:S(2)}) collective-permute-start(bf16[256,768]{1,0:T(8,128)(2,1)S(1)} %constant_dynamic-update-slice_fusion.4.refs_5_.refs_0_), channel_id=1, source_target_pairs={{0,6},{1,7},{2,0},{3,1},{4,2},{5,3},{6,4},{7,5},{8,14},{9,15},{10,... | collective-permute-start | bytes 1179656 | tf_op jit(solution)/shard_map/ppermute | solution.py:24
  15.8 17.6 %collective-permute-start.12 = (bf16[256,768]{1,0:T(8,128)(2,1)S(1)}, bf16[256,768]{1,0:T(8,128)(2,1)S(1)}, u32[]{:S(2)}, u32[]{:S(2)}) collective-permute-start(bf16[256,768]{1,0:T(8,128)(2,1)S(1)} %constant_dynamic-update-slice_fusion.4.refs_5_.refs_0_), channel_id=1, source_target_pairs={{0,8},{1,9},{2,10},{3,11},{4,12},{5,13},{6,14},{7,15},{8,0},{9,1},... | collective-permute-start | bytes 1179656 | tf_op jit(solution)/shard_map/ppermute | solution.py:24
  17.5 10.0 %collective-permute-start.2 = (bf16[128,768]{1,0:T(8,128)(2,1)S(1)}, bf16[128,768]{1,0:T(8,128)(2,1)S(1)}, u32[]{:S(2)}, u32[]{:S(2)}) collective-permute-start(bf16[128,768]{1,0:T(8,128)(2,1)S(1)} %collective-permute-done), channel_id=1, source_target_pairs={{0,32},{1,33},{2,34},{3,35},{4,36},{5,37},{6,38},{7,39},{8,40},{9,... | collective-permute-start | bytes 589832 | tf_op jit(solution)/shard_map/ppermute | solution.py:24
  22.5 5.7 %collective-permute-start.4 = (bf16[128,768]{1,0:T(8,128)(2,1)S(1)}, bf16[128,768]{1,0:T(8,128)(2,1)S(1)}, u32[]{:S(2)}, u32[]{:S(2)}) collective-permute-start(bf16[128,768]{1,0:T(8,128)(2,1)S(1)} %collective-permute-done), channel_id=1, source_target_pairs={{0,224},{1,225},{2,226},{3,227},{4,228},{5,229},{6,230},{7,231},{8... | collective-permute-start | bytes 589832 | tf_op jit(solution)/shard_map/ppermute | solution.py:24
  24.6 7.0 %collective-permute-start.10 = (bf16[128,768]{1,0:T(8,128)(2,1)S(1)}, bf16[128,768]{1,0:T(8,128)(2,1)S(1)}, u32[]{:S(2)}, u32[]{:S(2)}) collective-permute-start(bf16[128,768]{1,0:T(8,128)(2,1)S(1)} %slice.52), channel_id=1, source_target_pairs={{0,2},{1,3},{2,4},{3,5},{4,6},{5,7},{6,0},{7,1},{8,10},{9,11},{10,... | collective-permute-start | bytes 589832 | tf_op jit(solution)/shard_map/ppermute | solution.py:24
  27.4 10.4 %collective-permute-start.5 = (bf16[256,768]{1,0:T(8,128)(2,1)S(1)}, bf16[256,768]{1,0:T(8,128)(2,1)S(1)}, u32[]{:S(2)}, u32[]{:S(2)}) collective-permute-start(bf16[256,768]{1,0:T(8,128)(2,1)S(1)} %constant_dynamic-update-slice_fusion.refs_1_), channel_id=1, source_target_pairs={{0,32},{1,33},{2,34},{3,35},{4,36},{5,37},{6,38},{7,39},{8,40},{9,... | collective-permute-start | bytes 1179656 | tf_op jit(solution)/shard_map/ppermute | solution.py:24
  27.6 5.7 %collective-permute-start.11 = (bf16[128,768]{1,0:T(8,128)(2,1)S(1)}, bf16[128,768]{1,0:T(8,128)(2,1)S(1)}, u32[]{:S(2)}, u32[]{:S(2)}) collective-permute-start(bf16[128,768]{1,0:T(8,128)(2,1)S(1)} %slice.53), channel_id=1, source_target_pairs={{0,6},{1,7},{2,0},{3,1},{4,2},{5,3},{6,4},{7,5},{8,14},{9,15},{10,... | collective-permute-start | bytes 589832 | tf_op jit(solution)/shard_map/ppermute | solution.py:24
  28.2 9.7 %collective-permute-start.6 = (bf16[256,768]{1,0:T(8,128)(2,1)S(1)}, bf16[256,768]{1,0:T(8,128)(2,1)}, u32[]{:S(2)}, u32[]{:S(2)}) collective-permute-start(bf16[256,768]{1,0:T(8,128)(2,1)S(1)} %constant_dynamic-update-slice_fusion.2.refs_2_), channel_id=1, source_target_pairs={{0,224},{1,225},{2,226},{3,227},{4,228},{5,229},{6,230},{7,231},{8... | collective-permute-start | bytes 1179656 | tf_op jit(solution)/shard_map/ppermute | solution.py:24
  31.5 6.4 %collective-permute-start.14 = (bf16[256,768]{1,0:T(8,128)(2,1)S(1)}, bf16[256,768]{1,0:T(8,128)(2,1)S(1)}, u32[]{:S(2)}, u32[]{:S(2)}) collective-permute-start(bf16[256,768]{1,0:T(8,128)(2,1)S(1)} %collective-permute-done.9.refs_7_.refs_2_), channel_id=1, source_target_pairs={{0,8},{1,9},{2,10},{3,11},{4,12},{5,13},{6,14},{7,15},{8,0},{9,1},... | collective-permute-start | bytes 1179656 | tf_op jit(solution)/shard_map/ppermute | solution.py:24
  33.3 5.4 %collective-permute-start.13 = (bf16[256,768]{1,0:T(8,128)(2,1)S(1)}, bf16[256,768]{1,0:T(8,128)(2,1)}, u32[]{:S(2)}, u32[]{:S(2)}) collective-permute-start(bf16[256,768]{1,0:T(8,128)(2,1)S(1)} %collective-permute-done.8.refs_6_.refs_1_), channel_id=1, source_target_pairs={{0,8},{1,9},{2,10},{3,11},{4,12},{5,13},{6,14},{7,15},{8,0},{9,1},... | collective-permute-start | bytes 1179656 | tf_op jit(solution)/shard_map/ppermute | solution.py:24
  33.3 5.3 %collective-permute-start.15 = (bf16[256,768]{1,0:T(8,128)(2,1)S(1)}, bf16[256,768]{1,0:T(8,128)(2,1)}, u32[]{:S(2)}, u32[]{:S(2)}) collective-permute-start(bf16[256,768]{1,0:T(8,128)(2,1)S(1)} %constant_dynamic-update-slice_fusion.6.refs_8_.refs_3_), channel_id=1, source_target_pairs={{0,8},{1,9},{2,10},{3,11},{4,12},{5,13},{6,14},{7,15},{8,0},{9,1},... | collective-permute-start | bytes 1179656 | tf_op jit(solution)/shard_map/ppermute | solution.py:24
  51.0 40.7 %copy-start = (bf16[256,768]{1,0:T(8,128)(2,1)}, bf16[256,768]{1,0:T(8,128)(2,1)S(1)}, u32[]{:S(2)}) copy-start(bf16[256,768]{1,0:T(8,128)(2,1)S(1)} %get-tuple-element.20.refs_0_) | copy-start | bytes 1179652
  51.0 8.8 %collective-permute-start.18 = (bf16[256,768]{1,0:T(8,128)(2,1)S(1)}, bf16[256,768]{1,0:T(8,128)(2,1)S(1)}, u32[]{:S(2)}, u32[]{:S(2)}) collective-permute-start(bf16[256,768]{1,0:T(8,128)(2,1)S(1)} %get-tuple-element.25), channel_id=1, source_target_pairs={{0,8},{1,9},{2,10},{3,11},{4,12},{5,13},{6,14},{7,15},{8,0},{9,1},... | collective-permute-start | bytes 1179656 | tf_op jit(solution)/shard_map/ppermute | solution.py:24
  56.5 43.5 %copy-start.1 = (bf16[256,768]{1,0:T(8,128)(2,1)}, bf16[256,768]{1,0:T(8,128)(2,1)S(1)}, u32[]{:S(2)}) copy-start(bf16[256,768]{1,0:T(8,128)(2,1)S(1)} %get-tuple-element.29.refs_0_) | copy-start | bytes 1179652
  56.5 13.6 %collective-permute-start.25 = (bf16[256,768]{1,0:T(8,128)(2,1)S(1)}, bf16[256,768]{1,0:T(8,128)(2,1)S(1)}, u32[]{:S(2)}, u32[]{:S(2)}) collective-permute-start(bf16[256,768]{1,0:T(8,128)(2,1)S(1)} %get-tuple-element.31), channel_id=1, source_target_pairs={{0,32},{1,33},{2,34},{3,35},{4,36},{5,37},{6,38},{7,39},{8,40},{9,... | collective-permute-start | bytes 1179656 | tf_op jit(solution)/shard_map/ppermute | solution.py:24
  59.1 32.2 %collective-permute-start.16 = (bf16[256,768]{1,0:T(8,128)(2,1)S(1)}, bf16[256,768]{1,0:T(8,128)(2,1)S(1)}, u32[]{:S(2)}, u32[]{:S(2)}) collective-permute-start(bf16[256,768]{1,0:T(8,128)(2,1)S(1)} %get-tuple-element.21), channel_id=1, source_target_pairs={{0,8},{1,9},{2,10},{3,11},{4,12},{5,13},{6,14},{7,15},{8,0},{9,1},... | collective-permute-start | bytes 1179656 | tf_op jit(solution)/shard_map/ppermute | solution.py:24
  59.3 13.2 %collective-permute-start.17 = (bf16[256,768]{1,0:T(8,128)(2,1)S(1)}, bf16[256,768]{1,0:T(8,128)(2,1)S(1)}, u32[]{:S(2)}, u32[]{:S(2)}) collective-permute-start(bf16[256,768]{1,0:T(8,128)(2,1)S(1)} %get-tuple-element.23), channel_id=1, source_target_pairs={{0,8},{1,9},{2,10},{3,11},{4,12},{5,13},{6,14},{7,15},{8,0},{9,1},... | collective-permute-start | bytes 1179656 | tf_op jit(solution)/shard_map/ppermute | solution.py:24
  59.6 21.6 %collective-permute-start.21 = (bf16[256,768]{1,0:T(8,128)(2,1)S(1)}, bf16[256,768]{1,0:T(8,128)(2,1)S(1)}, u32[]{:S(2)}, u32[]{:S(2)}) collective-permute-start(bf16[256,768]{1,0:T(8,128)(2,1)S(1)} %get-tuple-element.27), channel_id=1, source_target_pairs={{0,8},{1,9},{2,10},{3,11},{4,12},{5,13},{6,14},{7,15},{8,0},{9,1},... | collective-permute-start | bytes 1179656 | tf_op jit(solution)/shard_map/ppermute | solution.py:24
  59.8 12.2 %collective-permute-start.27 = (bf16[256,768]{1,0:T(8,128)(2,1)S(1)}, bf16[256,768]{1,0:T(8,128)(2,1)S(1)}, u32[]{:S(2)}, u32[]{:S(2)}) collective-permute-start(bf16[256,768]{1,0:T(8,128)(2,1)S(1)} %get-tuple-element.33), channel_id=1, source_target_pairs={{0,224},{1,225},{2,226},{3,227},{4,228},{5,229},{6,230},{7,231},{8... | collective-permute-start | bytes 1179656 | tf_op jit(solution)/shard_map/ppermute | solution.py:24
  70.2 11.6 %collective-permute-start.22 = (bf16[128,768]{1,0:T(8,128)(2,1)S(1)}, bf16[128,768]{1,0:T(8,128)(2,1)S(1)}, u32[]{:S(2)}, u32[]{:S(2)}) collective-permute-start(bf16[128,768]{1,0:T(8,128)(2,1)S(1)} %get-tuple-element.34), channel_id=1, source_target_pairs={{0,6},{1,7},{2,0},{3,1},{4,2},{5,3},{6,4},{7,5},{8,14},{9,15},{10,... | collective-permute-start | bytes 589832 | tf_op jit(solution)/shard_map/ppermute | solution.py:24
  72.0 7.9 %collective-permute-start.19 = (bf16[128,768]{1,0:T(8,128)(2,1)S(1)}, bf16[128,768]{1,0:T(8,128)(2,1)S(1)}, u32[]{:S(2)}, u32[]{:S(2)}) collective-permute-start(bf16[128,768]{1,0:T(8,128)(2,1)S(1)} %get-tuple-element.35), channel_id=1, source_target_pairs={{0,2},{1,3},{2,4},{3,5},{4,6},{5,7},{6,0},{7,1},{8,10},{9,11},{10,... | collective-permute-start | bytes 589832 | tf_op jit(solution)/shard_map/ppermute | solution.py:24
  72.5 12.3 %collective-permute-start.26 = (bf16[256,768]{1,0:T(8,128)(2,1)S(1)}, bf16[256,768]{1,0:T(8,128)(2,1)S(1)}, u32[]{:S(2)}, u32[]{:S(2)}) collective-permute-start(bf16[256,768]{1,0:T(8,128)(2,1)S(1)} %add_convert_fusion.1), channel_id=1, source_target_pairs={{0,32},{1,33},{2,34},{3,35},{4,36},{5,37},{6,38},{7,39},{8,40},{9,... | collective-permute-start | bytes 1179656 | tf_op jit(solution)/shard_map/ppermute | solution.py:24
  79.9 11.2 %collective-permute-start.28 = (bf16[256,768]{1,0:T(8,128)(2,1)S(1)}, bf16[256,768]{1,0:T(8,128)(2,1)S(1)}, u32[]{:S(2)}, u32[]{:S(2)}) collective-permute-start(bf16[256,768]{1,0:T(8,128)(2,1)S(1)} %add_convert_fusion), channel_id=1, source_target_pairs={{0,224},{1,225},{2,226},{3,227},{4,228},{5,229},{6,230},{7,231},{8... | collective-permute-start | bytes 1179656 | tf_op jit(solution)/shard_map/ppermute | solution.py:24
  81.2 10.4 %collective-permute-start.20 = (bf16[256,768]{1,0:T(8,128)(2,1)S(1)}, bf16[256,768]{1,0:T(8,128)(2,1)S(1)}, u32[]{:S(2)}, u32[]{:S(2)}) collective-permute-start(bf16[256,768]{1,0:T(8,128)(2,1)S(1)} %add_convert_fusion.3), channel_id=1, source_target_pairs={{0,2},{1,3},{2,4},{3,5},{4,6},{5,7},{6,0},{7,1},{8,10},{9,11},{10,... | collective-permute-start | bytes 1179656 | tf_op jit(solution)/shard_map/ppermute | solution.py:24
  81.9 9.8 %collective-permute-start.23 = (bf16[256,768]{1,0:T(8,128)(2,1)S(1)}, bf16[256,768]{1,0:T(8,128)(2,1)S(1)}, u32[]{:S(2)}, u32[]{:S(2)}) collective-permute-start(bf16[256,768]{1,0:T(8,128)(2,1)S(1)} %add_convert_fusion.2), channel_id=1, source_target_pairs={{0,6},{1,7},{2,0},{3,1},{4,2},{5,3},{6,4},{7,5},{8,14},{9,15},{10,... | collective-permute-start | bytes 1179656 | tf_op jit(solution)/shard_map/ppermute | solution.py:24
  91.1 8.8 %collective-permute-start.29 = (bf16[128,768]{1,0:T(8,128)(2,1)S(1)}, bf16[128,768]{1,0:T(8,128)(2,1)S(1)}, u32[]{:S(2)}, u32[]{:S(2)}) collective-permute-start(bf16[128,768]{1,0:T(8,128)(2,1)S(1)} %add_convert_fusion.4), channel_id=1, source_target_pairs={{0,16},{1,17},{2,18},{3,19},{4,20},{5,21},{6,22},{7,23},{8,24},{9,... | collective-permute-start | bytes 589832 | tf_op jit(solution)/shard_map/ppermute | solution.py:24
  91.7 11.3 %collective-permute-start.24 = (bf16[128,768]{1,0:T(8,128)(2,1)S(1)}, bf16[128,768]{1,0:T(8,128)(2,1)S(1)}, u32[]{:S(2)}, u32[]{:S(2)}) collective-permute-start(bf16[128,768]{1,0:T(8,128)(2,1)S(1)} %add_convert_fusion.5), channel_id=1, source_target_pairs={{0,1},{1,0},{2,3},{3,2},{4,5},{5,4},{6,7},{7,6},{8,9},{9,8},{10,11... | collective-permute-start | bytes 589832 | tf_op jit(solution)/shard_map/ppermute | solution.py:24
  (10 other events, 77.8 us)

commit v2 on v1

v2 whole, which is shorter than its diff:
```python
import functools

import jax
import jax.numpy as jnp
from jax import lax
from jax.experimental import pallas as pl
from jax.experimental.pallas import tpu as pltpu
from jax.sharding import PartitionSpec as P

EPSILON = 1e-06
NZ, NX = 8, 4
AXES = ("blk", "bulk")
ANY = pl.BlockSpec(memory_space=pl.ANY)
SMEM = pl.BlockSpec(memory_space=pltpu.SMEM)


def move(block, x=0, z=0, y_lo=0, y_hi=0, core=0):
    pairs = []
    for blk in range(4 * NZ):
        for bulk in range(2 * NX):
            to_z = (blk // 4 + z) % NZ
            to_x = (bulk // 2 + x) % NX
            to_blk = to_z * 4 + (((blk // 2) % 2) ^ y_hi) * 2 + ((blk % 2) ^ core)
            to_bulk = to_x * 2 + ((bulk % 2) ^ y_lo)
            pairs.append((blk * 2 * NX + bulk, to_blk * 2 * NX + to_bulk))
    return lax.ppermute(block, AXES, pairs)


def add(*parts):
    total = parts[0].astype(jnp.float32)
    for part in parts[1:]:
        total = total + part.astype(jnp.float32)
    return total.astype(jnp.bfloat16)


def unit_rows(embedding):
    values = embedding.astype(jnp.float32)
    inverse = lax.rsqrt(jnp.sum(values * values, axis=1, keepdims=True) + EPSILON)
    return values * inverse, inverse


def unit_kernel(video_ref, text_ref, video_out, text_out):
    text_out[...] = unit_rows(text_ref[...])[0].astype(jnp.bfloat16)
    video_out[...] = unit_rows(video_ref[...])[0].astype(jnp.bfloat16)


def unit_low(video, text):
    shape = jax.ShapeDtypeStruct(video.shape, jnp.bfloat16)
    return pl.pallas_call(
        unit_kernel,
        out_shape=(shape, shape),
        compiler_params=pltpu.CompilerParams(vmem_limit_bytes=4 * 1024 * 1024),
        name="unit_low",
    )(video, text)


def back_kernel(scale_ref, embedding_ref, *refs):
    *parts, out = refs
    rows = out.shape[0]
    total = parts[0][:rows, :].astype(jnp.float32)
    for part in parts[1:]:
        total = total + part[:rows, :].astype(jnp.float32)
    grad_unit = scale_ref[0] * total
    unit, inverse = unit_rows(embedding_ref[...])
    along = jnp.sum(unit * grad_unit, axis=1, keepdims=True)
    out[...] = (grad_unit - unit * along) * inverse


def back_rows(scale, embedding, parts):
    vmem = pl.BlockSpec(memory_space=pltpu.VMEM)
    return pl.pallas_call(
        back_kernel,
        out_shape=jax.ShapeDtypeStruct(embedding.shape, jnp.float32),
        in_specs=[SMEM] + [vmem] * (1 + len(parts)),
        out_specs=vmem,
        compiler_params=pltpu.CompilerParams(vmem_limit_bytes=8 * 1024 * 1024),
        name="back_rows",
    )(scale, embedding, *parts)


PAIR, D = 256, 768
N_TEXT, N_VIDEO = 5, 8
LOG2_E = 1.4426950408889634


def put(target, blocks):
    place = 0
    for block in blocks:
        target[pl.ds(place, block.shape[0]), :] = block[...]
        place += block.shape[0]


def weigh(scale_ref, offset_ref, place_ref, weights, text, video, has_own_text):
    core, y_hi = place_ref[0], place_ref[1]
    factor = -LOG2_E * scale_ref[0]
    shift = -LOG2_E * offset_ref[0]
    tile = video.shape[0] // 2
    row = lax.broadcasted_iota(jnp.int32, (tile, PAIR), 0)
    column = lax.broadcasted_iota(jnp.int32, (tile, PAIR), 1)
    same = (row == column) & (row < PAIR // 2)
    half = lax.broadcasted_iota(jnp.int32, (1, PAIR), 1) < PAIR // 2

    @pl.loop(0, 2)
    def _(step):
        rows = pl.ds(pl.multiple_of(step * tile, tile), tile)
        video_tile = video[rows, :]
        own = step == 0
        below = jnp.where(half, jnp.where(own | (core == 1), 1.0, 0.0), jnp.where(y_hi == 0, 1.0, 0.0))
        above = jnp.where(half, jnp.where(own | (core == 0), 1.0, 0.0), jnp.where(y_hi == 1, 1.0, 0.0))
        for i in range(N_TEXT):
            products = lax.dot_general(
                video_tile,
                text[pl.ds(i * PAIR, PAIR), :],
                (((1,), (1,)), ((), ())),
                preferred_element_type=jnp.float32,
            )
            weight = pl.reciprocal(1.0 + jnp.exp2(products * factor + shift), approx=True)
            if i == 0 and has_own_text:
                weight = weight - jnp.where(same, jnp.where(own, 1.0, 0.0), 0.0)
            elif i == 3:
                weight = weight * below
            elif i == 4:
                weight = weight * above
            weights[rows, pl.ds(i * PAIR, PAIR)] = weight.astype(jnp.bfloat16)


def near_kernel(scale_ref, offset_ref, place_ref, *refs):
    texts, videos = refs[:9], refs[9:-3]
    weights, text, video = refs[-3:]
    put(text, texts[:7] + texts[8:] + texts[7:])
    put(video, videos)
    weigh(scale_ref, offset_ref, place_ref, weights, text, video, True)


def far_kernel(scale_ref, offset_ref, place_ref, text, *refs):
    *videos, weights, video = refs
    put(video, videos)
    weigh(scale_ref, offset_ref, place_ref, weights, text, video, False)


def text_kernel(first, near_weights, near_video, far_weights, far_video, *outs):
    for i, block in enumerate(outs):
        columns = pl.ds((first + i) * PAIR, PAIR)
        contract = (((0,), (0,)), ((), ()))
        near = lax.dot_general(
            near_weights[:, columns], near_video[...], contract, preferred_element_type=jnp.float32
        )
        far = lax.dot_general(
            far_weights[:, columns], far_video[...], contract, preferred_element_type=jnp.float32
        )
        block[...] = (near + far).astype(jnp.bfloat16)


def video_kernel(half, near_weights, far_weights, text, out):
    near_rows, far_rows = near_weights.shape[0] // 2, far_weights.shape[0] // 2
    for weights, rows, place in ((near_weights, near_rows, 0), (far_weights, far_rows, near_rows)):
        out[pl.ds(place, rows), :] = jnp.dot(
            weights[pl.ds(half * rows, rows), :], text[...], preferred_element_type=jnp.float32
        ).astype(jnp.bfloat16)


VMEM = pl.BlockSpec(memory_space=pltpu.VMEM)
MIB = 1024 * 1024
FLOPS = 2 * N_VIDEO * N_TEXT * PAIR * PAIR * D


def low(rows, columns=D):
    return jax.ShapeDtypeStruct((rows, columns), jnp.bfloat16)


def cost(flops, transcendentals=0):
    return pl.CostEstimate(flops=flops, bytes_accessed=0, transcendentals=transcendentals)


def near_weights(scalars, texts, videos):
    rows = sum(block.shape[0] for block in videos)
    return pl.pallas_call(
        near_kernel,
        out_shape=[low(rows, N_TEXT * PAIR), low(N_TEXT * PAIR), low(rows)],
        in_specs=[SMEM] * 3 + [VMEM] * (9 + len(videos)),
        out_specs=[VMEM] * 3,
        compiler_params=pltpu.CompilerParams(vmem_limit_bytes=20 * MIB),
        cost_estimate=cost(FLOPS * 3 // 4, 2 * rows * N_TEXT * PAIR),
        name="near_weights",
    )(*scalars, *texts, *videos)


def far_weights(scalars, text, videos):
    rows = sum(block.shape[0] for block in videos)
    return pl.pallas_call(
        far_kernel,
        out_shape=[low(rows, N_TEXT * PAIR), low(rows)],
        in_specs=[SMEM] * 3 + [VMEM] * (1 + len(videos)),
        out_specs=[VMEM] * 2,
        compiler_params=pltpu.CompilerParams(vmem_limit_bytes=12 * MIB),
        cost_estimate=cost(FLOPS // 4, 2 * rows * N_TEXT * PAIR),
        name="far_weights",
    )(*scalars, text, *videos)


def text_grads(near, near_video, far, far_video, first, count):
    return pl.pallas_call(
        functools.partial(text_kernel, first),
        out_shape=[low(PAIR)] * count,
        in_specs=[VMEM] * 4,
        out_specs=[VMEM] * count,
        compiler_params=pltpu.CompilerParams(vmem_limit_bytes=16 * MIB),
        cost_estimate=cost(FLOPS * count // N_TEXT),
        name="text_grads",
    )(near, near_video, far, far_video)


def video_grads(near, far, text, half):
    return pl.pallas_call(
        functools.partial(video_kernel, half),
        out_shape=low(N_VIDEO * PAIR // 2),
        in_specs=[VMEM] * 3,
        out_specs=VMEM,
        compiler_params=pltpu.CompilerParams(vmem_limit_bytes=16 * MIB),
        cost_estimate=cost(FLOPS // 2),
        name="video_grads",
    )(near, far, text)


def local(footage_embeds, caption_embeds, score_scale, score_offset):
    blk = lax.axis_index("blk")
    core, y_hi = blk % 2, (blk // 2) % 2
    scalars = score_scale, score_offset, jnp.stack([core, y_hi]).astype(jnp.int32)
    rows = footage_embeds.shape[0]
    v0, t0 = unit_low(footage_embeds, caption_embeds)

    tp, v1 = move(t0, y_hi=1), move(v0, y_lo=1)
    a1m, a1p = move(t0, z=1), move(t0, z=-1)
    v1, tp, a1m, a1p = lax.optimization_barrier((v1, tp, a1m, a1p))
    v01 = jnp.concatenate([v0, v1])
    vm, vp = move(v01, x=1), move(v01, x=-1)
    a2m, a2p = move(a1m, z=1), move(a1p, z=-1)
    b1m, b1p = move(tp, z=1), move(tp, z=-1)
    vm, vp, b1m, b1p, a2m, a2p = lax.optimization_barrier((vm, vp, b1m, b1p, a2m, a2p))
    b2 = move_by_y_hi(jnp.where(y_hi == 1, b1p, b1m))
    v2 = jnp.concatenate([move(vm[:rows], x=1), move(vp[rows:], x=-1)])
    own = jnp.concatenate([v01, vm, vp])
    videos = [own, move(own, core=1)]
    texts = [t0, tp, a1m, b1m, a1p, b1p, a2m, a2p, b2]

    near, text, near_video = near_weights(scalars, texts, videos)
    far, far_video = far_weights(scalars, text, [v2, move(v2, core=1)])

    hmm, hqq = text_grads(near, near_video, far, far_video, 3, 2)
    near, hmm, hqq = lax.optimization_barrier((near, hmm, hqq))
    sibling = video_grads(near, far, text, 1)
    near, sibling = lax.optimization_barrier((near, sibling))
    own = video_grads(near, far, text, 0)
    near, own = lax.optimization_barrier((near, own))
    h01, hm, hq = text_grads(near, near_video, far, far_video, 0, 3)
    hmm, hqq, other, own, h01, hm, hq = lax.optimization_barrier(
        (move(hmm, z=-1), move(hqq, z=1), move(sibling, core=1), own, h01, hm, hq)
    )

    up, down = move(add(hq, hqq), z=1), move(add(hm, hmm), z=-1)
    last = move(add(h01[rows:], up[rows:], down[rows:]), y_hi=1)
    text_parts = [h01, up, down, last]

    def total(index, *more):
        place = slice(index * rows, (index + 1) * rows)
        return add(own[place], other[place], *more)

    to_m, to_p = lax.optimization_barrier((move(total(6), x=-1), move(total(7), x=1)))
    gm = jnp.concatenate([total(2, to_m), total(3)])
    gp = jnp.concatenate([total(4), total(5, to_p)])
    from_p, from_m = move(gp, x=1), move(gm, x=-1)
    last = move(total(1, from_p[rows:], from_m[rows:]), y_lo=1)
    video_parts = [own, other, from_p, from_m, last]

    video_grad = back_rows(score_scale, footage_embeds, video_parts)
    text_grad = back_rows(score_scale, caption_embeds, text_parts)
    return (video_grad, text_grad)


def move_by_y_hi(block):
    pairs = []
    for blk in range(4 * NZ):
        step = 1 if (blk // 2) % 2 == 0 else -1
        to_blk = ((blk // 4 + step) % NZ) * 4 + blk % 4
        for bulk in range(2 * NX):
            pairs.append((blk * 2 * NX + bulk, to_blk * 2 * NX + bulk))
    return lax.ppermute(block, AXES, pairs)


def solution(mesh):
    assert mesh.shape["blk"] == 4 * NZ and mesh.shape["bulk"] == 2 * NX
    return jax.shard_map(
        local,
        mesh=mesh,
        in_specs=(P(AXES, None), P(AXES, None), P(), P()),
        out_specs=(P(AXES, None), P(AXES, None)),
        check_vma=False,
    )
```

time: 107 us -> 100 us (0.935)
  the two profiles are of different devices: /device:TPU:16 before, /device:TPU:2 now
where the time goes in v2:
time: 100 us; the launch traced here: 99.8 us
  waiting for transfers between devices  40.3 us (40%)
  starting transfers between devices  32.9 us (33%)
  Pallas kernels  18.1 us (18%)
  local copies, waits for them, and re-layouts  5.4 us (5%)
  between operations  2.2 us (2%)
    ppermute x25, waiting for transfers between devices, move(): return lax.ppermute(block, AXES, pairs)  40.3 us
    ppermute x25, starting transfers between devices, move(): return lax.ppermute(block, AXES, pairs)  32.8 us
    pallas_call x1, Pallas kernels, near_weights(): pl.pallas_call(near_kernel, out_shape=[low(rows, N_TEXT * PAIR), low(N_TE...  4.93 us
    pallas_call x2, Pallas kernels, text_grads(): pl.pallas_call(functools.partial(text_kernel, first), out_shape=[low(PAIR...  4.48 us
    pallas_call x2, Pallas kernels, video_grads(): pl.pallas_call(functools.partial(video_kernel, half), out_shape=low(N_VID...  4.39 us
    unnamed x24, local copies, waits for them, and re-layouts  3.43 us
    pallas_call x1, Pallas kernels, far_weights(): pl.pallas_call(far_kernel, out_shape=[low(rows, N_TEXT * PAIR), low(rows)...  2.12 us
    pallas_call x2, Pallas kernels, back_rows(): pl.pallas_call(back_kernel, out_shape=jax.ShapeDtypeStruct(embedding.shap...  2.05 us
  transfers between devices with their start and end apart: 26, of which 17 were waited for; matrix products, arithmetic and copies ran while one was open for 3% of the time, Pallas kernels for 11%

profile of v2, /device:TPU:2, one launch (start us, length us, event | category | flops | bytes accessed | tf_op | source)
XLA Modules:
  0.0 99.8 jit_solution(14514602764577345858)
XLA Ops:
  2.7 1.7 %collective-permute-start = (bf16[128,768]{1,0:T(8,128)(2,1)S(1)}, bf16[128,768]{1,0:T(8,128)(2,1)S(1)}, u32[]{:S(2)}, u32[]{:S(2)}) collective-permute-start(bf16[128,768]{1,0:T(8,128)(2,1)S(1)} %get-tuple-element.41), channel_id=1, source_target_pairs={{0,1},{1,0},{2,3},{3,2},{4,5},{5,4},{6,7},{7,6},{8,9},{9,8},{10,11... | collective-permute-start | bytes 589832 | tf_op jit(solution)/shard_map/ppermute | solution.py:26
  4.3 5.9 %collective-permute-start.3 = (bf16[128,768]{1,0:T(8,128)(2,1)S(1)}, bf16[128,768]{1,0:T(8,128)(2,1)S(1)}, u32[]{:S(2)}, u32[]{:S(2)}) collective-permute-start(bf16[128,768]{1,0:T(8,128)(2,1)S(1)} %get-tuple-element.40.refs_0_), channel_id=1, source_target_pairs={{0,224},{1,225},{2,226},{3,227},{4,228},{5,229},{6,230},{7,231},{8... | collective-permute-start | bytes 589832 | tf_op jit(solution)/shard_map/ppermute | solution.py:26
  10.2 2.9 %collective-permute-start.1 = (bf16[128,768]{1,0:T(8,128)(2,1)S(1)}, bf16[128,768]{1,0:T(8,128)(2,1)S(1)}, u32[]{:S(2)}, u32[]{:S(2)}) collective-permute-start(bf16[128,768]{1,0:T(8,128)(2,1)S(1)} %get-tuple-element.40.refs_0_), channel_id=1, source_target_pairs={{0,16},{1,17},{2,18},{3,19},{4,20},{5,21},{6,22},{7,23},{8,24},{9,... | collective-permute-start | bytes 589832 | tf_op jit(solution)/shard_map/ppermute | solution.py:26
  14.1 3.4 %collective-permute-done.2.refs_2_ = bf16[128,768]{1,0:T(8,128)(2,1)S(1)} collective-permute-done((bf16[128,768]{1,0:T(8,128)(2,1)S(1)}, bf16[128,768]{1,0:T(8,128)(2,1)S(1)}, u32[]{:S(2)}, u32[]{:S(2)}) %collective-permute-start.2) | collective-permute-done | bytes 196640 | tf_op jit(solution)/shard_map/ppermute | solution.py:26
  18.6 1.5 %collective-permute-start.4 = (bf16[256,768]{1,0:T(8,128)(2,1)S(1)}, bf16[256,768]{1,0:T(8,128)(2,1)S(1)}, u32[]{:S(2)}, u32[]{:S(2)}) collective-permute-start(bf16[256,768]{1,0:T(8,128)(2,1)S(1)} %get-tuple-element.85), channel_id=1, source_target_pairs={{0,2},{1,3},{2,4},{3,5},{4,6},{5,7},{6,0},{7,1},{8,10},{9,11},{10,... | collective-permute-start | bytes 1179656 | tf_op jit(solution)/shard_map/ppermute | solution.py:26
  20.1 3.9 %collective-permute-start.9 = (bf16[128,768]{1,0:T(8,128)(2,1)S(1)}, bf16[128,768]{1,0:T(8,128)(2,1)S(1)}, u32[]{:S(2)}, u32[]{:S(2)}) collective-permute-start(bf16[128,768]{1,0:T(8,128)(2,1)S(1)} %collective-permute-done.3.refs_4_), channel_id=1, source_target_pairs={{0,224},{1,225},{2,226},{3,227},{4,228},{5,229},{6,230},{7,231},{8... | collective-permute-start | bytes 589832 | tf_op jit(solution)/shard_map/ppermute | solution.py:26
  24.0 2.0 %collective-permute-start.7 = (bf16[128,768]{1,0:T(8,128)(2,1)S(1)}, bf16[128,768]{1,0:T(8,128)(2,1)S(1)}, u32[]{:S(2)}, u32[]{:S(2)}) collective-permute-start(bf16[128,768]{1,0:T(8,128)(2,1)S(1)} %collective-permute-done.1.refs_1_), channel_id=1, source_target_pairs={{0,224},{1,225},{2,226},{3,227},{4,228},{5,229},{6,230},{7,231},{8... | collective-permute-start | bytes 589832 | tf_op jit(solution)/shard_map/ppermute | solution.py:26
  26.8 2.1 %collective-permute-done.9.refs_7_ = bf16[128,768]{1,0:T(8,128)(2,1)S(1)} collective-permute-done((bf16[128,768]{1,0:T(8,128)(2,1)S(1)}, bf16[128,768]{1,0:T(8,128)(2,1)S(1)}, u32[]{:S(2)}, u32[]{:S(2)}) %collective-permute-start.9) | collective-permute-done | bytes 196640 | tf_op jit(solution)/shard_map/ppermute | solution.py:26
  28.9 2.1 %collective-permute-done.7.refs_5_ = bf16[128,768]{1,0:T(8,128)(2,1)S(1)} collective-permute-done((bf16[128,768]{1,0:T(8,128)(2,1)S(1)}, bf16[128,768]{1,0:T(8,128)(2,1)S(1)}, u32[]{:S(2)}, u32[]{:S(2)}) %collective-permute-start.7) | collective-permute-done | bytes 196640 | tf_op jit(solution)/shard_map/ppermute | solution.py:26
  31.0 2.6 %collective-permute-done.6.refs_3_ = bf16[128,768]{1,0:T(8,128)(2,1)S(1)} collective-permute-done((bf16[128,768]{1,0:T(8,128)(2,1)S(1)}, bf16[128,768]{1,0:T(8,128)(2,1)S(1)}, u32[]{:S(2)}, u32[]{:S(2)}) %collective-permute-start.6) | collective-permute-done | bytes 196640 | tf_op jit(solution)/shard_map/ppermute | solution.py:26
  37.8 1.4 %collective-permute-start.13 = (bf16[128,768]{1,0:T(8,128)(2,1)S(1)}, bf16[128,768]{1,0:T(8,128)(2,1)S(1)}, u32[]{:S(2)}, u32[]{:S(2)}) collective-permute-start(bf16[128,768]{1,0:T(8,128)(2,1)S(1)} %slice.64), channel_id=1, source_target_pairs={{0,6},{1,7},{2,0},{3,1},{4,2},{5,3},{6,4},{7,5},{8,14},{9,15},{10,... | collective-permute-start | bytes 589832 | tf_op jit(solution)/shard_map/ppermute | solution.py:26
  40.0 7.5 %collective-permute-done.12 = bf16[128,768]{1,0:T(8,128)(2,1)S(1)} collective-permute-done((bf16[128,768]{1,0:T(8,128)(2,1)S(1)}, bf16[128,768]{1,0:T(8,128)(2,1)S(1)}, u32[]{:S(2)}, u32[]{:S(2)}) %collective-permute-start.12) | collective-permute-done | bytes 196640 | tf_op jit(solution)/shard_map/ppermute | solution.py:26
  48.0 4.9 %near_weights.1 = (bf16[1536,1280]{1,0:T(8,128)(2,1)S(1)}, bf16[1280,768]{1,0:T(8,128)(2,1)S(1)}, bf16[1536,768]{1,0:T(8,128)(2,1)S(1)}) custom-call(f32[1]{0:T(128)S(6)} %copy.11.scale_ref, f32[1]{0:T(128)S(6)} %copy.12.offset_ref, s32[2]{0:T(128)S(1)} %pad_add_fusion.place_ref, bf16[128,768]{1,0:T(8,128)(2,1)S(1)} %get-tuple-element.40.refs_0_, ...), custom_call_target="tpu_custom_call" | custom-call | flops 3019898880 | tf_op jit(solution)/shard_map/near_weights/pallas_call | solution.py:177
  52.9 2.1 %far_weights.1 = (bf16[512,1280]{1,0:T(8,128)(2,1)S(1)}, bf16[512,768]{1,0:T(8,128)(2,1)S(1)}) custom-call(f32[1]{0:T(128)S(6)} %copy.11.scale_ref, f32[1]{0:T(128)S(6)} %copy.12.offset_ref, s32[2]{0:T(128)S(1)} %pad_add_fusion.place_ref, bf16[1280,768]{1,0:T(8,128)(2,1)S(1)} %get-tuple-element.54.text, ...), custom_call_target="tpu_custom_call" | custom-call | flops 1006632960 | tf_op jit(solution)/shard_map/far_weights/pallas_call | solution.py:190
  55.0 1.8 %text_grads.2 = (bf16[256,768]{1,0:T(8,128)(2,1)S(1)}, bf16[256,768]{1,0:T(8,128)(2,1)S(1)}) custom-call(bf16[1536,1280]{1,0:T(8,128)(2,1)S(1)} %get-tuple-element.65.near_weights, bf16[1536,768]{1,0:T(8,128)(2,1)S(1)} %get-tuple-element.53.near_video, bf16[512,1280]{1,0:T(8,128)(2,1)S(1)} %get-tuple-element.55.far_weights, ...), custom_call_target="tpu_custom_call" | custom-call | flops 1610612736 | tf_op jit(solution)/shard_map/text_grads/pallas_call | solution.py:202
  56.9 2.2 %video_grads.2 = bf16[1024,768]{1,0:T(8,128)(2,1)S(1)} custom-call(bf16[1536,1280]{1,0:T(8,128)(2,1)S(1)} %get-tuple-element.65.near_weights, bf16[512,1280]{1,0:T(8,128)(2,1)S(1)} %get-tuple-element.55.far_weights, bf16[1280,768]{1,0:T(8,128)(2,1)S(1)} %get-tuple-element.54.text), custom_call_target="tpu_custom_call" | custom-call | flops 2013265920 | tf_op jit(solution)/shard_map/video_grads/pallas_call | solution.py:214
  61.7 2.2 %video_grads.3.refs_0_ = bf16[1024,768]{1,0:T(8,128)(2,1)S(1)} custom-call(bf16[1536,1280]{1,0:T(8,128)(2,1)S(1)} %get-tuple-element.65.near_weights, bf16[512,1280]{1,0:T(8,128)(2,1)S(1)} %get-tuple-element.55.far_weights, bf16[1280,768]{1,0:T(8,128)(2,1)S(1)} %get-tuple-element.54.text), custom_call_target="tpu_custom_call" | custom-call | flops 2013265920 | tf_op jit(solution)/shard_map/video_grads/pallas_call | solution.py:214
  63.9 2.6 %text_grads.3 = (bf16[256,768]{1,0:T(8,128)(2,1)S(1)}, bf16[256,768]{1,0:T(8,128)(2,1)S(1)}, bf16[256,768]{1,0:T(8,128)(2,1)S(1)}) custom-call(bf16[1536,1280]{1,0:T(8,128)(2,1)S(1)} %get-tuple-element.65.near_weights, bf16[1536,768]{1,0:T(8,128)(2,1)S(1)} %get-tuple-element.53.near_video, bf16[512,1280]{1,0:T(8,128)(2,1)S(1)} %get-tuple-element.55.far_weights, ...), custom_call_target="tpu_custom_call" | custom-call | flops 2415919104 | tf_op jit(solution)/shard_map/text_grads/pallas_call | solution.py:202
  66.5 4.2 %collective-permute-done.15 = bf16[256,768]{1,0:T(8,128)(2,1)S(1)} collective-permute-done((bf16[256,768]{1,0:T(8,128)(2,1)S(1)}, bf16[256,768]{1,0:T(8,128)(2,1)S(1)}, u32[]{:S(2)}, u32[]{:S(2)}) %collective-permute-start.15) | collective-permute-done | bytes 393248 | tf_op jit(solution)/shard_map/ppermute | solution.py:26
  70.8 2.0 %collective-permute-done.16 = bf16[256,768]{1,0:T(8,128)(2,1)S(1)} collective-permute-done((bf16[256,768]{1,0:T(8,128)(2,1)S(1)}, bf16[256,768]{1,0:T(8,128)(2,1)S(1)}, u32[]{:S(2)}, u32[]{:S(2)}) %collective-permute-start.16) | collective-permute-done | bytes 393248 | tf_op jit(solution)/shard_map/ppermute | solution.py:26
  72.8 1.6 %collective-permute-start.19 = (bf16[128,768]{1,0:T(8,128)(2,1)S(1)}, bf16[128,768]{1,0:T(8,128)(2,1)S(1)}, u32[]{:S(2)}, u32[]{:S(2)}) collective-permute-start(bf16[128,768]{1,0:T(8,128)(2,1)S(1)} %get-tuple-element.82), channel_id=1, source_target_pairs={{0,2},{1,3},{2,4},{3,5},{4,6},{5,7},{6,0},{7,1},{8,10},{9,11},{10,... | collective-permute-start | bytes 589832 | tf_op jit(solution)/shard_map/ppermute | solution.py:26
  74.4 1.8 %collective-permute-start.18 = (bf16[128,768]{1,0:T(8,128)(2,1)S(1)}, bf16[128,768]{1,0:T(8,128)(2,1)S(1)}, u32[]{:S(2)}, u32[]{:S(2)}) collective-permute-start(bf16[128,768]{1,0:T(8,128)(2,1)S(1)} %get-tuple-element.83), channel_id=1, source_target_pairs={{0,6},{1,7},{2,0},{3,1},{4,2},{5,3},{6,4},{7,5},{8,14},{9,15},{10,... | collective-permute-start | bytes 589832 | tf_op jit(solution)/shard_map/ppermute | solution.py:26
  76.7 1.8 %collective-permute-start.23 = (bf16[256,768]{1,0:T(8,128)(2,1)S(1)}, bf16[256,768]{1,0:T(8,128)(2,1)S(1)}, u32[]{:S(2)}, u32[]{:S(2)}) collective-permute-start(bf16[256,768]{1,0:T(8,128)(2,1)S(1)} %add_convert_fusion.1), channel_id=1, source_target_pairs={{0,32},{1,33},{2,34},{3,35},{4,36},{5,37},{6,38},{7,39},{8,40},{9,... | collective-permute-start | bytes 1179656 | tf_op jit(solution)/shard_map/ppermute | solution.py:26
  78.6 1.5 %collective-permute-done.19 = bf16[128,768]{1,0:T(8,128)(2,1)S(1)} collective-permute-done((bf16[128,768]{1,0:T(8,128)(2,1)S(1)}, bf16[128,768]{1,0:T(8,128)(2,1)S(1)}, u32[]{:S(2)}, u32[]{:S(2)}) %collective-permute-start.19) | collective-permute-done | bytes 196640 | tf_op jit(solution)/shard_map/ppermute | solution.py:26
  80.1 1.5 %collective-permute-done.18 = bf16[128,768]{1,0:T(8,128)(2,1)S(1)} collective-permute-done((bf16[128,768]{1,0:T(8,128)(2,1)S(1)}, bf16[128,768]{1,0:T(8,128)(2,1)S(1)}, u32[]{:S(2)}, u32[]{:S(2)}) %collective-permute-start.18) | collective-permute-done | bytes 196640 | tf_op jit(solution)/shard_map/ppermute | solution.py:26
  81.9 1.8 %collective-permute-start.20 = (bf16[256,768]{1,0:T(8,128)(2,1)S(1)}, bf16[256,768]{1,0:T(8,128)(2,1)S(1)}, u32[]{:S(2)}, u32[]{:S(2)}) collective-permute-start(bf16[256,768]{1,0:T(8,128)(2,1)S(1)} %pad_maximum_fusion), channel_id=1, source_target_pairs={{0,2},{1,3},{2,4},{3,5},{4,6},{5,7},{6,0},{7,1},{8,10},{9,11},{10,... | collective-permute-start | bytes 1179656 | tf_op jit(solution)/shard_map/ppermute | solution.py:26
  84.1 1.9 %collective-permute-done.24.refs_2_ = bf16[256,768]{1,0:T(8,128)(2,1)S(1)} collective-permute-done((bf16[256,768]{1,0:T(8,128)(2,1)S(1)}, bf16[256,768]{1,0:T(8,128)(2,1)S(1)}, u32[]{:S(2)}, u32[]{:S(2)}) %collective-permute-start.24) | collective-permute-done | bytes 393248 | tf_op jit(solution)/shard_map/ppermute | solution.py:26
  86.0 1.7 %collective-permute-done.23.refs_1_ = bf16[256,768]{1,0:T(8,128)(2,1)S(1)} collective-permute-done((bf16[256,768]{1,0:T(8,128)(2,1)S(1)}, bf16[256,768]{1,0:T(8,128)(2,1)S(1)}, u32[]{:S(2)}, u32[]{:S(2)}) %collective-permute-start.23) | collective-permute-done | bytes 393248 | tf_op jit(solution)/shard_map/ppermute | solution.py:26
  87.8 1.2 %collective-permute-start.25 = (bf16[128,768]{1,0:T(8,128)(2,1)S(1)}, bf16[128,768]{1,0:T(8,128)(2,1)S(1)}, u32[]{:S(2)}, u32[]{:S(2)}) collective-permute-start(bf16[128,768]{1,0:T(8,128)(2,1)S(1)} %add_convert_fusion.2), channel_id=1, source_target_pairs={{0,16},{1,17},{2,18},{3,19},{4,20},{5,21},{6,22},{7,23},{8,24},{9,... | collective-permute-start | bytes 589832 | tf_op jit(solution)/shard_map/ppermute | solution.py:26
  89.0 2.6 %collective-permute-done.20.refs_2_ = bf16[256,768]{1,0:T(8,128)(2,1)S(1)} collective-permute-done((bf16[256,768]{1,0:T(8,128)(2,1)S(1)}, bf16[256,768]{1,0:T(8,128)(2,1)S(1)}, u32[]{:S(2)}, u32[]{:S(2)}) %collective-permute-start.20) | collective-permute-done | bytes 393248 | tf_op jit(solution)/shard_map/ppermute | solution.py:26
  91.6 1.3 %collective-permute-done.21.refs_3_ = bf16[256,768]{1,0:T(8,128)(2,1)S(1)} collective-permute-done((bf16[256,768]{1,0:T(8,128)(2,1)S(1)}, bf16[256,768]{1,0:T(8,128)(2,1)S(1)}, u32[]{:S(2)}, u32[]{:S(2)}) %collective-permute-start.21) | collective-permute-done | bytes 393248 | tf_op jit(solution)/shard_map/ppermute | solution.py:26
  93.2 3.8 %collective-permute-done.25.refs_3_ = bf16[128,768]{1,0:T(8,128)(2,1)S(1)} collective-permute-done((bf16[128,768]{1,0:T(8,128)(2,1)S(1)}, bf16[128,768]{1,0:T(8,128)(2,1)S(1)}, u32[]{:S(2)}, u32[]{:S(2)}) %collective-permute-start.25) | collective-permute-done | bytes 196640 | tf_op jit(solution)/shard_map/ppermute | solution.py:26
  (67 shorter events, 15.9 us)
Async XLA Ops:
  0.6 0.9 copy-start
  2.7 10.5 %collective-permute-start = (bf16[128,768]{1,0:T(8,128)(2,1)S(1)}, bf16[128,768]{1,0:T(8,128)(2,1)S(1)}, u32[]{:S(2)}, u32[]{:S(2)}) collective-permute-start(bf16[128,768]{1,0:T(8,128)(2,1)S(1)} %get-tuple-element.41), channel_id=1, source_target_pairs={{0,1},{1,0},{2,3},{3,2},{4,5},{5,4},{6,7},{7,6},{8,9},{9,8},{10,11... | collective-permute-start | bytes 589832 | tf_op jit(solution)/shard_map/ppermute | solution.py:26
  4.3 9.7 %collective-permute-start.3 = (bf16[128,768]{1,0:T(8,128)(2,1)S(1)}, bf16[128,768]{1,0:T(8,128)(2,1)S(1)}, u32[]{:S(2)}, u32[]{:S(2)}) collective-permute-start(bf16[128,768]{1,0:T(8,128)(2,1)S(1)} %get-tuple-element.40.refs_0_), channel_id=1, source_target_pairs={{0,224},{1,225},{2,226},{3,227},{4,228},{5,229},{6,230},{7,231},{8... | collective-permute-start | bytes 589832 | tf_op jit(solution)/shard_map/ppermute | solution.py:26
  10.2 7.3 %collective-permute-start.2 = (bf16[128,768]{1,0:T(8,128)(2,1)S(1)}, bf16[128,768]{1,0:T(8,128)(2,1)S(1)}, u32[]{:S(2)}, u32[]{:S(2)}) collective-permute-start(bf16[128,768]{1,0:T(8,128)(2,1)S(1)} %get-tuple-element.40.refs_0_), channel_id=1, source_target_pairs={{0,32},{1,33},{2,34},{3,35},{4,36},{5,37},{6,38},{7,39},{8,40},{9,... | collective-permute-start | bytes 589832 | tf_op jit(solution)/shard_map/ppermute | solution.py:26
  10.2 7.6 %collective-permute-start.1 = (bf16[128,768]{1,0:T(8,128)(2,1)S(1)}, bf16[128,768]{1,0:T(8,128)(2,1)S(1)}, u32[]{:S(2)}, u32[]{:S(2)}) collective-permute-start(bf16[128,768]{1,0:T(8,128)(2,1)S(1)} %get-tuple-element.40.refs_0_), channel_id=1, source_target_pairs={{0,16},{1,17},{2,18},{3,19},{4,20},{5,21},{6,22},{7,23},{8,24},{9,... | collective-permute-start | bytes 589832 | tf_op jit(solution)/shard_map/ppermute | solution.py:26
  17.8 8.3 %collective-permute-start.8 = (bf16[128,768]{1,0:T(8,128)(2,1)S(1)}, bf16[128,768]{1,0:T(8,128)(2,1)S(1)}, u32[]{:S(2)}, u32[]{:S(2)}) collective-permute-start(bf16[128,768]{1,0:T(8,128)(2,1)S(1)} %collective-permute-done.2.refs_2_), channel_id=1, source_target_pairs={{0,32},{1,33},{2,34},{3,35},{4,36},{5,37},{6,38},{7,39},{8,40},{9,... | collective-permute-start | bytes 589832 | tf_op jit(solution)/shard_map/ppermute | solution.py:26
  18.0 15.6 %collective-permute-start.5 = (bf16[256,768]{1,0:T(8,128)(2,1)S(1)}, bf16[256,768]{1,0:T(8,128)(2,1)S(1)}, u32[]{:S(2)}, u32[]{:S(2)}) collective-permute-start(bf16[256,768]{1,0:T(8,128)(2,1)S(1)} %get-tuple-element.85), channel_id=1, source_target_pairs={{0,6},{1,7},{2,0},{3,1},{4,2},{5,3},{6,4},{7,5},{8,14},{9,15},{10,... | collective-permute-start | bytes 1179656 | tf_op jit(solution)/shard_map/ppermute | solution.py:26
  18.6 15.0 %collective-permute-start.4 = (bf16[256,768]{1,0:T(8,128)(2,1)S(1)}, bf16[256,768]{1,0:T(8,128)(2,1)S(1)}, u32[]{:S(2)}, u32[]{:S(2)}) collective-permute-start(bf16[256,768]{1,0:T(8,128)(2,1)S(1)} %get-tuple-element.85), channel_id=1, source_target_pairs={{0,2},{1,3},{2,4},{3,5},{4,6},{5,7},{6,0},{7,1},{8,10},{9,11},{10,... | collective-permute-start | bytes 1179656 | tf_op jit(solution)/shard_map/ppermute | solution.py:26
  20.1 8.8 %collective-permute-start.9 = (bf16[128,768]{1,0:T(8,128)(2,1)S(1)}, bf16[128,768]{1,0:T(8,128)(2,1)S(1)}, u32[]{:S(2)}, u32[]{:S(2)}) collective-permute-start(bf16[128,768]{1,0:T(8,128)(2,1)S(1)} %collective-permute-done.3.refs_4_), channel_id=1, source_target_pairs={{0,224},{1,225},{2,226},{3,227},{4,228},{5,229},{6,230},{7,231},{8... | collective-permute-start | bytes 589832 | tf_op jit(solution)/shard_map/ppermute | solution.py:26
  24.0 6.9 %collective-permute-start.7 = (bf16[128,768]{1,0:T(8,128)(2,1)S(1)}, bf16[128,768]{1,0:T(8,128)(2,1)S(1)}, u32[]{:S(2)}, u32[]{:S(2)}) collective-permute-start(bf16[128,768]{1,0:T(8,128)(2,1)S(1)} %collective-permute-done.1.refs_1_), channel_id=1, source_target_pairs={{0,224},{1,225},{2,226},{3,227},{4,228},{5,229},{6,230},{7,231},{8... | collective-permute-start | bytes 589832 | tf_op jit(solution)/shard_map/ppermute | solution.py:26
  26.7 6.9 %collective-permute-start.6 = (bf16[128,768]{1,0:T(8,128)(2,1)S(1)}, bf16[128,768]{1,0:T(8,128)(2,1)S(1)}, u32[]{:S(2)}, u32[]{:S(2)}) collective-permute-start(bf16[128,768]{1,0:T(8,128)(2,1)S(1)} %collective-permute-done.1.refs_1_), channel_id=1, source_target_pairs={{0,32},{1,33},{2,34},{3,35},{4,36},{5,37},{6,38},{7,39},{8,40},{9,... | collective-permute-start | bytes 589832 | tf_op jit(solution)/shard_map/ppermute | solution.py:26
  28.9 4.8 %copy-start.6 = (bf16[128,768]{1,0:T(8,128)(2,1)}, bf16[128,768]{1,0:T(8,128)(2,1)S(1)}, u32[]{:S(2)}) copy-start(bf16[128,768]{1,0:T(8,128)(2,1)S(1)} %collective-permute-done.9.refs_7_) | copy-start | bytes 589828
  34.4 13.6 %collective-permute-start.11 = (bf16[768,768]{1,0:T(8,128)(2,1)S(1)}, bf16[768,768]{1,0:T(8,128)(2,1)S(1)}, u32[]{:S(2)}, u32[]{:S(2)}) collective-permute-start(bf16[768,768]{1,0:T(8,128)(2,1)S(1)} %constant_dynamic-update-slice_fusion.2.refs_9_), channel_id=1, source_target_pairs={{0,8},{1,9},{2,10},{3,11},{4,12},{5,13},{6,14},{7,15},{8,0},{9,1},... | collective-permute-start | bytes 3538952 | tf_op jit(solution)/shard_map/ppermute | solution.py:26
  35.8 12.1 %copy-start.5 = (bf16[128,768]{1,0:T(8,128)(2,1)S(1)}, bf16[128,768]{1,0:T(8,128)(2,1)}, u32[]{:S(2)}) copy-start(bf16[128,768]{1,0:T(8,128)(2,1)} %copy-done.4) | copy-start | bytes 589828
  35.8 12.1 %copy-start.7 = (bf16[128,768]{1,0:T(8,128)(2,1)S(1)}, bf16[128,768]{1,0:T(8,128)(2,1)}, u32[]{:S(2)}) copy-start(bf16[128,768]{1,0:T(8,128)(2,1)} %copy-done.6) | copy-start | bytes 589828
  37.8 9.8 %collective-permute-start.13 = (bf16[128,768]{1,0:T(8,128)(2,1)S(1)}, bf16[128,768]{1,0:T(8,128)(2,1)S(1)}, u32[]{:S(2)}, u32[]{:S(2)}) collective-permute-start(bf16[128,768]{1,0:T(8,128)(2,1)S(1)} %slice.64), channel_id=1, source_target_pairs={{0,6},{1,7},{2,0},{3,1},{4,2},{5,3},{6,4},{7,5},{8,14},{9,15},{10,... | collective-permute-start | bytes 589832 | tf_op jit(solution)/shard_map/ppermute | solution.py:26
  39.1 8.4 %collective-permute-start.12 = (bf16[128,768]{1,0:T(8,128)(2,1)S(1)}, bf16[128,768]{1,0:T(8,128)(2,1)S(1)}, u32[]{:S(2)}, u32[]{:S(2)}) collective-permute-start(bf16[128,768]{1,0:T(8,128)(2,1)S(1)} %slice.63), channel_id=1, source_target_pairs={{0,2},{1,3},{2,4},{3,5},{4,6},{5,7},{6,0},{7,1},{8,10},{9,11},{10,... | collective-permute-start | bytes 589832 | tf_op jit(solution)/shard_map/ppermute | solution.py:26
  39.9 8.0 %collective-permute-start.10 = (bf16[128,768]{1,0:T(8,128)(2,1)S(1)}, bf16[128,768]{1,0:T(8,128)(2,1)S(1)}, u32[]{:S(2)}, u32[]{:S(2)}) collective-permute-start(bf16[128,768]{1,0:T(8,128)(2,1)S(1)} %broadcast_select_fusion), channel_id=1, source_target_pairs={{0,32},{1,33},{2,34},{3,35},{4,36},{5,37},{6,38},{7,39},{8,40},{9,... | collective-permute-start | bytes 589832 | tf_op jit(solution)/shard_map/ppermute | solution.py:287
  47.6 5.3 %collective-permute-start.14 = (bf16[256,768]{1,0:T(8,128)(2,1)S(1)}, bf16[256,768]{1,0:T(8,128)(2,1)S(1)}, u32[]{:S(2)}, u32[]{:S(2)}) collective-permute-start(bf16[256,768]{1,0:T(8,128)(2,1)S(1)} %constant_dynamic-update-slice_fusion.6.refs_0_), channel_id=1, source_target_pairs={{0,8},{1,9},{2,10},{3,11},{4,12},{5,13},{6,14},{7,15},{8,0},{9,1},... | collective-permute-start | bytes 1179656 | tf_op jit(solution)/shard_map/ppermute | solution.py:26
  59.1 13.7 %collective-permute-start.17 = (bf16[1024,768]{1,0:T(8,128)(2,1)S(1)}, bf16[1024,768]{1,0:T(8,128)(2,1)S(1)}, u32[]{:S(2)}, u32[]{:S(2)}) collective-permute-start(bf16[1024,768]{1,0:T(8,128)(2,1)S(1)} %video_grads.2), channel_id=1, source_target_pairs={{0,8},{1,9},{2,10},{3,11},{4,12},{5,13},{6,14},{7,15},{8,0},{9,1},... | collective-permute-start | bytes 4718600 | tf_op jit(solution)/shard_map/ppermute | solution.py:26
  59.7 11.1 %collective-permute-start.15 = (bf16[256,768]{1,0:T(8,128)(2,1)S(1)}, bf16[256,768]{1,0:T(8,128)(2,1)S(1)}, u32[]{:S(2)}, u32[]{:S(2)}) collective-permute-start(bf16[256,768]{1,0:T(8,128)(2,1)S(1)} %get-tuple-element.59), channel_id=1, source_target_pairs={{0,224},{1,225},{2,226},{3,227},{4,228},{5,229},{6,230},{7,231},{8... | collective-permute-start | bytes 1179656 | tf_op jit(solution)/shard_map/ppermute | solution.py:26
  60.7 12.0 %collective-permute-start.16 = (bf16[256,768]{1,0:T(8,128)(2,1)S(1)}, bf16[256,768]{1,0:T(8,128)(2,1)S(1)}, u32[]{:S(2)}, u32[]{:S(2)}) collective-permute-start(bf16[256,768]{1,0:T(8,128)(2,1)S(1)} %get-tuple-element.60), channel_id=1, source_target_pairs={{0,32},{1,33},{2,34},{3,35},{4,36},{5,37},{6,38},{7,39},{8,40},{9,... | collective-permute-start | bytes 1179656 | tf_op jit(solution)/shard_map/ppermute | solution.py:26
  72.8 7.2 %collective-permute-start.19 = (bf16[128,768]{1,0:T(8,128)(2,1)S(1)}, bf16[128,768]{1,0:T(8,128)(2,1)S(1)}, u32[]{:S(2)}, u32[]{:S(2)}) collective-permute-start(bf16[128,768]{1,0:T(8,128)(2,1)S(1)} %get-tuple-element.82), channel_id=1, source_target_pairs={{0,2},{1,3},{2,4},{3,5},{4,6},{5,7},{6,0},{7,1},{8,10},{9,11},{10,... | collective-permute-start | bytes 589832 | tf_op jit(solution)/shard_map/ppermute | solution.py:26
  74.4 7.2 %collective-permute-start.18 = (bf16[128,768]{1,0:T(8,128)(2,1)S(1)}, bf16[128,768]{1,0:T(8,128)(2,1)S(1)}, u32[]{:S(2)}, u32[]{:S(2)}) collective-permute-start(bf16[128,768]{1,0:T(8,128)(2,1)S(1)} %get-tuple-element.83), channel_id=1, source_target_pairs={{0,6},{1,7},{2,0},{3,1},{4,2},{5,3},{6,4},{7,5},{8,14},{9,15},{10,... | collective-permute-start | bytes 589832 | tf_op jit(solution)/shard_map/ppermute | solution.py:26
  76.3 9.7 %collective-permute-start.24 = (bf16[256,768]{1,0:T(8,128)(2,1)S(1)}, bf16[256,768]{1,0:T(8,128)(2,1)S(1)}, u32[]{:S(2)}, u32[]{:S(2)}) collective-permute-start(bf16[256,768]{1,0:T(8,128)(2,1)S(1)} %add_convert_fusion), channel_id=1, source_target_pairs={{0,224},{1,225},{2,226},{3,227},{4,228},{5,229},{6,230},{7,231},{8... | collective-permute-start | bytes 1179656 | tf_op jit(solution)/shard_map/ppermute | solution.py:26
  76.7 11.0 %collective-permute-start.23 = (bf16[256,768]{1,0:T(8,128)(2,1)S(1)}, bf16[256,768]{1,0:T(8,128)(2,1)S(1)}, u32[]{:S(2)}, u32[]{:S(2)}) collective-permute-start(bf16[256,768]{1,0:T(8,128)(2,1)S(1)} %add_convert_fusion.1), channel_id=1, source_target_pairs={{0,32},{1,33},{2,34},{3,35},{4,36},{5,37},{6,38},{7,39},{8,40},{9,... | collective-permute-start | bytes 1179656 | tf_op jit(solution)/shard_map/ppermute | solution.py:26
  81.9 15.1 %copy-start.3 = (bf16[128,768]{1,0:T(8,128)(2,1)S(1)}, bf16[128,768]{1,0:T(8,128)(2,1)}, u32[]{:S(2)}) copy-start(bf16[128,768]{1,0:T(8,128)(2,1)} %embedding_ref.3) | copy-start | bytes 589828
  81.9 9.7 %collective-permute-start.20 = (bf16[256,768]{1,0:T(8,128)(2,1)S(1)}, bf16[256,768]{1,0:T(8,128)(2,1)S(1)}, u32[]{:S(2)}, u32[]{:S(2)}) collective-permute-start(bf16[256,768]{1,0:T(8,128)(2,1)S(1)} %pad_maximum_fusion), channel_id=1, source_target_pairs={{0,2},{1,3},{2,4},{3,5},{4,6},{5,7},{6,0},{7,1},{8,10},{9,11},{10,... | collective-permute-start | bytes 1179656 | tf_op jit(solution)/shard_map/ppermute | solution.py:26
  83.7 9.1 %collective-permute-start.21 = (bf16[256,768]{1,0:T(8,128)(2,1)S(1)}, bf16[256,768]{1,0:T(8,128)(2,1)S(1)}, u32[]{:S(2)}, u32[]{:S(2)}) collective-permute-start(bf16[256,768]{1,0:T(8,128)(2,1)S(1)} %pad_maximum_fusion.1), channel_id=1, source_target_pairs={{0,6},{1,7},{2,0},{3,1},{4,2},{5,3},{6,4},{7,5},{8,14},{9,15},{10,... | collective-permute-start | bytes 1179656 | tf_op jit(solution)/shard_map/ppermute | solution.py:26
  87.8 10.9 %copy-start.1 = (bf16[128,768]{1,0:T(8,128)(2,1)S(1)}, bf16[128,768]{1,0:T(8,128)(2,1)}, u32[]{:S(2)}) copy-start(bf16[128,768]{1,0:T(8,128)(2,1)} %embedding_ref.2) | copy-start | bytes 589828
  87.8 9.2 %collective-permute-start.25 = (bf16[128,768]{1,0:T(8,128)(2,1)S(1)}, bf16[128,768]{1,0:T(8,128)(2,1)S(1)}, u32[]{:S(2)}, u32[]{:S(2)}) collective-permute-start(bf16[128,768]{1,0:T(8,128)(2,1)S(1)} %add_convert_fusion.2), channel_id=1, source_target_pairs={{0,16},{1,17},{2,18},{3,19},{4,20},{5,21},{6,22},{7,23},{8,24},{9,... | collective-permute-start | bytes 589832 | tf_op jit(solution)/shard_map/ppermute | solution.py:26
  93.0 5.8 %collective-permute-start.22 = (bf16[128,768]{1,0:T(8,128)(2,1)S(1)}, bf16[128,768]{1,0:T(8,128)(2,1)S(1)}, u32[]{:S(2)}, u32[]{:S(2)}) collective-permute-start(bf16[128,768]{1,0:T(8,128)(2,1)S(1)} %add_convert_fusion.3), channel_id=1, source_target_pairs={{0,1},{1,0},{2,3},{3,2},{4,5},{5,4},{6,7},{7,6},{8,9},{9,8},{10,11... | collective-permute-start | bytes 589832 | tf_op jit(solution)/shard_map/ppermute | solution.py:26
  (4 other events, 3.2 us)

commit v3 on v2

v3 whole, which is shorter than its diff:
```python
import functools

import jax
import jax.numpy as jnp
from jax import lax
from jax.experimental import pallas as pl
from jax.experimental.pallas import tpu as pltpu
from jax.sharding import PartitionSpec as P

EPSILON = 1e-06
NZ, NX = 8, 4
AXES = ("blk", "bulk")
ANY = pl.BlockSpec(memory_space=pl.ANY)
SMEM = pl.BlockSpec(memory_space=pltpu.SMEM)


def move(block, x=0, z=0, y_lo=0, y_hi=0, core=0):
    pairs = []
    for blk in range(4 * NZ):
        for bulk in range(2 * NX):
            to_z = (blk // 4 + z) % NZ
            to_x = (bulk // 2 + x) % NX
            to_blk = to_z * 4 + (((blk // 2) % 2) ^ y_hi) * 2 + ((blk % 2) ^ core)
            to_bulk = to_x * 2 + ((bulk % 2) ^ y_lo)
            pairs.append((blk * 2 * NX + bulk, to_blk * 2 * NX + to_bulk))
    return lax.ppermute(block, AXES, pairs)


def add(*parts):
    total = parts[0].astype(jnp.float32)
    for part in parts[1:]:
        total = total + part.astype(jnp.float32)
    return total.astype(jnp.bfloat16)


def unit_rows(embedding):
    values = embedding.astype(jnp.float32)
    inverse = lax.rsqrt(jnp.sum(values * values, axis=1, keepdims=True) + EPSILON)
    return values * inverse, inverse


def unit_kernel(video_ref, text_ref, video_out, text_out):
    text_out[...] = unit_rows(text_ref[...])[0].astype(jnp.bfloat16)
    video_out[...] = unit_rows(video_ref[...])[0].astype(jnp.bfloat16)


def unit_low(video, text):
    shape = jax.ShapeDtypeStruct(video.shape, jnp.bfloat16)
    return pl.pallas_call(unit_kernel, out_shape=(shape, shape), name="unit_low")(video, text)


def back_kernel(scale_ref, embedding_ref, *refs):
    *parts, out = refs
    rows = out.shape[0]
    total = parts[0][:rows, :].astype(jnp.float32)
    for part in parts[1:]:
        total = total + part[:rows, :].astype(jnp.float32)
    grad_unit = scale_ref[0] * total
    unit, inverse = unit_rows(embedding_ref[...])
    along = jnp.sum(unit * grad_unit, axis=1, keepdims=True)
    out[...] = (grad_unit - unit * along) * inverse


def back_rows(scale, embedding, parts):
    vmem = pl.BlockSpec(memory_space=pltpu.VMEM)
    return pl.pallas_call(
        back_kernel,
        out_shape=jax.ShapeDtypeStruct(embedding.shape, jnp.float32),
        in_specs=[SMEM] + [vmem] * (1 + len(parts)),
        out_specs=vmem,
        compiler_params=pltpu.CompilerParams(vmem_limit_bytes=8 * 1024 * 1024),
        name="back_rows",
    )(scale, embedding, *parts)


PAIR, D = 256, 768
N_TEXT, N_VIDEO = 5, 8
LOG2_E = 1.4426950408889634


def put(target, blocks):
    place = 0
    for block in blocks:
        target[pl.ds(place, block.shape[0]), :] = block[...]
        place += block.shape[0]


def pair_weight(scale_ref, offset_ref, video, text):
    products = lax.dot_general(
        video, text, (((1,), (1,)), ((), ())), preferred_element_type=jnp.float32
    )
    shifted = products * (-LOG2_E * scale_ref[0]) + -LOG2_E * offset_ref[0]
    return pl.reciprocal(1.0 + jnp.exp2(shifted), approx=True)


def edge_mask(core, own):
    half = lax.broadcasted_iota(jnp.int32, (1, PAIR), 1) < PAIR // 2
    below, above = own | (core == 1), own | (core == 0)
    return jnp.where(half, jnp.where(below, 1.0, 0.0), jnp.where(above, 1.0, 0.0))


def tile_rows(step, tile):
    return pl.ds(pl.multiple_of(step * tile, tile), tile)


def near_kernel(scale_ref, offset_ref, place_ref, *refs):
    texts, videos = refs[:8], refs[8:-4]
    weights, text, video, sems = refs[-4:]
    copies = []
    for target, blocks in ((text, texts), (video, videos)):
        place = 0
        for block in blocks:
            part = target.at[pl.ds(place, block.shape[0]), :]
            copies.append(pltpu.make_async_copy(block, part, sems.at[len(copies)]))
            place += block.shape[0]
    for copy in copies:
        copy.start()
    for copy in copies:
        copy.wait()
    core = place_ref[0]
    tile = video.shape[0] // 2
    row = lax.broadcasted_iota(jnp.int32, (tile, PAIR), 0)
    column = lax.broadcasted_iota(jnp.int32, (tile, PAIR), 1)
    same = (row == column) & (row < PAIR // 2)

    @pl.loop(0, 2)
    def _(step):
        rows = tile_rows(step, tile)
        video_tile = video[rows, :]
        own = step == 0
        for i in range(4):
            columns = pl.ds(i * PAIR, PAIR)
            weight = pair_weight(scale_ref, offset_ref, video_tile, text[columns, :])
            if i == 0:
                weight = weight - jnp.where(same, jnp.where(own, 1.0, 0.0), 0.0)
            elif i == 3:
                weight = weight * edge_mask(core, own)
            weights[rows, columns] = weight.astype(jnp.bfloat16)


def text_sum(*pairs):
    total = None
    for weights, video in pairs:
        part = lax.dot_general(
            weights, video[...], (((0,), (0,)), ((), ())), preferred_element_type=jnp.float32
        )
        total = part if total is None else total + part
    return total


def video_sums(half, near, last_weights, far, text, last, outs):
    def dot(a, b):
        return jnp.dot(a, b[...], preferred_element_type=jnp.float32)

    tile = near.shape[0] // 2
    rows = pl.ds(half * tile, tile)
    total = dot(near[rows, :], text) + dot(last_weights[rows, :], last)
    for i, out in enumerate(outs[:3]):
        out[...] = total[i * PAIR : (i + 1) * PAIR].astype(jnp.bfloat16)
    rows = pl.ds(half * PAIR, PAIR)
    total = dot(far[rows, : 4 * PAIR], text) + dot(far[rows, 4 * PAIR :], last)
    outs[3][...] = total.astype(jnp.bfloat16)


def far_kernel(scale_ref, offset_ref, place_ref, near, text, near_video, last, *refs):
    videos, (last_weights, weights, video, below, above, *outs) = refs[:2], refs[2:]
    put(video, videos)
    core, y_hi = place_ref[0], place_ref[1]
    near_tile, rows = near_video.shape[0] // 2, PAIR // 2

    @pl.loop(0, 2)
    def _(step):
        rows = tile_rows(step, near_tile)
        weight = pair_weight(scale_ref, offset_ref, near_video[rows, :], last[...])
        last_weights[rows, :] = weight.astype(jnp.bfloat16)
        rows = tile_rows(step, PAIR)
        video_tile = video[rows, :]
        for i in range(4):
            columns = pl.ds(i * PAIR, PAIR)
            weight = pair_weight(scale_ref, offset_ref, video_tile, text[columns, :])
            if i == 3:
                weight = weight * edge_mask(core, step == 0)
            weights[rows, columns] = weight.astype(jnp.bfloat16)
        weight = pair_weight(scale_ref, offset_ref, video_tile, last[...])
        weights[rows, pl.ds(4 * PAIR, PAIR // 2)] = weight.astype(jnp.bfloat16)

    video_sums(1, near, last_weights, weights, text, last, outs)
    columns = pl.ds(3 * PAIR, PAIR)
    edges = text_sum((near[:, columns], near_video), (weights[:, columns], video))
    columns = pl.ds(4 * PAIR, rows)
    total = text_sum((last_weights[...], near_video), (weights[:, columns], video))
    below[:rows, :] = edges[:rows].astype(jnp.bfloat16)
    above[:rows, :] = edges[rows:].astype(jnp.bfloat16)
    below[rows:, :] = (total * jnp.where(y_hi == 0, 1.0, 0.0)).astype(jnp.bfloat16)
    above[rows:, :] = (total * jnp.where(y_hi == 1, 1.0, 0.0)).astype(jnp.bfloat16)


def last_kernel(near, last_weights, far, text, last, near_video, far_video, *outs):
    video_sums(0, near, last_weights, far, text, last, outs[:4])
    for i, block in enumerate(outs[4:]):
        columns = pl.ds(i * PAIR, PAIR)
        total = text_sum((near[:, columns], near_video), (far[:, columns], far_video))
        block[...] = total.astype(jnp.bfloat16)


VMEM = pl.BlockSpec(memory_space=pltpu.VMEM)
MIB = 1024 * 1024
FLOPS = 2 * N_VIDEO * N_TEXT * PAIR * PAIR * D


def low(rows, columns=D):
    return jax.ShapeDtypeStruct((rows, columns), jnp.bfloat16)


def cost(flops, transcendentals=0):
    return pl.CostEstimate(flops=flops, bytes_accessed=0, transcendentals=transcendentals)


def call(kernel, name, scalars, arrays, outs, grant, flops, transcendentals=0, copies=0):
    return pl.pallas_call(
        kernel,
        out_shape=outs,
        in_specs=[SMEM] * len(scalars) + [ANY if copies else VMEM] * len(arrays),
        out_specs=[VMEM] * len(outs),
        scratch_shapes=[pltpu.SemaphoreType.DMA((copies,))] if copies else [],
        compiler_params=pltpu.CompilerParams(vmem_limit_bytes=grant * MIB),
        cost_estimate=cost(flops, transcendentals),
        name=name,
    )(*scalars, *arrays)


def local(footage_embeds, caption_embeds, score_scale, score_offset):
    blk = lax.axis_index("blk")
    core, y_hi = blk % 2, (blk // 2) % 2
    place = jnp.stack([core, y_hi]).astype(jnp.int32)
    scalars = [score_scale, score_offset, place]
    rows = footage_embeds.shape[0]
    v0, t0 = unit_low(footage_embeds, caption_embeds)

    tp, v1 = move(t0, y_hi=1), move(v0, y_lo=1)
    a1m, a1p = move(t0, z=1), move(t0, z=-1)
    v1, tp, a1m, a1p = lax.optimization_barrier((v1, tp, a1m, a1p))
    v01 = jnp.concatenate([v0, v1])
    vm, vp = move(v01, x=1), move(v01, x=-1)
    a2m, a2p = move(a1m, z=1), move(a1p, z=-1)
    b1m, b1p = move(tp, z=1), move(tp, z=-1)
    vm, vp, b1m, b1p, a2m, a2p = lax.optimization_barrier((vm, vp, b1m, b1p, a2m, a2p))
    b2 = move_by_y_hi(jnp.where(y_hi == 1, b1p, b1m))
    v2 = move_by_core(jnp.where(core == 1, vp, vm), 1)
    own = [v01, vm, vp]
    videos = own + [move(block, core=1) for block in own]
    texts = [t0, tp, a1m, b1m, a1p, b1p, a2m, a2p]

    near_rows, far_rows = 6 * PAIR, 2 * PAIR
    near, text, near_video = call(
        near_kernel,
        "near_weights",
        scalars,
        texts + videos,
        [low(near_rows, 4 * PAIR), low(4 * PAIR), low(near_rows)],
        20,
        FLOPS * 3 // 5,
        2 * near_rows * 4 * PAIR,
        len(texts + videos),
    )
    v2, b2, near = lax.optimization_barrier((v2, b2, near))
    last, far, far_video, hmm, hqq, s01, sm, sp, s2 = call(
        far_kernel,
        "far_weights_and_sums",
        scalars,
        [near, text, near_video, b2, v2, move(v2, core=1)],
        [low(near_rows, PAIR // 2), low(far_rows, 4 * PAIR + PAIR // 2), low(far_rows)]
        + [low(PAIR)] * 6,
        24,
        FLOPS * 5 // 4,
        2 * far_rows * 5 * PAIR,
    )

    r2 = move(s2, core=1)
    g01, gm, gp, g2, h01, hm, hq = call(
        last_kernel,
        "own_video_and_near_text_sums",
        [],
        [near, last, far, text, b2, near_video, far_video],
        [low(PAIR)] * 7,
        24,
        FLOPS,
    )
    hmm, hqq, r2, g01, gm, gp, g2, h01, hm, hq = lax.optimization_barrier(
        (move(hmm, z=-1), move(hqq, z=1), r2, g01, gm, gp, g2, h01, hm, hq)
    )

    up, down = move(add(hq, hqq), z=1), move(add(hm, hmm), z=-1)
    last = move(add(h01[rows:], up[rows:], down[rows:]), y_hi=1)
    text_parts = [h01, up, down, last]

    back = move_by_core(add(g2, r2), -1)
    r01, rm, rp = [move(block, core=1) for block in (s01, sm, sp)]
    none = jnp.zeros((), jnp.bfloat16)
    gm = add(gm, rm, jnp.where(core == 0, back, none))
    gp = add(gp, rp, jnp.where(core == 1, back, none))
    from_p, from_m = move(gp, x=1), move(gm, x=-1)
    last = move(add(g01[rows:], r01[rows:], from_p[rows:], from_m[rows:]), y_lo=1)
    video_parts = [g01, r01, from_p, from_m, last]

    video_grad = back_rows(score_scale, footage_embeds, video_parts)
    text_grad = back_rows(score_scale, caption_embeds, text_parts)
    return (video_grad, text_grad)


def move_by_core(block, sign):
    pairs = []
    for blk in range(4 * NZ):
        step = sign if blk % 2 == 0 else -sign
        for bulk in range(2 * NX):
            to_bulk = ((bulk // 2 + step) % NX) * 2 + bulk % 2
            pairs.append((blk * 2 * NX + bulk, blk * 2 * NX + to_bulk))
    return lax.ppermute(block, AXES, pairs)


def move_by_y_hi(block):
    pairs = []
    for blk in range(4 * NZ):
        step = 1 if (blk // 2) % 2 == 0 else -1
        to_blk = ((blk // 4 + step) % NZ) * 4 + blk % 4
        for bulk in range(2 * NX):
            pairs.append((blk * 2 * NX + bulk, to_blk * 2 * NX + bulk))
    return lax.ppermute(block, AXES, pairs)


def solution(mesh):
    assert mesh.shape["blk"] == 4 * NZ and mesh.shape["bulk"] == 2 * NX
    return jax.shard_map(
        local,
        mesh=mesh,
        in_specs=(P(AXES, None), P(AXES, None), P(), P()),
        out_specs=(P(AXES, None), P(AXES, None)),
        check_vma=False,
    )
```

time: 100 us -> 101 us (1.010)
  waiting for transfers between devices: 40.3 us -> 29.5 us
  local copies, waits for them, and re-layouts: 5.4 us -> 10.4 us
  Pallas kernels: 18.1 us -> 22.1 us
  other arithmetic: 0.84 us -> 2.9 us
    ppermute x25 -> x26, waiting for transfers between devices: 40.3 us -> 28 us  [move(): return lax.ppermute(block, AXES, pairs)]
    unnamed x24 -> x27, local copies, waits for them, and re-layouts: 3.43 us -> 10.4 us
    pallas_call x7 -> x4, Pallas kernels: 16.1 us -> 20.1 us  [the longest x3 18.2 us: call(): pl.pallas_call(kernel, out_shape=outs, in_specs=[SMEM] * len(scalars) + [...]
    ppermute x0 -> x2, starting transfers between devices: none -> 3.83 us  [move_by_core(): return lax.ppermute(block, AXES, pairs)]
    ppermute x25 -> x26, starting transfers between devices: 32.8 us -> 29.4 us  [move(): return lax.ppermute(block, AXES, pairs)]
    convert_element_type x6, other arithmetic: 0.69 us -> 2.76 us  [add(): return total.astype(jnp.bfloat16)]
    slice x2 -> x0, local copies, waits for them, and re-layouts: 1.94 us -> none  [local(): v2 = jnp.concatenate([move(vm[:rows], x=1), move(vp[rows:], x=-1)])]
    ppermute x0 -> x2, waiting for transfers between devices: none -> 1.36 us  [move_by_core(): return lax.ppermute(block, AXES, pairs)]
  transfers between devices with their start and end apart: 26 -> 29, of which waited for: 17 -> 14; matrix products, arithmetic and copies ran while one was open for 3% -> 4% of each run, Pallas kernels for 11% -> 13%
where the time goes in v3:
time: 101 us
  starting transfers between devices  33.5 us (33%)
  waiting for transfers between devices  29.5 us (29%)
  Pallas kernels  22.1 us (22%)
  local copies, waits for them, and re-layouts  10.4 us (10%)
  other arithmetic  2.9 us (3%)
  between operations  2.2 us (2%)
    ppermute x26, starting transfers between devices, move(): return lax.ppermute(block, AXES, pairs)  29.4 us
    ppermute x26, waiting for transfers between devices, move(): return lax.ppermute(block, AXES, pairs)  28 us
    pallas_call x3, Pallas kernels, call(): pl.pallas_call(kernel, out_shape=outs, in_specs=[SMEM] * len(scalars) + [...  18.2 us
    unnamed x27, local copies, waits for them, and re-layouts  10.4 us
    ppermute x2, starting transfers between devices, move_by_core(): return lax.ppermute(block, AXES, pairs)  3.83 us
    convert_element_type x6, other arithmetic, add(): return total.astype(jnp.bfloat16)  2.76 us
    pallas_call x2, Pallas kernels, back_rows(): pl.pallas_call(back_kernel, out_shape=jax.ShapeDtypeStruct(embedding.shap...  2.05 us
  transfers between devices with their start and end apart: 29, of which 14 were waited for; matrix products, arithmetic and copies ran while one was open for 4% of the time, Pallas kernels for 13%

profile of v3, /device:TPU:2, one launch (start us, length us, event | category | flops | bytes accessed | tf_op | source)
XLA Modules:
  0.0 100.6 jit_solution(5269105656431653553)
XLA Ops:
  0.6 1.9 %unit_low.1 = (bf16[128,768]{1,0:T(8,128)(2,1)}, bf16[128,768]{1,0:T(8,128)(2,1)}) custom-call(bf16[128,768]{1,0:T(8,128)(2,1)} %embedding_ref.2, bf16[128,768]{1,0:T(8,128)(2,1)} %embedding_ref.3), custom_call_target="tpu_custom_call" | custom-call | tf_op jit(solution)/shard_map/unit_low/pallas_call | solution.py:49
  2.5 1.6 %collective-permute-start = (bf16[128,768]{1,0:T(8,128)(2,1)}, bf16[128,768]{1,0:T(8,128)(2,1)S(1)}, u32[]{:S(2)}, u32[]{:S(2)}) collective-permute-start(bf16[128,768]{1,0:T(8,128)(2,1)} %get-tuple-element.46), channel_id=1, source_target_pairs={{0,1},{1,0},{2,3},{3,2},{4,5},{5,4},{6,7},{7,6},{8,9},{9,8},{10,11... | collective-permute-start | bytes 589832 | tf_op jit(solution)/shard_map/ppermute | solution.py:26
  4.1 5.9 %collective-permute-start.3 = (bf16[128,768]{1,0:T(8,128)(2,1)}, bf16[128,768]{1,0:T(8,128)(2,1)S(1)}, u32[]{:S(2)}, u32[]{:S(2)}) collective-permute-start(bf16[128,768]{1,0:T(8,128)(2,1)} %get-tuple-element.47.refs_0_), channel_id=1, source_target_pairs={{0,224},{1,225},{2,226},{3,227},{4,228},{5,229},{6,230},{7,231},{8... | collective-permute-start | bytes 589832 | tf_op jit(solution)/shard_map/ppermute | solution.py:26
  10.0 2.9 %collective-permute-start.1 = (bf16[128,768]{1,0:T(8,128)(2,1)}, bf16[128,768]{1,0:T(8,128)(2,1)S(1)}, u32[]{:S(2)}, u32[]{:S(2)}) collective-permute-start(bf16[128,768]{1,0:T(8,128)(2,1)} %get-tuple-element.47.refs_0_), channel_id=1, source_target_pairs={{0,16},{1,17},{2,18},{3,19},{4,20},{5,21},{6,22},{7,23},{8,24},{9,... | collective-permute-start | bytes 589832 | tf_op jit(solution)/shard_map/ppermute | solution.py:26
  14.2 3.3 %collective-permute-done.2.refs_2_ = bf16[128,768]{1,0:T(8,128)(2,1)S(1)} collective-permute-done((bf16[128,768]{1,0:T(8,128)(2,1)}, bf16[128,768]{1,0:T(8,128)(2,1)S(1)}, u32[]{:S(2)}, u32[]{:S(2)}) %collective-permute-start.2) | collective-permute-done | bytes 196640 | tf_op jit(solution)/shard_map/ppermute | solution.py:26
  18.6 1.5 %collective-permute-start.4 = (bf16[256,768]{1,0:T(8,128)(2,1)S(1)}, bf16[256,768]{1,0:T(8,128)(2,1)S(1)}, u32[]{:S(2)}, u32[]{:S(2)}) collective-permute-start(bf16[256,768]{1,0:T(8,128)(2,1)S(1)} %constant_dynamic-update-slice_fusion.refs_8_), channel_id=1, source_target_pairs={{0,2},{1,3},{2,4},{3,5},{4,6},{5,7},{6,0},{7,1},{8,10},{9,11},{10,... | collective-permute-start | bytes 1179656 | tf_op jit(solution)/shard_map/ppermute | solution.py:26
  20.1 3.9 %collective-permute-start.9 = (bf16[128,768]{1,0:T(8,128)(2,1)S(1)}, bf16[128,768]{1,0:T(8,128)(2,1)S(1)}, u32[]{:S(2)}, u32[]{:S(2)}) collective-permute-start(bf16[128,768]{1,0:T(8,128)(2,1)S(1)} %collective-permute-done.3.refs_4_), channel_id=1, source_target_pairs={{0,224},{1,225},{2,226},{3,227},{4,228},{5,229},{6,230},{7,231},{8... | collective-permute-start | bytes 589832 | tf_op jit(solution)/shard_map/ppermute | solution.py:26
  24.0 2.0 %collective-permute-start.7 = (bf16[128,768]{1,0:T(8,128)(2,1)S(1)}, bf16[128,768]{1,0:T(8,128)(2,1)S(1)}, u32[]{:S(2)}, u32[]{:S(2)}) collective-permute-start(bf16[128,768]{1,0:T(8,128)(2,1)S(1)} %collective-permute-done.1.refs_1_), channel_id=1, source_target_pairs={{0,224},{1,225},{2,226},{3,227},{4,228},{5,229},{6,230},{7,231},{8... | collective-permute-start | bytes 589832 | tf_op jit(solution)/shard_map/ppermute | solution.py:26
  27.4 1.4 %collective-permute-done.9.refs_7_ = bf16[128,768]{1,0:T(8,128)(2,1)S(1)} collective-permute-done((bf16[128,768]{1,0:T(8,128)(2,1)S(1)}, bf16[128,768]{1,0:T(8,128)(2,1)S(1)}, u32[]{:S(2)}, u32[]{:S(2)}) %collective-permute-start.9) | collective-permute-done | bytes 196640 | tf_op jit(solution)/shard_map/ppermute | solution.py:26
  28.9 2.1 %collective-permute-done.7.refs_5_ = bf16[128,768]{1,0:T(8,128)(2,1)S(1)} collective-permute-done((bf16[128,768]{1,0:T(8,128)(2,1)S(1)}, bf16[128,768]{1,0:T(8,128)(2,1)S(1)}, u32[]{:S(2)}, u32[]{:S(2)}) %collective-permute-start.7) | collective-permute-done | bytes 196640 | tf_op jit(solution)/shard_map/ppermute | solution.py:26
  31.0 2.0 %collective-permute-done.6.refs_3_ = bf16[128,768]{1,0:T(8,128)(2,1)S(1)} collective-permute-done((bf16[128,768]{1,0:T(8,128)(2,1)S(1)}, bf16[128,768]{1,0:T(8,128)(2,1)S(1)}, u32[]{:S(2)}, u32[]{:S(2)}) %collective-permute-start.6) | collective-permute-done | bytes 196640 | tf_op jit(solution)/shard_map/ppermute | solution.py:26
  33.5 1.6 %collective-permute-start.10 = (bf16[256,768]{1,0:T(8,128)(2,1)S(1)}, bf16[256,768]{1,0:T(8,128)(2,1)S(1)}, u32[]{:S(2)}, u32[]{:S(2)}) collective-permute-start(bf16[256,768]{1,0:T(8,128)(2,1)S(1)} %broadcast_select_fusion), channel_id=1, source_target_pairs={{0,2},{1,3},{2,4},{3,5},{4,6},{5,7},{6,0},{7,1},{8,14},{9,15},{10,... | collective-permute-start | bytes 1179656 | tf_op jit(solution)/shard_map/ppermute | solution.py:318
  35.4 7.5 %near_weights.1 = (bf16[1536,1024]{1,0:T(8,128)(2,1)S(1)}, bf16[1024,768]{1,0:T(8,128)(2,1)S(1)}, bf16[1536,768]{1,0:T(8,128)(2,1)S(1)}) custom-call(f32[1]{0:T(128)S(6)} %copy.7.scale_ref, f32[1]{0:T(128)S(6)} %copy.8.offset_ref, s32[2]{0:T(128)S(1)} %pad_add_fusion.place_ref, bf16[128,768]{1,0:T(8,128)(2,1)S(1)} %copy-done.2, ...), custom_call_target="tpu_custom_call" | custom-call | flops 2415919104 | tf_op jit(solution)/shard_map/near_weights/pallas_call | solution.py:220
  43.0 1.7 %collective-permute-done.15.refs_1_ = bf16[256,768]{1,0:T(8,128)(2,1)S(1)} collective-permute-done((bf16[256,768]{1,0:T(8,128)(2,1)S(1)}, bf16[256,768]{1,0:T(8,128)(2,1)S(1)}, u32[]{:S(2)}, u32[]{:S(2)}) %collective-permute-start.15) | collective-permute-done | bytes 393248 | tf_op jit(solution)/shard_map/ppermute | solution.py:26
  44.7 6.1 %far_weights_and_sums.1 = (bf16[1536,128]{1,0:T(8,128)(2,1)S(1)}, bf16[512,1152]{1,0:T(8,128)(2,1)S(1)}, bf16[512,768]{1,0:T(8,128)(2,1)S(1)}, bf16[256,768]{1,0...) custom-call(f32[1]{0:T(128)S(6)} %copy.7.scale_ref, ...), custom_call_target="tpu_custom_call" | custom-call | flops 5033164800 | tf_op jit(solution)/shard_map/far_weights_and_sums/pallas_call | solution.py:220
  50.9 1.1 %copy-done.9 = bf16[512,1152]{1,0:T(8,128)(2,1)} copy-done((bf16[512,1152]{1,0:T(8,128)(2,1)}, bf16[512,1152]{1,0:T(8,128)(2,1)S(1)}, u32[]{:S(2)}) %copy-start.9) | copy-done | bytes 1179672
  52.9 3.2 %collective-permute-start.16 = (bf16[256,768]{1,0:T(8,128)(2,1)S(1)}, bf16[256,768]{1,0:T(8,128)(2,1)}, u32[]{:S(2)}, u32[]{:S(2)}) collective-permute-start(bf16[256,768]{1,0:T(8,128)(2,1)S(1)} %get-tuple-element.64), channel_id=1, source_target_pairs={{0,224},{1,225},{2,226},{3,227},{4,228},{5,229},{6,230},{7,231},{8... | collective-permute-start | bytes 1179656 | tf_op jit(solution)/shard_map/ppermute | solution.py:26
  56.7 1.9 %copy-done.4 = bf16[1536,1024]{1,0:T(8,128)(2,1)S(1)} copy-done((bf16[1536,1024]{1,0:T(8,128)(2,1)S(1)}, bf16[1536,1024]{1,0:T(8,128)(2,1)}, u32[]{:S(2)}) %copy-start.4) | copy-done | bytes 3145752
  58.5 1.7 %copy-done.6 = bf16[1536,768]{1,0:T(8,128)(2,1)S(1)} copy-done((bf16[1536,768]{1,0:T(8,128)(2,1)S(1)}, bf16[1536,768]{1,0:T(8,128)(2,1)}, u32[]{:S(2)}) %copy-start.6) | copy-done | bytes 2359320
  60.2 1.4 %copy-done.8 = bf16[1024,768]{1,0:T(8,128)(2,1)S(1)} copy-done((bf16[1024,768]{1,0:T(8,128)(2,1)S(1)}, bf16[1024,768]{1,0:T(8,128)(2,1)}, u32[]{:S(2)}) %copy-start.8) | copy-done | bytes 1572888
  61.6 1.3 %copy-done.10 = bf16[512,1152]{1,0:T(8,128)(2,1)S(1)} copy-done((bf16[512,1152]{1,0:T(8,128)(2,1)S(1)}, bf16[512,1152]{1,0:T(8,128)(2,1)}, u32[]{:S(2)}) %copy-start.10) | copy-done | bytes 1179672
  62.9 1.1 %copy-done.12 = bf16[512,768]{1,0:T(8,128)(2,1)S(1)} copy-done((bf16[512,768]{1,0:T(8,128)(2,1)S(1)}, bf16[512,768]{1,0:T(8,128)(2,1)}, u32[]{:S(2)}) %copy-start.12) | copy-done | bytes 786456
  64.0 4.6 %own_video_and_near_text_sums.1 = (bf16[256,768]{1,0:T(8,128)(2,1)S(1)}, bf16[256,768]{1,0:T(8,128)(2,1)S(1)}, bf16[256,768]{1,0:T(8,128)(2,1)S(1)}, bf16[256,76...) custom-call(bf16[1536,1024]{1,0:T(8,128)(2,1)S(1)} %copy-done.4, ...), custom_call_target="tpu_custom_call" | custom-call | flops 4026531840 | tf_op jit(solution)/shard_map/own_video_and_near_text_sums/pallas_call | solution.py:220
  69.3 1.1 %add_convert_fusion.4 = bf16[256,768]{1,0:T(8,128)(2,1)S(1)} fusion(bf16[256,768]{1,0:T(8,128)(2,1)} %collective-permute-done.18, bf16[256,768]{1,0:T(8,128)(2,1)S(1)} %get-tuple-element.81), kind=kLoop, calls=%fused_computation.4 | loop fusion | flops 786432 | bytes 1179648 | tf_op jit(solution)/shard_map/convert_element_type | solution.py:33
  70.4 2.3 %collective-permute-start.21 = (bf16[256,768]{1,0:T(8,128)(2,1)S(1)}, bf16[256,768]{1,0:T(8,128)(2,1)S(1)}, u32[]{:S(2)}, u32[]{:S(2)}) collective-permute-start(bf16[256,768]{1,0:T(8,128)(2,1)S(1)} %add_convert_fusion.4), channel_id=1, source_target_pairs={{0,6},{1,7},{2,0},{3,1},{4,2},{5,3},{6,4},{7,5},{8,10},{9,11},{10,... | collective-permute-start | bytes 1179656 | tf_op jit(solution)/shard_map/ppermute | solution.py:318
  73.7 3.3 %collective-permute-start.27 = (bf16[256,768]{1,0:T(8,128)(2,1)S(1)}, bf16[256,768]{1,0:T(8,128)(2,1)S(1)}, u32[]{:S(2)}, u32[]{:S(2)}) collective-permute-start(bf16[256,768]{1,0:T(8,128)(2,1)S(1)} %add_convert_fusion), channel_id=1, source_target_pairs={{0,224},{1,225},{2,226},{3,227},{4,228},{5,229},{6,230},{7,231},{8... | collective-permute-start | bytes 1179656 | tf_op jit(solution)/shard_map/ppermute | solution.py:26
  77.2 1.4 %collective-permute-done.21 = bf16[256,768]{1,0:T(8,128)(2,1)S(1)} collective-permute-done((bf16[256,768]{1,0:T(8,128)(2,1)S(1)}, bf16[256,768]{1,0:T(8,128)(2,1)S(1)}, u32[]{:S(2)}, u32[]{:S(2)}) %collective-permute-start.21) | collective-permute-done | bytes 393248 | tf_op jit(solution)/shard_map/ppermute | solution.py:318
  78.9 1.9 %collective-permute-start.24 = (bf16[256,768]{1,0:T(8,128)(2,1)S(1)}, bf16[256,768]{1,0:T(8,128)(2,1)S(1)}, u32[]{:S(2)}, u32[]{:S(2)}) collective-permute-start(bf16[256,768]{1,0:T(8,128)(2,1)S(1)} %get-tuple-element.90), channel_id=1, source_target_pairs={{0,6},{1,7},{2,0},{3,1},{4,2},{5,3},{6,4},{7,5},{8,14},{9,15},{10,... | collective-permute-start | bytes 1179656 | tf_op jit(solution)/shard_map/ppermute | solution.py:26
  81.1 4.4 %collective-permute-done.27.refs_2_ = bf16[256,768]{1,0:T(8,128)(2,1)S(1)} collective-permute-done((bf16[256,768]{1,0:T(8,128)(2,1)S(1)}, bf16[256,768]{1,0:T(8,128)(2,1)S(1)}, u32[]{:S(2)}, u32[]{:S(2)}) %collective-permute-start.27) | collective-permute-done | bytes 393248 | tf_op jit(solution)/shard_map/ppermute | solution.py:26
  85.5 3.6 %collective-permute-done.26.refs_1_ = bf16[256,768]{1,0:T(8,128)(2,1)S(1)} collective-permute-done((bf16[256,768]{1,0:T(8,128)(2,1)S(1)}, bf16[256,768]{1,0:T(8,128)(2,1)S(1)}, u32[]{:S(2)}, u32[]{:S(2)}) %collective-permute-start.26) | collective-permute-done | bytes 393248 | tf_op jit(solution)/shard_map/ppermute | solution.py:26
  89.5 2.2 %collective-permute-done.22.refs_2_ = bf16[256,768]{1,0:T(8,128)(2,1)S(1)} collective-permute-done((bf16[256,768]{1,0:T(8,128)(2,1)S(1)}, bf16[256,768]{1,0:T(8,128)(2,1)S(1)}, u32[]{:S(2)}, u32[]{:S(2)}) %collective-permute-start.22) | collective-permute-done | bytes 393248 | tf_op jit(solution)/shard_map/ppermute | solution.py:26
  92.0 6.5 %collective-permute-done.28.refs_3_ = bf16[128,768]{1,0:T(8,128)(2,1)S(1)} collective-permute-done((bf16[128,768]{1,0:T(8,128)(2,1)S(1)}, bf16[128,768]{1,0:T(8,128)(2,1)S(1)}, u32[]{:S(2)}, u32[]{:S(2)}) %collective-permute-start.28) | collective-permute-done | bytes 196640 | tf_op jit(solution)/shard_map/ppermute | solution.py:26
  (69 shorter events, 10.1 us)
Async XLA Ops:
  2.5 32.9 %copy-start.2 = (bf16[128,768]{1,0:T(8,128)(2,1)S(1)}, bf16[128,768]{1,0:T(8,128)(2,1)}, u32[]{:S(2)}) copy-start(bf16[128,768]{1,0:T(8,128)(2,1)} %get-tuple-element.47.refs_0_) | copy-start | bytes 589828
  2.5 11.3 %collective-permute-start = (bf16[128,768]{1,0:T(8,128)(2,1)}, bf16[128,768]{1,0:T(8,128)(2,1)S(1)}, u32[]{:S(2)}, u32[]{:S(2)}) collective-permute-start(bf16[128,768]{1,0:T(8,128)(2,1)} %get-tuple-element.46), channel_id=1, source_target_pairs={{0,1},{1,0},{2,3},{3,2},{4,5},{5,4},{6,7},{7,6},{8,9},{9,8},{10,11... | collective-permute-start | bytes 589832 | tf_op jit(solution)/shard_map/ppermute | solution.py:26
  4.1 10.1 %collective-permute-start.3 = (bf16[128,768]{1,0:T(8,128)(2,1)}, bf16[128,768]{1,0:T(8,128)(2,1)S(1)}, u32[]{:S(2)}, u32[]{:S(2)}) collective-permute-start(bf16[128,768]{1,0:T(8,128)(2,1)} %get-tuple-element.47.refs_0_), channel_id=1, source_target_pairs={{0,224},{1,225},{2,226},{3,227},{4,228},{5,229},{6,230},{7,231},{8... | collective-permute-start | bytes 589832 | tf_op jit(solution)/shard_map/ppermute | solution.py:26
  10.0 7.5 %collective-permute-start.2 = (bf16[128,768]{1,0:T(8,128)(2,1)}, bf16[128,768]{1,0:T(8,128)(2,1)S(1)}, u32[]{:S(2)}, u32[]{:S(2)}) collective-permute-start(bf16[128,768]{1,0:T(8,128)(2,1)} %get-tuple-element.47.refs_0_), channel_id=1, source_target_pairs={{0,32},{1,33},{2,34},{3,35},{4,36},{5,37},{6,38},{7,39},{8,40},{9,... | collective-permute-start | bytes 589832 | tf_op jit(solution)/shard_map/ppermute | solution.py:26
  10.0 7.8 %collective-permute-start.1 = (bf16[128,768]{1,0:T(8,128)(2,1)}, bf16[128,768]{1,0:T(8,128)(2,1)S(1)}, u32[]{:S(2)}, u32[]{:S(2)}) collective-permute-start(bf16[128,768]{1,0:T(8,128)(2,1)} %get-tuple-element.47.refs_0_), channel_id=1, source_target_pairs={{0,16},{1,17},{2,18},{3,19},{4,20},{5,21},{6,22},{7,23},{8,24},{9,... | collective-permute-start | bytes 589832 | tf_op jit(solution)/shard_map/ppermute | solution.py:26
  17.8 8.3 %collective-permute-start.8 = (bf16[128,768]{1,0:T(8,128)(2,1)S(1)}, bf16[128,768]{1,0:T(8,128)(2,1)S(1)}, u32[]{:S(2)}, u32[]{:S(2)}) collective-permute-start(bf16[128,768]{1,0:T(8,128)(2,1)S(1)} %collective-permute-done.2.refs_2_), channel_id=1, source_target_pairs={{0,32},{1,33},{2,34},{3,35},{4,36},{5,37},{6,38},{7,39},{8,40},{9,... | collective-permute-start | bytes 589832 | tf_op jit(solution)/shard_map/ppermute | solution.py:26
  18.0 15.0 %collective-permute-start.5 = (bf16[256,768]{1,0:T(8,128)(2,1)S(1)}, bf16[256,768]{1,0:T(8,128)(2,1)S(1)}, u32[]{:S(2)}, u32[]{:S(2)}) collective-permute-start(bf16[256,768]{1,0:T(8,128)(2,1)S(1)} %constant_dynamic-update-slice_fusion.refs_8_), channel_id=1, source_target_pairs={{0,6},{1,7},{2,0},{3,1},{4,2},{5,3},{6,4},{7,5},{8,14},{9,15},{10,... | collective-permute-start | bytes 1179656 | tf_op jit(solution)/shard_map/ppermute | solution.py:26
  18.6 14.3 %collective-permute-start.4 = (bf16[256,768]{1,0:T(8,128)(2,1)S(1)}, bf16[256,768]{1,0:T(8,128)(2,1)S(1)}, u32[]{:S(2)}, u32[]{:S(2)}) collective-permute-start(bf16[256,768]{1,0:T(8,128)(2,1)S(1)} %constant_dynamic-update-slice_fusion.refs_8_), channel_id=1, source_target_pairs={{0,2},{1,3},{2,4},{3,5},{4,6},{5,7},{6,0},{7,1},{8,10},{9,11},{10,... | collective-permute-start | bytes 1179656 | tf_op jit(solution)/shard_map/ppermute | solution.py:26
  20.1 8.8 %collective-permute-start.9 = (bf16[128,768]{1,0:T(8,128)(2,1)S(1)}, bf16[128,768]{1,0:T(8,128)(2,1)S(1)}, u32[]{:S(2)}, u32[]{:S(2)}) collective-permute-start(bf16[128,768]{1,0:T(8,128)(2,1)S(1)} %collective-permute-done.3.refs_4_), channel_id=1, source_target_pairs={{0,224},{1,225},{2,226},{3,227},{4,228},{5,229},{6,230},{7,231},{8... | collective-permute-start | bytes 589832 | tf_op jit(solution)/shard_map/ppermute | solution.py:26
  24.0 6.9 %collective-permute-start.7 = (bf16[128,768]{1,0:T(8,128)(2,1)S(1)}, bf16[128,768]{1,0:T(8,128)(2,1)S(1)}, u32[]{:S(2)}, u32[]{:S(2)}) collective-permute-start(bf16[128,768]{1,0:T(8,128)(2,1)S(1)} %collective-permute-done.1.refs_1_), channel_id=1, source_target_pairs={{0,224},{1,225},{2,226},{3,227},{4,228},{5,229},{6,230},{7,231},{8... | collective-permute-start | bytes 589832 | tf_op jit(solution)/shard_map/ppermute | solution.py:26
  26.0 6.9 %collective-permute-start.6 = (bf16[128,768]{1,0:T(8,128)(2,1)S(1)}, bf16[128,768]{1,0:T(8,128)(2,1)S(1)}, u32[]{:S(2)}, u32[]{:S(2)}) collective-permute-start(bf16[128,768]{1,0:T(8,128)(2,1)S(1)} %collective-permute-done.1.refs_1_), channel_id=1, source_target_pairs={{0,32},{1,33},{2,34},{3,35},{4,36},{5,37},{6,38},{7,39},{8,40},{9,... | collective-permute-start | bytes 589832 | tf_op jit(solution)/shard_map/ppermute | solution.py:26
  28.9 6.5 %collective-permute-start.12 = (bf16[256,768]{1,0:T(8,128)(2,1)S(1)}, bf16[256,768]{1,0:T(8,128)(2,1)S(1)}, u32[]{:S(2)}, u32[]{:S(2)}) collective-permute-start(bf16[256,768]{1,0:T(8,128)(2,1)S(1)} %constant_dynamic-update-slice_fusion.refs_8_), channel_id=1, source_target_pairs={{0,8},{1,9},{2,10},{3,11},{4,12},{5,13},{6,14},{7,15},{8,0},{9,1},... | collective-permute-start | bytes 1179656 | tf_op jit(solution)/shard_map/ppermute | solution.py:26
  32.9 2.4 %collective-permute-start.14 = (bf16[256,768]{1,0:T(8,128)(2,1)S(1)}, bf16[256,768]{1,0:T(8,128)(2,1)S(1)}, u32[]{:S(2)}, u32[]{:S(2)}) collective-permute-start(bf16[256,768]{1,0:T(8,128)(2,1)S(1)} %collective-permute-done.5.refs_10_), channel_id=1, source_target_pairs={{0,8},{1,9},{2,10},{3,11},{4,12},{5,13},{6,14},{7,15},{8,0},{9,1},... | collective-permute-start | bytes 1179656 | tf_op jit(solution)/shard_map/ppermute | solution.py:26
  32.9 2.4 %collective-permute-start.13 = (bf16[256,768]{1,0:T(8,128)(2,1)S(1)}, bf16[256,768]{1,0:T(8,128)(2,1)S(1)}, u32[]{:S(2)}, u32[]{:S(2)}) collective-permute-start(bf16[256,768]{1,0:T(8,128)(2,1)S(1)} %collective-permute-done.4.refs_9_), channel_id=1, source_target_pairs={{0,8},{1,9},{2,10},{3,11},{4,12},{5,13},{6,14},{7,15},{8,0},{9,1},... | collective-permute-start | bytes 1179656 | tf_op jit(solution)/shard_map/ppermute | solution.py:26
  33.5 9.5 %collective-permute-start.10 = (bf16[256,768]{1,0:T(8,128)(2,1)S(1)}, bf16[256,768]{1,0:T(8,128)(2,1)S(1)}, u32[]{:S(2)}, u32[]{:S(2)}) collective-permute-start(bf16[256,768]{1,0:T(8,128)(2,1)S(1)} %broadcast_select_fusion), channel_id=1, source_target_pairs={{0,2},{1,3},{2,4},{3,5},{4,6},{5,7},{6,0},{7,1},{8,14},{9,15},{10,... | collective-permute-start | bytes 1179656 | tf_op jit(solution)/shard_map/ppermute | solution.py:318
  35.1 7.9 %collective-permute-start.11 = (bf16[128,768]{1,0:T(8,128)(2,1)S(1)}, bf16[128,768]{1,0:T(8,128)(2,1)S(1)}, u32[]{:S(2)}, u32[]{:S(2)}) collective-permute-start(bf16[128,768]{1,0:T(8,128)(2,1)S(1)} %broadcast_select_fusion.1), channel_id=1, source_target_pairs={{0,32},{1,33},{2,34},{3,35},{4,36},{5,37},{6,38},{7,39},{8,40},{9,... | collective-permute-start | bytes 589832 | tf_op jit(solution)/shard_map/ppermute | solution.py:328
  43.0 1.8 %collective-permute-start.15 = (bf16[256,768]{1,0:T(8,128)(2,1)S(1)}, bf16[256,768]{1,0:T(8,128)(2,1)S(1)}, u32[]{:S(2)}, u32[]{:S(2)}) collective-permute-start(bf16[256,768]{1,0:T(8,128)(2,1)S(1)} %collective-permute-done.10.refs_0_), channel_id=1, source_target_pairs={{0,8},{1,9},{2,10},{3,11},{4,12},{5,13},{6,14},{7,15},{8,0},{9,1},... | collective-permute-start | bytes 1179656 | tf_op jit(solution)/shard_map/ppermute | solution.py:26
  52.9 15.7 %collective-permute-start.16 = (bf16[256,768]{1,0:T(8,128)(2,1)S(1)}, bf16[256,768]{1,0:T(8,128)(2,1)}, u32[]{:S(2)}, u32[]{:S(2)}) collective-permute-start(bf16[256,768]{1,0:T(8,128)(2,1)S(1)} %get-tuple-element.64), channel_id=1, source_target_pairs={{0,224},{1,225},{2,226},{3,227},{4,228},{5,229},{6,230},{7,231},{8... | collective-permute-start | bytes 1179656 | tf_op jit(solution)/shard_map/ppermute | solution.py:26
  56.1 13.1 %collective-permute-start.17 = (bf16[256,768]{1,0:T(8,128)(2,1)S(1)}, bf16[256,768]{1,0:T(8,128)(2,1)S(1)}, u32[]{:S(2)}, u32[]{:S(2)}) collective-permute-start(bf16[256,768]{1,0:T(8,128)(2,1)S(1)} %get-tuple-element.65), channel_id=1, source_target_pairs={{0,32},{1,33},{2,34},{3,35},{4,36},{5,37},{6,38},{7,39},{8,40},{9,... | collective-permute-start | bytes 1179656 | tf_op jit(solution)/shard_map/ppermute | solution.py:26
  56.1 13.1 %collective-permute-start.18 = (bf16[256,768]{1,0:T(8,128)(2,1)S(1)}, bf16[256,768]{1,0:T(8,128)(2,1)}, u32[]{:S(2)}, u32[]{:S(2)}) collective-permute-start(bf16[256,768]{1,0:T(8,128)(2,1)S(1)} %get-tuple-element.66), channel_id=1, source_target_pairs={{0,8},{1,9},{2,10},{3,11},{4,12},{5,13},{6,14},{7,15},{8,0},{9,1},... | collective-permute-start | bytes 1179656 | tf_op jit(solution)/shard_map/ppermute | solution.py:26
  56.1 33.2 %collective-permute-start.19 = (bf16[256,768]{1,0:T(8,128)(2,1)S(1)}, bf16[256,768]{1,0:T(8,128)(2,1)S(1)}, u32[]{:S(2)}, u32[]{:S(2)}) collective-permute-start(bf16[256,768]{1,0:T(8,128)(2,1)S(1)} %get-tuple-element.78), channel_id=1, source_target_pairs={{0,8},{1,9},{2,10},{3,11},{4,12},{5,13},{6,14},{7,15},{8,0},{9,1},... | collective-permute-start | bytes 1179656 | tf_op jit(solution)/shard_map/ppermute | solution.py:26
  56.6 20.5 %collective-permute-start.20 = (bf16[256,768]{1,0:T(8,128)(2,1)S(1)}, bf16[256,768]{1,0:T(8,128)(2,1)S(1)}, u32[]{:S(2)}, u32[]{:S(2)}) collective-permute-start(bf16[256,768]{1,0:T(8,128)(2,1)S(1)} %get-tuple-element.80), channel_id=1, source_target_pairs={{0,8},{1,9},{2,10},{3,11},{4,12},{5,13},{6,14},{7,15},{8,0},{9,1},... | collective-permute-start | bytes 1179656 | tf_op jit(solution)/shard_map/ppermute | solution.py:26
  68.7 8.6 %collective-permute-start.23 = (bf16[256,768]{1,0:T(8,128)(2,1)S(1)}, bf16[256,768]{1,0:T(8,128)(2,1)S(1)}, u32[]{:S(2)}, u32[]{:S(2)}) collective-permute-start(bf16[256,768]{1,0:T(8,128)(2,1)S(1)} %get-tuple-element.84), channel_id=1, source_target_pairs={{0,8},{1,9},{2,10},{3,11},{4,12},{5,13},{6,14},{7,15},{8,0},{9,1},... | collective-permute-start | bytes 1179656 | tf_op jit(solution)/shard_map/ppermute | solution.py:26
  70.4 8.2 %collective-permute-start.21 = (bf16[256,768]{1,0:T(8,128)(2,1)S(1)}, bf16[256,768]{1,0:T(8,128)(2,1)S(1)}, u32[]{:S(2)}, u32[]{:S(2)}) collective-permute-start(bf16[256,768]{1,0:T(8,128)(2,1)S(1)} %add_convert_fusion.4), channel_id=1, source_target_pairs={{0,6},{1,7},{2,0},{3,1},{4,2},{5,3},{6,4},{7,5},{8,10},{9,11},{10,... | collective-permute-start | bytes 1179656 | tf_op jit(solution)/shard_map/ppermute | solution.py:318
  73.7 11.8 %collective-permute-start.27 = (bf16[256,768]{1,0:T(8,128)(2,1)S(1)}, bf16[256,768]{1,0:T(8,128)(2,1)S(1)}, u32[]{:S(2)}, u32[]{:S(2)}) collective-permute-start(bf16[256,768]{1,0:T(8,128)(2,1)S(1)} %add_convert_fusion), channel_id=1, source_target_pairs={{0,224},{1,225},{2,226},{3,227},{4,228},{5,229},{6,230},{7,231},{8... | collective-permute-start | bytes 1179656 | tf_op jit(solution)/shard_map/ppermute | solution.py:26
  77.1 21.4 %copy-start = (bf16[128,768]{1,0:T(8,128)(2,1)S(1)}, bf16[128,768]{1,0:T(8,128)(2,1)}, u32[]{:S(2)}) copy-start(bf16[128,768]{1,0:T(8,128)(2,1)} %embedding_ref.3) | copy-start | bytes 589828
  77.1 12.0 %collective-permute-start.26 = (bf16[256,768]{1,0:T(8,128)(2,1)S(1)}, bf16[256,768]{1,0:T(8,128)(2,1)S(1)}, u32[]{:S(2)}, u32[]{:S(2)}) collective-permute-start(bf16[256,768]{1,0:T(8,128)(2,1)S(1)} %add_convert_fusion.1), channel_id=1, source_target_pairs={{0,32},{1,33},{2,34},{3,35},{4,36},{5,37},{6,38},{7,39},{8,40},{9,... | collective-permute-start | bytes 1179656 | tf_op jit(solution)/shard_map/ppermute | solution.py:26
  78.9 20.6 %copy-start.1 = (bf16[128,768]{1,0:T(8,128)(2,1)S(1)}, bf16[128,768]{1,0:T(8,128)(2,1)}, u32[]{:S(2)}) copy-start(bf16[128,768]{1,0:T(8,128)(2,1)} %embedding_ref.2) | copy-start | bytes 589828
  78.9 10.6 %collective-permute-start.24 = (bf16[256,768]{1,0:T(8,128)(2,1)S(1)}, bf16[256,768]{1,0:T(8,128)(2,1)S(1)}, u32[]{:S(2)}, u32[]{:S(2)}) collective-permute-start(bf16[256,768]{1,0:T(8,128)(2,1)S(1)} %get-tuple-element.90), channel_id=1, source_target_pairs={{0,6},{1,7},{2,0},{3,1},{4,2},{5,3},{6,4},{7,5},{8,14},{9,15},{10,... | collective-permute-start | bytes 1179656 | tf_op jit(solution)/shard_map/ppermute | solution.py:26
  80.8 10.9 %collective-permute-start.22 = (bf16[256,768]{1,0:T(8,128)(2,1)S(1)}, bf16[256,768]{1,0:T(8,128)(2,1)S(1)}, u32[]{:S(2)}, u32[]{:S(2)}) collective-permute-start(bf16[256,768]{1,0:T(8,128)(2,1)S(1)} %get-tuple-element.91), channel_id=1, source_target_pairs={{0,2},{1,3},{2,4},{3,5},{4,6},{5,7},{6,0},{7,1},{8,10},{9,11},{10,... | collective-permute-start | bytes 1179656 | tf_op jit(solution)/shard_map/ppermute | solution.py:26
  89.2 9.3 %collective-permute-start.28 = (bf16[128,768]{1,0:T(8,128)(2,1)S(1)}, bf16[128,768]{1,0:T(8,128)(2,1)S(1)}, u32[]{:S(2)}, u32[]{:S(2)}) collective-permute-start(bf16[128,768]{1,0:T(8,128)(2,1)S(1)} %add_convert_fusion.5), channel_id=1, source_target_pairs={{0,16},{1,17},{2,18},{3,19},{4,20},{5,21},{6,22},{7,23},{8,24},{9,... | collective-permute-start | bytes 589832 | tf_op jit(solution)/shard_map/ppermute | solution.py:26
  91.8 7.8 %collective-permute-start.25 = (bf16[128,768]{1,0:T(8,128)(2,1)S(1)}, bf16[128,768]{1,0:T(8,128)(2,1)S(1)}, u32[]{:S(2)}, u32[]{:S(2)}) collective-permute-start(bf16[128,768]{1,0:T(8,128)(2,1)S(1)} %add_convert_fusion.6), channel_id=1, source_target_pairs={{0,1},{1,0},{2,3},{3,2},{4,5},{5,4},{6,7},{7,6},{8,9},{9,8},{10,11... | collective-permute-start | bytes 589832 | tf_op jit(solution)/shard_map/ppermute | solution.py:26
  (10 other events, 33.4 us)

commit v4 on v3

--- a/solution.py
+++ b/solution.py
@@ -45,7 +45,7 @@
 
 
 def unit_low(video, text):
-    shape = jax.ShapeDtypeStruct(video.shape, jnp.bfloat16)
+    shape = pltpu.VMEM(video.shape, jnp.bfloat16)
     return pl.pallas_call(unit_kernel, out_shape=(shape, shape), name="unit_low")(video, text)
 
 
@@ -115,26 +115,27 @@
             place += block.shape[0]
     for copy in copies:
         copy.start()
-    for copy in copies:
-        copy.wait()
     core = place_ref[0]
     tile = video.shape[0] // 2
     row = lax.broadcasted_iota(jnp.int32, (tile, PAIR), 0)
     column = lax.broadcasted_iota(jnp.int32, (tile, PAIR), 1)
     same = (row == column) & (row < PAIR // 2)
 
-    @pl.loop(0, 2)
-    def _(step):
-        rows = tile_rows(step, tile)
+    for step in range(2):
+        for copy in copies[8 + 3 * step : 11 + 3 * step]:
+            copy.wait()
+        rows = pl.ds(step * tile, tile)
         video_tile = video[rows, :]
-        own = step == 0
         for i in range(4):
+            if step == 0:
+                copies[2 * i].wait()
+                copies[2 * i + 1].wait()
             columns = pl.ds(i * PAIR, PAIR)
             weight = pair_weight(scale_ref, offset_ref, video_tile, text[columns, :])
-            if i == 0:
-                weight = weight - jnp.where(same, jnp.where(own, 1.0, 0.0), 0.0)
-            elif i == 3:
-                weight = weight * edge_mask(core, own)
+            if i == 0 and step == 0:
+                weight = weight - jnp.where(same, 1.0, 0.0)
+            elif i == 3 and step == 1:
+                weight = weight * edge_mask(core, False)
             weights[rows, columns] = weight.astype(jnp.bfloat16)
 
 
@@ -209,7 +210,7 @@
 
 
 def low(rows, columns=D):
-    return jax.ShapeDtypeStruct((rows, columns), jnp.bfloat16)
+    return pltpu.VMEM((rows, columns), jnp.bfloat16)
 
 
 def cost(flops, transcendentals=0):

time: 101 us -> 102 us (level)
    pallas_call x3, Pallas kernels: 18.2 us -> 19.7 us  [call(): pl.pallas_call(kernel, out_shape=outs, in_specs=[SMEM] * len(scalars) + [...]
    unnamed x27 -> x25, local copies, waits for them, and re-layouts: 10.4 us -> 9.45 us
  transfers between devices with their start and end apart: 29 -> 29, of which waited for: 14 -> 13; matrix products, arithmetic and copies ran while one was open for 4% -> 3% of each run, Pallas kernels for 13% -> 14%
where the time goes in v4:
time: 102 us; the launch traced here: 101 us
  starting transfers between devices  33.6 us (33%)
  waiting for transfers between devices  30.1 us (30%)
  Pallas kernels  23 us (23%)
  local copies, waits for them, and re-layouts  9.47 us (9%)
  other arithmetic  2.9 us (3%)
  between operations  2.21 us (2%)
    ppermute x26, starting transfers between devices, move(): return lax.ppermute(block, AXES, pairs)  29.5 us
    ppermute x26, waiting for transfers between devices, move(): return lax.ppermute(block, AXES, pairs)  28.8 us
    pallas_call x3, Pallas kernels, call(): pl.pallas_call(kernel, out_shape=outs, in_specs=[SMEM] * len(scalars) + [...  19.7 us
    unnamed x25, local copies, waits for them, and re-layouts  9.45 us
    ppermute x2, starting transfers between devices, move_by_core(): return lax.ppermute(block, AXES, pairs)  3.83 us
    convert_element_type x6, other arithmetic, add(): return total.astype(jnp.bfloat16)  2.76 us
    pallas_call x2, Pallas kernels, back_rows(): pl.pallas_call(back_kernel, out_shape=jax.ShapeDtypeStruct(embedding.shap...  2.05 us
  transfers between devices with their start and end apart: 29, of which 13 were waited for; matrix products, arithmetic and copies ran while one was open for 3% of the time, Pallas kernels for 14%

profile of v4, /device:TPU:2, one launch (start us, length us, event | category | flops | bytes accessed | tf_op | source)
XLA Modules:
  0.0 101.3 jit_solution(6577894628631515022)
XLA Ops:
  0.6 1.2 %unit_low.1 = (bf16[128,768]{1,0:T(8,128)(2,1)S(1)}, bf16[128,768]{1,0:T(8,128)(2,1)S(1)}) custom-call(bf16[128,768]{1,0:T(8,128)(2,1)} %embedding_ref.2, bf16[128,768]{1,0:T(8,128)(2,1)} %embedding_ref.3), custom_call_target="tpu_custom_call" | custom-call | tf_op jit(solution)/shard_map/unit_low/pallas_call | solution.py:49
  1.8 1.7 %collective-permute-start = (bf16[128,768]{1,0:T(8,128)(2,1)S(1)}, bf16[128,768]{1,0:T(8,128)(2,1)S(1)}, u32[]{:S(2)}, u32[]{:S(2)}) collective-permute-start(bf16[128,768]{1,0:T(8,128)(2,1)S(1)} %get-tuple-element.46), channel_id=1, source_target_pairs={{0,1},{1,0},{2,3},{3,2},{4,5},{5,4},{6,7},{7,6},{8,9},{9,8},{10,11... | collective-permute-start | bytes 589832 | tf_op jit(solution)/shard_map/ppermute | solution.py:26
  3.5 5.9 %collective-permute-start.3 = (bf16[128,768]{1,0:T(8,128)(2,1)S(1)}, bf16[128,768]{1,0:T(8,128)(2,1)S(1)}, u32[]{:S(2)}, u32[]{:S(2)}) collective-permute-start(bf16[128,768]{1,0:T(8,128)(2,1)S(1)} %get-tuple-element.47.refs_0_), channel_id=1, source_target_pairs={{0,224},{1,225},{2,226},{3,227},{4,228},{5,229},{6,230},{7,231},{8... | collective-permute-start | bytes 589832 | tf_op jit(solution)/shard_map/ppermute | solution.py:26
  9.3 2.9 %collective-permute-start.1 = (bf16[128,768]{1,0:T(8,128)(2,1)S(1)}, bf16[128,768]{1,0:T(8,128)(2,1)S(1)}, u32[]{:S(2)}, u32[]{:S(2)}) collective-permute-start(bf16[128,768]{1,0:T(8,128)(2,1)S(1)} %get-tuple-element.47.refs_0_), channel_id=1, source_target_pairs={{0,16},{1,17},{2,18},{3,19},{4,20},{5,21},{6,22},{7,23},{8,24},{9,... | collective-permute-start | bytes 589832 | tf_op jit(solution)/shard_map/ppermute | solution.py:26
  13.2 3.4 %collective-permute-done.2.refs_2_ = bf16[128,768]{1,0:T(8,128)(2,1)S(1)} collective-permute-done((bf16[128,768]{1,0:T(8,128)(2,1)S(1)}, bf16[128,768]{1,0:T(8,128)(2,1)S(1)}, u32[]{:S(2)}, u32[]{:S(2)}) %collective-permute-start.2) | collective-permute-done | bytes 196640 | tf_op jit(solution)/shard_map/ppermute | solution.py:26
  17.8 1.5 %collective-permute-start.4 = (bf16[256,768]{1,0:T(8,128)(2,1)S(1)}, bf16[256,768]{1,0:T(8,128)(2,1)S(1)}, u32[]{:S(2)}, u32[]{:S(2)}) collective-permute-start(bf16[256,768]{1,0:T(8,128)(2,1)S(1)} %constant_dynamic-update-slice_fusion.refs_8_), channel_id=1, source_target_pairs={{0,2},{1,3},{2,4},{3,5},{4,6},{5,7},{6,0},{7,1},{8,10},{9,11},{10,... | collective-permute-start | bytes 1179656 | tf_op jit(solution)/shard_map/ppermute | solution.py:26
  19.2 3.9 %collective-permute-start.9 = (bf16[128,768]{1,0:T(8,128)(2,1)S(1)}, bf16[128,768]{1,0:T(8,128)(2,1)S(1)}, u32[]{:S(2)}, u32[]{:S(2)}) collective-permute-start(bf16[128,768]{1,0:T(8,128)(2,1)S(1)} %collective-permute-done.3.refs_4_), channel_id=1, source_target_pairs={{0,224},{1,225},{2,226},{3,227},{4,228},{5,229},{6,230},{7,231},{8... | collective-permute-start | bytes 589832 | tf_op jit(solution)/shard_map/ppermute | solution.py:26
  23.2 2.0 %collective-permute-start.7 = (bf16[128,768]{1,0:T(8,128)(2,1)S(1)}, bf16[128,768]{1,0:T(8,128)(2,1)S(1)}, u32[]{:S(2)}, u32[]{:S(2)}) collective-permute-start(bf16[128,768]{1,0:T(8,128)(2,1)S(1)} %collective-permute-done.1.refs_1_), channel_id=1, source_target_pairs={{0,224},{1,225},{2,226},{3,227},{4,228},{5,229},{6,230},{7,231},{8... | collective-permute-start | bytes 589832 | tf_op jit(solution)/shard_map/ppermute | solution.py:26
  26.6 1.4 %collective-permute-done.9.refs_7_ = bf16[128,768]{1,0:T(8,128)(2,1)S(1)} collective-permute-done((bf16[128,768]{1,0:T(8,128)(2,1)S(1)}, bf16[128,768]{1,0:T(8,128)(2,1)S(1)}, u32[]{:S(2)}, u32[]{:S(2)}) %collective-permute-start.9) | collective-permute-done | bytes 196640 | tf_op jit(solution)/shard_map/ppermute | solution.py:26
  28.0 2.1 %collective-permute-done.7.refs_5_ = bf16[128,768]{1,0:T(8,128)(2,1)S(1)} collective-permute-done((bf16[128,768]{1,0:T(8,128)(2,1)S(1)}, bf16[128,768]{1,0:T(8,128)(2,1)S(1)}, u32[]{:S(2)}, u32[]{:S(2)}) %collective-permute-start.7) | collective-permute-done | bytes 196640 | tf_op jit(solution)/shard_map/ppermute | solution.py:26
  30.1 2.0 %collective-permute-done.6.refs_3_ = bf16[128,768]{1,0:T(8,128)(2,1)S(1)} collective-permute-done((bf16[128,768]{1,0:T(8,128)(2,1)S(1)}, bf16[128,768]{1,0:T(8,128)(2,1)S(1)}, u32[]{:S(2)}, u32[]{:S(2)}) %collective-permute-start.6) | collective-permute-done | bytes 196640 | tf_op jit(solution)/shard_map/ppermute | solution.py:26
  32.7 1.6 %collective-permute-start.10 = (bf16[256,768]{1,0:T(8,128)(2,1)S(1)}, bf16[256,768]{1,0:T(8,128)(2,1)S(1)}, u32[]{:S(2)}, u32[]{:S(2)}) collective-permute-start(bf16[256,768]{1,0:T(8,128)(2,1)S(1)} %broadcast_select_fusion), channel_id=1, source_target_pairs={{0,2},{1,3},{2,4},{3,5},{4,6},{5,7},{6,0},{7,1},{8,14},{9,15},{10,... | collective-permute-start | bytes 1179656 | tf_op jit(solution)/shard_map/ppermute | solution.py:319
  34.6 9.0 %near_weights.1 = (bf16[1536,1024]{1,0:T(8,128)(2,1)S(1)}, bf16[1024,768]{1,0:T(8,128)(2,1)S(1)}, bf16[1536,768]{1,0:T(8,128)(2,1)S(1)}) custom-call(f32[1]{0:T(128)S(6)} %copy.7.scale_ref, f32[1]{0:T(128)S(6)} %copy.8.offset_ref, s32[2]{0:T(128)S(1)} %pad_add_fusion.place_ref, bf16[128,768]{1,0:T(8,128)(2,1)S(1)} %get-tuple-element.47.refs_0_, ...), custom_call_target="tpu_custom_call" | custom-call | flops 2415919104 | tf_op jit(solution)/shard_map/near_weights/pallas_call | solution.py:221
  43.7 1.7 %collective-permute-done.15.refs_1_ = bf16[256,768]{1,0:T(8,128)(2,1)S(1)} collective-permute-done((bf16[256,768]{1,0:T(8,128)(2,1)S(1)}, bf16[256,768]{1,0:T(8,128)(2,1)S(1)}, u32[]{:S(2)}, u32[]{:S(2)}) %collective-permute-start.15) | collective-permute-done | bytes 393248 | tf_op jit(solution)/shard_map/ppermute | solution.py:26
  45.4 6.1 %far_weights_and_sums.1 = (bf16[1536,128]{1,0:T(8,128)(2,1)S(1)}, bf16[512,1152]{1,0:T(8,128)(2,1)S(1)}, bf16[512,768]{1,0:T(8,128)(2,1)S(1)}, bf16[256,768]{1,0...) custom-call(f32[1]{0:T(128)S(6)} %copy.7.scale_ref, ...), custom_call_target="tpu_custom_call" | custom-call | flops 5033164800 | tf_op jit(solution)/shard_map/far_weights_and_sums/pallas_call | solution.py:221
  51.6 1.1 %copy-done.8 = bf16[512,1152]{1,0:T(8,128)(2,1)} copy-done((bf16[512,1152]{1,0:T(8,128)(2,1)}, bf16[512,1152]{1,0:T(8,128)(2,1)S(1)}, u32[]{:S(2)}) %copy-start.8) | copy-done | bytes 1179672
  53.6 3.2 %collective-permute-start.16 = (bf16[256,768]{1,0:T(8,128)(2,1)S(1)}, bf16[256,768]{1,0:T(8,128)(2,1)}, u32[]{:S(2)}, u32[]{:S(2)}) collective-permute-start(bf16[256,768]{1,0:T(8,128)(2,1)S(1)} %get-tuple-element.64), channel_id=1, source_target_pairs={{0,224},{1,225},{2,226},{3,227},{4,228},{5,229},{6,230},{7,231},{8... | collective-permute-start | bytes 1179656 | tf_op jit(solution)/shard_map/ppermute | solution.py:26
  57.4 1.9 %copy-done.3 = bf16[1536,1024]{1,0:T(8,128)(2,1)S(1)} copy-done((bf16[1536,1024]{1,0:T(8,128)(2,1)S(1)}, bf16[1536,1024]{1,0:T(8,128)(2,1)}, u32[]{:S(2)}) %copy-start.3) | copy-done | bytes 3145752
  59.3 1.7 %copy-done.5 = bf16[1536,768]{1,0:T(8,128)(2,1)S(1)} copy-done((bf16[1536,768]{1,0:T(8,128)(2,1)S(1)}, bf16[1536,768]{1,0:T(8,128)(2,1)}, u32[]{:S(2)}) %copy-start.5) | copy-done | bytes 2359320
  60.9 1.4 %copy-done.7 = bf16[1024,768]{1,0:T(8,128)(2,1)S(1)} copy-done((bf16[1024,768]{1,0:T(8,128)(2,1)S(1)}, bf16[1024,768]{1,0:T(8,128)(2,1)}, u32[]{:S(2)}) %copy-start.7) | copy-done | bytes 1572888
  62.3 1.3 %copy-done.9 = bf16[512,1152]{1,0:T(8,128)(2,1)S(1)} copy-done((bf16[512,1152]{1,0:T(8,128)(2,1)S(1)}, bf16[512,1152]{1,0:T(8,128)(2,1)}, u32[]{:S(2)}) %copy-start.9) | copy-done | bytes 1179672
  63.6 1.1 %copy-done.11 = bf16[512,768]{1,0:T(8,128)(2,1)S(1)} copy-done((bf16[512,768]{1,0:T(8,128)(2,1)S(1)}, bf16[512,768]{1,0:T(8,128)(2,1)}, u32[]{:S(2)}) %copy-start.11) | copy-done | bytes 786456
  64.7 4.6 %own_video_and_near_text_sums.1 = (bf16[256,768]{1,0:T(8,128)(2,1)S(1)}, bf16[256,768]{1,0:T(8,128)(2,1)S(1)}, bf16[256,768]{1,0:T(8,128)(2,1)S(1)}, bf16[256,76...) custom-call(bf16[1536,1024]{1,0:T(8,128)(2,1)S(1)} %copy-done.3, ...), custom_call_target="tpu_custom_call" | custom-call | flops 4026531840 | tf_op jit(solution)/shard_map/own_video_and_near_text_sums/pallas_call | solution.py:221
  70.0 1.1 %add_convert_fusion.4 = bf16[256,768]{1,0:T(8,128)(2,1)S(1)} fusion(bf16[256,768]{1,0:T(8,128)(2,1)} %collective-permute-done.18, bf16[256,768]{1,0:T(8,128)(2,1)S(1)} %get-tuple-element.81), kind=kLoop, calls=%fused_computation.4 | loop fusion | flops 786432 | bytes 1179648 | tf_op jit(solution)/shard_map/convert_element_type | solution.py:33
  71.1 2.3 %collective-permute-start.21 = (bf16[256,768]{1,0:T(8,128)(2,1)S(1)}, bf16[256,768]{1,0:T(8,128)(2,1)S(1)}, u32[]{:S(2)}, u32[]{:S(2)}) collective-permute-start(bf16[256,768]{1,0:T(8,128)(2,1)S(1)} %add_convert_fusion.4), channel_id=1, source_target_pairs={{0,6},{1,7},{2,0},{3,1},{4,2},{5,3},{6,4},{7,5},{8,10},{9,11},{10,... | collective-permute-start | bytes 1179656 | tf_op jit(solution)/shard_map/ppermute | solution.py:319
  74.4 3.3 %collective-permute-start.27 = (bf16[256,768]{1,0:T(8,128)(2,1)S(1)}, bf16[256,768]{1,0:T(8,128)(2,1)S(1)}, u32[]{:S(2)}, u32[]{:S(2)}) collective-permute-start(bf16[256,768]{1,0:T(8,128)(2,1)S(1)} %add_convert_fusion), channel_id=1, source_target_pairs={{0,224},{1,225},{2,226},{3,227},{4,228},{5,229},{6,230},{7,231},{8... | collective-permute-start | bytes 1179656 | tf_op jit(solution)/shard_map/ppermute | solution.py:26
  77.9 1.4 %collective-permute-done.21 = bf16[256,768]{1,0:T(8,128)(2,1)S(1)} collective-permute-done((bf16[256,768]{1,0:T(8,128)(2,1)S(1)}, bf16[256,768]{1,0:T(8,128)(2,1)S(1)}, u32[]{:S(2)}, u32[]{:S(2)}) %collective-permute-start.21) | collective-permute-done | bytes 393248 | tf_op jit(solution)/shard_map/ppermute | solution.py:319
  79.6 1.9 %collective-permute-start.24 = (bf16[256,768]{1,0:T(8,128)(2,1)S(1)}, bf16[256,768]{1,0:T(8,128)(2,1)S(1)}, u32[]{:S(2)}, u32[]{:S(2)}) collective-permute-start(bf16[256,768]{1,0:T(8,128)(2,1)S(1)} %get-tuple-element.90), channel_id=1, source_target_pairs={{0,6},{1,7},{2,0},{3,1},{4,2},{5,3},{6,4},{7,5},{8,14},{9,15},{10,... | collective-permute-start | bytes 1179656 | tf_op jit(solution)/shard_map/ppermute | solution.py:26
  81.8 4.4 %collective-permute-done.27.refs_2_ = bf16[256,768]{1,0:T(8,128)(2,1)S(1)} collective-permute-done((bf16[256,768]{1,0:T(8,128)(2,1)S(1)}, bf16[256,768]{1,0:T(8,128)(2,1)S(1)}, u32[]{:S(2)}, u32[]{:S(2)}) %collective-permute-start.27) | collective-permute-done | bytes 393248 | tf_op jit(solution)/shard_map/ppermute | solution.py:26
  86.2 3.6 %collective-permute-done.26.refs_1_ = bf16[256,768]{1,0:T(8,128)(2,1)S(1)} collective-permute-done((bf16[256,768]{1,0:T(8,128)(2,1)S(1)}, bf16[256,768]{1,0:T(8,128)(2,1)S(1)}, u32[]{:S(2)}, u32[]{:S(2)}) %collective-permute-start.26) | collective-permute-done | bytes 393248 | tf_op jit(solution)/shard_map/ppermute | solution.py:26
  90.2 2.2 %collective-permute-done.22.refs_2_ = bf16[256,768]{1,0:T(8,128)(2,1)S(1)} collective-permute-done((bf16[256,768]{1,0:T(8,128)(2,1)S(1)}, bf16[256,768]{1,0:T(8,128)(2,1)S(1)}, u32[]{:S(2)}, u32[]{:S(2)}) %collective-permute-start.22) | collective-permute-done | bytes 393248 | tf_op jit(solution)/shard_map/ppermute | solution.py:26
  92.7 6.5 %collective-permute-done.28.refs_3_ = bf16[128,768]{1,0:T(8,128)(2,1)S(1)} collective-permute-done((bf16[128,768]{1,0:T(8,128)(2,1)S(1)}, bf16[128,768]{1,0:T(8,128)(2,1)S(1)}, u32[]{:S(2)}, u32[]{:S(2)}) %collective-permute-start.28) | collective-permute-done | bytes 196640 | tf_op jit(solution)/shard_map/ppermute | solution.py:26
  (67 shorter events, 9.8 us)
Async XLA Ops:
  1.8 10.4 %collective-permute-start = (bf16[128,768]{1,0:T(8,128)(2,1)S(1)}, bf16[128,768]{1,0:T(8,128)(2,1)S(1)}, u32[]{:S(2)}, u32[]{:S(2)}) collective-permute-start(bf16[128,768]{1,0:T(8,128)(2,1)S(1)} %get-tuple-element.46), channel_id=1, source_target_pairs={{0,1},{1,0},{2,3},{3,2},{4,5},{5,4},{6,7},{7,6},{8,9},{9,8},{10,11... | collective-permute-start | bytes 589832 | tf_op jit(solution)/shard_map/ppermute | solution.py:26
  3.5 9.7 %collective-permute-start.3 = (bf16[128,768]{1,0:T(8,128)(2,1)S(1)}, bf16[128,768]{1,0:T(8,128)(2,1)S(1)}, u32[]{:S(2)}, u32[]{:S(2)}) collective-permute-start(bf16[128,768]{1,0:T(8,128)(2,1)S(1)} %get-tuple-element.47.refs_0_), channel_id=1, source_target_pairs={{0,224},{1,225},{2,226},{3,227},{4,228},{5,229},{6,230},{7,231},{8... | collective-permute-start | bytes 589832 | tf_op jit(solution)/shard_map/ppermute | solution.py:26
  9.3 7.3 %collective-permute-start.2 = (bf16[128,768]{1,0:T(8,128)(2,1)S(1)}, bf16[128,768]{1,0:T(8,128)(2,1)S(1)}, u32[]{:S(2)}, u32[]{:S(2)}) collective-permute-start(bf16[128,768]{1,0:T(8,128)(2,1)S(1)} %get-tuple-element.47.refs_0_), channel_id=1, source_target_pairs={{0,32},{1,33},{2,34},{3,35},{4,36},{5,37},{6,38},{7,39},{8,40},{9,... | collective-permute-start | bytes 589832 | tf_op jit(solution)/shard_map/ppermute | solution.py:26
  9.3 7.6 %collective-permute-start.1 = (bf16[128,768]{1,0:T(8,128)(2,1)S(1)}, bf16[128,768]{1,0:T(8,128)(2,1)S(1)}, u32[]{:S(2)}, u32[]{:S(2)}) collective-permute-start(bf16[128,768]{1,0:T(8,128)(2,1)S(1)} %get-tuple-element.47.refs_0_), channel_id=1, source_target_pairs={{0,16},{1,17},{2,18},{3,19},{4,20},{5,21},{6,22},{7,23},{8,24},{9,... | collective-permute-start | bytes 589832 | tf_op jit(solution)/shard_map/ppermute | solution.py:26
  16.9 8.3 %collective-permute-start.8 = (bf16[128,768]{1,0:T(8,128)(2,1)S(1)}, bf16[128,768]{1,0:T(8,128)(2,1)S(1)}, u32[]{:S(2)}, u32[]{:S(2)}) collective-permute-start(bf16[128,768]{1,0:T(8,128)(2,1)S(1)} %collective-permute-done.2.refs_2_), channel_id=1, source_target_pairs={{0,32},{1,33},{2,34},{3,35},{4,36},{5,37},{6,38},{7,39},{8,40},{9,... | collective-permute-start | bytes 589832 | tf_op jit(solution)/shard_map/ppermute | solution.py:26
  17.1 15.0 %collective-permute-start.5 = (bf16[256,768]{1,0:T(8,128)(2,1)S(1)}, bf16[256,768]{1,0:T(8,128)(2,1)S(1)}, u32[]{:S(2)}, u32[]{:S(2)}) collective-permute-start(bf16[256,768]{1,0:T(8,128)(2,1)S(1)} %constant_dynamic-update-slice_fusion.refs_8_), channel_id=1, source_target_pairs={{0,6},{1,7},{2,0},{3,1},{4,2},{5,3},{6,4},{7,5},{8,14},{9,15},{10,... | collective-permute-start | bytes 1179656 | tf_op jit(solution)/shard_map/ppermute | solution.py:26
  17.8 14.3 %collective-permute-start.4 = (bf16[256,768]{1,0:T(8,128)(2,1)S(1)}, bf16[256,768]{1,0:T(8,128)(2,1)S(1)}, u32[]{:S(2)}, u32[]{:S(2)}) collective-permute-start(bf16[256,768]{1,0:T(8,128)(2,1)S(1)} %constant_dynamic-update-slice_fusion.refs_8_), channel_id=1, source_target_pairs={{0,2},{1,3},{2,4},{3,5},{4,6},{5,7},{6,0},{7,1},{8,10},{9,11},{10,... | collective-permute-start | bytes 1179656 | tf_op jit(solution)/shard_map/ppermute | solution.py:26
  19.2 8.8 %collective-permute-start.9 = (bf16[128,768]{1,0:T(8,128)(2,1)S(1)}, bf16[128,768]{1,0:T(8,128)(2,1)S(1)}, u32[]{:S(2)}, u32[]{:S(2)}) collective-permute-start(bf16[128,768]{1,0:T(8,128)(2,1)S(1)} %collective-permute-done.3.refs_4_), channel_id=1, source_target_pairs={{0,224},{1,225},{2,226},{3,227},{4,228},{5,229},{6,230},{7,231},{8... | collective-permute-start | bytes 589832 | tf_op jit(solution)/shard_map/ppermute | solution.py:26
  23.2 6.9 %collective-permute-start.7 = (bf16[128,768]{1,0:T(8,128)(2,1)S(1)}, bf16[128,768]{1,0:T(8,128)(2,1)S(1)}, u32[]{:S(2)}, u32[]{:S(2)}) collective-permute-start(bf16[128,768]{1,0:T(8,128)(2,1)S(1)} %collective-permute-done.1.refs_1_), channel_id=1, source_target_pairs={{0,224},{1,225},{2,226},{3,227},{4,228},{5,229},{6,230},{7,231},{8... | collective-permute-start | bytes 589832 | tf_op jit(solution)/shard_map/ppermute | solution.py:26
  25.2 6.9 %collective-permute-start.6 = (bf16[128,768]{1,0:T(8,128)(2,1)S(1)}, bf16[128,768]{1,0:T(8,128)(2,1)S(1)}, u32[]{:S(2)}, u32[]{:S(2)}) collective-permute-start(bf16[128,768]{1,0:T(8,128)(2,1)S(1)} %collective-permute-done.1.refs_1_), channel_id=1, source_target_pairs={{0,32},{1,33},{2,34},{3,35},{4,36},{5,37},{6,38},{7,39},{8,40},{9,... | collective-permute-start | bytes 589832 | tf_op jit(solution)/shard_map/ppermute | solution.py:26
  28.0 6.5 %collective-permute-start.12 = (bf16[256,768]{1,0:T(8,128)(2,1)S(1)}, bf16[256,768]{1,0:T(8,128)(2,1)S(1)}, u32[]{:S(2)}, u32[]{:S(2)}) collective-permute-start(bf16[256,768]{1,0:T(8,128)(2,1)S(1)} %constant_dynamic-update-slice_fusion.refs_8_), channel_id=1, source_target_pairs={{0,8},{1,9},{2,10},{3,11},{4,12},{5,13},{6,14},{7,15},{8,0},{9,1},... | collective-permute-start | bytes 1179656 | tf_op jit(solution)/shard_map/ppermute | solution.py:26
  32.1 2.4 %collective-permute-start.14 = (bf16[256,768]{1,0:T(8,128)(2,1)S(1)}, bf16[256,768]{1,0:T(8,128)(2,1)S(1)}, u32[]{:S(2)}, u32[]{:S(2)}) collective-permute-start(bf16[256,768]{1,0:T(8,128)(2,1)S(1)} %collective-permute-done.5.refs_10_), channel_id=1, source_target_pairs={{0,8},{1,9},{2,10},{3,11},{4,12},{5,13},{6,14},{7,15},{8,0},{9,1},... | collective-permute-start | bytes 1179656 | tf_op jit(solution)/shard_map/ppermute | solution.py:26
  32.1 2.4 %collective-permute-start.13 = (bf16[256,768]{1,0:T(8,128)(2,1)S(1)}, bf16[256,768]{1,0:T(8,128)(2,1)S(1)}, u32[]{:S(2)}, u32[]{:S(2)}) collective-permute-start(bf16[256,768]{1,0:T(8,128)(2,1)S(1)} %collective-permute-done.4.refs_9_), channel_id=1, source_target_pairs={{0,8},{1,9},{2,10},{3,11},{4,12},{5,13},{6,14},{7,15},{8,0},{9,1},... | collective-permute-start | bytes 1179656 | tf_op jit(solution)/shard_map/ppermute | solution.py:26
  32.7 10.9 %collective-permute-start.10 = (bf16[256,768]{1,0:T(8,128)(2,1)S(1)}, bf16[256,768]{1,0:T(8,128)(2,1)S(1)}, u32[]{:S(2)}, u32[]{:S(2)}) collective-permute-start(bf16[256,768]{1,0:T(8,128)(2,1)S(1)} %broadcast_select_fusion), channel_id=1, source_target_pairs={{0,2},{1,3},{2,4},{3,5},{4,6},{5,7},{6,0},{7,1},{8,14},{9,15},{10,... | collective-permute-start | bytes 1179656 | tf_op jit(solution)/shard_map/ppermute | solution.py:319
  34.3 9.3 %collective-permute-start.11 = (bf16[128,768]{1,0:T(8,128)(2,1)S(1)}, bf16[128,768]{1,0:T(8,128)(2,1)S(1)}, u32[]{:S(2)}, u32[]{:S(2)}) collective-permute-start(bf16[128,768]{1,0:T(8,128)(2,1)S(1)} %broadcast_select_fusion.1), channel_id=1, source_target_pairs={{0,32},{1,33},{2,34},{3,35},{4,36},{5,37},{6,38},{7,39},{8,40},{9,... | collective-permute-start | bytes 589832 | tf_op jit(solution)/shard_map/ppermute | solution.py:329
  43.6 8.0 %copy-start.2 = (bf16[1536,1024]{1,0:T(8,128)(2,1)}, bf16[1536,1024]{1,0:T(8,128)(2,1)S(1)}, u32[]{:S(2)}) copy-start(bf16[1536,1024]{1,0:T(8,128)(2,1)S(1)} %get-tuple-element.59.near) | copy-start | bytes 9437188
  43.6 1.8 %collective-permute-start.15 = (bf16[256,768]{1,0:T(8,128)(2,1)S(1)}, bf16[256,768]{1,0:T(8,128)(2,1)S(1)}, u32[]{:S(2)}, u32[]{:S(2)}) collective-permute-start(bf16[256,768]{1,0:T(8,128)(2,1)S(1)} %collective-permute-done.10.refs_0_), channel_id=1, source_target_pairs={{0,8},{1,9},{2,10},{3,11},{4,12},{5,13},{6,14},{7,15},{8,0},{9,1},... | collective-permute-start | bytes 1179656 | tf_op jit(solution)/shard_map/ppermute | solution.py:26
  53.6 15.7 %collective-permute-start.16 = (bf16[256,768]{1,0:T(8,128)(2,1)S(1)}, bf16[256,768]{1,0:T(8,128)(2,1)}, u32[]{:S(2)}, u32[]{:S(2)}) collective-permute-start(bf16[256,768]{1,0:T(8,128)(2,1)S(1)} %get-tuple-element.64), channel_id=1, source_target_pairs={{0,224},{1,225},{2,226},{3,227},{4,228},{5,229},{6,230},{7,231},{8... | collective-permute-start | bytes 1179656 | tf_op jit(solution)/shard_map/ppermute | solution.py:26
  56.8 13.1 %collective-permute-start.17 = (bf16[256,768]{1,0:T(8,128)(2,1)S(1)}, bf16[256,768]{1,0:T(8,128)(2,1)S(1)}, u32[]{:S(2)}, u32[]{:S(2)}) collective-permute-start(bf16[256,768]{1,0:T(8,128)(2,1)S(1)} %get-tuple-element.65), channel_id=1, source_target_pairs={{0,32},{1,33},{2,34},{3,35},{4,36},{5,37},{6,38},{7,39},{8,40},{9,... | collective-permute-start | bytes 1179656 | tf_op jit(solution)/shard_map/ppermute | solution.py:26
  56.8 13.1 %collective-permute-start.18 = (bf16[256,768]{1,0:T(8,128)(2,1)S(1)}, bf16[256,768]{1,0:T(8,128)(2,1)}, u32[]{:S(2)}, u32[]{:S(2)}) collective-permute-start(bf16[256,768]{1,0:T(8,128)(2,1)S(1)} %get-tuple-element.66), channel_id=1, source_target_pairs={{0,8},{1,9},{2,10},{3,11},{4,12},{5,13},{6,14},{7,15},{8,0},{9,1},... | collective-permute-start | bytes 1179656 | tf_op jit(solution)/shard_map/ppermute | solution.py:26
  56.8 33.2 %collective-permute-start.19 = (bf16[256,768]{1,0:T(8,128)(2,1)S(1)}, bf16[256,768]{1,0:T(8,128)(2,1)S(1)}, u32[]{:S(2)}, u32[]{:S(2)}) collective-permute-start(bf16[256,768]{1,0:T(8,128)(2,1)S(1)} %get-tuple-element.78), channel_id=1, source_target_pairs={{0,8},{1,9},{2,10},{3,11},{4,12},{5,13},{6,14},{7,15},{8,0},{9,1},... | collective-permute-start | bytes 1179656 | tf_op jit(solution)/shard_map/ppermute | solution.py:26
  57.4 20.5 %collective-permute-start.20 = (bf16[256,768]{1,0:T(8,128)(2,1)S(1)}, bf16[256,768]{1,0:T(8,128)(2,1)S(1)}, u32[]{:S(2)}, u32[]{:S(2)}) collective-permute-start(bf16[256,768]{1,0:T(8,128)(2,1)S(1)} %get-tuple-element.80), channel_id=1, source_target_pairs={{0,8},{1,9},{2,10},{3,11},{4,12},{5,13},{6,14},{7,15},{8,0},{9,1},... | collective-permute-start | bytes 1179656 | tf_op jit(solution)/shard_map/ppermute | solution.py:26
  69.4 8.6 %collective-permute-start.23 = (bf16[256,768]{1,0:T(8,128)(2,1)S(1)}, bf16[256,768]{1,0:T(8,128)(2,1)S(1)}, u32[]{:S(2)}, u32[]{:S(2)}) collective-permute-start(bf16[256,768]{1,0:T(8,128)(2,1)S(1)} %get-tuple-element.84), channel_id=1, source_target_pairs={{0,8},{1,9},{2,10},{3,11},{4,12},{5,13},{6,14},{7,15},{8,0},{9,1},... | collective-permute-start | bytes 1179656 | tf_op jit(solution)/shard_map/ppermute | solution.py:26
  71.1 8.2 %collective-permute-start.21 = (bf16[256,768]{1,0:T(8,128)(2,1)S(1)}, bf16[256,768]{1,0:T(8,128)(2,1)S(1)}, u32[]{:S(2)}, u32[]{:S(2)}) collective-permute-start(bf16[256,768]{1,0:T(8,128)(2,1)S(1)} %add_convert_fusion.4), channel_id=1, source_target_pairs={{0,6},{1,7},{2,0},{3,1},{4,2},{5,3},{6,4},{7,5},{8,10},{9,11},{10,... | collective-permute-start | bytes 1179656 | tf_op jit(solution)/shard_map/ppermute | solution.py:319
  74.4 11.8 %collective-permute-start.27 = (bf16[256,768]{1,0:T(8,128)(2,1)S(1)}, bf16[256,768]{1,0:T(8,128)(2,1)S(1)}, u32[]{:S(2)}, u32[]{:S(2)}) collective-permute-start(bf16[256,768]{1,0:T(8,128)(2,1)S(1)} %add_convert_fusion), channel_id=1, source_target_pairs={{0,224},{1,225},{2,226},{3,227},{4,228},{5,229},{6,230},{7,231},{8... | collective-permute-start | bytes 1179656 | tf_op jit(solution)/shard_map/ppermute | solution.py:26
  77.8 21.4 %copy-start = (bf16[128,768]{1,0:T(8,128)(2,1)S(1)}, bf16[128,768]{1,0:T(8,128)(2,1)}, u32[]{:S(2)}) copy-start(bf16[128,768]{1,0:T(8,128)(2,1)} %embedding_ref.3) | copy-start | bytes 589828
  77.8 12.0 %collective-permute-start.26 = (bf16[256,768]{1,0:T(8,128)(2,1)S(1)}, bf16[256,768]{1,0:T(8,128)(2,1)S(1)}, u32[]{:S(2)}, u32[]{:S(2)}) collective-permute-start(bf16[256,768]{1,0:T(8,128)(2,1)S(1)} %add_convert_fusion.1), channel_id=1, source_target_pairs={{0,32},{1,33},{2,34},{3,35},{4,36},{5,37},{6,38},{7,39},{8,40},{9,... | collective-permute-start | bytes 1179656 | tf_op jit(solution)/shard_map/ppermute | solution.py:26
  79.6 20.6 %copy-start.1 = (bf16[128,768]{1,0:T(8,128)(2,1)S(1)}, bf16[128,768]{1,0:T(8,128)(2,1)}, u32[]{:S(2)}) copy-start(bf16[128,768]{1,0:T(8,128)(2,1)} %embedding_ref.2) | copy-start | bytes 589828
  79.6 10.6 %collective-permute-start.24 = (bf16[256,768]{1,0:T(8,128)(2,1)S(1)}, bf16[256,768]{1,0:T(8,128)(2,1)S(1)}, u32[]{:S(2)}, u32[]{:S(2)}) collective-permute-start(bf16[256,768]{1,0:T(8,128)(2,1)S(1)} %get-tuple-element.90), channel_id=1, source_target_pairs={{0,6},{1,7},{2,0},{3,1},{4,2},{5,3},{6,4},{7,5},{8,14},{9,15},{10,... | collective-permute-start | bytes 1179656 | tf_op jit(solution)/shard_map/ppermute | solution.py:26
  81.5 10.9 %collective-permute-start.22 = (bf16[256,768]{1,0:T(8,128)(2,1)S(1)}, bf16[256,768]{1,0:T(8,128)(2,1)S(1)}, u32[]{:S(2)}, u32[]{:S(2)}) collective-permute-start(bf16[256,768]{1,0:T(8,128)(2,1)S(1)} %get-tuple-element.91), channel_id=1, source_target_pairs={{0,2},{1,3},{2,4},{3,5},{4,6},{5,7},{6,0},{7,1},{8,10},{9,11},{10,... | collective-permute-start | bytes 1179656 | tf_op jit(solution)/shard_map/ppermute | solution.py:26
  89.9 9.3 %collective-permute-start.28 = (bf16[128,768]{1,0:T(8,128)(2,1)S(1)}, bf16[128,768]{1,0:T(8,128)(2,1)S(1)}, u32[]{:S(2)}, u32[]{:S(2)}) collective-permute-start(bf16[128,768]{1,0:T(8,128)(2,1)S(1)} %add_convert_fusion.5), channel_id=1, source_target_pairs={{0,16},{1,17},{2,18},{3,19},{4,20},{5,21},{6,22},{7,23},{8,24},{9,... | collective-permute-start | bytes 589832 | tf_op jit(solution)/shard_map/ppermute | solution.py:26
  92.5 7.7 %collective-permute-start.25 = (bf16[128,768]{1,0:T(8,128)(2,1)S(1)}, bf16[128,768]{1,0:T(8,128)(2,1)S(1)}, u32[]{:S(2)}, u32[]{:S(2)}) collective-permute-start(bf16[128,768]{1,0:T(8,128)(2,1)S(1)} %add_convert_fusion.6), channel_id=1, source_target_pairs={{0,1},{1,0},{2,3},{3,2},{4,5},{5,4},{6,7},{7,6},{8,9},{9,8},{10,11... | collective-permute-start | bytes 589832 | tf_op jit(solution)/shard_map/ppermute | solution.py:26
  (9 other events, 25.4 us)

commit v5 on v3

--- a/solution.py
+++ b/solution.py
@@ -10,7 +10,6 @@
 EPSILON = 1e-06
 NZ, NX = 8, 4
 AXES = ("blk", "bulk")
-ANY = pl.BlockSpec(memory_space=pl.ANY)
 SMEM = pl.BlockSpec(memory_space=pltpu.SMEM)
 
 
@@ -45,7 +44,7 @@
 
 
 def unit_low(video, text):
-    shape = jax.ShapeDtypeStruct(video.shape, jnp.bfloat16)
+    shape = pltpu.VMEM(video.shape, jnp.bfloat16)
     return pl.pallas_call(unit_kernel, out_shape=(shape, shape), name="unit_low")(video, text)
 
 
@@ -68,7 +67,7 @@
         out_shape=jax.ShapeDtypeStruct(embedding.shape, jnp.float32),
         in_specs=[SMEM] + [vmem] * (1 + len(parts)),
         out_specs=vmem,
-        compiler_params=pltpu.CompilerParams(vmem_limit_bytes=8 * 1024 * 1024),
+        compiler_params=pltpu.CompilerParams(vmem_limit_bytes=5 * 1024 * 1024),
         name="back_rows",
     )(scale, embedding, *parts)
 
@@ -104,19 +103,10 @@
 
 
 def near_kernel(scale_ref, offset_ref, place_ref, *refs):
-    texts, videos = refs[:8], refs[8:-4]
-    weights, text, video, sems = refs[-4:]
-    copies = []
-    for target, blocks in ((text, texts), (video, videos)):
-        place = 0
-        for block in blocks:
-            part = target.at[pl.ds(place, block.shape[0]), :]
-            copies.append(pltpu.make_async_copy(block, part, sems.at[len(copies)]))
-            place += block.shape[0]
-    for copy in copies:
-        copy.start()
-    for copy in copies:
-        copy.wait()
+    texts, videos = refs[:8], refs[8:-3]
+    weights, text, video = refs[-3:]
+    put(text, texts)
+    put(video, videos)
     core = place_ref[0]
     tile = video.shape[0] // 2
     row = lax.broadcasted_iota(jnp.int32, (tile, PAIR), 0)
@@ -209,20 +199,19 @@
 
 
 def low(rows, columns=D):
-    return jax.ShapeDtypeStruct((rows, columns), jnp.bfloat16)
+    return pltpu.VMEM((rows, columns), jnp.bfloat16)
 
 
 def cost(flops, transcendentals=0):
     return pl.CostEstimate(flops=flops, bytes_accessed=0, transcendentals=transcendentals)
 
 
-def call(kernel, name, scalars, arrays, outs, grant, flops, transcendentals=0, copies=0):
+def call(kernel, name, scalars, arrays, outs, grant, flops, transcendentals=0):
     return pl.pallas_call(
         kernel,
         out_shape=outs,
-        in_specs=[SMEM] * len(scalars) + [ANY if copies else VMEM] * len(arrays),
+        in_specs=[SMEM] * len(scalars) + [VMEM] * len(arrays),
         out_specs=[VMEM] * len(outs),
-        scratch_shapes=[pltpu.SemaphoreType.DMA((copies,))] if copies else [],
         compiler_params=pltpu.CompilerParams(vmem_limit_bytes=grant * MIB),
         cost_estimate=cost(flops, transcendentals),
         name=name,
@@ -258,10 +247,9 @@
         scalars,
         texts + videos,
         [low(near_rows, 4 * PAIR), low(4 * PAIR), low(near_rows)],
-        20,
+        8,
         FLOPS * 3 // 5,
         2 * near_rows * 4 * PAIR,
-        len(texts + videos),
     )
     v2, b2, near = lax.optimization_barrier((v2, b2, near))
     last, far, far_video, hmm, hqq, s01, sm, sp, s2 = call(
@@ -271,7 +259,7 @@
         [near, text, near_video, b2, v2, move(v2, core=1)],
         [low(near_rows, PAIR // 2), low(far_rows, 4 * PAIR + PAIR // 2), low(far_rows)]
         + [low(PAIR)] * 6,
-        24,
+        11,
         FLOPS * 5 // 4,
         2 * far_rows * 5 * PAIR,
     )
@@ -283,7 +271,7 @@
         [],
         [near, last, far, text, b2, near_video, far_video],
         [low(PAIR)] * 7,
-        24,
+        11,
         FLOPS,
     )
     hmm, hqq, r2, g01, gm, gp, g2, h01, hm, hq = lax.optimization_barrier(

time: 101 us -> 97.5 us (0.965)
  Pallas kernels: 22.1 us -> 18.3 us
  waiting for transfers between devices: 29.5 us -> 30.6 us
    pallas_call x3, Pallas kernels: 18.2 us -> 15 us  [call(): pl.pallas_call(kernel, out_shape=outs, in_specs=[SMEM] * len(scalars) + [...]
    ppermute x1, waiting for transfers between devices: 0.06 us -> 3.21 us  [move_by_y_hi(): return lax.ppermute(block, AXES, pairs)]
    ppermute x26, waiting for transfers between devices: 28 us -> 25.2 us  [move(): return lax.ppermute(block, AXES, pairs)]
    unnamed x27 -> x25, local copies, waits for them, and re-layouts: 10.4 us -> 9.45 us
  transfers between devices with their start and end apart: 29 -> 29, of which waited for: 14 -> 14; matrix products, arithmetic and copies ran while one was open for 4% -> 3% of each run, Pallas kernels for 13% -> 10%
where the time goes in v5:
time: 97.5 us; the launch traced here: 96.5 us
  starting transfers between devices  33.1 us (34%)
  waiting for transfers between devices  30.6 us (31%)
  Pallas kernels  18.3 us (19%)
  local copies, waits for them, and re-layouts  9.47 us (10%)
  other arithmetic  2.9 us (3%)
  between operations  2.17 us (2%)
    ppermute x26, starting transfers between devices, move(): return lax.ppermute(block, AXES, pairs)  29.8 us
    ppermute x26, waiting for transfers between devices, move(): return lax.ppermute(block, AXES, pairs)  25.2 us
    pallas_call x3, Pallas kernels, call(): pl.pallas_call(kernel, out_shape=outs, in_specs=[SMEM] * len(scalars) + [...  15 us
    unnamed x25, local copies, waits for them, and re-layouts  9.45 us
    ppermute x1, waiting for transfers between devices, move_by_y_hi(): return lax.ppermute(block, AXES, pairs)  3.21 us
    ppermute x2, starting transfers between devices, move_by_core(): return lax.ppermute(block, AXES, pairs)  3.02 us
    convert_element_type x6, other arithmetic, add(): return total.astype(jnp.bfloat16)  2.76 us
    ppermute x2, waiting for transfers between devices, move_by_core(): return lax.ppermute(block, AXES, pairs)  2.22 us
  transfers between devices with their start and end apart: 29, of which 14 were waited for; matrix products, arithmetic and copies ran while one was open for 3% of the time, Pallas kernels for 10%

profile of v5, /device:TPU:2, one launch (start us, length us, event | category | flops | bytes accessed | tf_op | source)
XLA Modules:
  0.0 96.5 jit_solution(6974599502489915201)
XLA Ops:
  0.6 1.2 %unit_low.1 = (bf16[128,768]{1,0:T(8,128)(2,1)S(1)}, bf16[128,768]{1,0:T(8,128)(2,1)S(1)}) custom-call(bf16[128,768]{1,0:T(8,128)(2,1)} %embedding_ref.2, bf16[128,768]{1,0:T(8,128)(2,1)} %embedding_ref.3), custom_call_target="tpu_custom_call" | custom-call | tf_op jit(solution)/shard_map/unit_low/pallas_call | solution.py:48
  1.8 1.7 %collective-permute-start = (bf16[128,768]{1,0:T(8,128)(2,1)S(1)}, bf16[128,768]{1,0:T(8,128)(2,1)S(1)}, u32[]{:S(2)}, u32[]{:S(2)}) collective-permute-start(bf16[128,768]{1,0:T(8,128)(2,1)S(1)} %get-tuple-element.46), channel_id=1, source_target_pairs={{0,1},{1,0},{2,3},{3,2},{4,5},{5,4},{6,7},{7,6},{8,9},{9,8},{10,11... | collective-permute-start | bytes 589832 | tf_op jit(solution)/shard_map/ppermute | solution.py:25
  3.5 5.9 %collective-permute-start.3 = (bf16[128,768]{1,0:T(8,128)(2,1)S(1)}, bf16[128,768]{1,0:T(8,128)(2,1)S(1)}, u32[]{:S(2)}, u32[]{:S(2)}) collective-permute-start(bf16[128,768]{1,0:T(8,128)(2,1)S(1)} %get-tuple-element.47.refs_0_), channel_id=1, source_target_pairs={{0,224},{1,225},{2,226},{3,227},{4,228},{5,229},{6,230},{7,231},{8... | collective-permute-start | bytes 589832 | tf_op jit(solution)/shard_map/ppermute | solution.py:25
  9.3 2.9 %collective-permute-start.1 = (bf16[128,768]{1,0:T(8,128)(2,1)S(1)}, bf16[128,768]{1,0:T(8,128)(2,1)S(1)}, u32[]{:S(2)}, u32[]{:S(2)}) collective-permute-start(bf16[128,768]{1,0:T(8,128)(2,1)S(1)} %get-tuple-element.47.refs_0_), channel_id=1, source_target_pairs={{0,16},{1,17},{2,18},{3,19},{4,20},{5,21},{6,22},{7,23},{8,24},{9,... | collective-permute-start | bytes 589832 | tf_op jit(solution)/shard_map/ppermute | solution.py:25
  13.2 3.4 %collective-permute-done.2.refs_2_ = bf16[128,768]{1,0:T(8,128)(2,1)S(1)} collective-permute-done((bf16[128,768]{1,0:T(8,128)(2,1)S(1)}, bf16[128,768]{1,0:T(8,128)(2,1)S(1)}, u32[]{:S(2)}, u32[]{:S(2)}) %collective-permute-start.2) | collective-permute-done | bytes 196640 | tf_op jit(solution)/shard_map/ppermute | solution.py:25
  17.8 1.5 %collective-permute-start.4 = (bf16[256,768]{1,0:T(8,128)(2,1)S(1)}, bf16[256,768]{1,0:T(8,128)(2,1)S(1)}, u32[]{:S(2)}, u32[]{:S(2)}) collective-permute-start(bf16[256,768]{1,0:T(8,128)(2,1)S(1)} %constant_dynamic-update-slice_fusion.refs_8_), channel_id=1, source_target_pairs={{0,2},{1,3},{2,4},{3,5},{4,6},{5,7},{6,0},{7,1},{8,10},{9,11},{10,... | collective-permute-start | bytes 1179656 | tf_op jit(solution)/shard_map/ppermute | solution.py:25
  19.2 3.9 %collective-permute-start.9 = (bf16[128,768]{1,0:T(8,128)(2,1)S(1)}, bf16[128,768]{1,0:T(8,128)(2,1)S(1)}, u32[]{:S(2)}, u32[]{:S(2)}) collective-permute-start(bf16[128,768]{1,0:T(8,128)(2,1)S(1)} %collective-permute-done.3.refs_4_), channel_id=1, source_target_pairs={{0,224},{1,225},{2,226},{3,227},{4,228},{5,229},{6,230},{7,231},{8... | collective-permute-start | bytes 589832 | tf_op jit(solution)/shard_map/ppermute | solution.py:25
  23.2 2.0 %collective-permute-start.7 = (bf16[128,768]{1,0:T(8,128)(2,1)S(1)}, bf16[128,768]{1,0:T(8,128)(2,1)S(1)}, u32[]{:S(2)}, u32[]{:S(2)}) collective-permute-start(bf16[128,768]{1,0:T(8,128)(2,1)S(1)} %collective-permute-done.1.refs_1_), channel_id=1, source_target_pairs={{0,224},{1,225},{2,226},{3,227},{4,228},{5,229},{6,230},{7,231},{8... | collective-permute-start | bytes 589832 | tf_op jit(solution)/shard_map/ppermute | solution.py:25
  26.6 1.4 %collective-permute-done.9.refs_7_ = bf16[128,768]{1,0:T(8,128)(2,1)S(1)} collective-permute-done((bf16[128,768]{1,0:T(8,128)(2,1)S(1)}, bf16[128,768]{1,0:T(8,128)(2,1)S(1)}, u32[]{:S(2)}, u32[]{:S(2)}) %collective-permute-start.9) | collective-permute-done | bytes 196640 | tf_op jit(solution)/shard_map/ppermute | solution.py:25
  28.0 2.1 %collective-permute-done.7.refs_5_ = bf16[128,768]{1,0:T(8,128)(2,1)S(1)} collective-permute-done((bf16[128,768]{1,0:T(8,128)(2,1)S(1)}, bf16[128,768]{1,0:T(8,128)(2,1)S(1)}, u32[]{:S(2)}, u32[]{:S(2)}) %collective-permute-start.7) | collective-permute-done | bytes 196640 | tf_op jit(solution)/shard_map/ppermute | solution.py:25
  30.1 2.0 %collective-permute-done.6.refs_3_ = bf16[128,768]{1,0:T(8,128)(2,1)S(1)} collective-permute-done((bf16[128,768]{1,0:T(8,128)(2,1)S(1)}, bf16[128,768]{1,0:T(8,128)(2,1)S(1)}, u32[]{:S(2)}, u32[]{:S(2)}) %collective-permute-start.6) | collective-permute-done | bytes 196640 | tf_op jit(solution)/shard_map/ppermute | solution.py:25
  32.7 1.6 %collective-permute-start.10 = (bf16[256,768]{1,0:T(8,128)(2,1)S(1)}, bf16[256,768]{1,0:T(8,128)(2,1)S(1)}, u32[]{:S(2)}, u32[]{:S(2)}) collective-permute-start(bf16[256,768]{1,0:T(8,128)(2,1)S(1)} %broadcast_select_fusion), channel_id=1, source_target_pairs={{0,2},{1,3},{2,4},{3,5},{4,6},{5,7},{6,0},{7,1},{8,14},{9,15},{10,... | collective-permute-start | bytes 1179656 | tf_op jit(solution)/shard_map/ppermute | solution.py:306
  34.6 4.3 %near_weights.1 = (bf16[1536,1024]{1,0:T(8,128)(2,1)S(1)}, bf16[1024,768]{1,0:T(8,128)(2,1)S(1)}, bf16[1536,768]{1,0:T(8,128)(2,1)S(1)}) custom-call(f32[1]{0:T(128)S(6)} %copy.7.scale_ref, f32[1]{0:T(128)S(6)} %copy.8.offset_ref, s32[2]{0:T(128)S(1)} %pad_add_fusion.place_ref, bf16[128,768]{1,0:T(8,128)(2,1)S(1)} %get-tuple-element.47.refs_0_, ...), custom_call_target="tpu_custom_call" | custom-call | flops 2415919104 | tf_op jit(solution)/shard_map/near_weights/pallas_call | solution.py:210
  38.9 3.2 %collective-permute-done.11.last = bf16[128,768]{1,0:T(8,128)(2,1)S(1)} collective-permute-done((bf16[128,768]{1,0:T(8,128)(2,1)S(1)}, bf16[128,768]{1,0:T(8,128)(2,1)S(1)}, u32[]{:S(2)}, u32[]{:S(2)}) %collective-permute-start.11) | collective-permute-done | bytes 196640 | tf_op jit(solution)/shard_map/ppermute | solution.py:316
  42.1 1.7 %collective-permute-done.15.refs_1_ = bf16[256,768]{1,0:T(8,128)(2,1)S(1)} collective-permute-done((bf16[256,768]{1,0:T(8,128)(2,1)S(1)}, bf16[256,768]{1,0:T(8,128)(2,1)S(1)}, u32[]{:S(2)}, u32[]{:S(2)}) %collective-permute-start.15) | collective-permute-done | bytes 393248 | tf_op jit(solution)/shard_map/ppermute | solution.py:25
  43.9 6.1 %far_weights_and_sums.1 = (bf16[1536,128]{1,0:T(8,128)(2,1)S(1)}, bf16[512,1152]{1,0:T(8,128)(2,1)S(1)}, bf16[512,768]{1,0:T(8,128)(2,1)S(1)}, bf16[256,768]{1,0...) custom-call(f32[1]{0:T(128)S(6)} %copy.7.scale_ref, ...), custom_call_target="tpu_custom_call" | custom-call | flops 5033164800 | tf_op jit(solution)/shard_map/far_weights_and_sums/pallas_call | solution.py:210
  52.9 1.1 %collective-permute-start.17 = (bf16[256,768]{1,0:T(8,128)(2,1)S(1)}, bf16[256,768]{1,0:T(8,128)(2,1)S(1)}, u32[]{:S(2)}, u32[]{:S(2)}) collective-permute-start(bf16[256,768]{1,0:T(8,128)(2,1)S(1)} %get-tuple-element.65), channel_id=1, source_target_pairs={{0,32},{1,33},{2,34},{3,35},{4,36},{5,37},{6,38},{7,39},{8,40},{9,... | collective-permute-start | bytes 1179656 | tf_op jit(solution)/shard_map/ppermute | solution.py:25
  54.6 1.9 %copy-done.3 = bf16[1536,1024]{1,0:T(8,128)(2,1)S(1)} copy-done((bf16[1536,1024]{1,0:T(8,128)(2,1)S(1)}, bf16[1536,1024]{1,0:T(8,128)(2,1)}, u32[]{:S(2)}) %copy-start.3) | copy-done | bytes 3145752
  56.5 1.7 %copy-done.5 = bf16[1536,768]{1,0:T(8,128)(2,1)S(1)} copy-done((bf16[1536,768]{1,0:T(8,128)(2,1)S(1)}, bf16[1536,768]{1,0:T(8,128)(2,1)}, u32[]{:S(2)}) %copy-start.5) | copy-done | bytes 2359320
  58.2 1.4 %copy-done.7 = bf16[1024,768]{1,0:T(8,128)(2,1)S(1)} copy-done((bf16[1024,768]{1,0:T(8,128)(2,1)S(1)}, bf16[1024,768]{1,0:T(8,128)(2,1)}, u32[]{:S(2)}) %copy-start.7) | copy-done | bytes 1572888
  59.6 1.3 %copy-done.9 = bf16[512,1152]{1,0:T(8,128)(2,1)S(1)} copy-done((bf16[512,1152]{1,0:T(8,128)(2,1)S(1)}, bf16[512,1152]{1,0:T(8,128)(2,1)}, u32[]{:S(2)}) %copy-start.9) | copy-done | bytes 1179672
  60.8 1.1 %copy-done.11 = bf16[512,768]{1,0:T(8,128)(2,1)S(1)} copy-done((bf16[512,768]{1,0:T(8,128)(2,1)S(1)}, bf16[512,768]{1,0:T(8,128)(2,1)}, u32[]{:S(2)}) %copy-start.11) | copy-done | bytes 786456
  62.0 4.6 %own_video_and_near_text_sums.1 = (bf16[256,768]{1,0:T(8,128)(2,1)S(1)}, bf16[256,768]{1,0:T(8,128)(2,1)S(1)}, bf16[256,768]{1,0:T(8,128)(2,1)S(1)}, bf16[256,76...) custom-call(bf16[1536,1024]{1,0:T(8,128)(2,1)S(1)} %copy-done.3, ...), custom_call_target="tpu_custom_call" | custom-call | flops 4026531840 | tf_op jit(solution)/shard_map/own_video_and_near_text_sums/pallas_call | solution.py:210
  68.3 1.5 %collective-permute-start.21 = (bf16[256,768]{1,0:T(8,128)(2,1)S(1)}, bf16[256,768]{1,0:T(8,128)(2,1)S(1)}, u32[]{:S(2)}, u32[]{:S(2)}) collective-permute-start(bf16[256,768]{1,0:T(8,128)(2,1)S(1)} %add_convert_fusion.4), channel_id=1, source_target_pairs={{0,6},{1,7},{2,0},{3,1},{4,2},{5,3},{6,4},{7,5},{8,10},{9,11},{10,... | collective-permute-start | bytes 1179656 | tf_op jit(solution)/shard_map/ppermute | solution.py:306
  70.8 2.9 %collective-permute-start.27 = (bf16[256,768]{1,0:T(8,128)(2,1)S(1)}, bf16[256,768]{1,0:T(8,128)(2,1)S(1)}, u32[]{:S(2)}, u32[]{:S(2)}) collective-permute-start(bf16[256,768]{1,0:T(8,128)(2,1)S(1)} %add_convert_fusion), channel_id=1, source_target_pairs={{0,224},{1,225},{2,226},{3,227},{4,228},{5,229},{6,230},{7,231},{8... | collective-permute-start | bytes 1179656 | tf_op jit(solution)/shard_map/ppermute | solution.py:25
  73.9 2.2 %collective-permute-done.21 = bf16[256,768]{1,0:T(8,128)(2,1)S(1)} collective-permute-done((bf16[256,768]{1,0:T(8,128)(2,1)S(1)}, bf16[256,768]{1,0:T(8,128)(2,1)S(1)}, u32[]{:S(2)}, u32[]{:S(2)}) %collective-permute-start.21) | collective-permute-done | bytes 393248 | tf_op jit(solution)/shard_map/ppermute | solution.py:306
  76.5 1.5 %collective-permute-start.24 = (bf16[256,768]{1,0:T(8,128)(2,1)S(1)}, bf16[256,768]{1,0:T(8,128)(2,1)S(1)}, u32[]{:S(2)}, u32[]{:S(2)}) collective-permute-start(bf16[256,768]{1,0:T(8,128)(2,1)S(1)} %get-tuple-element.90), channel_id=1, source_target_pairs={{0,6},{1,7},{2,0},{3,1},{4,2},{5,3},{6,4},{7,5},{8,14},{9,15},{10,... | collective-permute-start | bytes 1179656 | tf_op jit(solution)/shard_map/ppermute | solution.py:25
  78.6 3.4 %collective-permute-done.27.refs_2_ = bf16[256,768]{1,0:T(8,128)(2,1)S(1)} collective-permute-done((bf16[256,768]{1,0:T(8,128)(2,1)S(1)}, bf16[256,768]{1,0:T(8,128)(2,1)S(1)}, u32[]{:S(2)}, u32[]{:S(2)}) %collective-permute-start.27) | collective-permute-done | bytes 393248 | tf_op jit(solution)/shard_map/ppermute | solution.py:25
  82.0 3.2 %collective-permute-done.26.refs_1_ = bf16[256,768]{1,0:T(8,128)(2,1)S(1)} collective-permute-done((bf16[256,768]{1,0:T(8,128)(2,1)S(1)}, bf16[256,768]{1,0:T(8,128)(2,1)S(1)}, u32[]{:S(2)}, u32[]{:S(2)}) %collective-permute-start.26) | collective-permute-done | bytes 393248 | tf_op jit(solution)/shard_map/ppermute | solution.py:25
  85.2 2.2 %collective-permute-start.28 = (bf16[128,768]{1,0:T(8,128)(2,1)S(1)}, bf16[128,768]{1,0:T(8,128)(2,1)S(1)}, u32[]{:S(2)}, u32[]{:S(2)}) collective-permute-start(bf16[128,768]{1,0:T(8,128)(2,1)S(1)} %add_convert_fusion.5), channel_id=1, source_target_pairs={{0,16},{1,17},{2,18},{3,19},{4,20},{5,21},{6,22},{7,23},{8,24},{9,... | collective-permute-start | bytes 589832 | tf_op jit(solution)/shard_map/ppermute | solution.py:25
  87.4 1.4 %collective-permute-done.22.refs_2_ = bf16[256,768]{1,0:T(8,128)(2,1)S(1)} collective-permute-done((bf16[256,768]{1,0:T(8,128)(2,1)S(1)}, bf16[256,768]{1,0:T(8,128)(2,1)S(1)}, u32[]{:S(2)}, u32[]{:S(2)}) %collective-permute-start.22) | collective-permute-done | bytes 393248 | tf_op jit(solution)/shard_map/ppermute | solution.py:25
  89.1 4.7 %collective-permute-done.28.refs_3_ = bf16[128,768]{1,0:T(8,128)(2,1)S(1)} collective-permute-done((bf16[128,768]{1,0:T(8,128)(2,1)S(1)}, bf16[128,768]{1,0:T(8,128)(2,1)S(1)}, u32[]{:S(2)}, u32[]{:S(2)}) %collective-permute-start.28) | collective-permute-done | bytes 196640 | tf_op jit(solution)/shard_map/ppermute | solution.py:25
  (67 shorter events, 13.5 us)
Async XLA Ops:
  1.8 10.4 %collective-permute-start = (bf16[128,768]{1,0:T(8,128)(2,1)S(1)}, bf16[128,768]{1,0:T(8,128)(2,1)S(1)}, u32[]{:S(2)}, u32[]{:S(2)}) collective-permute-start(bf16[128,768]{1,0:T(8,128)(2,1)S(1)} %get-tuple-element.46), channel_id=1, source_target_pairs={{0,1},{1,0},{2,3},{3,2},{4,5},{5,4},{6,7},{7,6},{8,9},{9,8},{10,11... | collective-permute-start | bytes 589832 | tf_op jit(solution)/shard_map/ppermute | solution.py:25
  3.5 9.7 %collective-permute-start.3 = (bf16[128,768]{1,0:T(8,128)(2,1)S(1)}, bf16[128,768]{1,0:T(8,128)(2,1)S(1)}, u32[]{:S(2)}, u32[]{:S(2)}) collective-permute-start(bf16[128,768]{1,0:T(8,128)(2,1)S(1)} %get-tuple-element.47.refs_0_), channel_id=1, source_target_pairs={{0,224},{1,225},{2,226},{3,227},{4,228},{5,229},{6,230},{7,231},{8... | collective-permute-start | bytes 589832 | tf_op jit(solution)/shard_map/ppermute | solution.py:25
  9.3 7.3 %collective-permute-start.2 = (bf16[128,768]{1,0:T(8,128)(2,1)S(1)}, bf16[128,768]{1,0:T(8,128)(2,1)S(1)}, u32[]{:S(2)}, u32[]{:S(2)}) collective-permute-start(bf16[128,768]{1,0:T(8,128)(2,1)S(1)} %get-tuple-element.47.refs_0_), channel_id=1, source_target_pairs={{0,32},{1,33},{2,34},{3,35},{4,36},{5,37},{6,38},{7,39},{8,40},{9,... | collective-permute-start | bytes 589832 | tf_op jit(solution)/shard_map/ppermute | solution.py:25
  9.3 7.6 %collective-permute-start.1 = (bf16[128,768]{1,0:T(8,128)(2,1)S(1)}, bf16[128,768]{1,0:T(8,128)(2,1)S(1)}, u32[]{:S(2)}, u32[]{:S(2)}) collective-permute-start(bf16[128,768]{1,0:T(8,128)(2,1)S(1)} %get-tuple-element.47.refs_0_), channel_id=1, source_target_pairs={{0,16},{1,17},{2,18},{3,19},{4,20},{5,21},{6,22},{7,23},{8,24},{9,... | collective-permute-start | bytes 589832 | tf_op jit(solution)/shard_map/ppermute | solution.py:25
  16.9 8.3 %collective-permute-start.8 = (bf16[128,768]{1,0:T(8,128)(2,1)S(1)}, bf16[128,768]{1,0:T(8,128)(2,1)S(1)}, u32[]{:S(2)}, u32[]{:S(2)}) collective-permute-start(bf16[128,768]{1,0:T(8,128)(2,1)S(1)} %collective-permute-done.2.refs_2_), channel_id=1, source_target_pairs={{0,32},{1,33},{2,34},{3,35},{4,36},{5,37},{6,38},{7,39},{8,40},{9,... | collective-permute-start | bytes 589832 | tf_op jit(solution)/shard_map/ppermute | solution.py:25
  17.1 15.0 %collective-permute-start.5 = (bf16[256,768]{1,0:T(8,128)(2,1)S(1)}, bf16[256,768]{1,0:T(8,128)(2,1)S(1)}, u32[]{:S(2)}, u32[]{:S(2)}) collective-permute-start(bf16[256,768]{1,0:T(8,128)(2,1)S(1)} %constant_dynamic-update-slice_fusion.refs_8_), channel_id=1, source_target_pairs={{0,6},{1,7},{2,0},{3,1},{4,2},{5,3},{6,4},{7,5},{8,14},{9,15},{10,... | collective-permute-start | bytes 1179656 | tf_op jit(solution)/shard_map/ppermute | solution.py:25
  17.8 14.3 %collective-permute-start.4 = (bf16[256,768]{1,0:T(8,128)(2,1)S(1)}, bf16[256,768]{1,0:T(8,128)(2,1)S(1)}, u32[]{:S(2)}, u32[]{:S(2)}) collective-permute-start(bf16[256,768]{1,0:T(8,128)(2,1)S(1)} %constant_dynamic-update-slice_fusion.refs_8_), channel_id=1, source_target_pairs={{0,2},{1,3},{2,4},{3,5},{4,6},{5,7},{6,0},{7,1},{8,10},{9,11},{10,... | collective-permute-start | bytes 1179656 | tf_op jit(solution)/shard_map/ppermute | solution.py:25
  19.2 8.8 %collective-permute-start.9 = (bf16[128,768]{1,0:T(8,128)(2,1)S(1)}, bf16[128,768]{1,0:T(8,128)(2,1)S(1)}, u32[]{:S(2)}, u32[]{:S(2)}) collective-permute-start(bf16[128,768]{1,0:T(8,128)(2,1)S(1)} %collective-permute-done.3.refs_4_), channel_id=1, source_target_pairs={{0,224},{1,225},{2,226},{3,227},{4,228},{5,229},{6,230},{7,231},{8... | collective-permute-start | bytes 589832 | tf_op jit(solution)/shard_map/ppermute | solution.py:25
  23.2 6.9 %collective-permute-start.7 = (bf16[128,768]{1,0:T(8,128)(2,1)S(1)}, bf16[128,768]{1,0:T(8,128)(2,1)S(1)}, u32[]{:S(2)}, u32[]{:S(2)}) collective-permute-start(bf16[128,768]{1,0:T(8,128)(2,1)S(1)} %collective-permute-done.1.refs_1_), channel_id=1, source_target_pairs={{0,224},{1,225},{2,226},{3,227},{4,228},{5,229},{6,230},{7,231},{8... | collective-permute-start | bytes 589832 | tf_op jit(solution)/shard_map/ppermute | solution.py:25
  25.2 6.9 %collective-permute-start.6 = (bf16[128,768]{1,0:T(8,128)(2,1)S(1)}, bf16[128,768]{1,0:T(8,128)(2,1)S(1)}, u32[]{:S(2)}, u32[]{:S(2)}) collective-permute-start(bf16[128,768]{1,0:T(8,128)(2,1)S(1)} %collective-permute-done.1.refs_1_), channel_id=1, source_target_pairs={{0,32},{1,33},{2,34},{3,35},{4,36},{5,37},{6,38},{7,39},{8,40},{9,... | collective-permute-start | bytes 589832 | tf_op jit(solution)/shard_map/ppermute | solution.py:25
  28.0 6.5 %collective-permute-start.12 = (bf16[256,768]{1,0:T(8,128)(2,1)S(1)}, bf16[256,768]{1,0:T(8,128)(2,1)S(1)}, u32[]{:S(2)}, u32[]{:S(2)}) collective-permute-start(bf16[256,768]{1,0:T(8,128)(2,1)S(1)} %constant_dynamic-update-slice_fusion.refs_8_), channel_id=1, source_target_pairs={{0,8},{1,9},{2,10},{3,11},{4,12},{5,13},{6,14},{7,15},{8,0},{9,1},... | collective-permute-start | bytes 1179656 | tf_op jit(solution)/shard_map/ppermute | solution.py:25
  32.1 2.4 %collective-permute-start.14 = (bf16[256,768]{1,0:T(8,128)(2,1)S(1)}, bf16[256,768]{1,0:T(8,128)(2,1)S(1)}, u32[]{:S(2)}, u32[]{:S(2)}) collective-permute-start(bf16[256,768]{1,0:T(8,128)(2,1)S(1)} %collective-permute-done.5.refs_10_), channel_id=1, source_target_pairs={{0,8},{1,9},{2,10},{3,11},{4,12},{5,13},{6,14},{7,15},{8,0},{9,1},... | collective-permute-start | bytes 1179656 | tf_op jit(solution)/shard_map/ppermute | solution.py:25
  32.1 2.4 %collective-permute-start.13 = (bf16[256,768]{1,0:T(8,128)(2,1)S(1)}, bf16[256,768]{1,0:T(8,128)(2,1)S(1)}, u32[]{:S(2)}, u32[]{:S(2)}) collective-permute-start(bf16[256,768]{1,0:T(8,128)(2,1)S(1)} %collective-permute-done.4.refs_9_), channel_id=1, source_target_pairs={{0,8},{1,9},{2,10},{3,11},{4,12},{5,13},{6,14},{7,15},{8,0},{9,1},... | collective-permute-start | bytes 1179656 | tf_op jit(solution)/shard_map/ppermute | solution.py:25
  32.7 9.5 %collective-permute-start.10 = (bf16[256,768]{1,0:T(8,128)(2,1)S(1)}, bf16[256,768]{1,0:T(8,128)(2,1)S(1)}, u32[]{:S(2)}, u32[]{:S(2)}) collective-permute-start(bf16[256,768]{1,0:T(8,128)(2,1)S(1)} %broadcast_select_fusion), channel_id=1, source_target_pairs={{0,2},{1,3},{2,4},{3,5},{4,6},{5,7},{6,0},{7,1},{8,14},{9,15},{10,... | collective-permute-start | bytes 1179656 | tf_op jit(solution)/shard_map/ppermute | solution.py:306
  34.3 7.9 %collective-permute-start.11 = (bf16[128,768]{1,0:T(8,128)(2,1)S(1)}, bf16[128,768]{1,0:T(8,128)(2,1)S(1)}, u32[]{:S(2)}, u32[]{:S(2)}) collective-permute-start(bf16[128,768]{1,0:T(8,128)(2,1)S(1)} %broadcast_select_fusion.1), channel_id=1, source_target_pairs={{0,32},{1,33},{2,34},{3,35},{4,36},{5,37},{6,38},{7,39},{8,40},{9,... | collective-permute-start | bytes 589832 | tf_op jit(solution)/shard_map/ppermute | solution.py:316
  38.9 11.1 %copy-start.2 = (bf16[1536,1024]{1,0:T(8,128)(2,1)}, bf16[1536,1024]{1,0:T(8,128)(2,1)S(1)}, u32[]{:S(2)}) copy-start(bf16[1536,1024]{1,0:T(8,128)(2,1)S(1)} %get-tuple-element.59.near) | copy-start | bytes 9437188
  42.1 1.7 %collective-permute-start.15 = (bf16[256,768]{1,0:T(8,128)(2,1)S(1)}, bf16[256,768]{1,0:T(8,128)(2,1)S(1)}, u32[]{:S(2)}, u32[]{:S(2)}) collective-permute-start(bf16[256,768]{1,0:T(8,128)(2,1)S(1)} %collective-permute-done.10.refs_0_), channel_id=1, source_target_pairs={{0,8},{1,9},{2,10},{3,11},{4,12},{5,13},{6,14},{7,15},{8,0},{9,1},... | collective-permute-start | bytes 1179656 | tf_op jit(solution)/shard_map/ppermute | solution.py:25
  52.1 14.5 %collective-permute-start.16 = (bf16[256,768]{1,0:T(8,128)(2,1)S(1)}, bf16[256,768]{1,0:T(8,128)(2,1)}, u32[]{:S(2)}, u32[]{:S(2)}) collective-permute-start(bf16[256,768]{1,0:T(8,128)(2,1)S(1)} %get-tuple-element.64), channel_id=1, source_target_pairs={{0,224},{1,225},{2,226},{3,227},{4,228},{5,229},{6,230},{7,231},{8... | collective-permute-start | bytes 1179656 | tf_op jit(solution)/shard_map/ppermute | solution.py:25
  52.9 14.3 %collective-permute-start.17 = (bf16[256,768]{1,0:T(8,128)(2,1)S(1)}, bf16[256,768]{1,0:T(8,128)(2,1)S(1)}, u32[]{:S(2)}, u32[]{:S(2)}) collective-permute-start(bf16[256,768]{1,0:T(8,128)(2,1)S(1)} %get-tuple-element.65), channel_id=1, source_target_pairs={{0,32},{1,33},{2,34},{3,35},{4,36},{5,37},{6,38},{7,39},{8,40},{9,... | collective-permute-start | bytes 1179656 | tf_op jit(solution)/shard_map/ppermute | solution.py:25
  54.1 13.1 %collective-permute-start.18 = (bf16[256,768]{1,0:T(8,128)(2,1)S(1)}, bf16[256,768]{1,0:T(8,128)(2,1)}, u32[]{:S(2)}, u32[]{:S(2)}) collective-permute-start(bf16[256,768]{1,0:T(8,128)(2,1)S(1)} %get-tuple-element.66), channel_id=1, source_target_pairs={{0,8},{1,9},{2,10},{3,11},{4,12},{5,13},{6,14},{7,15},{8,0},{9,1},... | collective-permute-start | bytes 1179656 | tf_op jit(solution)/shard_map/ppermute | solution.py:25
  54.1 33.3 %collective-permute-start.19 = (bf16[256,768]{1,0:T(8,128)(2,1)S(1)}, bf16[256,768]{1,0:T(8,128)(2,1)S(1)}, u32[]{:S(2)}, u32[]{:S(2)}) collective-permute-start(bf16[256,768]{1,0:T(8,128)(2,1)S(1)} %get-tuple-element.78), channel_id=1, source_target_pairs={{0,8},{1,9},{2,10},{3,11},{4,12},{5,13},{6,14},{7,15},{8,0},{9,1},... | collective-permute-start | bytes 1179656 | tf_op jit(solution)/shard_map/ppermute | solution.py:25
  54.6 19.2 %collective-permute-start.20 = (bf16[256,768]{1,0:T(8,128)(2,1)S(1)}, bf16[256,768]{1,0:T(8,128)(2,1)S(1)}, u32[]{:S(2)}, u32[]{:S(2)}) collective-permute-start(bf16[256,768]{1,0:T(8,128)(2,1)S(1)} %get-tuple-element.80), channel_id=1, source_target_pairs={{0,8},{1,9},{2,10},{3,11},{4,12},{5,13},{6,14},{7,15},{8,0},{9,1},... | collective-permute-start | bytes 1179656 | tf_op jit(solution)/shard_map/ppermute | solution.py:25
  66.6 7.3 %collective-permute-start.23 = (bf16[256,768]{1,0:T(8,128)(2,1)S(1)}, bf16[256,768]{1,0:T(8,128)(2,1)S(1)}, u32[]{:S(2)}, u32[]{:S(2)}) collective-permute-start(bf16[256,768]{1,0:T(8,128)(2,1)S(1)} %get-tuple-element.84), channel_id=1, source_target_pairs={{0,8},{1,9},{2,10},{3,11},{4,12},{5,13},{6,14},{7,15},{8,0},{9,1},... | collective-permute-start | bytes 1179656 | tf_op jit(solution)/shard_map/ppermute | solution.py:25
  68.3 7.9 %collective-permute-start.21 = (bf16[256,768]{1,0:T(8,128)(2,1)S(1)}, bf16[256,768]{1,0:T(8,128)(2,1)S(1)}, u32[]{:S(2)}, u32[]{:S(2)}) collective-permute-start(bf16[256,768]{1,0:T(8,128)(2,1)S(1)} %add_convert_fusion.4), channel_id=1, source_target_pairs={{0,6},{1,7},{2,0},{3,1},{4,2},{5,3},{6,4},{7,5},{8,10},{9,11},{10,... | collective-permute-start | bytes 1179656 | tf_op jit(solution)/shard_map/ppermute | solution.py:306
  70.8 11.2 %collective-permute-start.27 = (bf16[256,768]{1,0:T(8,128)(2,1)S(1)}, bf16[256,768]{1,0:T(8,128)(2,1)S(1)}, u32[]{:S(2)}, u32[]{:S(2)}) collective-permute-start(bf16[256,768]{1,0:T(8,128)(2,1)S(1)} %add_convert_fusion), channel_id=1, source_target_pairs={{0,224},{1,225},{2,226},{3,227},{4,228},{5,229},{6,230},{7,231},{8... | collective-permute-start | bytes 1179656 | tf_op jit(solution)/shard_map/ppermute | solution.py:25
  73.8 20.0 %copy-start = (bf16[128,768]{1,0:T(8,128)(2,1)S(1)}, bf16[128,768]{1,0:T(8,128)(2,1)}, u32[]{:S(2)}) copy-start(bf16[128,768]{1,0:T(8,128)(2,1)} %embedding_ref.3) | copy-start | bytes 589828
  73.8 11.3 %collective-permute-start.26 = (bf16[256,768]{1,0:T(8,128)(2,1)S(1)}, bf16[256,768]{1,0:T(8,128)(2,1)S(1)}, u32[]{:S(2)}, u32[]{:S(2)}) collective-permute-start(bf16[256,768]{1,0:T(8,128)(2,1)S(1)} %add_convert_fusion.1), channel_id=1, source_target_pairs={{0,32},{1,33},{2,34},{3,35},{4,36},{5,37},{6,38},{7,39},{8,40},{9,... | collective-permute-start | bytes 1179656 | tf_op jit(solution)/shard_map/ppermute | solution.py:25
  76.5 19.0 %copy-start.1 = (bf16[128,768]{1,0:T(8,128)(2,1)S(1)}, bf16[128,768]{1,0:T(8,128)(2,1)}, u32[]{:S(2)}) copy-start(bf16[128,768]{1,0:T(8,128)(2,1)} %embedding_ref.2) | copy-start | bytes 589828
  76.5 10.9 %collective-permute-start.24 = (bf16[256,768]{1,0:T(8,128)(2,1)S(1)}, bf16[256,768]{1,0:T(8,128)(2,1)S(1)}, u32[]{:S(2)}, u32[]{:S(2)}) collective-permute-start(bf16[256,768]{1,0:T(8,128)(2,1)S(1)} %get-tuple-element.90), channel_id=1, source_target_pairs={{0,6},{1,7},{2,0},{3,1},{4,2},{5,3},{6,4},{7,5},{8,14},{9,15},{10,... | collective-permute-start | bytes 1179656 | tf_op jit(solution)/shard_map/ppermute | solution.py:25
  77.9 10.8 %collective-permute-start.22 = (bf16[256,768]{1,0:T(8,128)(2,1)S(1)}, bf16[256,768]{1,0:T(8,128)(2,1)S(1)}, u32[]{:S(2)}, u32[]{:S(2)}) collective-permute-start(bf16[256,768]{1,0:T(8,128)(2,1)S(1)} %get-tuple-element.91), channel_id=1, source_target_pairs={{0,2},{1,3},{2,4},{3,5},{4,6},{5,7},{6,0},{7,1},{8,10},{9,11},{10,... | collective-permute-start | bytes 1179656 | tf_op jit(solution)/shard_map/ppermute | solution.py:25
  85.2 8.6 %collective-permute-start.28 = (bf16[128,768]{1,0:T(8,128)(2,1)S(1)}, bf16[128,768]{1,0:T(8,128)(2,1)S(1)}, u32[]{:S(2)}, u32[]{:S(2)}) collective-permute-start(bf16[128,768]{1,0:T(8,128)(2,1)S(1)} %add_convert_fusion.5), channel_id=1, source_target_pairs={{0,16},{1,17},{2,18},{3,19},{4,20},{5,21},{6,22},{7,23},{8,24},{9,... | collective-permute-start | bytes 589832 | tf_op jit(solution)/shard_map/ppermute | solution.py:25
  88.9 6.6 %collective-permute-start.25 = (bf16[128,768]{1,0:T(8,128)(2,1)S(1)}, bf16[128,768]{1,0:T(8,128)(2,1)S(1)}, u32[]{:S(2)}, u32[]{:S(2)}) collective-permute-start(bf16[128,768]{1,0:T(8,128)(2,1)S(1)} %add_convert_fusion.6), channel_id=1, source_target_pairs={{0,1},{1,0},{2,3},{3,2},{4,5},{5,4},{6,7},{7,6},{8,9},{9,8},{10,11... | collective-permute-start | bytes 589832 | tf_op jit(solution)/shard_map/ppermute | solution.py:25
  (9 other events, 31.6 us)

commit v6 on v5

--- a/solution.py
+++ b/solution.py
@@ -153,7 +153,8 @@
 
 
 def far_kernel(scale_ref, offset_ref, place_ref, near, text, near_video, last, *refs):
-    videos, (last_weights, weights, video, below, above, *outs) = refs[:2], refs[2:]
+    videos, (below, above, *outs), scratch = refs[:2], refs[2:-3], refs[-3:]
+    last_weights, weights, video = scratch
     put(video, videos)
     core, y_hi = place_ref[0], place_ref[1]
     near_tile, rows = near_video.shape[0] // 2, PAIR // 2
@@ -174,7 +175,12 @@
         weight = pair_weight(scale_ref, offset_ref, video_tile, last[...])
         weights[rows, pl.ds(4 * PAIR, PAIR // 2)] = weight.astype(jnp.bfloat16)
 
-    video_sums(1, near, last_weights, weights, text, last, outs)
+    video_sums(1, near, last_weights, weights, text, last, outs[:4])
+    video_sums(0, near, last_weights, weights, text, last, outs[4:8])
+    for i, block in enumerate(outs[8:]):
+        columns = pl.ds(i * PAIR, PAIR)
+        total = text_sum((near[:, columns], near_video), (weights[:, columns], video))
+        block[...] = total.astype(jnp.bfloat16)
     columns = pl.ds(3 * PAIR, PAIR)
     edges = text_sum((near[:, columns], near_video), (weights[:, columns], video))
     columns = pl.ds(4 * PAIR, rows)
@@ -185,14 +191,6 @@
     above[rows:, :] = (total * jnp.where(y_hi == 1, 1.0, 0.0)).astype(jnp.bfloat16)
 
 
-def last_kernel(near, last_weights, far, text, last, near_video, far_video, *outs):
-    video_sums(0, near, last_weights, far, text, last, outs[:4])
-    for i, block in enumerate(outs[4:]):
-        columns = pl.ds(i * PAIR, PAIR)
-        total = text_sum((near[:, columns], near_video), (far[:, columns], far_video))
-        block[...] = total.astype(jnp.bfloat16)
-
-
 VMEM = pl.BlockSpec(memory_space=pltpu.VMEM)
 MIB = 1024 * 1024
 FLOPS = 2 * N_VIDEO * N_TEXT * PAIR * PAIR * D
@@ -206,12 +204,13 @@
     return pl.CostEstimate(flops=flops, bytes_accessed=0, transcendentals=transcendentals)
 
 
-def call(kernel, name, scalars, arrays, outs, grant, flops, transcendentals=0):
+def call(kernel, name, scalars, arrays, outs, grant, flops, transcendentals, scratch=()):
     return pl.pallas_call(
         kernel,
         out_shape=outs,
         in_specs=[SMEM] * len(scalars) + [VMEM] * len(arrays),
         out_specs=[VMEM] * len(outs),
+        scratch_shapes=scratch,
         compiler_params=pltpu.CompilerParams(vmem_limit_bytes=grant * MIB),
         cost_estimate=cost(flops, transcendentals),
         name=name,
@@ -252,37 +251,24 @@
         2 * near_rows * 4 * PAIR,
     )
     v2, b2, near = lax.optimization_barrier((v2, b2, near))
-    last, far, far_video, hmm, hqq, s01, sm, sp, s2 = call(
+    hmm, hqq, s01, sm, sp, s2, g01, gm, gp, g2, h01, hm, hq = call(
         far_kernel,
         "far_weights_and_sums",
         scalars,
         [near, text, near_video, b2, v2, move(v2, core=1)],
-        [low(near_rows, PAIR // 2), low(far_rows, 4 * PAIR + PAIR // 2), low(far_rows)]
-        + [low(PAIR)] * 6,
-        11,
-        FLOPS * 5 // 4,
+        [low(PAIR)] * 13,
+        14,
+        FLOPS * 9 // 4,
         2 * far_rows * 5 * PAIR,
+        [low(near_rows, PAIR // 2), low(far_rows, 4 * PAIR + PAIR // 2), low(far_rows)],
     )
 
-    r2 = move(s2, core=1)
-    g01, gm, gp, g2, h01, hm, hq = call(
-        last_kernel,
-        "own_video_and_near_text_sums",
-        [],
-        [near, last, far, text, b2, near_video, far_video],
-        [low(PAIR)] * 7,
-        11,
-        FLOPS,
-    )
-    hmm, hqq, r2, g01, gm, gp, g2, h01, hm, hq = lax.optimization_barrier(
-        (move(hmm, z=-1), move(hqq, z=1), r2, g01, gm, gp, g2, h01, hm, hq)
-    )
-
+    back = move_by_core(add(g2, move(s2, core=1)), -1)
+    hmm, hqq, back = lax.optimization_barrier((move(hmm, z=-1), move(hqq, z=1), back))
     up, down = move(add(hq, hqq), z=1), move(add(hm, hmm), z=-1)
     last = move(add(h01[rows:], up[rows:], down[rows:]), y_hi=1)
     text_parts = [h01, up, down, last]
 
-    back = move_by_core(add(g2, r2), -1)
     r01, rm, rp = [move(block, core=1) for block in (s01, sm, sp)]
     none = jnp.zeros((), jnp.bfloat16)
     gm = add(gm, rm, jnp.where(core == 0, back, none))

time: 97.5 us -> 95.7 us (0.982)
  local copies, waits for them, and re-layouts: 9.47 us -> 0.04 us
  waiting for transfers between devices: 30.6 us -> 35.2 us
  other arithmetic: 2.9 us -> 4.64 us
    unnamed x25 -> x5, local copies, waits for them, and re-layouts: 9.45 us -> 0.03 us
    ppermute x26, waiting for transfers between devices: 25.2 us -> 31.9 us  [move(): return lax.ppermute(block, AXES, pairs)]
    ppermute x2, waiting for transfers between devices: 2.22 us -> 0.01 us  [move_by_core(): return lax.ppermute(block, AXES, pairs)]
    convert_element_type x6, other arithmetic: 2.76 us -> 4.5 us  [add(): return total.astype(jnp.bfloat16)]
    pallas_call x3 -> x2, Pallas kernels: 15 us -> 15.8 us  [call(): pl.pallas_call(kernel, out_shape=outs, in_specs=[SMEM] * len(scalars) + [...]
  transfers between devices with their start and end apart: 29 -> 29, of which waited for: 14 -> 16; matrix products, arithmetic and copies ran while one was open for 3% -> 5% of each run, Pallas kernels for 10% -> 6%
where the time goes in v6:
time: 95.7 us; the launch traced here: 94.4 us
  waiting for transfers between devices  35.2 us (37%)
  starting transfers between devices  33.5 us (35%)
  Pallas kernels  19.1 us (20%)
  other arithmetic  4.64 us (5%)
  between operations  2.07 us (2%)
    ppermute x26, waiting for transfers between devices, move(): return lax.ppermute(block, AXES, pairs)  31.9 us
    ppermute x26, starting transfers between devices, move(): return lax.ppermute(block, AXES, pairs)  30 us
    pallas_call x2, Pallas kernels, call(): pl.pallas_call(kernel, out_shape=outs, in_specs=[SMEM] * len(scalars) + [...  15.8 us
    convert_element_type x6, other arithmetic, add(): return total.astype(jnp.bfloat16)  4.5 us
    ppermute x1, waiting for transfers between devices, move_by_y_hi(): return lax.ppermute(block, AXES, pairs)  3.24 us
    ppermute x2, starting transfers between devices, move_by_core(): return lax.ppermute(block, AXES, pairs)  3.15 us
    pallas_call x2, Pallas kernels, back_rows(): pl.pallas_call(back_kernel, out_shape=jax.ShapeDtypeStruct(embedding.shap...  2.05 us
  transfers between devices with their start and end apart: 29, of which 16 were waited for; matrix products, arithmetic and copies ran while one was open for 5% of the time, Pallas kernels for 6%

profile of v6, /device:TPU:2, one launch (start us, length us, event | category | flops | bytes accessed | tf_op | source)
XLA Modules:
  0.0 94.4 jit_solution(18155663213924471833)
XLA Ops:
  0.6 1.2 %unit_low.1 = (bf16[128,768]{1,0:T(8,128)(2,1)S(1)}, bf16[128,768]{1,0:T(8,128)(2,1)S(1)}) custom-call(bf16[128,768]{1,0:T(8,128)(2,1)} %embedding_ref.2, bf16[128,768]{1,0:T(8,128)(2,1)} %embedding_ref.3), custom_call_target="tpu_custom_call" | custom-call | tf_op jit(solution)/shard_map/unit_low/pallas_call | solution.py:48
  1.8 1.7 %collective-permute-start = (bf16[128,768]{1,0:T(8,128)(2,1)S(1)}, bf16[128,768]{1,0:T(8,128)(2,1)S(1)}, u32[]{:S(2)}, u32[]{:S(2)}) collective-permute-start(bf16[128,768]{1,0:T(8,128)(2,1)S(1)} %get-tuple-element.36), channel_id=1, source_target_pairs={{0,1},{1,0},{2,3},{3,2},{4,5},{5,4},{6,7},{7,6},{8,9},{9,8},{10,11... | collective-permute-start | bytes 589832 | tf_op jit(solution)/shard_map/ppermute | solution.py:25
  3.5 5.9 %collective-permute-start.3 = (bf16[128,768]{1,0:T(8,128)(2,1)S(1)}, bf16[128,768]{1,0:T(8,128)(2,1)S(1)}, u32[]{:S(2)}, u32[]{:S(2)}) collective-permute-start(bf16[128,768]{1,0:T(8,128)(2,1)S(1)} %get-tuple-element.37.refs_0_), channel_id=1, source_target_pairs={{0,224},{1,225},{2,226},{3,227},{4,228},{5,229},{6,230},{7,231},{8... | collective-permute-start | bytes 589832 | tf_op jit(solution)/shard_map/ppermute | solution.py:25
  9.3 2.9 %collective-permute-start.1 = (bf16[128,768]{1,0:T(8,128)(2,1)S(1)}, bf16[128,768]{1,0:T(8,128)(2,1)S(1)}, u32[]{:S(2)}, u32[]{:S(2)}) collective-permute-start(bf16[128,768]{1,0:T(8,128)(2,1)S(1)} %get-tuple-element.37.refs_0_), channel_id=1, source_target_pairs={{0,16},{1,17},{2,18},{3,19},{4,20},{5,21},{6,22},{7,23},{8,24},{9,... | collective-permute-start | bytes 589832 | tf_op jit(solution)/shard_map/ppermute | solution.py:25
  13.2 3.4 %collective-permute-done.2.refs_2_ = bf16[128,768]{1,0:T(8,128)(2,1)S(1)} collective-permute-done((bf16[128,768]{1,0:T(8,128)(2,1)S(1)}, bf16[128,768]{1,0:T(8,128)(2,1)S(1)}, u32[]{:S(2)}, u32[]{:S(2)}) %collective-permute-start.2) | collective-permute-done | bytes 196640 | tf_op jit(solution)/shard_map/ppermute | solution.py:25
  17.8 1.5 %collective-permute-start.4 = (bf16[256,768]{1,0:T(8,128)(2,1)S(1)}, bf16[256,768]{1,0:T(8,128)(2,1)S(1)}, u32[]{:S(2)}, u32[]{:S(2)}) collective-permute-start(bf16[256,768]{1,0:T(8,128)(2,1)S(1)} %constant_dynamic-update-slice_fusion.refs_8_), channel_id=1, source_target_pairs={{0,2},{1,3},{2,4},{3,5},{4,6},{5,7},{6,0},{7,1},{8,10},{9,11},{10,... | collective-permute-start | bytes 1179656 | tf_op jit(solution)/shard_map/ppermute | solution.py:25
  19.2 3.9 %collective-permute-start.9 = (bf16[128,768]{1,0:T(8,128)(2,1)S(1)}, bf16[128,768]{1,0:T(8,128)(2,1)S(1)}, u32[]{:S(2)}, u32[]{:S(2)}) collective-permute-start(bf16[128,768]{1,0:T(8,128)(2,1)S(1)} %collective-permute-done.3.refs_4_), channel_id=1, source_target_pairs={{0,224},{1,225},{2,226},{3,227},{4,228},{5,229},{6,230},{7,231},{8... | collective-permute-start | bytes 589832 | tf_op jit(solution)/shard_map/ppermute | solution.py:25
  23.2 2.0 %collective-permute-start.7 = (bf16[128,768]{1,0:T(8,128)(2,1)S(1)}, bf16[128,768]{1,0:T(8,128)(2,1)S(1)}, u32[]{:S(2)}, u32[]{:S(2)}) collective-permute-start(bf16[128,768]{1,0:T(8,128)(2,1)S(1)} %collective-permute-done.1.refs_1_), channel_id=1, source_target_pairs={{0,224},{1,225},{2,226},{3,227},{4,228},{5,229},{6,230},{7,231},{8... | collective-permute-start | bytes 589832 | tf_op jit(solution)/shard_map/ppermute | solution.py:25
  26.6 1.4 %collective-permute-done.9.refs_7_ = bf16[128,768]{1,0:T(8,128)(2,1)S(1)} collective-permute-done((bf16[128,768]{1,0:T(8,128)(2,1)S(1)}, bf16[128,768]{1,0:T(8,128)(2,1)S(1)}, u32[]{:S(2)}, u32[]{:S(2)}) %collective-permute-start.9) | collective-permute-done | bytes 196640 | tf_op jit(solution)/shard_map/ppermute | solution.py:25
  28.0 2.1 %collective-permute-done.7.refs_5_ = bf16[128,768]{1,0:T(8,128)(2,1)S(1)} collective-permute-done((bf16[128,768]{1,0:T(8,128)(2,1)S(1)}, bf16[128,768]{1,0:T(8,128)(2,1)S(1)}, u32[]{:S(2)}, u32[]{:S(2)}) %collective-permute-start.7) | collective-permute-done | bytes 196640 | tf_op jit(solution)/shard_map/ppermute | solution.py:25
  30.1 2.0 %collective-permute-done.6.refs_3_ = bf16[128,768]{1,0:T(8,128)(2,1)S(1)} collective-permute-done((bf16[128,768]{1,0:T(8,128)(2,1)S(1)}, bf16[128,768]{1,0:T(8,128)(2,1)S(1)}, u32[]{:S(2)}, u32[]{:S(2)}) %collective-permute-start.6) | collective-permute-done | bytes 196640 | tf_op jit(solution)/shard_map/ppermute | solution.py:25
  32.7 1.6 %collective-permute-start.10 = (bf16[256,768]{1,0:T(8,128)(2,1)S(1)}, bf16[256,768]{1,0:T(8,128)(2,1)S(1)}, u32[]{:S(2)}, u32[]{:S(2)}) collective-permute-start(bf16[256,768]{1,0:T(8,128)(2,1)S(1)} %broadcast_select_fusion), channel_id=1, source_target_pairs={{0,2},{1,3},{2,4},{3,5},{4,6},{5,7},{6,0},{7,1},{8,14},{9,15},{10,... | collective-permute-start | bytes 1179656 | tf_op jit(solution)/shard_map/ppermute | solution.py:292
  34.6 4.3 %near_weights.1 = (bf16[1536,1024]{1,0:T(8,128)(2,1)S(1)}, bf16[1024,768]{1,0:T(8,128)(2,1)S(1)}, bf16[1536,768]{1,0:T(8,128)(2,1)S(1)}) custom-call(f32[1]{0:T(128)S(6)} %copy.7.scale_ref, f32[1]{0:T(128)S(6)} %copy.8.offset_ref, s32[2]{0:T(128)S(1)} %pad_add_fusion.place_ref, bf16[128,768]{1,0:T(8,128)(2,1)S(1)} %get-tuple-element.37.refs_0_, ...), custom_call_target="tpu_custom_call" | custom-call | flops 2415919104 | tf_op jit(solution)/shard_map/near_weights/pallas_call | solution.py:208
  38.9 3.2 %collective-permute-done.11.last = bf16[128,768]{1,0:T(8,128)(2,1)S(1)} collective-permute-done((bf16[128,768]{1,0:T(8,128)(2,1)S(1)}, bf16[128,768]{1,0:T(8,128)(2,1)S(1)}, u32[]{:S(2)}, u32[]{:S(2)}) %collective-permute-start.11) | collective-permute-done | bytes 196640 | tf_op jit(solution)/shard_map/ppermute | solution.py:302
  42.1 1.7 %collective-permute-done.15.refs_1_ = bf16[256,768]{1,0:T(8,128)(2,1)S(1)} collective-permute-done((bf16[256,768]{1,0:T(8,128)(2,1)S(1)}, bf16[256,768]{1,0:T(8,128)(2,1)S(1)}, u32[]{:S(2)}, u32[]{:S(2)}) %collective-permute-start.15) | collective-permute-done | bytes 393248 | tf_op jit(solution)/shard_map/ppermute | solution.py:25
  43.9 11.5 %far_weights_and_sums.1 = (bf16[256,768]{1,0:T(8,128)(2,1)}, bf16[256,768]{1,0:T(8,128)(2,1)}, bf16[256,768]{1,0:T(8,128)(2,1)S(1)}, bf16[256,768]{1,0:T(8,128)(...) custom-call(f32[1]{0:T(128)S(6)} %copy.7.scale_ref, ...), custom_call_target="tpu_custom_call" | custom-call | flops 9059696640 | tf_op jit(solution)/shard_map/far_weights_and_sums/pallas_call | solution.py:208
  56.4 1.1 %collective-permute-start.19 = (bf16[256,768]{1,0:T(8,128)(2,1)}, bf16[256,768]{1,0:T(8,128)(2,1)}, u32[]{:S(2)}, u32[]{:S(2)}) collective-permute-start(bf16[256,768]{1,0:T(8,128)(2,1)} %get-tuple-element.59), channel_id=1, source_target_pairs={{0,32},{1,33},{2,34},{3,35},{4,36},{5,37},{6,38},{7,39},{8,40},{9,... | collective-permute-start | bytes 1179656 | tf_op jit(solution)/shard_map/ppermute | solution.py:25
  58.4 1.6 %collective-permute-start.21 = (bf16[256,768]{1,0:T(8,128)(2,1)}, bf16[256,768]{1,0:T(8,128)(2,1)}, u32[]{:S(2)}, u32[]{:S(2)}) collective-permute-start(bf16[256,768]{1,0:T(8,128)(2,1)} %add_convert_fusion.4), channel_id=1, source_target_pairs={{0,6},{1,7},{2,0},{3,1},{4,2},{5,3},{6,4},{7,5},{8,10},{9,11},{10,... | collective-permute-start | bytes 1179656 | tf_op jit(solution)/shard_map/ppermute | solution.py:292
  60.5 6.7 %collective-permute-done.18 = bf16[256,768]{1,0:T(8,128)(2,1)} collective-permute-done((bf16[256,768]{1,0:T(8,128)(2,1)}, bf16[256,768]{1,0:T(8,128)(2,1)}, u32[]{:S(2)}, u32[]{:S(2)}) %collective-permute-start.18) | collective-permute-done | bytes 393248 | tf_op jit(solution)/shard_map/ppermute | solution.py:25
  67.2 1.8 %collective-permute-done.19 = bf16[256,768]{1,0:T(8,128)(2,1)} collective-permute-done((bf16[256,768]{1,0:T(8,128)(2,1)}, bf16[256,768]{1,0:T(8,128)(2,1)}, u32[]{:S(2)}, u32[]{:S(2)}) %collective-permute-start.19) | collective-permute-done | bytes 393248 | tf_op jit(solution)/shard_map/ppermute | solution.py:25
  69.0 1.1 %add_convert_fusion.1 = bf16[256,768]{1,0:T(8,128)(2,1)S(1)} fusion(bf16[256,768]{1,0:T(8,128)(2,1)} %collective-permute-done.19, bf16[256,768]{1,0:T(8,128)(2,1)S(1)} %get-tuple-element.66), kind=kLoop, calls=%fused_computation.1 | loop fusion | flops 786432 | bytes 1179648 | tf_op jit(solution)/shard_map/convert_element_type | solution.py:32
  70.2 1.1 %add_convert_fusion = bf16[256,768]{1,0:T(8,128)(2,1)S(1)} fusion(bf16[256,768]{1,0:T(8,128)(2,1)} %collective-permute-done.18, bf16[256,768]{1,0:T(8,128)(2,1)S(1)} %get-tuple-element.68), kind=kLoop, calls=%fused_computation | loop fusion | flops 786432 | bytes 1179648 | tf_op jit(solution)/shard_map/convert_element_type | solution.py:32
  71.3 3.3 %collective-permute-start.27 = (bf16[256,768]{1,0:T(8,128)(2,1)S(1)}, bf16[256,768]{1,0:T(8,128)(2,1)S(1)}, u32[]{:S(2)}, u32[]{:S(2)}) collective-permute-start(bf16[256,768]{1,0:T(8,128)(2,1)S(1)} %add_convert_fusion), channel_id=1, source_target_pairs={{0,224},{1,225},{2,226},{3,227},{4,228},{5,229},{6,230},{7,231},{8... | collective-permute-start | bytes 1179656 | tf_op jit(solution)/shard_map/ppermute | solution.py:25
  74.6 1.3 %add_convert_fusion.2 = (bf16[256,768]{1,0:T(8,128)(2,1)S(1)}, bf16[256,768]{1,0:T(8,128)(2,1)S(1)}) fusion(bf16[256,768]{1,0:T(8,128)(2,1)S(1)} %collective-permute-done.23, bf16[256,768]{1,0:T(8,128)(2,1)S(1)} %get-tuple-element.63, bf16[256,768]{1,0:T(8,128)(2,1)} %collective-permute-done.21, pred[]{:T(512)S(6)} %eq.15, pred[]{:T(512)S(6)} %eq.13, ...), kind=kLoop, calls=%fused_computation.2 | loop fusion | flops 2752512 | bytes 2752514 | tf_op jit(solution)/shard_map/convert_element_type | solution.py:32
  76.0 2.2 %collective-permute-start.24 = (bf16[256,768]{1,0:T(8,128)(2,1)S(1)}, bf16[256,768]{1,0:T(8,128)(2,1)S(1)}, u32[]{:S(2)}, u32[]{:S(2)}) collective-permute-start(bf16[256,768]{1,0:T(8,128)(2,1)S(1)} %get-tuple-element.70), channel_id=1, source_target_pairs={{0,6},{1,7},{2,0},{3,1},{4,2},{5,3},{6,4},{7,5},{8,14},{9,15},{10,... | collective-permute-start | bytes 1179656 | tf_op jit(solution)/shard_map/ppermute | solution.py:25
  78.1 3.6 %collective-permute-done.26.refs_1_ = bf16[256,768]{1,0:T(8,128)(2,1)S(1)} collective-permute-done((bf16[256,768]{1,0:T(8,128)(2,1)S(1)}, bf16[256,768]{1,0:T(8,128)(2,1)S(1)}, u32[]{:S(2)}, u32[]{:S(2)}) %collective-permute-start.26) | collective-permute-done | bytes 393248 | tf_op jit(solution)/shard_map/ppermute | solution.py:25
  82.2 2.4 %collective-permute-start.28 = (bf16[128,768]{1,0:T(8,128)(2,1)S(1)}, bf16[128,768]{1,0:T(8,128)(2,1)S(1)}, u32[]{:S(2)}, u32[]{:S(2)}) collective-permute-start(bf16[128,768]{1,0:T(8,128)(2,1)S(1)} %add_convert_fusion.5), channel_id=1, source_target_pairs={{0,16},{1,17},{2,18},{3,19},{4,20},{5,21},{6,22},{7,23},{8,24},{9,... | collective-permute-start | bytes 589832 | tf_op jit(solution)/shard_map/ppermute | solution.py:25
  84.6 1.1 %collective-permute-done.24.refs_3_ = bf16[256,768]{1,0:T(8,128)(2,1)S(1)} collective-permute-done((bf16[256,768]{1,0:T(8,128)(2,1)S(1)}, bf16[256,768]{1,0:T(8,128)(2,1)S(1)}, u32[]{:S(2)}, u32[]{:S(2)}) %collective-permute-start.24) | collective-permute-done | bytes 393248 | tf_op jit(solution)/shard_map/ppermute | solution.py:25
  85.7 1.8 %collective-permute-done.22.refs_2_ = bf16[256,768]{1,0:T(8,128)(2,1)S(1)} collective-permute-done((bf16[256,768]{1,0:T(8,128)(2,1)S(1)}, bf16[256,768]{1,0:T(8,128)(2,1)S(1)}, u32[]{:S(2)}, u32[]{:S(2)}) %collective-permute-start.22) | collective-permute-done | bytes 393248 | tf_op jit(solution)/shard_map/ppermute | solution.py:25
  87.8 2.5 %collective-permute-done.28.refs_3_ = bf16[128,768]{1,0:T(8,128)(2,1)S(1)} collective-permute-done((bf16[128,768]{1,0:T(8,128)(2,1)S(1)}, bf16[128,768]{1,0:T(8,128)(2,1)S(1)}, u32[]{:S(2)}, u32[]{:S(2)}) %collective-permute-start.28) | collective-permute-done | bytes 196640 | tf_op jit(solution)/shard_map/ppermute | solution.py:25
  91.4 2.0 %collective-permute-done.25.refs_4_ = bf16[128,768]{1,0:T(8,128)(2,1)S(1)} collective-permute-done((bf16[128,768]{1,0:T(8,128)(2,1)S(1)}, bf16[128,768]{1,0:T(8,128)(2,1)S(1)}, u32[]{:S(2)}, u32[]{:S(2)}) %collective-permute-start.25) | collective-permute-done | bytes 196640 | tf_op jit(solution)/shard_map/ppermute | solution.py:25
  93.4 1.0 %back_rows.2 = f32[128,768]{1,0:T(8,128)} custom-call(f32[1]{0:T(128)S(6)} %copy.7.scale_ref, bf16[128,768]{1,0:T(8,128)(2,1)S(1)} %copy-done.1, bf16[256,768]{1,0:T(8,128)(2,1)S(1)} %get-tuple-element.54.refs_0_, bf16[256,768]{1,0:T(8,128)(2,1)S(1)} %collective-permute-done.16.refs_1_, bf16[256,768]{1,0:T(8,128)(2,1)S(1)} %collective-permute-done.22.refs_2_, ...), custom_call_target="tpu_custom_call" | custom-call | tf_op jit(solution)/shard_map/back_rows/pallas_call | solution.py:65
  (46 shorter events, 7.4 us)
Async XLA Ops:
  1.8 10.4 %collective-permute-start = (bf16[128,768]{1,0:T(8,128)(2,1)S(1)}, bf16[128,768]{1,0:T(8,128)(2,1)S(1)}, u32[]{:S(2)}, u32[]{:S(2)}) collective-permute-start(bf16[128,768]{1,0:T(8,128)(2,1)S(1)} %get-tuple-element.36), channel_id=1, source_target_pairs={{0,1},{1,0},{2,3},{3,2},{4,5},{5,4},{6,7},{7,6},{8,9},{9,8},{10,11... | collective-permute-start | bytes 589832 | tf_op jit(solution)/shard_map/ppermute | solution.py:25
  3.5 9.7 %collective-permute-start.3 = (bf16[128,768]{1,0:T(8,128)(2,1)S(1)}, bf16[128,768]{1,0:T(8,128)(2,1)S(1)}, u32[]{:S(2)}, u32[]{:S(2)}) collective-permute-start(bf16[128,768]{1,0:T(8,128)(2,1)S(1)} %get-tuple-element.37.refs_0_), channel_id=1, source_target_pairs={{0,224},{1,225},{2,226},{3,227},{4,228},{5,229},{6,230},{7,231},{8... | collective-permute-start | bytes 589832 | tf_op jit(solution)/shard_map/ppermute | solution.py:25
  9.3 7.3 %collective-permute-start.2 = (bf16[128,768]{1,0:T(8,128)(2,1)S(1)}, bf16[128,768]{1,0:T(8,128)(2,1)S(1)}, u32[]{:S(2)}, u32[]{:S(2)}) collective-permute-start(bf16[128,768]{1,0:T(8,128)(2,1)S(1)} %get-tuple-element.37.refs_0_), channel_id=1, source_target_pairs={{0,32},{1,33},{2,34},{3,35},{4,36},{5,37},{6,38},{7,39},{8,40},{9,... | collective-permute-start | bytes 589832 | tf_op jit(solution)/shard_map/ppermute | solution.py:25
  9.3 7.6 %collective-permute-start.1 = (bf16[128,768]{1,0:T(8,128)(2,1)S(1)}, bf16[128,768]{1,0:T(8,128)(2,1)S(1)}, u32[]{:S(2)}, u32[]{:S(2)}) collective-permute-start(bf16[128,768]{1,0:T(8,128)(2,1)S(1)} %get-tuple-element.37.refs_0_), channel_id=1, source_target_pairs={{0,16},{1,17},{2,18},{3,19},{4,20},{5,21},{6,22},{7,23},{8,24},{9,... | collective-permute-start | bytes 589832 | tf_op jit(solution)/shard_map/ppermute | solution.py:25
  16.9 8.3 %collective-permute-start.8 = (bf16[128,768]{1,0:T(8,128)(2,1)S(1)}, bf16[128,768]{1,0:T(8,128)(2,1)S(1)}, u32[]{:S(2)}, u32[]{:S(2)}) collective-permute-start(bf16[128,768]{1,0:T(8,128)(2,1)S(1)} %collective-permute-done.2.refs_2_), channel_id=1, source_target_pairs={{0,32},{1,33},{2,34},{3,35},{4,36},{5,37},{6,38},{7,39},{8,40},{9,... | collective-permute-start | bytes 589832 | tf_op jit(solution)/shard_map/ppermute | solution.py:25
  17.1 15.0 %collective-permute-start.5 = (bf16[256,768]{1,0:T(8,128)(2,1)S(1)}, bf16[256,768]{1,0:T(8,128)(2,1)S(1)}, u32[]{:S(2)}, u32[]{:S(2)}) collective-permute-start(bf16[256,768]{1,0:T(8,128)(2,1)S(1)} %constant_dynamic-update-slice_fusion.refs_8_), channel_id=1, source_target_pairs={{0,6},{1,7},{2,0},{3,1},{4,2},{5,3},{6,4},{7,5},{8,14},{9,15},{10,... | collective-permute-start | bytes 1179656 | tf_op jit(solution)/shard_map/ppermute | solution.py:25
  17.8 14.3 %collective-permute-start.4 = (bf16[256,768]{1,0:T(8,128)(2,1)S(1)}, bf16[256,768]{1,0:T(8,128)(2,1)S(1)}, u32[]{:S(2)}, u32[]{:S(2)}) collective-permute-start(bf16[256,768]{1,0:T(8,128)(2,1)S(1)} %constant_dynamic-update-slice_fusion.refs_8_), channel_id=1, source_target_pairs={{0,2},{1,3},{2,4},{3,5},{4,6},{5,7},{6,0},{7,1},{8,10},{9,11},{10,... | collective-permute-start | bytes 1179656 | tf_op jit(solution)/shard_map/ppermute | solution.py:25
  19.2 8.8 %collective-permute-start.9 = (bf16[128,768]{1,0:T(8,128)(2,1)S(1)}, bf16[128,768]{1,0:T(8,128)(2,1)S(1)}, u32[]{:S(2)}, u32[]{:S(2)}) collective-permute-start(bf16[128,768]{1,0:T(8,128)(2,1)S(1)} %collective-permute-done.3.refs_4_), channel_id=1, source_target_pairs={{0,224},{1,225},{2,226},{3,227},{4,228},{5,229},{6,230},{7,231},{8... | collective-permute-start | bytes 589832 | tf_op jit(solution)/shard_map/ppermute | solution.py:25
  23.2 6.9 %collective-permute-start.7 = (bf16[128,768]{1,0:T(8,128)(2,1)S(1)}, bf16[128,768]{1,0:T(8,128)(2,1)S(1)}, u32[]{:S(2)}, u32[]{:S(2)}) collective-permute-start(bf16[128,768]{1,0:T(8,128)(2,1)S(1)} %collective-permute-done.1.refs_1_), channel_id=1, source_target_pairs={{0,224},{1,225},{2,226},{3,227},{4,228},{5,229},{6,230},{7,231},{8... | collective-permute-start | bytes 589832 | tf_op jit(solution)/shard_map/ppermute | solution.py:25
  25.2 6.9 %collective-permute-start.6 = (bf16[128,768]{1,0:T(8,128)(2,1)S(1)}, bf16[128,768]{1,0:T(8,128)(2,1)S(1)}, u32[]{:S(2)}, u32[]{:S(2)}) collective-permute-start(bf16[128,768]{1,0:T(8,128)(2,1)S(1)} %collective-permute-done.1.refs_1_), channel_id=1, source_target_pairs={{0,32},{1,33},{2,34},{3,35},{4,36},{5,37},{6,38},{7,39},{8,40},{9,... | collective-permute-start | bytes 589832 | tf_op jit(solution)/shard_map/ppermute | solution.py:25
  28.0 6.5 %collective-permute-start.12 = (bf16[256,768]{1,0:T(8,128)(2,1)S(1)}, bf16[256,768]{1,0:T(8,128)(2,1)S(1)}, u32[]{:S(2)}, u32[]{:S(2)}) collective-permute-start(bf16[256,768]{1,0:T(8,128)(2,1)S(1)} %constant_dynamic-update-slice_fusion.refs_8_), channel_id=1, source_target_pairs={{0,8},{1,9},{2,10},{3,11},{4,12},{5,13},{6,14},{7,15},{8,0},{9,1},... | collective-permute-start | bytes 1179656 | tf_op jit(solution)/shard_map/ppermute | solution.py:25
  32.1 2.4 %collective-permute-start.14 = (bf16[256,768]{1,0:T(8,128)(2,1)S(1)}, bf16[256,768]{1,0:T(8,128)(2,1)S(1)}, u32[]{:S(2)}, u32[]{:S(2)}) collective-permute-start(bf16[256,768]{1,0:T(8,128)(2,1)S(1)} %collective-permute-done.5.refs_10_), channel_id=1, source_target_pairs={{0,8},{1,9},{2,10},{3,11},{4,12},{5,13},{6,14},{7,15},{8,0},{9,1},... | collective-permute-start | bytes 1179656 | tf_op jit(solution)/shard_map/ppermute | solution.py:25
  32.1 2.4 %collective-permute-start.13 = (bf16[256,768]{1,0:T(8,128)(2,1)S(1)}, bf16[256,768]{1,0:T(8,128)(2,1)S(1)}, u32[]{:S(2)}, u32[]{:S(2)}) collective-permute-start(bf16[256,768]{1,0:T(8,128)(2,1)S(1)} %collective-permute-done.4.refs_9_), channel_id=1, source_target_pairs={{0,8},{1,9},{2,10},{3,11},{4,12},{5,13},{6,14},{7,15},{8,0},{9,1},... | collective-permute-start | bytes 1179656 | tf_op jit(solution)/shard_map/ppermute | solution.py:25
  32.7 9.5 %collective-permute-start.10 = (bf16[256,768]{1,0:T(8,128)(2,1)S(1)}, bf16[256,768]{1,0:T(8,128)(2,1)S(1)}, u32[]{:S(2)}, u32[]{:S(2)}) collective-permute-start(bf16[256,768]{1,0:T(8,128)(2,1)S(1)} %broadcast_select_fusion), channel_id=1, source_target_pairs={{0,2},{1,3},{2,4},{3,5},{4,6},{5,7},{6,0},{7,1},{8,14},{9,15},{10,... | collective-permute-start | bytes 1179656 | tf_op jit(solution)/shard_map/ppermute | solution.py:292
  34.3 7.9 %collective-permute-start.11 = (bf16[128,768]{1,0:T(8,128)(2,1)S(1)}, bf16[128,768]{1,0:T(8,128)(2,1)S(1)}, u32[]{:S(2)}, u32[]{:S(2)}) collective-permute-start(bf16[128,768]{1,0:T(8,128)(2,1)S(1)} %broadcast_select_fusion.1), channel_id=1, source_target_pairs={{0,32},{1,33},{2,34},{3,35},{4,36},{5,37},{6,38},{7,39},{8,40},{9,... | collective-permute-start | bytes 589832 | tf_op jit(solution)/shard_map/ppermute | solution.py:302
  42.1 1.7 %collective-permute-start.15 = (bf16[256,768]{1,0:T(8,128)(2,1)S(1)}, bf16[256,768]{1,0:T(8,128)(2,1)S(1)}, u32[]{:S(2)}, u32[]{:S(2)}) collective-permute-start(bf16[256,768]{1,0:T(8,128)(2,1)S(1)} %collective-permute-done.10.refs_0_), channel_id=1, source_target_pairs={{0,8},{1,9},{2,10},{3,11},{4,12},{5,13},{6,14},{7,15},{8,0},{9,1},... | collective-permute-start | bytes 1179656 | tf_op jit(solution)/shard_map/ppermute | solution.py:25
  55.4 2.2 %collective-permute-start.20 = (bf16[256,768]{1,0:T(8,128)(2,1)S(1)}, bf16[256,768]{1,0:T(8,128)(2,1)S(1)}, u32[]{:S(2)}, u32[]{:S(2)}) collective-permute-start(bf16[256,768]{1,0:T(8,128)(2,1)S(1)} %get-tuple-element.61), channel_id=1, source_target_pairs={{0,8},{1,9},{2,10},{3,11},{4,12},{5,13},{6,14},{7,15},{8,0},{9,1},... | collective-permute-start | bytes 1179656 | tf_op jit(solution)/shard_map/ppermute | solution.py:25
  55.5 11.7 %collective-permute-start.18 = (bf16[256,768]{1,0:T(8,128)(2,1)}, bf16[256,768]{1,0:T(8,128)(2,1)}, u32[]{:S(2)}, u32[]{:S(2)}) collective-permute-start(bf16[256,768]{1,0:T(8,128)(2,1)} %get-tuple-element.58), channel_id=1, source_target_pairs={{0,224},{1,225},{2,226},{3,227},{4,228},{5,229},{6,230},{7,231},{8... | collective-permute-start | bytes 1179656 | tf_op jit(solution)/shard_map/ppermute | solution.py:25
  56.4 12.6 %collective-permute-start.19 = (bf16[256,768]{1,0:T(8,128)(2,1)}, bf16[256,768]{1,0:T(8,128)(2,1)}, u32[]{:S(2)}, u32[]{:S(2)}) collective-permute-start(bf16[256,768]{1,0:T(8,128)(2,1)} %get-tuple-element.59), channel_id=1, source_target_pairs={{0,32},{1,33},{2,34},{3,35},{4,36},{5,37},{6,38},{7,39},{8,40},{9,... | collective-permute-start | bytes 1179656 | tf_op jit(solution)/shard_map/ppermute | solution.py:25
  58.4 10.6 %collective-permute-start.21 = (bf16[256,768]{1,0:T(8,128)(2,1)}, bf16[256,768]{1,0:T(8,128)(2,1)}, u32[]{:S(2)}, u32[]{:S(2)}) collective-permute-start(bf16[256,768]{1,0:T(8,128)(2,1)} %add_convert_fusion.4), channel_id=1, source_target_pairs={{0,6},{1,7},{2,0},{3,1},{4,2},{5,3},{6,4},{7,5},{8,10},{9,11},{10,... | collective-permute-start | bytes 1179656 | tf_op jit(solution)/shard_map/ppermute | solution.py:292
  60.0 24.6 %collective-permute-start.16 = (bf16[256,768]{1,0:T(8,128)(2,1)S(1)}, bf16[256,768]{1,0:T(8,128)(2,1)S(1)}, u32[]{:S(2)}, u32[]{:S(2)}) collective-permute-start(bf16[256,768]{1,0:T(8,128)(2,1)S(1)} %get-tuple-element.55), channel_id=1, source_target_pairs={{0,8},{1,9},{2,10},{3,11},{4,12},{5,13},{6,14},{7,15},{8,0},{9,1},... | collective-permute-start | bytes 1179656 | tf_op jit(solution)/shard_map/ppermute | solution.py:25
  60.0 14.7 %collective-permute-start.17 = (bf16[256,768]{1,0:T(8,128)(2,1)S(1)}, bf16[256,768]{1,0:T(8,128)(2,1)S(1)}, u32[]{:S(2)}, u32[]{:S(2)}) collective-permute-start(bf16[256,768]{1,0:T(8,128)(2,1)S(1)} %get-tuple-element.57), channel_id=1, source_target_pairs={{0,8},{1,9},{2,10},{3,11},{4,12},{5,13},{6,14},{7,15},{8,0},{9,1},... | collective-permute-start | bytes 1179656 | tf_op jit(solution)/shard_map/ppermute | solution.py:25
  67.2 7.4 %collective-permute-start.23 = (bf16[256,768]{1,0:T(8,128)(2,1)S(1)}, bf16[256,768]{1,0:T(8,128)(2,1)S(1)}, u32[]{:S(2)}, u32[]{:S(2)}) collective-permute-start(bf16[256,768]{1,0:T(8,128)(2,1)S(1)} %get-tuple-element.64), channel_id=1, source_target_pairs={{0,8},{1,9},{2,10},{3,11},{4,12},{5,13},{6,14},{7,15},{8,0},{9,1},... | collective-permute-start | bytes 1179656 | tf_op jit(solution)/shard_map/ppermute | solution.py:25
  70.1 11.5 %collective-permute-start.26 = (bf16[256,768]{1,0:T(8,128)(2,1)S(1)}, bf16[256,768]{1,0:T(8,128)(2,1)S(1)}, u32[]{:S(2)}, u32[]{:S(2)}) collective-permute-start(bf16[256,768]{1,0:T(8,128)(2,1)S(1)} %add_convert_fusion.1), channel_id=1, source_target_pairs={{0,32},{1,33},{2,34},{3,35},{4,36},{5,37},{6,38},{7,39},{8,40},{9,... | collective-permute-start | bytes 1179656 | tf_op jit(solution)/shard_map/ppermute | solution.py:25
  71.3 19.0 %copy-start = (bf16[128,768]{1,0:T(8,128)(2,1)S(1)}, bf16[128,768]{1,0:T(8,128)(2,1)}, u32[]{:S(2)}) copy-start(bf16[128,768]{1,0:T(8,128)(2,1)} %embedding_ref.3) | copy-start | bytes 589828
  71.3 10.8 %collective-permute-start.27 = (bf16[256,768]{1,0:T(8,128)(2,1)S(1)}, bf16[256,768]{1,0:T(8,128)(2,1)S(1)}, u32[]{:S(2)}, u32[]{:S(2)}) collective-permute-start(bf16[256,768]{1,0:T(8,128)(2,1)S(1)} %add_convert_fusion), channel_id=1, source_target_pairs={{0,224},{1,225},{2,226},{3,227},{4,228},{5,229},{6,230},{7,231},{8... | collective-permute-start | bytes 1179656 | tf_op jit(solution)/shard_map/ppermute | solution.py:25
  76.0 17.5 %copy-start.1 = (bf16[128,768]{1,0:T(8,128)(2,1)S(1)}, bf16[128,768]{1,0:T(8,128)(2,1)}, u32[]{:S(2)}) copy-start(bf16[128,768]{1,0:T(8,128)(2,1)} %embedding_ref.2) | copy-start | bytes 589828
  76.0 9.8 %collective-permute-start.24 = (bf16[256,768]{1,0:T(8,128)(2,1)S(1)}, bf16[256,768]{1,0:T(8,128)(2,1)S(1)}, u32[]{:S(2)}, u32[]{:S(2)}) collective-permute-start(bf16[256,768]{1,0:T(8,128)(2,1)S(1)} %get-tuple-element.70), channel_id=1, source_target_pairs={{0,6},{1,7},{2,0},{3,1},{4,2},{5,3},{6,4},{7,5},{8,14},{9,15},{10,... | collective-permute-start | bytes 1179656 | tf_op jit(solution)/shard_map/ppermute | solution.py:25
  78.1 9.4 %collective-permute-start.22 = (bf16[256,768]{1,0:T(8,128)(2,1)S(1)}, bf16[256,768]{1,0:T(8,128)(2,1)S(1)}, u32[]{:S(2)}, u32[]{:S(2)}) collective-permute-start(bf16[256,768]{1,0:T(8,128)(2,1)S(1)} %get-tuple-element.71), channel_id=1, source_target_pairs={{0,2},{1,3},{2,4},{3,5},{4,6},{5,7},{6,0},{7,1},{8,10},{9,11},{10,... | collective-permute-start | bytes 1179656 | tf_op jit(solution)/shard_map/ppermute | solution.py:25
  82.2 8.1 %collective-permute-start.28 = (bf16[128,768]{1,0:T(8,128)(2,1)S(1)}, bf16[128,768]{1,0:T(8,128)(2,1)S(1)}, u32[]{:S(2)}, u32[]{:S(2)}) collective-permute-start(bf16[128,768]{1,0:T(8,128)(2,1)S(1)} %add_convert_fusion.5), channel_id=1, source_target_pairs={{0,16},{1,17},{2,18},{3,19},{4,20},{5,21},{6,22},{7,23},{8,24},{9,... | collective-permute-start | bytes 589832 | tf_op jit(solution)/shard_map/ppermute | solution.py:25
  87.6 5.8 %collective-permute-start.25 = (bf16[128,768]{1,0:T(8,128)(2,1)S(1)}, bf16[128,768]{1,0:T(8,128)(2,1)S(1)}, u32[]{:S(2)}, u32[]{:S(2)}) collective-permute-start(bf16[128,768]{1,0:T(8,128)(2,1)S(1)} %add_convert_fusion.6), channel_id=1, source_target_pairs={{0,1},{1,0},{2,3},{3,2},{4,5},{5,4},{6,7},{7,6},{8,9},{9,8},{10,11... | collective-permute-start | bytes 589832 | tf_op jit(solution)/shard_map/ppermute | solution.py:25

commit v7 on v5

--- a/solution.py
+++ b/solution.py
@@ -142,11 +142,10 @@
     def dot(a, b):
         return jnp.dot(a, b[...], preferred_element_type=jnp.float32)
 
-    tile = near.shape[0] // 2
-    rows = pl.ds(half * tile, tile)
-    total = dot(near[rows, :], text) + dot(last_weights[rows, :], last)
     for i, out in enumerate(outs[:3]):
-        out[...] = total[i * PAIR : (i + 1) * PAIR].astype(jnp.bfloat16)
+        rows = pl.ds(half * (near.shape[0] // 2) + i * PAIR, PAIR)
+        total = dot(near[rows, :], text) + dot(last_weights[rows, :], last)
+        out[...] = total.astype(jnp.bfloat16)
     rows = pl.ds(half * PAIR, PAIR)
     total = dot(far[rows, : 4 * PAIR], text) + dot(far[rows, 4 * PAIR :], last)
     outs[3][...] = total.astype(jnp.bfloat16)
@@ -247,7 +246,7 @@
         scalars,
         texts + videos,
         [low(near_rows, 4 * PAIR), low(4 * PAIR), low(near_rows)],
-        8,
+        4,
         FLOPS * 3 // 5,
         2 * near_rows * 4 * PAIR,
     )
@@ -259,7 +258,7 @@
         [near, text, near_video, b2, v2, move(v2, core=1)],
         [low(near_rows, PAIR // 2), low(far_rows, 4 * PAIR + PAIR // 2), low(far_rows)]
         + [low(PAIR)] * 6,
-        11,
+        4,
         FLOPS * 5 // 4,
         2 * far_rows * 5 * PAIR,
     )
@@ -271,18 +270,18 @@
         [],
         [near, last, far, text, b2, near_video, far_video],
         [low(PAIR)] * 7,
-        11,
+        4,
         FLOPS,
     )
-    hmm, hqq, r2, g01, gm, gp, g2, h01, hm, hq = lax.optimization_barrier(
-        (move(hmm, z=-1), move(hqq, z=1), r2, g01, gm, gp, g2, h01, hm, hq)
+    back = move_by_core(add(g2, r2), -1)
+    hmm, hqq, back, g01, gm, gp, h01, hm, hq = lax.optimization_barrier(
+        (move(hmm, z=-1), move(hqq, z=1), back, g01, gm, gp, h01, hm, hq)
     )
 
     up, down = move(add(hq, hqq), z=1), move(add(hm, hmm), z=-1)
     last = move(add(h01[rows:], up[rows:], down[rows:]), y_hi=1)
     text_parts = [h01, up, down, last]
 
-    back = move_by_core(add(g2, r2), -1)
     r01, rm, rp = [move(block, core=1) for block in (s01, sm, sp)]
     none = jnp.zeros((), jnp.bfloat16)
     gm = add(gm, rm, jnp.where(core == 0, back, none))

time: 97.5 us -> 95.1 us (0.975)
  the two profiles are of different devices: /device:TPU:2 before, /device:TPU:8 now
where the time goes in v7:
time: 95.1 us; the launch traced here: 94.9 us
  waiting for transfers between devices  34.7 us (36%)
  starting transfers between devices  34.2 us (36%)
  Pallas kernels  19.2 us (20%)
  other arithmetic  4.64 us (5%)
  between operations  2.08 us (2%)
    ppermute x26, starting transfers between devices, move(): return lax.ppermute(block, AXES, pairs)  31.1 us
    ppermute x26, waiting for transfers between devices, move(): return lax.ppermute(block, AXES, pairs)  30 us
    pallas_call x3, Pallas kernels, call(): pl.pallas_call(kernel, out_shape=outs, in_specs=[SMEM] * len(scalars) + [...  16 us
    convert_element_type x6, other arithmetic, add(): return total.astype(jnp.bfloat16)  4.5 us
    ppermute x2, starting transfers between devices, move_by_core(): return lax.ppermute(block, AXES, pairs)  2.79 us
    ppermute x1, waiting for transfers between devices, move_by_y_hi(): return lax.ppermute(block, AXES, pairs)  2.72 us
    pallas_call x2, Pallas kernels, back_rows(): pl.pallas_call(back_kernel, out_shape=jax.ShapeDtypeStruct(embedding.shap...  2.05 us
    ppermute x2, waiting for transfers between devices, move_by_core(): return lax.ppermute(block, AXES, pairs)  2.03 us
  transfers between devices with their start and end apart: 29, of which 18 were waited for; matrix products, arithmetic and copies ran while one was open for 5% of the time, Pallas kernels for 11%

profile of v7, /device:TPU:8, one launch (start us, length us, event | category | flops | bytes accessed | tf_op | source)
XLA Modules:
  0.0 94.9 jit_solution(14186053646253508099)
XLA Ops:
  0.6 1.2 %unit_low.1 = (bf16[128,768]{1,0:T(8,128)(2,1)S(1)}, bf16[128,768]{1,0:T(8,128)(2,1)S(1)}) custom-call(bf16[128,768]{1,0:T(8,128)(2,1)} %embedding_ref.2, bf16[128,768]{1,0:T(8,128)(2,1)} %embedding_ref.3), custom_call_target="tpu_custom_call" | custom-call | tf_op jit(solution)/shard_map/unit_low/pallas_call | solution.py:48
  1.8 2.3 %collective-permute-start = (bf16[128,768]{1,0:T(8,128)(2,1)S(1)}, bf16[128,768]{1,0:T(8,128)(2,1)S(1)}, u32[]{:S(2)}, u32[]{:S(2)}) collective-permute-start(bf16[128,768]{1,0:T(8,128)(2,1)S(1)} %get-tuple-element.45), channel_id=1, source_target_pairs={{0,1},{1,0},{2,3},{3,2},{4,5},{5,4},{6,7},{7,6},{8,9},{9,8},{10,11... | collective-permute-start | bytes 589832 | tf_op jit(solution)/shard_map/ppermute | solution.py:25
  4.1 4.1 %collective-permute-start.3 = (bf16[128,768]{1,0:T(8,128)(2,1)S(1)}, bf16[128,768]{1,0:T(8,128)(2,1)S(1)}, u32[]{:S(2)}, u32[]{:S(2)}) collective-permute-start(bf16[128,768]{1,0:T(8,128)(2,1)S(1)} %get-tuple-element.46.refs_0_), channel_id=1, source_target_pairs={{0,224},{1,225},{2,226},{3,227},{4,228},{5,229},{6,230},{7,231},{8... | collective-permute-start | bytes 589832 | tf_op jit(solution)/shard_map/ppermute | solution.py:25
  8.2 2.6 %collective-permute-start.1 = (bf16[128,768]{1,0:T(8,128)(2,1)S(1)}, bf16[128,768]{1,0:T(8,128)(2,1)S(1)}, u32[]{:S(2)}, u32[]{:S(2)}) collective-permute-start(bf16[128,768]{1,0:T(8,128)(2,1)S(1)} %get-tuple-element.46.refs_0_), channel_id=1, source_target_pairs={{0,16},{1,17},{2,18},{3,19},{4,20},{5,21},{6,22},{7,23},{8,24},{9,... | collective-permute-start | bytes 589832 | tf_op jit(solution)/shard_map/ppermute | solution.py:25
  10.8 1.3 %collective-permute-done.3.refs_4_ = bf16[128,768]{1,0:T(8,128)(2,1)S(1)} collective-permute-done((bf16[128,768]{1,0:T(8,128)(2,1)S(1)}, bf16[128,768]{1,0:T(8,128)(2,1)S(1)}, u32[]{:S(2)}, u32[]{:S(2)}) %collective-permute-start.3) | collective-permute-done | bytes 196640 | tf_op jit(solution)/shard_map/ppermute | solution.py:25
  12.1 3.4 %collective-permute-done.2.refs_2_ = bf16[128,768]{1,0:T(8,128)(2,1)S(1)} collective-permute-done((bf16[128,768]{1,0:T(8,128)(2,1)S(1)}, bf16[128,768]{1,0:T(8,128)(2,1)S(1)}, u32[]{:S(2)}, u32[]{:S(2)}) %collective-permute-start.2) | collective-permute-done | bytes 196640 | tf_op jit(solution)/shard_map/ppermute | solution.py:25
  15.8 2.8 %collective-permute-start.5 = (bf16[256,768]{1,0:T(8,128)(2,1)S(1)}, bf16[256,768]{1,0:T(8,128)(2,1)S(1)}, u32[]{:S(2)}, u32[]{:S(2)}) collective-permute-start(bf16[256,768]{1,0:T(8,128)(2,1)S(1)} %constant_dynamic-update-slice_fusion.refs_8_), channel_id=1, source_target_pairs={{0,6},{1,7},{2,0},{3,1},{4,2},{5,3},{6,4},{7,5},{8,14},{9,15},{10,... | collective-permute-start | bytes 1179656 | tf_op jit(solution)/shard_map/ppermute | solution.py:25
  18.7 3.8 %collective-permute-start.9 = (bf16[128,768]{1,0:T(8,128)(2,1)S(1)}, bf16[128,768]{1,0:T(8,128)(2,1)S(1)}, u32[]{:S(2)}, u32[]{:S(2)}) collective-permute-start(bf16[128,768]{1,0:T(8,128)(2,1)S(1)} %collective-permute-done.3.refs_4_), channel_id=1, source_target_pairs={{0,224},{1,225},{2,226},{3,227},{4,228},{5,229},{6,230},{7,231},{8... | collective-permute-start | bytes 589832 | tf_op jit(solution)/shard_map/ppermute | solution.py:25
  22.5 2.0 %collective-permute-start.7 = (bf16[128,768]{1,0:T(8,128)(2,1)S(1)}, bf16[128,768]{1,0:T(8,128)(2,1)S(1)}, u32[]{:S(2)}, u32[]{:S(2)}) collective-permute-start(bf16[128,768]{1,0:T(8,128)(2,1)S(1)} %collective-permute-done.1.refs_1_), channel_id=1, source_target_pairs={{0,224},{1,225},{2,226},{3,227},{4,228},{5,229},{6,230},{7,231},{8... | collective-permute-start | bytes 589832 | tf_op jit(solution)/shard_map/ppermute | solution.py:25
  25.9 1.7 %collective-permute-done.9.refs_7_ = bf16[128,768]{1,0:T(8,128)(2,1)S(1)} collective-permute-done((bf16[128,768]{1,0:T(8,128)(2,1)S(1)}, bf16[128,768]{1,0:T(8,128)(2,1)S(1)}, u32[]{:S(2)}, u32[]{:S(2)}) %collective-permute-start.9) | collective-permute-done | bytes 196640 | tf_op jit(solution)/shard_map/ppermute | solution.py:25
  27.6 2.1 %collective-permute-done.7.refs_5_ = bf16[128,768]{1,0:T(8,128)(2,1)S(1)} collective-permute-done((bf16[128,768]{1,0:T(8,128)(2,1)S(1)}, bf16[128,768]{1,0:T(8,128)(2,1)S(1)}, u32[]{:S(2)}, u32[]{:S(2)}) %collective-permute-start.7) | collective-permute-done | bytes 196640 | tf_op jit(solution)/shard_map/ppermute | solution.py:25
  29.7 1.7 %collective-permute-done.6.refs_3_ = bf16[128,768]{1,0:T(8,128)(2,1)S(1)} collective-permute-done((bf16[128,768]{1,0:T(8,128)(2,1)S(1)}, bf16[128,768]{1,0:T(8,128)(2,1)S(1)}, u32[]{:S(2)}, u32[]{:S(2)}) %collective-permute-start.6) | collective-permute-done | bytes 196640 | tf_op jit(solution)/shard_map/ppermute | solution.py:25
  33.7 4.3 %near_weights.1 = (bf16[1536,1024]{1,0:T(8,128)(2,1)S(1)}, bf16[1024,768]{1,0:T(8,128)(2,1)S(1)}, bf16[1536,768]{1,0:T(8,128)(2,1)S(1)}) custom-call(f32[1]{0:T(128)S(6)} %copy.7.scale_ref, f32[1]{0:T(128)S(6)} %copy.8.offset_ref, s32[2]{0:T(128)S(1)} %pad_add_fusion.place_ref, bf16[128,768]{1,0:T(8,128)(2,1)S(1)} %get-tuple-element.46.refs_0_, ...), custom_call_target="tpu_custom_call" | custom-call | flops 2415919104 | tf_op jit(solution)/shard_map/near_weights/pallas_call | solution.py:209
  38.0 2.7 %collective-permute-done.11.last = bf16[128,768]{1,0:T(8,128)(2,1)S(1)} collective-permute-done((bf16[128,768]{1,0:T(8,128)(2,1)S(1)}, bf16[128,768]{1,0:T(8,128)(2,1)S(1)}, u32[]{:S(2)}, u32[]{:S(2)}) %collective-permute-start.11) | collective-permute-done | bytes 196640 | tf_op jit(solution)/shard_map/ppermute | solution.py:315
  41.9 1.3 %collective-permute-done.15.refs_1_ = bf16[256,768]{1,0:T(8,128)(2,1)S(1)} collective-permute-done((bf16[256,768]{1,0:T(8,128)(2,1)S(1)}, bf16[256,768]{1,0:T(8,128)(2,1)S(1)}, u32[]{:S(2)}, u32[]{:S(2)}) %collective-permute-start.15) | collective-permute-done | bytes 393248 | tf_op jit(solution)/shard_map/ppermute | solution.py:25
  43.2 7.0 %far_weights_and_sums.1 = (bf16[1536,128]{1,0:T(8,128)(2,1)S(1)}, bf16[512,1152]{1,0:T(8,128)(2,1)S(1)}, bf16[512,768]{1,0:T(8,128)(2,1)S(1)}, bf16[256,768]{1,0...) custom-call(f32[1]{0:T(128)S(6)} %copy.7.scale_ref, ...), custom_call_target="tpu_custom_call" | custom-call | flops 5033164800 | tf_op jit(solution)/shard_map/far_weights_and_sums/pallas_call | solution.py:209
  50.6 1.4 %collective-permute-start.16 = (bf16[256,768]{1,0:T(8,128)(2,1)}, bf16[256,768]{1,0:T(8,128)(2,1)}, u32[]{:S(2)}, u32[]{:S(2)}) collective-permute-start(bf16[256,768]{1,0:T(8,128)(2,1)} %get-tuple-element.63), channel_id=1, source_target_pairs={{0,224},{1,225},{2,226},{3,227},{4,228},{5,229},{6,230},{7,231},{8... | collective-permute-start | bytes 1179656 | tf_op jit(solution)/shard_map/ppermute | solution.py:25
  52.6 4.7 %own_video_and_near_text_sums.1 = (bf16[256,768]{1,0:T(8,128)(2,1)S(1)}, bf16[256,768]{1,0:T(8,128)(2,1)S(1)}, bf16[256,768]{1,0:T(8,128)(2,1)S(1)}, bf16[256,76...) custom-call(bf16[1536,1024]{1,0:T(8,128)(2,1)S(1)} %get-tuple-elemen, ...), custom_call_target="tpu_custom_call" | custom-call | flops 4026531840 | tf_op jit(solution)/shard_map/own_video_and_near_text_sums/pallas_call | solution.py:209
  58.2 2.0 %collective-permute-start.19 = (bf16[256,768]{1,0:T(8,128)(2,1)}, bf16[256,768]{1,0:T(8,128)(2,1)}, u32[]{:S(2)}, u32[]{:S(2)}) collective-permute-start(bf16[256,768]{1,0:T(8,128)(2,1)} %add_convert_fusion.4), channel_id=1, source_target_pairs={{0,6},{1,7},{2,0},{3,1},{4,2},{5,3},{6,4},{7,5},{8,10},{9,11},{10,... | collective-permute-start | bytes 1179656 | tf_op jit(solution)/shard_map/ppermute | solution.py:305
  60.6 1.4 %collective-permute-done.16 = bf16[256,768]{1,0:T(8,128)(2,1)} collective-permute-done((bf16[256,768]{1,0:T(8,128)(2,1)}, bf16[256,768]{1,0:T(8,128)(2,1)}, u32[]{:S(2)}, u32[]{:S(2)}) %collective-permute-start.16) | collective-permute-done | bytes 393248 | tf_op jit(solution)/shard_map/ppermute | solution.py:25
  62.1 2.5 %collective-permute-done.17 = bf16[256,768]{1,0:T(8,128)(2,1)} collective-permute-done((bf16[256,768]{1,0:T(8,128)(2,1)}, bf16[256,768]{1,0:T(8,128)(2,1)}, u32[]{:S(2)}, u32[]{:S(2)}) %collective-permute-start.17) | collective-permute-done | bytes 393248 | tf_op jit(solution)/shard_map/ppermute | solution.py:25
  64.6 1.7 %collective-permute-done.19 = bf16[256,768]{1,0:T(8,128)(2,1)} collective-permute-done((bf16[256,768]{1,0:T(8,128)(2,1)}, bf16[256,768]{1,0:T(8,128)(2,1)}, u32[]{:S(2)}, u32[]{:S(2)}) %collective-permute-start.19) | collective-permute-done | bytes 393248 | tf_op jit(solution)/shard_map/ppermute | solution.py:305
  66.3 1.1 %add_convert_fusion = bf16[256,768]{1,0:T(8,128)(2,1)S(1)} fusion(bf16[256,768]{1,0:T(8,128)(2,1)} %collective-permute-done.16, bf16[256,768]{1,0:T(8,128)(2,1)S(1)} %get-tuple-element.86), kind=kLoop, calls=%fused_computation | loop fusion | flops 786432 | bytes 1179648 | tf_op jit(solution)/shard_map/convert_element_type | solution.py:32
  67.4 2.7 %collective-permute-start.27 = (bf16[256,768]{1,0:T(8,128)(2,1)S(1)}, bf16[256,768]{1,0:T(8,128)(2,1)S(1)}, u32[]{:S(2)}, u32[]{:S(2)}) collective-permute-start(bf16[256,768]{1,0:T(8,128)(2,1)S(1)} %add_convert_fusion), channel_id=1, source_target_pairs={{0,224},{1,225},{2,226},{3,227},{4,228},{5,229},{6,230},{7,231},{8... | collective-permute-start | bytes 1179656 | tf_op jit(solution)/shard_map/ppermute | solution.py:25
  70.0 1.1 %add_convert_fusion.1 = bf16[256,768]{1,0:T(8,128)(2,1)S(1)} fusion(bf16[256,768]{1,0:T(8,128)(2,1)} %collective-permute-done.17, bf16[256,768]{1,0:T(8,128)(2,1)S(1)} %get-tuple-element.84), kind=kLoop, calls=%fused_computation.1 | loop fusion | flops 786432 | bytes 1179648 | tf_op jit(solution)/shard_map/convert_element_type | solution.py:32
  71.2 1.3 %add_convert_fusion.2 = (bf16[256,768]{1,0:T(8,128)(2,1)S(1)}, bf16[256,768]{1,0:T(8,128)(2,1)S(1)}) fusion(bf16[256,768]{1,0:T(8,128)(2,1)S(1)} %collective-permute-done.23, bf16[256,768]{1,0:T(8,128)(2,1)S(1)} %get-tuple-element.81, bf16[256,768]{1,0:T(8,128)(2,1)} %collective-permute-done.19, pred[]{:T(512)S(6)} %eq.15, pred[]{:T(512)S(6)} %eq.13, ...), kind=kLoop, calls=%fused_computation.2 | loop fusion | flops 2752512 | bytes 2752514 | tf_op jit(solution)/shard_map/convert_element_type | solution.py:32
  72.6 3.0 %collective-permute-start.24 = (bf16[256,768]{1,0:T(8,128)(2,1)S(1)}, bf16[256,768]{1,0:T(8,128)(2,1)S(1)}, u32[]{:S(2)}, u32[]{:S(2)}) collective-permute-start(bf16[256,768]{1,0:T(8,128)(2,1)S(1)} %get-tuple-element.88), channel_id=1, source_target_pairs={{0,6},{1,7},{2,0},{3,1},{4,2},{5,3},{6,4},{7,5},{8,14},{9,15},{10,... | collective-permute-start | bytes 1179656 | tf_op jit(solution)/shard_map/ppermute | solution.py:25
  75.6 2.8 %collective-permute-done.27.refs_2_ = bf16[256,768]{1,0:T(8,128)(2,1)S(1)} collective-permute-done((bf16[256,768]{1,0:T(8,128)(2,1)S(1)}, bf16[256,768]{1,0:T(8,128)(2,1)S(1)}, u32[]{:S(2)}, u32[]{:S(2)}) %collective-permute-start.27) | collective-permute-done | bytes 393248 | tf_op jit(solution)/shard_map/ppermute | solution.py:25
  78.4 4.6 %collective-permute-done.26.refs_1_ = bf16[256,768]{1,0:T(8,128)(2,1)S(1)} collective-permute-done((bf16[256,768]{1,0:T(8,128)(2,1)S(1)}, bf16[256,768]{1,0:T(8,128)(2,1)S(1)}, u32[]{:S(2)}, u32[]{:S(2)}) %collective-permute-start.26) | collective-permute-done | bytes 393248 | tf_op jit(solution)/shard_map/ppermute | solution.py:25
  83.1 1.4 %collective-permute-start.28 = (bf16[128,768]{1,0:T(8,128)(2,1)S(1)}, bf16[128,768]{1,0:T(8,128)(2,1)S(1)}, u32[]{:S(2)}, u32[]{:S(2)}) collective-permute-start(bf16[128,768]{1,0:T(8,128)(2,1)S(1)} %add_convert_fusion.5), channel_id=1, source_target_pairs={{0,16},{1,17},{2,18},{3,19},{4,20},{5,21},{6,22},{7,23},{8,24},{9,... | collective-permute-start | bytes 589832 | tf_op jit(solution)/shard_map/ppermute | solution.py:25
  85.1 2.0 %collective-permute-start.25 = (bf16[128,768]{1,0:T(8,128)(2,1)S(1)}, bf16[128,768]{1,0:T(8,128)(2,1)S(1)}, u32[]{:S(2)}, u32[]{:S(2)}) collective-permute-start(bf16[128,768]{1,0:T(8,128)(2,1)S(1)} %add_convert_fusion.6), channel_id=1, source_target_pairs={{0,1},{1,0},{2,3},{3,2},{4,5},{5,4},{6,7},{7,6},{8,9},{9,8},{10,11... | collective-permute-start | bytes 589832 | tf_op jit(solution)/shard_map/ppermute | solution.py:25
  87.1 5.2 %collective-permute-done.28.refs_3_ = bf16[128,768]{1,0:T(8,128)(2,1)S(1)} collective-permute-done((bf16[128,768]{1,0:T(8,128)(2,1)S(1)}, bf16[128,768]{1,0:T(8,128)(2,1)S(1)}, u32[]{:S(2)}, u32[]{:S(2)}) %collective-permute-start.28) | collective-permute-done | bytes 196640 | tf_op jit(solution)/shard_map/ppermute | solution.py:25
  (47 shorter events, 9.6 us)
Async XLA Ops:
  1.8 9.0 %collective-permute-start = (bf16[128,768]{1,0:T(8,128)(2,1)S(1)}, bf16[128,768]{1,0:T(8,128)(2,1)S(1)}, u32[]{:S(2)}, u32[]{:S(2)}) collective-permute-start(bf16[128,768]{1,0:T(8,128)(2,1)S(1)} %get-tuple-element.45), channel_id=1, source_target_pairs={{0,1},{1,0},{2,3},{3,2},{4,5},{5,4},{6,7},{7,6},{8,9},{9,8},{10,11... | collective-permute-start | bytes 589832 | tf_op jit(solution)/shard_map/ppermute | solution.py:25
  4.1 8.0 %collective-permute-start.3 = (bf16[128,768]{1,0:T(8,128)(2,1)S(1)}, bf16[128,768]{1,0:T(8,128)(2,1)S(1)}, u32[]{:S(2)}, u32[]{:S(2)}) collective-permute-start(bf16[128,768]{1,0:T(8,128)(2,1)S(1)} %get-tuple-element.46.refs_0_), channel_id=1, source_target_pairs={{0,224},{1,225},{2,226},{3,227},{4,228},{5,229},{6,230},{7,231},{8... | collective-permute-start | bytes 589832 | tf_op jit(solution)/shard_map/ppermute | solution.py:25
  8.2 7.3 %collective-permute-start.2 = (bf16[128,768]{1,0:T(8,128)(2,1)S(1)}, bf16[128,768]{1,0:T(8,128)(2,1)S(1)}, u32[]{:S(2)}, u32[]{:S(2)}) collective-permute-start(bf16[128,768]{1,0:T(8,128)(2,1)S(1)} %get-tuple-element.46.refs_0_), channel_id=1, source_target_pairs={{0,32},{1,33},{2,34},{3,35},{4,36},{5,37},{6,38},{7,39},{8,40},{9,... | collective-permute-start | bytes 589832 | tf_op jit(solution)/shard_map/ppermute | solution.py:25
  8.2 7.6 %collective-permute-start.1 = (bf16[128,768]{1,0:T(8,128)(2,1)S(1)}, bf16[128,768]{1,0:T(8,128)(2,1)S(1)}, u32[]{:S(2)}, u32[]{:S(2)}) collective-permute-start(bf16[128,768]{1,0:T(8,128)(2,1)S(1)} %get-tuple-element.46.refs_0_), channel_id=1, source_target_pairs={{0,16},{1,17},{2,18},{3,19},{4,20},{5,21},{6,22},{7,23},{8,24},{9,... | collective-permute-start | bytes 589832 | tf_op jit(solution)/shard_map/ppermute | solution.py:25
  15.8 8.7 %collective-permute-start.8 = (bf16[128,768]{1,0:T(8,128)(2,1)S(1)}, bf16[128,768]{1,0:T(8,128)(2,1)S(1)}, u32[]{:S(2)}, u32[]{:S(2)}) collective-permute-start(bf16[128,768]{1,0:T(8,128)(2,1)S(1)} %collective-permute-done.2.refs_2_), channel_id=1, source_target_pairs={{0,32},{1,33},{2,34},{3,35},{4,36},{5,37},{6,38},{7,39},{8,40},{9,... | collective-permute-start | bytes 589832 | tf_op jit(solution)/shard_map/ppermute | solution.py:25
  15.8 15.6 %collective-permute-start.5 = (bf16[256,768]{1,0:T(8,128)(2,1)S(1)}, bf16[256,768]{1,0:T(8,128)(2,1)S(1)}, u32[]{:S(2)}, u32[]{:S(2)}) collective-permute-start(bf16[256,768]{1,0:T(8,128)(2,1)S(1)} %constant_dynamic-update-slice_fusion.refs_8_), channel_id=1, source_target_pairs={{0,6},{1,7},{2,0},{3,1},{4,2},{5,3},{6,4},{7,5},{8,14},{9,15},{10,... | collective-permute-start | bytes 1179656 | tf_op jit(solution)/shard_map/ppermute | solution.py:25
  18.7 12.7 %collective-permute-start.4 = (bf16[256,768]{1,0:T(8,128)(2,1)S(1)}, bf16[256,768]{1,0:T(8,128)(2,1)S(1)}, u32[]{:S(2)}, u32[]{:S(2)}) collective-permute-start(bf16[256,768]{1,0:T(8,128)(2,1)S(1)} %constant_dynamic-update-slice_fusion.refs_8_), channel_id=1, source_target_pairs={{0,2},{1,3},{2,4},{3,5},{4,6},{5,7},{6,0},{7,1},{8,10},{9,11},{10,... | collective-permute-start | bytes 1179656 | tf_op jit(solution)/shard_map/ppermute | solution.py:25
  18.7 8.9 %collective-permute-start.9 = (bf16[128,768]{1,0:T(8,128)(2,1)S(1)}, bf16[128,768]{1,0:T(8,128)(2,1)S(1)}, u32[]{:S(2)}, u32[]{:S(2)}) collective-permute-start(bf16[128,768]{1,0:T(8,128)(2,1)S(1)} %collective-permute-done.3.refs_4_), channel_id=1, source_target_pairs={{0,224},{1,225},{2,226},{3,227},{4,228},{5,229},{6,230},{7,231},{8... | collective-permute-start | bytes 589832 | tf_op jit(solution)/shard_map/ppermute | solution.py:25
  22.5 7.2 %collective-permute-start.7 = (bf16[128,768]{1,0:T(8,128)(2,1)S(1)}, bf16[128,768]{1,0:T(8,128)(2,1)S(1)}, u32[]{:S(2)}, u32[]{:S(2)}) collective-permute-start(bf16[128,768]{1,0:T(8,128)(2,1)S(1)} %collective-permute-done.1.refs_1_), channel_id=1, source_target_pairs={{0,224},{1,225},{2,226},{3,227},{4,228},{5,229},{6,230},{7,231},{8... | collective-permute-start | bytes 589832 | tf_op jit(solution)/shard_map/ppermute | solution.py:25
  24.5 6.9 %collective-permute-start.6 = (bf16[128,768]{1,0:T(8,128)(2,1)S(1)}, bf16[128,768]{1,0:T(8,128)(2,1)S(1)}, u32[]{:S(2)}, u32[]{:S(2)}) collective-permute-start(bf16[128,768]{1,0:T(8,128)(2,1)S(1)} %collective-permute-done.1.refs_1_), channel_id=1, source_target_pairs={{0,32},{1,33},{2,34},{3,35},{4,36},{5,37},{6,38},{7,39},{8,40},{9,... | collective-permute-start | bytes 589832 | tf_op jit(solution)/shard_map/ppermute | solution.py:25
  27.6 5.5 %collective-permute-start.12 = (bf16[256,768]{1,0:T(8,128)(2,1)S(1)}, bf16[256,768]{1,0:T(8,128)(2,1)S(1)}, u32[]{:S(2)}, u32[]{:S(2)}) collective-permute-start(bf16[256,768]{1,0:T(8,128)(2,1)S(1)} %constant_dynamic-update-slice_fusion.refs_8_), channel_id=1, source_target_pairs={{0,8},{1,9},{2,10},{3,11},{4,12},{5,13},{6,14},{7,15},{8,0},{9,1},... | collective-permute-start | bytes 1179656 | tf_op jit(solution)/shard_map/ppermute | solution.py:25
  31.4 1.7 %collective-permute-start.14 = (bf16[256,768]{1,0:T(8,128)(2,1)S(1)}, bf16[256,768]{1,0:T(8,128)(2,1)S(1)}, u32[]{:S(2)}, u32[]{:S(2)}) collective-permute-start(bf16[256,768]{1,0:T(8,128)(2,1)S(1)} %collective-permute-done.5.refs_10_), channel_id=1, source_target_pairs={{0,8},{1,9},{2,10},{3,11},{4,12},{5,13},{6,14},{7,15},{8,0},{9,1},... | collective-permute-start | bytes 1179656 | tf_op jit(solution)/shard_map/ppermute | solution.py:25
  31.4 2.3 %collective-permute-start.13 = (bf16[256,768]{1,0:T(8,128)(2,1)S(1)}, bf16[256,768]{1,0:T(8,128)(2,1)S(1)}, u32[]{:S(2)}, u32[]{:S(2)}) collective-permute-start(bf16[256,768]{1,0:T(8,128)(2,1)S(1)} %collective-permute-done.4.refs_9_), channel_id=1, source_target_pairs={{0,8},{1,9},{2,10},{3,11},{4,12},{5,13},{6,14},{7,15},{8,0},{9,1},... | collective-permute-start | bytes 1179656 | tf_op jit(solution)/shard_map/ppermute | solution.py:25
  32.0 9.1 %collective-permute-start.10 = (bf16[256,768]{1,0:T(8,128)(2,1)S(1)}, bf16[256,768]{1,0:T(8,128)(2,1)S(1)}, u32[]{:S(2)}, u32[]{:S(2)}) collective-permute-start(bf16[256,768]{1,0:T(8,128)(2,1)S(1)} %broadcast_select_fusion), channel_id=1, source_target_pairs={{0,2},{1,3},{2,4},{3,5},{4,6},{5,7},{6,0},{7,1},{8,14},{9,15},{10,... | collective-permute-start | bytes 1179656 | tf_op jit(solution)/shard_map/ppermute | solution.py:305
  32.8 7.9 %collective-permute-start.11 = (bf16[128,768]{1,0:T(8,128)(2,1)S(1)}, bf16[128,768]{1,0:T(8,128)(2,1)S(1)}, u32[]{:S(2)}, u32[]{:S(2)}) collective-permute-start(bf16[128,768]{1,0:T(8,128)(2,1)S(1)} %broadcast_select_fusion.1), channel_id=1, source_target_pairs={{0,32},{1,33},{2,34},{3,35},{4,36},{5,37},{6,38},{7,39},{8,40},{9,... | collective-permute-start | bytes 589832 | tf_op jit(solution)/shard_map/ppermute | solution.py:315
  41.0 2.2 %collective-permute-start.15 = (bf16[256,768]{1,0:T(8,128)(2,1)S(1)}, bf16[256,768]{1,0:T(8,128)(2,1)S(1)}, u32[]{:S(2)}, u32[]{:S(2)}) collective-permute-start(bf16[256,768]{1,0:T(8,128)(2,1)S(1)} %collective-permute-done.10.refs_0_), channel_id=1, source_target_pairs={{0,8},{1,9},{2,10},{3,11},{4,12},{5,13},{6,14},{7,15},{8,0},{9,1},... | collective-permute-start | bytes 1179656 | tf_op jit(solution)/shard_map/ppermute | solution.py:25
  50.2 7.1 %collective-permute-start.18 = (bf16[256,768]{1,0:T(8,128)(2,1)S(1)}, bf16[256,768]{1,0:T(8,128)(2,1)S(1)}, u32[]{:S(2)}, u32[]{:S(2)}) collective-permute-start(bf16[256,768]{1,0:T(8,128)(2,1)S(1)} %get-tuple-element.69), channel_id=1, source_target_pairs={{0,8},{1,9},{2,10},{3,11},{4,12},{5,13},{6,14},{7,15},{8,0},{9,1},... | collective-permute-start | bytes 1179656 | tf_op jit(solution)/shard_map/ppermute | solution.py:25
  50.6 11.5 %collective-permute-start.16 = (bf16[256,768]{1,0:T(8,128)(2,1)}, bf16[256,768]{1,0:T(8,128)(2,1)}, u32[]{:S(2)}, u32[]{:S(2)}) collective-permute-start(bf16[256,768]{1,0:T(8,128)(2,1)} %get-tuple-element.63), channel_id=1, source_target_pairs={{0,224},{1,225},{2,226},{3,227},{4,228},{5,229},{6,230},{7,231},{8... | collective-permute-start | bytes 1179656 | tf_op jit(solution)/shard_map/ppermute | solution.py:25
  51.9 12.6 %collective-permute-start.17 = (bf16[256,768]{1,0:T(8,128)(2,1)}, bf16[256,768]{1,0:T(8,128)(2,1)}, u32[]{:S(2)}, u32[]{:S(2)}) collective-permute-start(bf16[256,768]{1,0:T(8,128)(2,1)} %get-tuple-element.64), channel_id=1, source_target_pairs={{0,32},{1,33},{2,34},{3,35},{4,36},{5,37},{6,38},{7,39},{8,40},{9,... | collective-permute-start | bytes 1179656 | tf_op jit(solution)/shard_map/ppermute | solution.py:25
  58.2 8.1 %collective-permute-start.19 = (bf16[256,768]{1,0:T(8,128)(2,1)}, bf16[256,768]{1,0:T(8,128)(2,1)}, u32[]{:S(2)}, u32[]{:S(2)}) collective-permute-start(bf16[256,768]{1,0:T(8,128)(2,1)} %add_convert_fusion.4), channel_id=1, source_target_pairs={{0,6},{1,7},{2,0},{3,1},{4,2},{5,3},{6,4},{7,5},{8,10},{9,11},{10,... | collective-permute-start | bytes 1179656 | tf_op jit(solution)/shard_map/ppermute | solution.py:305
  60.1 24.4 %collective-permute-start.20 = (bf16[256,768]{1,0:T(8,128)(2,1)S(1)}, bf16[256,768]{1,0:T(8,128)(2,1)S(1)}, u32[]{:S(2)}, u32[]{:S(2)}) collective-permute-start(bf16[256,768]{1,0:T(8,128)(2,1)S(1)} %get-tuple-element.77), channel_id=1, source_target_pairs={{0,8},{1,9},{2,10},{3,11},{4,12},{5,13},{6,14},{7,15},{8,0},{9,1},... | collective-permute-start | bytes 1179656 | tf_op jit(solution)/shard_map/ppermute | solution.py:25
  60.1 11.1 %collective-permute-start.21 = (bf16[256,768]{1,0:T(8,128)(2,1)S(1)}, bf16[256,768]{1,0:T(8,128)(2,1)S(1)}, u32[]{:S(2)}, u32[]{:S(2)}) collective-permute-start(bf16[256,768]{1,0:T(8,128)(2,1)S(1)} %get-tuple-element.79), channel_id=1, source_target_pairs={{0,8},{1,9},{2,10},{3,11},{4,12},{5,13},{6,14},{7,15},{8,0},{9,1},... | collective-permute-start | bytes 1179656 | tf_op jit(solution)/shard_map/ppermute | solution.py:25
  62.1 9.2 %collective-permute-start.23 = (bf16[256,768]{1,0:T(8,128)(2,1)S(1)}, bf16[256,768]{1,0:T(8,128)(2,1)S(1)}, u32[]{:S(2)}, u32[]{:S(2)}) collective-permute-start(bf16[256,768]{1,0:T(8,128)(2,1)S(1)} %get-tuple-element.82), channel_id=1, source_target_pairs={{0,8},{1,9},{2,10},{3,11},{4,12},{5,13},{6,14},{7,15},{8,0},{9,1},... | collective-permute-start | bytes 1179656 | tf_op jit(solution)/shard_map/ppermute | solution.py:25
  67.4 11.1 %collective-permute-start.27 = (bf16[256,768]{1,0:T(8,128)(2,1)S(1)}, bf16[256,768]{1,0:T(8,128)(2,1)S(1)}, u32[]{:S(2)}, u32[]{:S(2)}) collective-permute-start(bf16[256,768]{1,0:T(8,128)(2,1)S(1)} %add_convert_fusion), channel_id=1, source_target_pairs={{0,224},{1,225},{2,226},{3,227},{4,228},{5,229},{6,230},{7,231},{8... | collective-permute-start | bytes 1179656 | tf_op jit(solution)/shard_map/ppermute | solution.py:25
  71.1 21.2 %copy-start = (bf16[128,768]{1,0:T(8,128)(2,1)S(1)}, bf16[128,768]{1,0:T(8,128)(2,1)}, u32[]{:S(2)}) copy-start(bf16[128,768]{1,0:T(8,128)(2,1)} %embedding_ref.3) | copy-start | bytes 589828
  71.1 11.9 %collective-permute-start.26 = (bf16[256,768]{1,0:T(8,128)(2,1)S(1)}, bf16[256,768]{1,0:T(8,128)(2,1)S(1)}, u32[]{:S(2)}, u32[]{:S(2)}) collective-permute-start(bf16[256,768]{1,0:T(8,128)(2,1)S(1)} %add_convert_fusion.1), channel_id=1, source_target_pairs={{0,32},{1,33},{2,34},{3,35},{4,36},{5,37},{6,38},{7,39},{8,40},{9,... | collective-permute-start | bytes 1179656 | tf_op jit(solution)/shard_map/ppermute | solution.py:25
  72.5 21.3 %copy-start.1 = (bf16[128,768]{1,0:T(8,128)(2,1)S(1)}, bf16[128,768]{1,0:T(8,128)(2,1)}, u32[]{:S(2)}) copy-start(bf16[128,768]{1,0:T(8,128)(2,1)} %embedding_ref.2) | copy-start | bytes 589828
  72.6 11.9 %collective-permute-start.24 = (bf16[256,768]{1,0:T(8,128)(2,1)S(1)}, bf16[256,768]{1,0:T(8,128)(2,1)S(1)}, u32[]{:S(2)}, u32[]{:S(2)}) collective-permute-start(bf16[256,768]{1,0:T(8,128)(2,1)S(1)} %get-tuple-element.88), channel_id=1, source_target_pairs={{0,6},{1,7},{2,0},{3,1},{4,2},{5,3},{6,4},{7,5},{8,14},{9,15},{10,... | collective-permute-start | bytes 1179656 | tf_op jit(solution)/shard_map/ppermute | solution.py:25
  75.6 9.4 %collective-permute-start.22 = (bf16[256,768]{1,0:T(8,128)(2,1)S(1)}, bf16[256,768]{1,0:T(8,128)(2,1)S(1)}, u32[]{:S(2)}, u32[]{:S(2)}) collective-permute-start(bf16[256,768]{1,0:T(8,128)(2,1)S(1)} %get-tuple-element.89), channel_id=1, source_target_pairs={{0,2},{1,3},{2,4},{3,5},{4,6},{5,7},{6,0},{7,1},{8,10},{9,11},{10,... | collective-permute-start | bytes 1179656 | tf_op jit(solution)/shard_map/ppermute | solution.py:25
  83.1 9.2 %collective-permute-start.28 = (bf16[128,768]{1,0:T(8,128)(2,1)S(1)}, bf16[128,768]{1,0:T(8,128)(2,1)S(1)}, u32[]{:S(2)}, u32[]{:S(2)}) collective-permute-start(bf16[128,768]{1,0:T(8,128)(2,1)S(1)} %add_convert_fusion.5), channel_id=1, source_target_pairs={{0,16},{1,17},{2,18},{3,19},{4,20},{5,21},{6,22},{7,23},{8,24},{9,... | collective-permute-start | bytes 589832 | tf_op jit(solution)/shard_map/ppermute | solution.py:25
  85.1 8.7 %collective-permute-start.25 = (bf16[128,768]{1,0:T(8,128)(2,1)S(1)}, bf16[128,768]{1,0:T(8,128)(2,1)S(1)}, u32[]{:S(2)}, u32[]{:S(2)}) collective-permute-start(bf16[128,768]{1,0:T(8,128)(2,1)S(1)} %add_convert_fusion.6), channel_id=1, source_target_pairs={{0,1},{1,0},{2,3},{3,2},{4,5},{5,4},{6,7},{7,6},{8,9},{9,8},{10,11... | collective-permute-start | bytes 589832 | tf_op jit(solution)/shard_map/ppermute | solution.py:25

commit v8 on v7

--- a/solution.py
+++ b/solution.py
@@ -225,9 +225,9 @@
     rows = footage_embeds.shape[0]
     v0, t0 = unit_low(footage_embeds, caption_embeds)
 
-    tp, v1 = move(t0, y_hi=1), move(v0, y_lo=1)
     a1m, a1p = move(t0, z=1), move(t0, z=-1)
-    v1, tp, a1m, a1p = lax.optimization_barrier((v1, tp, a1m, a1p))
+    v1, tp = move(v0, y_lo=1), move(t0, y_hi=1)
+    a1m, a1p, v1, tp = lax.optimization_barrier((a1m, a1p, v1, tp))
     v01 = jnp.concatenate([v0, v1])
     vm, vp = move(v01, x=1), move(v01, x=-1)
     a2m, a2p = move(a1m, z=1), move(a1p, z=-1)

time: 95.1 us -> 94.9 us (level)
  the two profiles are of different devices: /device:TPU:8 before, /device:TPU:2 now
where the time goes in v8:
time: 94.9 us; the launch traced here: 93.3 us
  waiting for transfers between devices  36.7 us (39%)
  starting transfers between devices  30.6 us (32%)
  Pallas kernels  19.2 us (20%)
  other arithmetic  4.64 us (5%)
  between operations  2.1 us (2%)
    ppermute x26, waiting for transfers between devices, move(): return lax.ppermute(block, AXES, pairs)  32 us
    ppermute x26, starting transfers between devices, move(): return lax.ppermute(block, AXES, pairs)  26.5 us
    pallas_call x3, Pallas kernels, call(): pl.pallas_call(kernel, out_shape=outs, in_specs=[SMEM] * len(scalars) + [...  16 us
    convert_element_type x6, other arithmetic, add(): return total.astype(jnp.bfloat16)  4.5 us
    ppermute x2, starting transfers between devices, move_by_core(): return lax.ppermute(block, AXES, pairs)  3.89 us
    ppermute x1, waiting for transfers between devices, move_by_y_hi(): return lax.ppermute(block, AXES, pairs)  2.53 us
    ppermute x2, waiting for transfers between devices, move_by_core(): return lax.ppermute(block, AXES, pairs)  2.12 us
    pallas_call x2, Pallas kernels, back_rows(): pl.pallas_call(back_kernel, out_shape=jax.ShapeDtypeStruct(embedding.shap...  2.05 us
  transfers between devices with their start and end apart: 29, of which 16 were waited for; matrix products, arithmetic and copies ran while one was open for 5% of the time, Pallas kernels for 11%

profile of v8, /device:TPU:2, one launch (start us, length us, event | category | flops | bytes accessed | tf_op | source)
XLA Modules:
  0.0 93.3 jit_solution(7643120079175881678)
XLA Ops:
  0.6 1.2 %unit_low.1 = (bf16[128,768]{1,0:T(8,128)(2,1)S(1)}, bf16[128,768]{1,0:T(8,128)(2,1)S(1)}) custom-call(bf16[128,768]{1,0:T(8,128)(2,1)} %embedding_ref.2, bf16[128,768]{1,0:T(8,128)(2,1)} %embedding_ref.3), custom_call_target="tpu_custom_call" | custom-call | tf_op jit(solution)/shard_map/unit_low/pallas_call | solution.py:48
  1.8 1.7 %collective-permute-start.2 = (bf16[128,768]{1,0:T(8,128)(2,1)S(1)}, bf16[128,768]{1,0:T(8,128)(2,1)S(1)}, u32[]{:S(2)}, u32[]{:S(2)}) collective-permute-start(bf16[128,768]{1,0:T(8,128)(2,1)S(1)} %get-tuple-element.45), channel_id=1, source_target_pairs={{0,1},{1,0},{2,3},{3,2},{4,5},{5,4},{6,7},{7,6},{8,9},{9,8},{10,11... | collective-permute-start | bytes 589832 | tf_op jit(solution)/shard_map/ppermute | solution.py:25
  3.5 2.9 %collective-permute-start.3 = (bf16[128,768]{1,0:T(8,128)(2,1)S(1)}, bf16[128,768]{1,0:T(8,128)(2,1)S(1)}, u32[]{:S(2)}, u32[]{:S(2)}) collective-permute-start(bf16[128,768]{1,0:T(8,128)(2,1)S(1)} %get-tuple-element.46.refs_0_), channel_id=1, source_target_pairs={{0,16},{1,17},{2,18},{3,19},{4,20},{5,21},{6,22},{7,23},{8,24},{9,... | collective-permute-start | bytes 589832 | tf_op jit(solution)/shard_map/ppermute | solution.py:25
  6.4 5.9 %collective-permute-start.1 = (bf16[128,768]{1,0:T(8,128)(2,1)S(1)}, bf16[128,768]{1,0:T(8,128)(2,1)S(1)}, u32[]{:S(2)}, u32[]{:S(2)}) collective-permute-start(bf16[128,768]{1,0:T(8,128)(2,1)S(1)} %get-tuple-element.46.refs_0_), channel_id=1, source_target_pairs={{0,224},{1,225},{2,226},{3,227},{4,228},{5,229},{6,230},{7,231},{8... | collective-permute-start | bytes 589832 | tf_op jit(solution)/shard_map/ppermute | solution.py:25
  12.3 2.9 %collective-permute-done.3.refs_1_ = bf16[128,768]{1,0:T(8,128)(2,1)S(1)} collective-permute-done((bf16[128,768]{1,0:T(8,128)(2,1)S(1)}, bf16[128,768]{1,0:T(8,128)(2,1)S(1)}, u32[]{:S(2)}, u32[]{:S(2)}) %collective-permute-start.3) | collective-permute-done | bytes 196640 | tf_op jit(solution)/shard_map/ppermute | solution.py:25
  15.8 3.4 %collective-permute-done.refs_2_ = bf16[128,768]{1,0:T(8,128)(2,1)S(1)} collective-permute-done((bf16[128,768]{1,0:T(8,128)(2,1)S(1)}, bf16[128,768]{1,0:T(8,128)(2,1)S(1)}, u32[]{:S(2)}, u32[]{:S(2)}) %collective-permute-start) | collective-permute-done | bytes 196640 | tf_op jit(solution)/shard_map/ppermute | solution.py:25
  19.9 1.5 %collective-permute-start.4 = (bf16[256,768]{1,0:T(8,128)(2,1)S(1)}, bf16[256,768]{1,0:T(8,128)(2,1)S(1)}, u32[]{:S(2)}, u32[]{:S(2)}) collective-permute-start(bf16[256,768]{1,0:T(8,128)(2,1)S(1)} %constant_dynamic-update-slice_fusion.refs_8_), channel_id=1, source_target_pairs={{0,2},{1,3},{2,4},{3,5},{4,6},{5,7},{6,0},{7,1},{8,10},{9,11},{10,... | collective-permute-start | bytes 1179656 | tf_op jit(solution)/shard_map/ppermute | solution.py:25
  21.4 3.2 %collective-permute-start.9 = (bf16[128,768]{1,0:T(8,128)(2,1)S(1)}, bf16[128,768]{1,0:T(8,128)(2,1)S(1)}, u32[]{:S(2)}, u32[]{:S(2)}) collective-permute-start(bf16[128,768]{1,0:T(8,128)(2,1)S(1)} %collective-permute-done.1.refs_4_), channel_id=1, source_target_pairs={{0,224},{1,225},{2,226},{3,227},{4,228},{5,229},{6,230},{7,231},{8... | collective-permute-start | bytes 589832 | tf_op jit(solution)/shard_map/ppermute | solution.py:25
  28.4 2.1 %collective-permute-done.7.refs_5_ = bf16[128,768]{1,0:T(8,128)(2,1)S(1)} collective-permute-done((bf16[128,768]{1,0:T(8,128)(2,1)S(1)}, bf16[128,768]{1,0:T(8,128)(2,1)S(1)}, u32[]{:S(2)}, u32[]{:S(2)}) %collective-permute-start.7) | collective-permute-done | bytes 196640 | tf_op jit(solution)/shard_map/ppermute | solution.py:25
  30.5 2.5 %collective-permute-done.6.refs_3_ = bf16[128,768]{1,0:T(8,128)(2,1)S(1)} collective-permute-done((bf16[128,768]{1,0:T(8,128)(2,1)S(1)}, bf16[128,768]{1,0:T(8,128)(2,1)S(1)}, u32[]{:S(2)}, u32[]{:S(2)}) %collective-permute-start.6) | collective-permute-done | bytes 196640 | tf_op jit(solution)/shard_map/ppermute | solution.py:25
  33.6 1.6 %collective-permute-start.10 = (bf16[256,768]{1,0:T(8,128)(2,1)S(1)}, bf16[256,768]{1,0:T(8,128)(2,1)S(1)}, u32[]{:S(2)}, u32[]{:S(2)}) collective-permute-start(bf16[256,768]{1,0:T(8,128)(2,1)S(1)} %broadcast_select_fusion), channel_id=1, source_target_pairs={{0,2},{1,3},{2,4},{3,5},{4,6},{5,7},{6,0},{7,1},{8,14},{9,15},{10,... | collective-permute-start | bytes 1179656 | tf_op jit(solution)/shard_map/ppermute | solution.py:305
  35.5 4.3 %near_weights.1 = (bf16[1536,1024]{1,0:T(8,128)(2,1)S(1)}, bf16[1024,768]{1,0:T(8,128)(2,1)S(1)}, bf16[1536,768]{1,0:T(8,128)(2,1)S(1)}) custom-call(f32[1]{0:T(128)S(6)} %copy.7.scale_ref, f32[1]{0:T(128)S(6)} %copy.8.offset_ref, s32[2]{0:T(128)S(1)} %pad_add_fusion.place_ref, bf16[128,768]{1,0:T(8,128)(2,1)S(1)} %get-tuple-element.46.refs_0_, ...), custom_call_target="tpu_custom_call" | custom-call | flops 2415919104 | tf_op jit(solution)/shard_map/near_weights/pallas_call | solution.py:209
  39.8 2.5 %collective-permute-done.11.last = bf16[128,768]{1,0:T(8,128)(2,1)S(1)} collective-permute-done((bf16[128,768]{1,0:T(8,128)(2,1)S(1)}, bf16[128,768]{1,0:T(8,128)(2,1)S(1)}, u32[]{:S(2)}, u32[]{:S(2)}) %collective-permute-start.11) | collective-permute-done | bytes 196640 | tf_op jit(solution)/shard_map/ppermute | solution.py:315
  42.3 1.7 %collective-permute-done.15.refs_1_ = bf16[256,768]{1,0:T(8,128)(2,1)S(1)} collective-permute-done((bf16[256,768]{1,0:T(8,128)(2,1)S(1)}, bf16[256,768]{1,0:T(8,128)(2,1)S(1)}, u32[]{:S(2)}, u32[]{:S(2)}) %collective-permute-start.15) | collective-permute-done | bytes 393248 | tf_op jit(solution)/shard_map/ppermute | solution.py:25
  44.0 7.0 %far_weights_and_sums.1 = (bf16[1536,128]{1,0:T(8,128)(2,1)S(1)}, bf16[512,1152]{1,0:T(8,128)(2,1)S(1)}, bf16[512,768]{1,0:T(8,128)(2,1)S(1)}, bf16[256,768]{1,0...) custom-call(f32[1]{0:T(128)S(6)} %copy.7.scale_ref, ...), custom_call_target="tpu_custom_call" | custom-call | flops 5033164800 | tf_op jit(solution)/shard_map/far_weights_and_sums/pallas_call | solution.py:209
  52.1 1.1 %collective-permute-start.17 = (bf16[256,768]{1,0:T(8,128)(2,1)}, bf16[256,768]{1,0:T(8,128)(2,1)}, u32[]{:S(2)}, u32[]{:S(2)}) collective-permute-start(bf16[256,768]{1,0:T(8,128)(2,1)} %get-tuple-element.64), channel_id=1, source_target_pairs={{0,32},{1,33},{2,34},{3,35},{4,36},{5,37},{6,38},{7,39},{8,40},{9,... | collective-permute-start | bytes 1179656 | tf_op jit(solution)/shard_map/ppermute | solution.py:25
  53.2 4.7 %own_video_and_near_text_sums.1 = (bf16[256,768]{1,0:T(8,128)(2,1)S(1)}, bf16[256,768]{1,0:T(8,128)(2,1)S(1)}, bf16[256,768]{1,0:T(8,128)(2,1)S(1)}, bf16[256,76...) custom-call(bf16[1536,1024]{1,0:T(8,128)(2,1)S(1)} %get-tuple-elemen, ...), custom_call_target="tpu_custom_call" | custom-call | flops 4026531840 | tf_op jit(solution)/shard_map/own_video_and_near_text_sums/pallas_call | solution.py:209
  58.8 2.3 %collective-permute-start.19 = (bf16[256,768]{1,0:T(8,128)(2,1)}, bf16[256,768]{1,0:T(8,128)(2,1)}, u32[]{:S(2)}, u32[]{:S(2)}) collective-permute-start(bf16[256,768]{1,0:T(8,128)(2,1)} %add_convert_fusion.4), channel_id=1, source_target_pairs={{0,6},{1,7},{2,0},{3,1},{4,2},{5,3},{6,4},{7,5},{8,10},{9,11},{10,... | collective-permute-start | bytes 1179656 | tf_op jit(solution)/shard_map/ppermute | solution.py:305
  61.6 1.3 %collective-permute-done.16 = bf16[256,768]{1,0:T(8,128)(2,1)} collective-permute-done((bf16[256,768]{1,0:T(8,128)(2,1)}, bf16[256,768]{1,0:T(8,128)(2,1)}, u32[]{:S(2)}, u32[]{:S(2)}) %collective-permute-start.16) | collective-permute-done | bytes 393248 | tf_op jit(solution)/shard_map/ppermute | solution.py:25
  62.8 1.9 %collective-permute-done.17 = bf16[256,768]{1,0:T(8,128)(2,1)} collective-permute-done((bf16[256,768]{1,0:T(8,128)(2,1)}, bf16[256,768]{1,0:T(8,128)(2,1)}, u32[]{:S(2)}, u32[]{:S(2)}) %collective-permute-start.17) | collective-permute-done | bytes 393248 | tf_op jit(solution)/shard_map/ppermute | solution.py:25
  64.7 2.1 %collective-permute-done.19 = bf16[256,768]{1,0:T(8,128)(2,1)} collective-permute-done((bf16[256,768]{1,0:T(8,128)(2,1)}, bf16[256,768]{1,0:T(8,128)(2,1)}, u32[]{:S(2)}, u32[]{:S(2)}) %collective-permute-start.19) | collective-permute-done | bytes 393248 | tf_op jit(solution)/shard_map/ppermute | solution.py:305
  66.8 1.1 %add_convert_fusion = bf16[256,768]{1,0:T(8,128)(2,1)S(1)} fusion(bf16[256,768]{1,0:T(8,128)(2,1)} %collective-permute-done.16, bf16[256,768]{1,0:T(8,128)(2,1)S(1)} %get-tuple-element.86), kind=kLoop, calls=%fused_computation | loop fusion | flops 786432 | bytes 1179648 | tf_op jit(solution)/shard_map/convert_element_type | solution.py:32
  67.9 2.2 %collective-permute-start.27 = (bf16[256,768]{1,0:T(8,128)(2,1)S(1)}, bf16[256,768]{1,0:T(8,128)(2,1)S(1)}, u32[]{:S(2)}, u32[]{:S(2)}) collective-permute-start(bf16[256,768]{1,0:T(8,128)(2,1)S(1)} %add_convert_fusion), channel_id=1, source_target_pairs={{0,224},{1,225},{2,226},{3,227},{4,228},{5,229},{6,230},{7,231},{8... | collective-permute-start | bytes 1179656 | tf_op jit(solution)/shard_map/ppermute | solution.py:25
  70.2 1.1 %add_convert_fusion.1 = bf16[256,768]{1,0:T(8,128)(2,1)S(1)} fusion(bf16[256,768]{1,0:T(8,128)(2,1)} %collective-permute-done.17, bf16[256,768]{1,0:T(8,128)(2,1)S(1)} %get-tuple-element.84), kind=kLoop, calls=%fused_computation.1 | loop fusion | flops 786432 | bytes 1179648 | tf_op jit(solution)/shard_map/convert_element_type | solution.py:32
  71.4 1.3 %add_convert_fusion.2 = (bf16[256,768]{1,0:T(8,128)(2,1)S(1)}, bf16[256,768]{1,0:T(8,128)(2,1)S(1)}) fusion(bf16[256,768]{1,0:T(8,128)(2,1)S(1)} %collective-permute-done.23, bf16[256,768]{1,0:T(8,128)(2,1)S(1)} %get-tuple-element.81, bf16[256,768]{1,0:T(8,128)(2,1)} %collective-permute-done.19, pred[]{:T(512)S(6)} %eq.15, pred[]{:T(512)S(6)} %eq.13, ...), kind=kLoop, calls=%fused_computation.2 | loop fusion | flops 2752512 | bytes 2752514 | tf_op jit(solution)/shard_map/convert_element_type | solution.py:32
  72.7 2.2 %collective-permute-start.24 = (bf16[256,768]{1,0:T(8,128)(2,1)S(1)}, bf16[256,768]{1,0:T(8,128)(2,1)S(1)}, u32[]{:S(2)}, u32[]{:S(2)}) collective-permute-start(bf16[256,768]{1,0:T(8,128)(2,1)S(1)} %get-tuple-element.88), channel_id=1, source_target_pairs={{0,6},{1,7},{2,0},{3,1},{4,2},{5,3},{6,4},{7,5},{8,14},{9,15},{10,... | collective-permute-start | bytes 1179656 | tf_op jit(solution)/shard_map/ppermute | solution.py:25
  75.0 3.6 %collective-permute-done.27.refs_2_ = bf16[256,768]{1,0:T(8,128)(2,1)S(1)} collective-permute-done((bf16[256,768]{1,0:T(8,128)(2,1)S(1)}, bf16[256,768]{1,0:T(8,128)(2,1)S(1)}, u32[]{:S(2)}, u32[]{:S(2)}) %collective-permute-start.27) | collective-permute-done | bytes 393248 | tf_op jit(solution)/shard_map/ppermute | solution.py:25
  78.5 4.0 %collective-permute-done.26.refs_1_ = bf16[256,768]{1,0:T(8,128)(2,1)S(1)} collective-permute-done((bf16[256,768]{1,0:T(8,128)(2,1)S(1)}, bf16[256,768]{1,0:T(8,128)(2,1)S(1)}, u32[]{:S(2)}, u32[]{:S(2)}) %collective-permute-start.26) | collective-permute-done | bytes 393248 | tf_op jit(solution)/shard_map/ppermute | solution.py:25
  82.7 1.6 %collective-permute-start.28 = (bf16[128,768]{1,0:T(8,128)(2,1)S(1)}, bf16[128,768]{1,0:T(8,128)(2,1)S(1)}, u32[]{:S(2)}, u32[]{:S(2)}) collective-permute-start(bf16[128,768]{1,0:T(8,128)(2,1)S(1)} %add_convert_fusion.5), channel_id=1, source_target_pairs={{0,16},{1,17},{2,18},{3,19},{4,20},{5,21},{6,22},{7,23},{8,24},{9,... | collective-permute-start | bytes 589832 | tf_op jit(solution)/shard_map/ppermute | solution.py:25
  85.5 5.7 %collective-permute-done.28.refs_3_ = bf16[128,768]{1,0:T(8,128)(2,1)S(1)} collective-permute-done((bf16[128,768]{1,0:T(8,128)(2,1)S(1)}, bf16[128,768]{1,0:T(8,128)(2,1)S(1)}, u32[]{:S(2)}, u32[]{:S(2)}) %collective-permute-start.28) | collective-permute-done | bytes 196640 | tf_op jit(solution)/shard_map/ppermute | solution.py:25
  91.2 1.0 %back_rows.3 = f32[128,768]{1,0:T(8,128)} custom-call(f32[1]{0:T(128)S(6)} %copy.7.scale_ref, bf16[128,768]{1,0:T(8,128)(2,1)S(1)} %copy-done, bf16[256,768]{1,0:T(8,128)(2,1)S(1)} %get-tuple-element.83.refs_0_, bf16[256,768]{1,0:T(8,128)(2,1)S(1)} %collective-permute-done.26.refs_1_, bf16[256,768]{1,0:T(8,128)(2,1)S(1)} %collective-permute-done.27.refs_2_, ...), custom_call_target="tpu_custom_call" | custom-call | tf_op jit(solution)/shard_map/back_rows/pallas_call | solution.py:65
  92.3 1.0 %back_rows.2 = f32[128,768]{1,0:T(8,128)} custom-call(f32[1]{0:T(128)S(6)} %copy.7.scale_ref, bf16[128,768]{1,0:T(8,128)(2,1)S(1)} %copy-done.1, bf16[256,768]{1,0:T(8,128)(2,1)S(1)} %get-tuple-element.76.refs_0_, bf16[256,768]{1,0:T(8,128)(2,1)S(1)} %collective-permute-done.20.refs_1_, bf16[256,768]{1,0:T(8,128)(2,1)S(1)} %collective-permute-done.22.refs_2_, ...), custom_call_target="tpu_custom_call" | custom-call | tf_op jit(solution)/shard_map/back_rows/pallas_call | solution.py:65
  (47 shorter events, 8.5 us)
Async XLA Ops:
  1.8 10.4 %collective-permute-start.2 = (bf16[128,768]{1,0:T(8,128)(2,1)S(1)}, bf16[128,768]{1,0:T(8,128)(2,1)S(1)}, u32[]{:S(2)}, u32[]{:S(2)}) collective-permute-start(bf16[128,768]{1,0:T(8,128)(2,1)S(1)} %get-tuple-element.45), channel_id=1, source_target_pairs={{0,1},{1,0},{2,3},{3,2},{4,5},{5,4},{6,7},{7,6},{8,9},{9,8},{10,11... | collective-permute-start | bytes 589832 | tf_op jit(solution)/shard_map/ppermute | solution.py:25
  3.5 11.7 %collective-permute-start.3 = (bf16[128,768]{1,0:T(8,128)(2,1)S(1)}, bf16[128,768]{1,0:T(8,128)(2,1)S(1)}, u32[]{:S(2)}, u32[]{:S(2)}) collective-permute-start(bf16[128,768]{1,0:T(8,128)(2,1)S(1)} %get-tuple-element.46.refs_0_), channel_id=1, source_target_pairs={{0,16},{1,17},{2,18},{3,19},{4,20},{5,21},{6,22},{7,23},{8,24},{9,... | collective-permute-start | bytes 589832 | tf_op jit(solution)/shard_map/ppermute | solution.py:25
  6.4 9.5 %collective-permute-start.1 = (bf16[128,768]{1,0:T(8,128)(2,1)S(1)}, bf16[128,768]{1,0:T(8,128)(2,1)S(1)}, u32[]{:S(2)}, u32[]{:S(2)}) collective-permute-start(bf16[128,768]{1,0:T(8,128)(2,1)S(1)} %get-tuple-element.46.refs_0_), channel_id=1, source_target_pairs={{0,224},{1,225},{2,226},{3,227},{4,228},{5,229},{6,230},{7,231},{8... | collective-permute-start | bytes 589832 | tf_op jit(solution)/shard_map/ppermute | solution.py:25
  12.2 7.0 %collective-permute-start = (bf16[128,768]{1,0:T(8,128)(2,1)S(1)}, bf16[128,768]{1,0:T(8,128)(2,1)S(1)}, u32[]{:S(2)}, u32[]{:S(2)}) collective-permute-start(bf16[128,768]{1,0:T(8,128)(2,1)S(1)} %get-tuple-element.46.refs_0_), channel_id=1, source_target_pairs={{0,32},{1,33},{2,34},{3,35},{4,36},{5,37},{6,38},{7,39},{8,40},{9,... | collective-permute-start | bytes 589832 | tf_op jit(solution)/shard_map/ppermute | solution.py:25
  19.3 6.9 %collective-permute-start.8 = (bf16[128,768]{1,0:T(8,128)(2,1)S(1)}, bf16[128,768]{1,0:T(8,128)(2,1)S(1)}, u32[]{:S(2)}, u32[]{:S(2)}) collective-permute-start(bf16[128,768]{1,0:T(8,128)(2,1)S(1)} %collective-permute-done.refs_2_), channel_id=1, source_target_pairs={{0,32},{1,33},{2,34},{3,35},{4,36},{5,37},{6,38},{7,39},{8,40},{9,... | collective-permute-start | bytes 589832 | tf_op jit(solution)/shard_map/ppermute | solution.py:25
  19.3 13.7 %collective-permute-start.5 = (bf16[256,768]{1,0:T(8,128)(2,1)S(1)}, bf16[256,768]{1,0:T(8,128)(2,1)S(1)}, u32[]{:S(2)}, u32[]{:S(2)}) collective-permute-start(bf16[256,768]{1,0:T(8,128)(2,1)S(1)} %constant_dynamic-update-slice_fusion.refs_8_), channel_id=1, source_target_pairs={{0,6},{1,7},{2,0},{3,1},{4,2},{5,3},{6,4},{7,5},{8,14},{9,15},{10,... | collective-permute-start | bytes 1179656 | tf_op jit(solution)/shard_map/ppermute | solution.py:25
  19.9 13.1 %collective-permute-start.4 = (bf16[256,768]{1,0:T(8,128)(2,1)S(1)}, bf16[256,768]{1,0:T(8,128)(2,1)S(1)}, u32[]{:S(2)}, u32[]{:S(2)}) collective-permute-start(bf16[256,768]{1,0:T(8,128)(2,1)S(1)} %constant_dynamic-update-slice_fusion.refs_8_), channel_id=1, source_target_pairs={{0,2},{1,3},{2,4},{3,5},{4,6},{5,7},{6,0},{7,1},{8,10},{9,11},{10,... | collective-permute-start | bytes 1179656 | tf_op jit(solution)/shard_map/ppermute | solution.py:25
  21.4 7.0 %collective-permute-start.9 = (bf16[128,768]{1,0:T(8,128)(2,1)S(1)}, bf16[128,768]{1,0:T(8,128)(2,1)S(1)}, u32[]{:S(2)}, u32[]{:S(2)}) collective-permute-start(bf16[128,768]{1,0:T(8,128)(2,1)S(1)} %collective-permute-done.1.refs_4_), channel_id=1, source_target_pairs={{0,224},{1,225},{2,226},{3,227},{4,228},{5,229},{6,230},{7,231},{8... | collective-permute-start | bytes 589832 | tf_op jit(solution)/shard_map/ppermute | solution.py:25
  24.6 5.9 %collective-permute-start.7 = (bf16[128,768]{1,0:T(8,128)(2,1)S(1)}, bf16[128,768]{1,0:T(8,128)(2,1)S(1)}, u32[]{:S(2)}, u32[]{:S(2)}) collective-permute-start(bf16[128,768]{1,0:T(8,128)(2,1)S(1)} %collective-permute-done.3.refs_1_), channel_id=1, source_target_pairs={{0,224},{1,225},{2,226},{3,227},{4,228},{5,229},{6,230},{7,231},{8... | collective-permute-start | bytes 589832 | tf_op jit(solution)/shard_map/ppermute | solution.py:25
  26.1 6.9 %collective-permute-start.6 = (bf16[128,768]{1,0:T(8,128)(2,1)S(1)}, bf16[128,768]{1,0:T(8,128)(2,1)S(1)}, u32[]{:S(2)}, u32[]{:S(2)}) collective-permute-start(bf16[128,768]{1,0:T(8,128)(2,1)S(1)} %collective-permute-done.3.refs_1_), channel_id=1, source_target_pairs={{0,32},{1,33},{2,34},{3,35},{4,36},{5,37},{6,38},{7,39},{8,40},{9,... | collective-permute-start | bytes 589832 | tf_op jit(solution)/shard_map/ppermute | solution.py:25
  28.4 7.1 %collective-permute-start.12 = (bf16[256,768]{1,0:T(8,128)(2,1)S(1)}, bf16[256,768]{1,0:T(8,128)(2,1)S(1)}, u32[]{:S(2)}, u32[]{:S(2)}) collective-permute-start(bf16[256,768]{1,0:T(8,128)(2,1)S(1)} %constant_dynamic-update-slice_fusion.refs_8_), channel_id=1, source_target_pairs={{0,8},{1,9},{2,10},{3,11},{4,12},{5,13},{6,14},{7,15},{8,0},{9,1},... | collective-permute-start | bytes 1179656 | tf_op jit(solution)/shard_map/ppermute | solution.py:25
  33.0 2.4 %collective-permute-start.14 = (bf16[256,768]{1,0:T(8,128)(2,1)S(1)}, bf16[256,768]{1,0:T(8,128)(2,1)S(1)}, u32[]{:S(2)}, u32[]{:S(2)}) collective-permute-start(bf16[256,768]{1,0:T(8,128)(2,1)S(1)} %collective-permute-done.5.refs_10_), channel_id=1, source_target_pairs={{0,8},{1,9},{2,10},{3,11},{4,12},{5,13},{6,14},{7,15},{8,0},{9,1},... | collective-permute-start | bytes 1179656 | tf_op jit(solution)/shard_map/ppermute | solution.py:25
  33.0 2.4 %collective-permute-start.13 = (bf16[256,768]{1,0:T(8,128)(2,1)S(1)}, bf16[256,768]{1,0:T(8,128)(2,1)S(1)}, u32[]{:S(2)}, u32[]{:S(2)}) collective-permute-start(bf16[256,768]{1,0:T(8,128)(2,1)S(1)} %collective-permute-done.4.refs_9_), channel_id=1, source_target_pairs={{0,8},{1,9},{2,10},{3,11},{4,12},{5,13},{6,14},{7,15},{8,0},{9,1},... | collective-permute-start | bytes 1179656 | tf_op jit(solution)/shard_map/ppermute | solution.py:25
  33.6 8.7 %collective-permute-start.10 = (bf16[256,768]{1,0:T(8,128)(2,1)S(1)}, bf16[256,768]{1,0:T(8,128)(2,1)S(1)}, u32[]{:S(2)}, u32[]{:S(2)}) collective-permute-start(bf16[256,768]{1,0:T(8,128)(2,1)S(1)} %broadcast_select_fusion), channel_id=1, source_target_pairs={{0,2},{1,3},{2,4},{3,5},{4,6},{5,7},{6,0},{7,1},{8,14},{9,15},{10,... | collective-permute-start | bytes 1179656 | tf_op jit(solution)/shard_map/ppermute | solution.py:305
  35.2 7.1 %collective-permute-start.11 = (bf16[128,768]{1,0:T(8,128)(2,1)S(1)}, bf16[128,768]{1,0:T(8,128)(2,1)S(1)}, u32[]{:S(2)}, u32[]{:S(2)}) collective-permute-start(bf16[128,768]{1,0:T(8,128)(2,1)S(1)} %broadcast_select_fusion.1), channel_id=1, source_target_pairs={{0,32},{1,33},{2,34},{3,35},{4,36},{5,37},{6,38},{7,39},{8,40},{9,... | collective-permute-start | bytes 589832 | tf_op jit(solution)/shard_map/ppermute | solution.py:315
  42.3 1.7 %collective-permute-start.15 = (bf16[256,768]{1,0:T(8,128)(2,1)S(1)}, bf16[256,768]{1,0:T(8,128)(2,1)S(1)}, u32[]{:S(2)}, u32[]{:S(2)}) collective-permute-start(bf16[256,768]{1,0:T(8,128)(2,1)S(1)} %collective-permute-done.10.refs_0_), channel_id=1, source_target_pairs={{0,8},{1,9},{2,10},{3,11},{4,12},{5,13},{6,14},{7,15},{8,0},{9,1},... | collective-permute-start | bytes 1179656 | tf_op jit(solution)/shard_map/ppermute | solution.py:25
  51.0 6.9 %collective-permute-start.18 = (bf16[256,768]{1,0:T(8,128)(2,1)S(1)}, bf16[256,768]{1,0:T(8,128)(2,1)S(1)}, u32[]{:S(2)}, u32[]{:S(2)}) collective-permute-start(bf16[256,768]{1,0:T(8,128)(2,1)S(1)} %get-tuple-element.69), channel_id=1, source_target_pairs={{0,8},{1,9},{2,10},{3,11},{4,12},{5,13},{6,14},{7,15},{8,0},{9,1},... | collective-permute-start | bytes 1179656 | tf_op jit(solution)/shard_map/ppermute | solution.py:25
  51.1 11.7 %collective-permute-start.16 = (bf16[256,768]{1,0:T(8,128)(2,1)}, bf16[256,768]{1,0:T(8,128)(2,1)}, u32[]{:S(2)}, u32[]{:S(2)}) collective-permute-start(bf16[256,768]{1,0:T(8,128)(2,1)} %get-tuple-element.63), channel_id=1, source_target_pairs={{0,224},{1,225},{2,226},{3,227},{4,228},{5,229},{6,230},{7,231},{8... | collective-permute-start | bytes 1179656 | tf_op jit(solution)/shard_map/ppermute | solution.py:25
  52.1 12.6 %collective-permute-start.17 = (bf16[256,768]{1,0:T(8,128)(2,1)}, bf16[256,768]{1,0:T(8,128)(2,1)}, u32[]{:S(2)}, u32[]{:S(2)}) collective-permute-start(bf16[256,768]{1,0:T(8,128)(2,1)} %get-tuple-element.64), channel_id=1, source_target_pairs={{0,32},{1,33},{2,34},{3,35},{4,36},{5,37},{6,38},{7,39},{8,40},{9,... | collective-permute-start | bytes 1179656 | tf_op jit(solution)/shard_map/ppermute | solution.py:25
  58.8 8.1 %collective-permute-start.19 = (bf16[256,768]{1,0:T(8,128)(2,1)}, bf16[256,768]{1,0:T(8,128)(2,1)}, u32[]{:S(2)}, u32[]{:S(2)}) collective-permute-start(bf16[256,768]{1,0:T(8,128)(2,1)} %add_convert_fusion.4), channel_id=1, source_target_pairs={{0,6},{1,7},{2,0},{3,1},{4,2},{5,3},{6,4},{7,5},{8,10},{9,11},{10,... | collective-permute-start | bytes 1179656 | tf_op jit(solution)/shard_map/ppermute | solution.py:305
  61.1 23.2 %collective-permute-start.20 = (bf16[256,768]{1,0:T(8,128)(2,1)S(1)}, bf16[256,768]{1,0:T(8,128)(2,1)S(1)}, u32[]{:S(2)}, u32[]{:S(2)}) collective-permute-start(bf16[256,768]{1,0:T(8,128)(2,1)S(1)} %get-tuple-element.77), channel_id=1, source_target_pairs={{0,8},{1,9},{2,10},{3,11},{4,12},{5,13},{6,14},{7,15},{8,0},{9,1},... | collective-permute-start | bytes 1179656 | tf_op jit(solution)/shard_map/ppermute | solution.py:25
  61.1 10.3 %collective-permute-start.21 = (bf16[256,768]{1,0:T(8,128)(2,1)S(1)}, bf16[256,768]{1,0:T(8,128)(2,1)S(1)}, u32[]{:S(2)}, u32[]{:S(2)}) collective-permute-start(bf16[256,768]{1,0:T(8,128)(2,1)S(1)} %get-tuple-element.79), channel_id=1, source_target_pairs={{0,8},{1,9},{2,10},{3,11},{4,12},{5,13},{6,14},{7,15},{8,0},{9,1},... | collective-permute-start | bytes 1179656 | tf_op jit(solution)/shard_map/ppermute | solution.py:25
  62.8 8.5 %collective-permute-start.23 = (bf16[256,768]{1,0:T(8,128)(2,1)S(1)}, bf16[256,768]{1,0:T(8,128)(2,1)S(1)}, u32[]{:S(2)}, u32[]{:S(2)}) collective-permute-start(bf16[256,768]{1,0:T(8,128)(2,1)S(1)} %get-tuple-element.82), channel_id=1, source_target_pairs={{0,8},{1,9},{2,10},{3,11},{4,12},{5,13},{6,14},{7,15},{8,0},{9,1},... | collective-permute-start | bytes 1179656 | tf_op jit(solution)/shard_map/ppermute | solution.py:25
  67.9 10.6 %collective-permute-start.27 = (bf16[256,768]{1,0:T(8,128)(2,1)S(1)}, bf16[256,768]{1,0:T(8,128)(2,1)S(1)}, u32[]{:S(2)}, u32[]{:S(2)}) collective-permute-start(bf16[256,768]{1,0:T(8,128)(2,1)S(1)} %add_convert_fusion), channel_id=1, source_target_pairs={{0,224},{1,225},{2,226},{3,227},{4,228},{5,229},{6,230},{7,231},{8... | collective-permute-start | bytes 1179656 | tf_op jit(solution)/shard_map/ppermute | solution.py:25
  71.3 20.0 %copy-start = (bf16[128,768]{1,0:T(8,128)(2,1)S(1)}, bf16[128,768]{1,0:T(8,128)(2,1)}, u32[]{:S(2)}) copy-start(bf16[128,768]{1,0:T(8,128)(2,1)} %embedding_ref.3) | copy-start | bytes 589828
  71.3 11.3 %collective-permute-start.26 = (bf16[256,768]{1,0:T(8,128)(2,1)S(1)}, bf16[256,768]{1,0:T(8,128)(2,1)S(1)}, u32[]{:S(2)}, u32[]{:S(2)}) collective-permute-start(bf16[256,768]{1,0:T(8,128)(2,1)S(1)} %add_convert_fusion.1), channel_id=1, source_target_pairs={{0,32},{1,33},{2,34},{3,35},{4,36},{5,37},{6,38},{7,39},{8,40},{9,... | collective-permute-start | bytes 1179656 | tf_op jit(solution)/shard_map/ppermute | solution.py:25
  72.7 19.5 %copy-start.1 = (bf16[128,768]{1,0:T(8,128)(2,1)S(1)}, bf16[128,768]{1,0:T(8,128)(2,1)}, u32[]{:S(2)}) copy-start(bf16[128,768]{1,0:T(8,128)(2,1)} %embedding_ref.2) | copy-start | bytes 589828
  72.7 11.5 %collective-permute-start.24 = (bf16[256,768]{1,0:T(8,128)(2,1)S(1)}, bf16[256,768]{1,0:T(8,128)(2,1)S(1)}, u32[]{:S(2)}, u32[]{:S(2)}) collective-permute-start(bf16[256,768]{1,0:T(8,128)(2,1)S(1)} %get-tuple-element.88), channel_id=1, source_target_pairs={{0,6},{1,7},{2,0},{3,1},{4,2},{5,3},{6,4},{7,5},{8,14},{9,15},{10,... | collective-permute-start | bytes 1179656 | tf_op jit(solution)/shard_map/ppermute | solution.py:25
  75.0 10.2 %collective-permute-start.22 = (bf16[256,768]{1,0:T(8,128)(2,1)S(1)}, bf16[256,768]{1,0:T(8,128)(2,1)S(1)}, u32[]{:S(2)}, u32[]{:S(2)}) collective-permute-start(bf16[256,768]{1,0:T(8,128)(2,1)S(1)} %get-tuple-element.89), channel_id=1, source_target_pairs={{0,2},{1,3},{2,4},{3,5},{4,6},{5,7},{6,0},{7,1},{8,10},{9,11},{10,... | collective-permute-start | bytes 1179656 | tf_op jit(solution)/shard_map/ppermute | solution.py:25
  82.7 8.6 %collective-permute-start.28 = (bf16[128,768]{1,0:T(8,128)(2,1)S(1)}, bf16[128,768]{1,0:T(8,128)(2,1)S(1)}, u32[]{:S(2)}, u32[]{:S(2)}) collective-permute-start(bf16[128,768]{1,0:T(8,128)(2,1)S(1)} %add_convert_fusion.5), channel_id=1, source_target_pairs={{0,16},{1,17},{2,18},{3,19},{4,20},{5,21},{6,22},{7,23},{8,24},{9,... | collective-permute-start | bytes 589832 | tf_op jit(solution)/shard_map/ppermute | solution.py:25
  85.3 7.0 %collective-permute-start.25 = (bf16[128,768]{1,0:T(8,128)(2,1)S(1)}, bf16[128,768]{1,0:T(8,128)(2,1)S(1)}, u32[]{:S(2)}, u32[]{:S(2)}) collective-permute-start(bf16[128,768]{1,0:T(8,128)(2,1)S(1)} %add_convert_fusion.6), channel_id=1, source_target_pairs={{0,1},{1,0},{2,3},{3,2},{4,5},{5,4},{6,7},{7,6},{8,9},{9,8},{10,11... | collective-permute-start | bytes 589832 | tf_op jit(solution)/shard_map/ppermute | solution.py:25

commit v9 on v8

--- a/solution.py
+++ b/solution.py
@@ -226,7 +226,7 @@
     v0, t0 = unit_low(footage_embeds, caption_embeds)
 
     a1m, a1p = move(t0, z=1), move(t0, z=-1)
-    v1, tp = move(v0, y_lo=1), move(t0, y_hi=1)
+    v1, tp = move(v0, y_lo=1), across_y(t0)
     a1m, a1p, v1, tp = lax.optimization_barrier((a1m, a1p, v1, tp))
     v01 = jnp.concatenate([v0, v1])
     vm, vp = move(v01, x=1), move(v01, x=-1)
@@ -279,7 +279,7 @@
     )
 
     up, down = move(add(hq, hqq), z=1), move(add(hm, hmm), z=-1)
-    last = move(add(h01[rows:], up[rows:], down[rows:]), y_hi=1)
+    last = across_y(add(h01[rows:], up[rows:], down[rows:]))
     text_parts = [h01, up, down, last]
 
     r01, rm, rp = [move(block, core=1) for block in (s01, sm, sp)]
@@ -293,6 +293,18 @@
     video_grad = back_rows(score_scale, footage_embeds, video_parts)
     text_grad = back_rows(score_scale, caption_embeds, text_parts)
     return (video_grad, text_grad)
+
+
+def across_y(block):
+    pairs = []
+    for blk in range(4 * NZ):
+        for bulk in range(2 * NX):
+            y = ((blk // 2) % 2) * 2 + bulk % 2
+            to_y = (y + (1 if blk % 2 == 0 else -1)) % 4
+            to_blk = (blk // 4) * 4 + (to_y // 2) * 2 + blk % 2
+            to_bulk = (bulk // 2) * 2 + to_y % 2
+            pairs.append((blk * 2 * NX + bulk, to_blk * 2 * NX + to_bulk))
+    return lax.ppermute(lax.ppermute(block, AXES, pairs), AXES, pairs)
 
 
 def move_by_core(block, sign):

time: 94.9 us -> 99.6 us (1.050)
  waiting for transfers between devices: 36.7 us -> 40.6 us
  starting transfers between devices: 30.6 us -> 32.4 us
    ppermute x0 -> x4, waiting for transfers between devices: none -> 6.85 us  [across_y(): return lax.ppermute(lax.ppermute(block, AXES, pairs), AXES, pairs)]
    ppermute x0 -> x4, starting transfers between devices: none -> 3.61 us  [across_y(): return lax.ppermute(lax.ppermute(block, AXES, pairs), AXES, pairs)]
    ppermute x26 -> x24, waiting for transfers between devices: 32 us -> 29.6 us  [move(): return lax.ppermute(block, AXES, pairs)]
    ppermute x26 -> x24, starting transfers between devices: 26.5 us -> 24.7 us  [move(): return lax.ppermute(block, AXES, pairs)]
  transfers between devices with their start and end apart: 29 -> 31, of which waited for: 16 -> 17; matrix products, arithmetic and copies ran while one was open for 5% -> 5% of each run, Pallas kernels for 11% -> 10%
where the time goes in v9:
time: 99.6 us; the launch traced here: 99 us
  waiting for transfers between devices  40.6 us (41%)
  starting transfers between devices  32.4 us (33%)
  Pallas kernels  19.2 us (19%)
  other arithmetic  4.64 us (5%)
  between operations  2.09 us (2%)
    ppermute x24, waiting for transfers between devices, move(): return lax.ppermute(block, AXES, pairs)  29.6 us
    ppermute x24, starting transfers between devices, move(): return lax.ppermute(block, AXES, pairs)  24.7 us
    pallas_call x3, Pallas kernels, call(): pl.pallas_call(kernel, out_shape=outs, in_specs=[SMEM] * len(scalars) + [...  16 us
    ppermute x4, waiting for transfers between devices, across_y(): return lax.ppermute(lax.ppermute(block, AXES, pairs), AXES, pairs)  6.85 us
    convert_element_type x6, other arithmetic, add(): return total.astype(jnp.bfloat16)  4.5 us
    ppermute x2, starting transfers between devices, move_by_core(): return lax.ppermute(block, AXES, pairs)  3.81 us
    ppermute x4, starting transfers between devices, across_y(): return lax.ppermute(lax.ppermute(block, AXES, pairs), AXES, pairs)  3.61 us
    ppermute x1, waiting for transfers between devices, move_by_y_hi(): return lax.ppermute(block, AXES, pairs)  2.6 us
  transfers between devices with their start and end apart: 31, of which 17 were waited for; matrix products, arithmetic and copies ran while one was open for 5% of the time, Pallas kernels for 10%

profile of v9, /device:TPU:2, one launch (start us, length us, event | category | flops | bytes accessed | tf_op | source)
XLA Modules:
  0.0 99.0 jit_solution(17873693295226343825)
XLA Ops:
  0.6 1.2 %unit_low.1 = (bf16[128,768]{1,0:T(8,128)(2,1)S(1)}, bf16[128,768]{1,0:T(8,128)(2,1)S(1)}) custom-call(bf16[128,768]{1,0:T(8,128)(2,1)} %embedding_ref.2, bf16[128,768]{1,0:T(8,128)(2,1)} %embedding_ref.3), custom_call_target="tpu_custom_call" | custom-call | tf_op jit(solution)/shard_map/unit_low/pallas_call | solution.py:48
  1.8 1.7 %collective-permute-start.3 = (bf16[128,768]{1,0:T(8,128)(2,1)S(1)}, bf16[128,768]{1,0:T(8,128)(2,1)S(1)}, u32[]{:S(2)}, u32[]{:S(2)}) collective-permute-start(bf16[128,768]{1,0:T(8,128)(2,1)S(1)} %get-tuple-element.46.refs_0_), channel_id=1, source_target_pairs={{0,1},{1,16},{2,3},{3,18},{4,5},{5,20},{6,7},{7,22},{8,25},{9,8},{... | collective-permute-start | bytes 589832 | tf_op jit(solution)/shard_map/ppermute | solution.py:307
  3.5 5.9 %collective-permute-start.1 = (bf16[128,768]{1,0:T(8,128)(2,1)S(1)}, bf16[128,768]{1,0:T(8,128)(2,1)S(1)}, u32[]{:S(2)}, u32[]{:S(2)}) collective-permute-start(bf16[128,768]{1,0:T(8,128)(2,1)S(1)} %get-tuple-element.46.refs_0_), channel_id=1, source_target_pairs={{0,224},{1,225},{2,226},{3,227},{4,228},{5,229},{6,230},{7,231},{8... | collective-permute-start | bytes 589832 | tf_op jit(solution)/shard_map/ppermute | solution.py:25
  9.3 1.6 %collective-permute-start.2 = (bf16[128,768]{1,0:T(8,128)(2,1)S(1)}, bf16[128,768]{1,0:T(8,128)(2,1)S(1)}, u32[]{:S(2)}, u32[]{:S(2)}) collective-permute-start(bf16[128,768]{1,0:T(8,128)(2,1)S(1)} %get-tuple-element.45), channel_id=1, source_target_pairs={{0,1},{1,0},{2,3},{3,2},{4,5},{5,4},{6,7},{7,6},{8,9},{9,8},{10,11... | collective-permute-start | bytes 589832 | tf_op jit(solution)/shard_map/ppermute | solution.py:25
  11.4 5.7 %collective-permute-done.2 = bf16[128,768]{1,0:T(8,128)(2,1)S(1)} collective-permute-done((bf16[128,768]{1,0:T(8,128)(2,1)S(1)}, bf16[128,768]{1,0:T(8,128)(2,1)S(1)}, u32[]{:S(2)}, u32[]{:S(2)}) %collective-permute-start.2) | collective-permute-done | bytes 196640 | tf_op jit(solution)/shard_map/ppermute | solution.py:25
  18.7 1.5 %collective-permute-start.5 = (bf16[256,768]{1,0:T(8,128)(2,1)S(1)}, bf16[256,768]{1,0:T(8,128)(2,1)S(1)}, u32[]{:S(2)}, u32[]{:S(2)}) collective-permute-start(bf16[256,768]{1,0:T(8,128)(2,1)S(1)} %constant_dynamic-update-slice_fusion.refs_8_), channel_id=1, source_target_pairs={{0,2},{1,3},{2,4},{3,5},{4,6},{5,7},{6,0},{7,1},{8,10},{9,11},{10,... | collective-permute-start | bytes 1179656 | tf_op jit(solution)/shard_map/ppermute | solution.py:25
  20.2 4.1 %collective-permute-start.10 = (bf16[128,768]{1,0:T(8,128)(2,1)S(1)}, bf16[128,768]{1,0:T(8,128)(2,1)S(1)}, u32[]{:S(2)}, u32[]{:S(2)}) collective-permute-start(bf16[128,768]{1,0:T(8,128)(2,1)S(1)} %collective-permute-done.1.refs_4_), channel_id=1, source_target_pairs={{0,224},{1,225},{2,226},{3,227},{4,228},{5,229},{6,230},{7,231},{8... | collective-permute-start | bytes 589832 | tf_op jit(solution)/shard_map/ppermute | solution.py:25
  24.3 2.0 %collective-permute-start.8 = (bf16[128,768]{1,0:T(8,128)(2,1)S(1)}, bf16[128,768]{1,0:T(8,128)(2,1)S(1)}, u32[]{:S(2)}, u32[]{:S(2)}) collective-permute-start(bf16[128,768]{1,0:T(8,128)(2,1)S(1)} %collective-permute-done.4.refs_1_), channel_id=1, source_target_pairs={{0,224},{1,225},{2,226},{3,227},{4,228},{5,229},{6,230},{7,231},{8... | collective-permute-start | bytes 589832 | tf_op jit(solution)/shard_map/ppermute | solution.py:25
  28.2 1.4 %collective-permute-done.10.refs_7_ = bf16[128,768]{1,0:T(8,128)(2,1)S(1)} collective-permute-done((bf16[128,768]{1,0:T(8,128)(2,1)S(1)}, bf16[128,768]{1,0:T(8,128)(2,1)S(1)}, u32[]{:S(2)}, u32[]{:S(2)}) %collective-permute-start.10) | collective-permute-done | bytes 196640 | tf_op jit(solution)/shard_map/ppermute | solution.py:25
  29.6 2.2 %collective-permute-done.8.refs_5_ = bf16[128,768]{1,0:T(8,128)(2,1)S(1)} collective-permute-done((bf16[128,768]{1,0:T(8,128)(2,1)S(1)}, bf16[128,768]{1,0:T(8,128)(2,1)S(1)}, u32[]{:S(2)}, u32[]{:S(2)}) %collective-permute-start.8) | collective-permute-done | bytes 196640 | tf_op jit(solution)/shard_map/ppermute | solution.py:25
  31.8 2.0 %collective-permute-done.7.refs_3_ = bf16[128,768]{1,0:T(8,128)(2,1)S(1)} collective-permute-done((bf16[128,768]{1,0:T(8,128)(2,1)S(1)}, bf16[128,768]{1,0:T(8,128)(2,1)S(1)}, u32[]{:S(2)}, u32[]{:S(2)}) %collective-permute-start.7) | collective-permute-done | bytes 196640 | tf_op jit(solution)/shard_map/ppermute | solution.py:25
  34.4 1.6 %collective-permute-start.11 = (bf16[256,768]{1,0:T(8,128)(2,1)S(1)}, bf16[256,768]{1,0:T(8,128)(2,1)S(1)}, u32[]{:S(2)}, u32[]{:S(2)}) collective-permute-start(bf16[256,768]{1,0:T(8,128)(2,1)S(1)} %broadcast_select_fusion), channel_id=1, source_target_pairs={{0,2},{1,3},{2,4},{3,5},{4,6},{5,7},{6,0},{7,1},{8,14},{9,15},{10,... | collective-permute-start | bytes 1179656 | tf_op jit(solution)/shard_map/ppermute | solution.py:317
  36.3 4.3 %near_weights.1 = (bf16[1536,1024]{1,0:T(8,128)(2,1)S(1)}, bf16[1024,768]{1,0:T(8,128)(2,1)S(1)}, bf16[1536,768]{1,0:T(8,128)(2,1)S(1)}) custom-call(f32[1]{0:T(128)S(6)} %copy.7.scale_ref, f32[1]{0:T(128)S(6)} %copy.8.offset_ref, s32[2]{0:T(128)S(1)} %pad_add_fusion.place_ref, bf16[128,768]{1,0:T(8,128)(2,1)S(1)} %get-tuple-element.46.refs_0_, ...), custom_call_target="tpu_custom_call" | custom-call | flops 2415919104 | tf_op jit(solution)/shard_map/near_weights/pallas_call | solution.py:209
  40.6 2.6 %collective-permute-done.12.last = bf16[128,768]{1,0:T(8,128)(2,1)S(1)} collective-permute-done((bf16[128,768]{1,0:T(8,128)(2,1)S(1)}, bf16[128,768]{1,0:T(8,128)(2,1)S(1)}, u32[]{:S(2)}, u32[]{:S(2)}) %collective-permute-start.12) | collective-permute-done | bytes 196640 | tf_op jit(solution)/shard_map/ppermute | solution.py:327
  43.2 1.7 %collective-permute-done.16.refs_1_ = bf16[256,768]{1,0:T(8,128)(2,1)S(1)} collective-permute-done((bf16[256,768]{1,0:T(8,128)(2,1)S(1)}, bf16[256,768]{1,0:T(8,128)(2,1)S(1)}, u32[]{:S(2)}, u32[]{:S(2)}) %collective-permute-start.16) | collective-permute-done | bytes 393248 | tf_op jit(solution)/shard_map/ppermute | solution.py:25
  44.9 7.0 %far_weights_and_sums.1 = (bf16[1536,128]{1,0:T(8,128)(2,1)S(1)}, bf16[512,1152]{1,0:T(8,128)(2,1)S(1)}, bf16[512,768]{1,0:T(8,128)(2,1)S(1)}, bf16[256,768]{1,0...) custom-call(f32[1]{0:T(128)S(6)} %copy.7.scale_ref, ...), custom_call_target="tpu_custom_call" | custom-call | flops 5033164800 | tf_op jit(solution)/shard_map/far_weights_and_sums/pallas_call | solution.py:209
  52.0 1.5 %collective-permute-start.17 = (bf16[256,768]{1,0:T(8,128)(2,1)}, bf16[256,768]{1,0:T(8,128)(2,1)}, u32[]{:S(2)}, u32[]{:S(2)}) collective-permute-start(bf16[256,768]{1,0:T(8,128)(2,1)} %get-tuple-element.63), channel_id=1, source_target_pairs={{0,224},{1,225},{2,226},{3,227},{4,228},{5,229},{6,230},{7,231},{8... | collective-permute-start | bytes 1179656 | tf_op jit(solution)/shard_map/ppermute | solution.py:25
  54.1 4.7 %own_video_and_near_text_sums.1 = (bf16[256,768]{1,0:T(8,128)(2,1)S(1)}, bf16[256,768]{1,0:T(8,128)(2,1)S(1)}, bf16[256,768]{1,0:T(8,128)(2,1)S(1)}, bf16[256,76...) custom-call(bf16[1536,1024]{1,0:T(8,128)(2,1)S(1)} %get-tuple-elemen, ...), custom_call_target="tpu_custom_call" | custom-call | flops 4026531840 | tf_op jit(solution)/shard_map/own_video_and_near_text_sums/pallas_call | solution.py:209
  59.6 2.2 %collective-permute-start.20 = (bf16[256,768]{1,0:T(8,128)(2,1)}, bf16[256,768]{1,0:T(8,128)(2,1)}, u32[]{:S(2)}, u32[]{:S(2)}) collective-permute-start(bf16[256,768]{1,0:T(8,128)(2,1)} %add_convert_fusion.4), channel_id=1, source_target_pairs={{0,6},{1,7},{2,0},{3,1},{4,2},{5,3},{6,4},{7,5},{8,10},{9,11},{10,... | collective-permute-start | bytes 1179656 | tf_op jit(solution)/shard_map/ppermute | solution.py:317
  62.4 1.3 %collective-permute-done.17 = bf16[256,768]{1,0:T(8,128)(2,1)} collective-permute-done((bf16[256,768]{1,0:T(8,128)(2,1)}, bf16[256,768]{1,0:T(8,128)(2,1)}, u32[]{:S(2)}, u32[]{:S(2)}) %collective-permute-start.17) | collective-permute-done | bytes 393248 | tf_op jit(solution)/shard_map/ppermute | solution.py:25
  63.7 2.5 %collective-permute-done.18 = bf16[256,768]{1,0:T(8,128)(2,1)} collective-permute-done((bf16[256,768]{1,0:T(8,128)(2,1)}, bf16[256,768]{1,0:T(8,128)(2,1)}, u32[]{:S(2)}, u32[]{:S(2)}) %collective-permute-start.18) | collective-permute-done | bytes 393248 | tf_op jit(solution)/shard_map/ppermute | solution.py:25
  66.2 1.5 %collective-permute-done.20 = bf16[256,768]{1,0:T(8,128)(2,1)} collective-permute-done((bf16[256,768]{1,0:T(8,128)(2,1)}, bf16[256,768]{1,0:T(8,128)(2,1)}, u32[]{:S(2)}, u32[]{:S(2)}) %collective-permute-start.20) | collective-permute-done | bytes 393248 | tf_op jit(solution)/shard_map/ppermute | solution.py:317
  67.7 1.1 %add_convert_fusion = bf16[256,768]{1,0:T(8,128)(2,1)S(1)} fusion(bf16[256,768]{1,0:T(8,128)(2,1)} %collective-permute-done.17, bf16[256,768]{1,0:T(8,128)(2,1)S(1)} %get-tuple-element.86), kind=kLoop, calls=%fused_computation | loop fusion | flops 786432 | bytes 1179648 | tf_op jit(solution)/shard_map/convert_element_type | solution.py:32
  68.8 2.8 %collective-permute-start.28 = (bf16[256,768]{1,0:T(8,128)(2,1)S(1)}, bf16[256,768]{1,0:T(8,128)(2,1)S(1)}, u32[]{:S(2)}, u32[]{:S(2)}) collective-permute-start(bf16[256,768]{1,0:T(8,128)(2,1)S(1)} %add_convert_fusion), channel_id=1, source_target_pairs={{0,224},{1,225},{2,226},{3,227},{4,228},{5,229},{6,230},{7,231},{8... | collective-permute-start | bytes 1179656 | tf_op jit(solution)/shard_map/ppermute | solution.py:25
  72.8 1.3 %add_convert_fusion.2 = (bf16[256,768]{1,0:T(8,128)(2,1)S(1)}, bf16[256,768]{1,0:T(8,128)(2,1)S(1)}) fusion(bf16[256,768]{1,0:T(8,128)(2,1)S(1)} %collective-permute-done.24, bf16[256,768]{1,0:T(8,128)(2,1)S(1)} %get-tuple-element.81, bf16[256,768]{1,0:T(8,128)(2,1)} %collective-permute-done.20, pred[]{:T(512)S(6)} %eq.15, pred[]{:T(512)S(6)} %eq.13, ...), kind=kLoop, calls=%fused_computation.2 | loop fusion | flops 2752512 | bytes 2752514 | tf_op jit(solution)/shard_map/convert_element_type | solution.py:32
  74.2 2.2 %collective-permute-start.25 = (bf16[256,768]{1,0:T(8,128)(2,1)S(1)}, bf16[256,768]{1,0:T(8,128)(2,1)S(1)}, u32[]{:S(2)}, u32[]{:S(2)}) collective-permute-start(bf16[256,768]{1,0:T(8,128)(2,1)S(1)} %get-tuple-element.88), channel_id=1, source_target_pairs={{0,6},{1,7},{2,0},{3,1},{4,2},{5,3},{6,4},{7,5},{8,14},{9,15},{10,... | collective-permute-start | bytes 1179656 | tf_op jit(solution)/shard_map/ppermute | solution.py:25
  76.3 3.1 %collective-permute-done.28.refs_2_ = bf16[256,768]{1,0:T(8,128)(2,1)S(1)} collective-permute-done((bf16[256,768]{1,0:T(8,128)(2,1)S(1)}, bf16[256,768]{1,0:T(8,128)(2,1)S(1)}, u32[]{:S(2)}, u32[]{:S(2)}) %collective-permute-start.28) | collective-permute-done | bytes 393248 | tf_op jit(solution)/shard_map/ppermute | solution.py:25
  79.4 4.6 %collective-permute-done.27.refs_1_ = bf16[256,768]{1,0:T(8,128)(2,1)S(1)} collective-permute-done((bf16[256,768]{1,0:T(8,128)(2,1)S(1)}, bf16[256,768]{1,0:T(8,128)(2,1)S(1)}, u32[]{:S(2)}, u32[]{:S(2)}) %collective-permute-start.27) | collective-permute-done | bytes 393248 | tf_op jit(solution)/shard_map/ppermute | solution.py:25
  84.9 1.7 %collective-permute-done.23.refs_2_ = bf16[256,768]{1,0:T(8,128)(2,1)S(1)} collective-permute-done((bf16[256,768]{1,0:T(8,128)(2,1)S(1)}, bf16[256,768]{1,0:T(8,128)(2,1)S(1)}, u32[]{:S(2)}, u32[]{:S(2)}) %collective-permute-start.23) | collective-permute-done | bytes 393248 | tf_op jit(solution)/shard_map/ppermute | solution.py:25
  87.5 3.5 %collective-permute-done.29 = bf16[128,768]{1,0:T(8,128)(2,1)S(1)} collective-permute-done((bf16[128,768]{1,0:T(8,128)(2,1)S(1)}, bf16[128,768]{1,0:T(8,128)(2,1)S(1)}, u32[]{:S(2)}, u32[]{:S(2)}) %collective-permute-start.29) | collective-permute-done | bytes 196640 | tf_op jit(solution)/shard_map/ppermute | solution.py:307
  91.8 1.8 %collective-permute-done.26.refs_4_ = bf16[128,768]{1,0:T(8,128)(2,1)S(1)} collective-permute-done((bf16[128,768]{1,0:T(8,128)(2,1)S(1)}, bf16[128,768]{1,0:T(8,128)(2,1)S(1)}, u32[]{:S(2)}, u32[]{:S(2)}) %collective-permute-start.26) | collective-permute-done | bytes 196640 | tf_op jit(solution)/shard_map/ppermute | solution.py:25
  94.6 3.3 %collective-permute-done.30.refs_3_ = bf16[128,768]{1,0:T(8,128)(2,1)S(1)} collective-permute-done((bf16[128,768]{1,0:T(8,128)(2,1)S(1)}, bf16[128,768]{1,0:T(8,128)(2,1)S(1)}, u32[]{:S(2)}, u32[]{:S(2)}) %collective-permute-start.30) | collective-permute-done | bytes 196640 | tf_op jit(solution)/shard_map/ppermute | solution.py:307
  (51 shorter events, 11.2 us)
Async XLA Ops:
  1.8 9.1 %collective-permute-start.3 = (bf16[128,768]{1,0:T(8,128)(2,1)S(1)}, bf16[128,768]{1,0:T(8,128)(2,1)S(1)}, u32[]{:S(2)}, u32[]{:S(2)}) collective-permute-start(bf16[128,768]{1,0:T(8,128)(2,1)S(1)} %get-tuple-element.46.refs_0_), channel_id=1, source_target_pairs={{0,1},{1,16},{2,3},{3,18},{4,5},{5,20},{6,7},{7,22},{8,25},{9,8},{... | collective-permute-start | bytes 589832 | tf_op jit(solution)/shard_map/ppermute | solution.py:307
  3.5 13.6 %collective-permute-start.1 = (bf16[128,768]{1,0:T(8,128)(2,1)S(1)}, bf16[128,768]{1,0:T(8,128)(2,1)S(1)}, u32[]{:S(2)}, u32[]{:S(2)}) collective-permute-start(bf16[128,768]{1,0:T(8,128)(2,1)S(1)} %get-tuple-element.46.refs_0_), channel_id=1, source_target_pairs={{0,224},{1,225},{2,226},{3,227},{4,228},{5,229},{6,230},{7,231},{8... | collective-permute-start | bytes 589832 | tf_op jit(solution)/shard_map/ppermute | solution.py:25
  9.3 7.8 %collective-permute-start.2 = (bf16[128,768]{1,0:T(8,128)(2,1)S(1)}, bf16[128,768]{1,0:T(8,128)(2,1)S(1)}, u32[]{:S(2)}, u32[]{:S(2)}) collective-permute-start(bf16[128,768]{1,0:T(8,128)(2,1)S(1)} %get-tuple-element.45), channel_id=1, source_target_pairs={{0,1},{1,0},{2,3},{3,2},{4,5},{5,4},{6,7},{7,6},{8,9},{9,8},{10,11... | collective-permute-start | bytes 589832 | tf_op jit(solution)/shard_map/ppermute | solution.py:25
  10.9 7.2 %collective-permute-start = (bf16[128,768]{1,0:T(8,128)(2,1)S(1)}, bf16[128,768]{1,0:T(8,128)(2,1)S(1)}, u32[]{:S(2)}, u32[]{:S(2)}) collective-permute-start(bf16[128,768]{1,0:T(8,128)(2,1)S(1)} %get-tuple-element.46.refs_0_), channel_id=1, source_target_pairs={{0,32},{1,33},{2,34},{3,35},{4,36},{5,37},{6,38},{7,39},{8,40},{9,... | collective-permute-start | bytes 589832 | tf_op jit(solution)/shard_map/ppermute | solution.py:25
  10.9 7.2 %collective-permute-start.4 = (bf16[128,768]{1,0:T(8,128)(2,1)S(1)}, bf16[128,768]{1,0:T(8,128)(2,1)S(1)}, u32[]{:S(2)}, u32[]{:S(2)}) collective-permute-start(bf16[128,768]{1,0:T(8,128)(2,1)S(1)} %collective-permute-done.3), channel_id=1, source_target_pairs={{0,1},{1,16},{2,3},{3,18},{4,5},{5,20},{6,7},{7,22},{8,25},{9,8},{... | collective-permute-start | bytes 589832 | tf_op jit(solution)/shard_map/ppermute | solution.py:307
  18.1 8.7 %collective-permute-start.9 = (bf16[128,768]{1,0:T(8,128)(2,1)S(1)}, bf16[128,768]{1,0:T(8,128)(2,1)S(1)}, u32[]{:S(2)}, u32[]{:S(2)}) collective-permute-start(bf16[128,768]{1,0:T(8,128)(2,1)S(1)} %collective-permute-done.refs_2_), channel_id=1, source_target_pairs={{0,32},{1,33},{2,34},{3,35},{4,36},{5,37},{6,38},{7,39},{8,40},{9,... | collective-permute-start | bytes 589832 | tf_op jit(solution)/shard_map/ppermute | solution.py:25
  18.1 15.7 %collective-permute-start.6 = (bf16[256,768]{1,0:T(8,128)(2,1)S(1)}, bf16[256,768]{1,0:T(8,128)(2,1)S(1)}, u32[]{:S(2)}, u32[]{:S(2)}) collective-permute-start(bf16[256,768]{1,0:T(8,128)(2,1)S(1)} %constant_dynamic-update-slice_fusion.refs_8_), channel_id=1, source_target_pairs={{0,6},{1,7},{2,0},{3,1},{4,2},{5,3},{6,4},{7,5},{8,14},{9,15},{10,... | collective-permute-start | bytes 1179656 | tf_op jit(solution)/shard_map/ppermute | solution.py:25
  18.7 15.1 %collective-permute-start.5 = (bf16[256,768]{1,0:T(8,128)(2,1)S(1)}, bf16[256,768]{1,0:T(8,128)(2,1)S(1)}, u32[]{:S(2)}, u32[]{:S(2)}) collective-permute-start(bf16[256,768]{1,0:T(8,128)(2,1)S(1)} %constant_dynamic-update-slice_fusion.refs_8_), channel_id=1, source_target_pairs={{0,2},{1,3},{2,4},{3,5},{4,6},{5,7},{6,0},{7,1},{8,10},{9,11},{10,... | collective-permute-start | bytes 1179656 | tf_op jit(solution)/shard_map/ppermute | solution.py:25
  20.2 9.4 %collective-permute-start.10 = (bf16[128,768]{1,0:T(8,128)(2,1)S(1)}, bf16[128,768]{1,0:T(8,128)(2,1)S(1)}, u32[]{:S(2)}, u32[]{:S(2)}) collective-permute-start(bf16[128,768]{1,0:T(8,128)(2,1)S(1)} %collective-permute-done.1.refs_4_), channel_id=1, source_target_pairs={{0,224},{1,225},{2,226},{3,227},{4,228},{5,229},{6,230},{7,231},{8... | collective-permute-start | bytes 589832 | tf_op jit(solution)/shard_map/ppermute | solution.py:25
  24.3 7.6 %collective-permute-start.8 = (bf16[128,768]{1,0:T(8,128)(2,1)S(1)}, bf16[128,768]{1,0:T(8,128)(2,1)S(1)}, u32[]{:S(2)}, u32[]{:S(2)}) collective-permute-start(bf16[128,768]{1,0:T(8,128)(2,1)S(1)} %collective-permute-done.4.refs_1_), channel_id=1, source_target_pairs={{0,224},{1,225},{2,226},{3,227},{4,228},{5,229},{6,230},{7,231},{8... | collective-permute-start | bytes 589832 | tf_op jit(solution)/shard_map/ppermute | solution.py:25
  26.8 7.0 %collective-permute-start.7 = (bf16[128,768]{1,0:T(8,128)(2,1)S(1)}, bf16[128,768]{1,0:T(8,128)(2,1)S(1)}, u32[]{:S(2)}, u32[]{:S(2)}) collective-permute-start(bf16[128,768]{1,0:T(8,128)(2,1)S(1)} %collective-permute-done.4.refs_1_), channel_id=1, source_target_pairs={{0,32},{1,33},{2,34},{3,35},{4,36},{5,37},{6,38},{7,39},{8,40},{9,... | collective-permute-start | bytes 589832 | tf_op jit(solution)/shard_map/ppermute | solution.py:25
  29.6 6.6 %collective-permute-start.13 = (bf16[256,768]{1,0:T(8,128)(2,1)S(1)}, bf16[256,768]{1,0:T(8,128)(2,1)S(1)}, u32[]{:S(2)}, u32[]{:S(2)}) collective-permute-start(bf16[256,768]{1,0:T(8,128)(2,1)S(1)} %constant_dynamic-update-slice_fusion.refs_8_), channel_id=1, source_target_pairs={{0,8},{1,9},{2,10},{3,11},{4,12},{5,13},{6,14},{7,15},{8,0},{9,1},... | collective-permute-start | bytes 1179656 | tf_op jit(solution)/shard_map/ppermute | solution.py:25
  33.8 2.4 %collective-permute-start.15 = (bf16[256,768]{1,0:T(8,128)(2,1)S(1)}, bf16[256,768]{1,0:T(8,128)(2,1)S(1)}, u32[]{:S(2)}, u32[]{:S(2)}) collective-permute-start(bf16[256,768]{1,0:T(8,128)(2,1)S(1)} %collective-permute-done.6.refs_10_), channel_id=1, source_target_pairs={{0,8},{1,9},{2,10},{3,11},{4,12},{5,13},{6,14},{7,15},{8,0},{9,1},... | collective-permute-start | bytes 1179656 | tf_op jit(solution)/shard_map/ppermute | solution.py:25
  33.8 2.4 %collective-permute-start.14 = (bf16[256,768]{1,0:T(8,128)(2,1)S(1)}, bf16[256,768]{1,0:T(8,128)(2,1)S(1)}, u32[]{:S(2)}, u32[]{:S(2)}) collective-permute-start(bf16[256,768]{1,0:T(8,128)(2,1)S(1)} %collective-permute-done.5.refs_9_), channel_id=1, source_target_pairs={{0,8},{1,9},{2,10},{3,11},{4,12},{5,13},{6,14},{7,15},{8,0},{9,1},... | collective-permute-start | bytes 1179656 | tf_op jit(solution)/shard_map/ppermute | solution.py:25
  34.4 8.8 %collective-permute-start.11 = (bf16[256,768]{1,0:T(8,128)(2,1)S(1)}, bf16[256,768]{1,0:T(8,128)(2,1)S(1)}, u32[]{:S(2)}, u32[]{:S(2)}) collective-permute-start(bf16[256,768]{1,0:T(8,128)(2,1)S(1)} %broadcast_select_fusion), channel_id=1, source_target_pairs={{0,2},{1,3},{2,4},{3,5},{4,6},{5,7},{6,0},{7,1},{8,14},{9,15},{10,... | collective-permute-start | bytes 1179656 | tf_op jit(solution)/shard_map/ppermute | solution.py:317
  36.0 7.2 %collective-permute-start.12 = (bf16[128,768]{1,0:T(8,128)(2,1)S(1)}, bf16[128,768]{1,0:T(8,128)(2,1)S(1)}, u32[]{:S(2)}, u32[]{:S(2)}) collective-permute-start(bf16[128,768]{1,0:T(8,128)(2,1)S(1)} %broadcast_select_fusion.1), channel_id=1, source_target_pairs={{0,32},{1,33},{2,34},{3,35},{4,36},{5,37},{6,38},{7,39},{8,40},{9,... | collective-permute-start | bytes 589832 | tf_op jit(solution)/shard_map/ppermute | solution.py:327
  43.2 1.7 %collective-permute-start.16 = (bf16[256,768]{1,0:T(8,128)(2,1)S(1)}, bf16[256,768]{1,0:T(8,128)(2,1)S(1)}, u32[]{:S(2)}, u32[]{:S(2)}) collective-permute-start(bf16[256,768]{1,0:T(8,128)(2,1)S(1)} %collective-permute-done.11.refs_0_), channel_id=1, source_target_pairs={{0,8},{1,9},{2,10},{3,11},{4,12},{5,13},{6,14},{7,15},{8,0},{9,1},... | collective-permute-start | bytes 1179656 | tf_op jit(solution)/shard_map/ppermute | solution.py:25
  51.9 6.9 %collective-permute-start.19 = (bf16[256,768]{1,0:T(8,128)(2,1)S(1)}, bf16[256,768]{1,0:T(8,128)(2,1)S(1)}, u32[]{:S(2)}, u32[]{:S(2)}) collective-permute-start(bf16[256,768]{1,0:T(8,128)(2,1)S(1)} %get-tuple-element.69), channel_id=1, source_target_pairs={{0,8},{1,9},{2,10},{3,11},{4,12},{5,13},{6,14},{7,15},{8,0},{9,1},... | collective-permute-start | bytes 1179656 | tf_op jit(solution)/shard_map/ppermute | solution.py:25
  52.0 11.7 %collective-permute-start.17 = (bf16[256,768]{1,0:T(8,128)(2,1)}, bf16[256,768]{1,0:T(8,128)(2,1)}, u32[]{:S(2)}, u32[]{:S(2)}) collective-permute-start(bf16[256,768]{1,0:T(8,128)(2,1)} %get-tuple-element.63), channel_id=1, source_target_pairs={{0,224},{1,225},{2,226},{3,227},{4,228},{5,229},{6,230},{7,231},{8... | collective-permute-start | bytes 1179656 | tf_op jit(solution)/shard_map/ppermute | solution.py:25
  53.6 12.6 %collective-permute-start.18 = (bf16[256,768]{1,0:T(8,128)(2,1)}, bf16[256,768]{1,0:T(8,128)(2,1)}, u32[]{:S(2)}, u32[]{:S(2)}) collective-permute-start(bf16[256,768]{1,0:T(8,128)(2,1)} %get-tuple-element.64), channel_id=1, source_target_pairs={{0,32},{1,33},{2,34},{3,35},{4,36},{5,37},{6,38},{7,39},{8,40},{9,... | collective-permute-start | bytes 1179656 | tf_op jit(solution)/shard_map/ppermute | solution.py:25
  59.6 8.1 %collective-permute-start.20 = (bf16[256,768]{1,0:T(8,128)(2,1)}, bf16[256,768]{1,0:T(8,128)(2,1)}, u32[]{:S(2)}, u32[]{:S(2)}) collective-permute-start(bf16[256,768]{1,0:T(8,128)(2,1)} %add_convert_fusion.4), channel_id=1, source_target_pairs={{0,6},{1,7},{2,0},{3,1},{4,2},{5,3},{6,4},{7,5},{8,10},{9,11},{10,... | collective-permute-start | bytes 1179656 | tf_op jit(solution)/shard_map/ppermute | solution.py:317
  61.9 23.0 %collective-permute-start.21 = (bf16[256,768]{1,0:T(8,128)(2,1)S(1)}, bf16[256,768]{1,0:T(8,128)(2,1)S(1)}, u32[]{:S(2)}, u32[]{:S(2)}) collective-permute-start(bf16[256,768]{1,0:T(8,128)(2,1)S(1)} %get-tuple-element.77), channel_id=1, source_target_pairs={{0,8},{1,9},{2,10},{3,11},{4,12},{5,13},{6,14},{7,15},{8,0},{9,1},... | collective-permute-start | bytes 1179656 | tf_op jit(solution)/shard_map/ppermute | solution.py:25
  61.9 10.9 %collective-permute-start.22 = (bf16[256,768]{1,0:T(8,128)(2,1)S(1)}, bf16[256,768]{1,0:T(8,128)(2,1)S(1)}, u32[]{:S(2)}, u32[]{:S(2)}) collective-permute-start(bf16[256,768]{1,0:T(8,128)(2,1)S(1)} %get-tuple-element.79), channel_id=1, source_target_pairs={{0,8},{1,9},{2,10},{3,11},{4,12},{5,13},{6,14},{7,15},{8,0},{9,1},... | collective-permute-start | bytes 1179656 | tf_op jit(solution)/shard_map/ppermute | solution.py:25
  63.7 9.1 %collective-permute-start.24 = (bf16[256,768]{1,0:T(8,128)(2,1)S(1)}, bf16[256,768]{1,0:T(8,128)(2,1)S(1)}, u32[]{:S(2)}, u32[]{:S(2)}) collective-permute-start(bf16[256,768]{1,0:T(8,128)(2,1)S(1)} %get-tuple-element.82), channel_id=1, source_target_pairs={{0,8},{1,9},{2,10},{3,11},{4,12},{5,13},{6,14},{7,15},{8,0},{9,1},... | collective-permute-start | bytes 1179656 | tf_op jit(solution)/shard_map/ppermute | solution.py:25
  68.8 10.6 %collective-permute-start.28 = (bf16[256,768]{1,0:T(8,128)(2,1)S(1)}, bf16[256,768]{1,0:T(8,128)(2,1)S(1)}, u32[]{:S(2)}, u32[]{:S(2)}) collective-permute-start(bf16[256,768]{1,0:T(8,128)(2,1)S(1)} %add_convert_fusion), channel_id=1, source_target_pairs={{0,224},{1,225},{2,226},{3,227},{4,228},{5,229},{6,230},{7,231},{8... | collective-permute-start | bytes 1179656 | tf_op jit(solution)/shard_map/ppermute | solution.py:25
  72.7 11.3 %collective-permute-start.27 = (bf16[256,768]{1,0:T(8,128)(2,1)S(1)}, bf16[256,768]{1,0:T(8,128)(2,1)S(1)}, u32[]{:S(2)}, u32[]{:S(2)}) collective-permute-start(bf16[256,768]{1,0:T(8,128)(2,1)S(1)} %add_convert_fusion.1), channel_id=1, source_target_pairs={{0,32},{1,33},{2,34},{3,35},{4,36},{5,37},{6,38},{7,39},{8,40},{9,... | collective-permute-start | bytes 1179656 | tf_op jit(solution)/shard_map/ppermute | solution.py:25
  74.2 23.8 %copy-start.1 = (bf16[128,768]{1,0:T(8,128)(2,1)S(1)}, bf16[128,768]{1,0:T(8,128)(2,1)}, u32[]{:S(2)}) copy-start(bf16[128,768]{1,0:T(8,128)(2,1)} %embedding_ref.3) | copy-start | bytes 589828
  74.2 10.7 %collective-permute-start.25 = (bf16[256,768]{1,0:T(8,128)(2,1)S(1)}, bf16[256,768]{1,0:T(8,128)(2,1)S(1)}, u32[]{:S(2)}, u32[]{:S(2)}) collective-permute-start(bf16[256,768]{1,0:T(8,128)(2,1)S(1)} %get-tuple-element.88), channel_id=1, source_target_pairs={{0,6},{1,7},{2,0},{3,1},{4,2},{5,3},{6,4},{7,5},{8,14},{9,15},{10,... | collective-permute-start | bytes 1179656 | tf_op jit(solution)/shard_map/ppermute | solution.py:25
  76.3 10.3 %collective-permute-start.23 = (bf16[256,768]{1,0:T(8,128)(2,1)S(1)}, bf16[256,768]{1,0:T(8,128)(2,1)S(1)}, u32[]{:S(2)}, u32[]{:S(2)}) collective-permute-start(bf16[256,768]{1,0:T(8,128)(2,1)S(1)} %get-tuple-element.89), channel_id=1, source_target_pairs={{0,2},{1,3},{2,4},{3,5},{4,6},{5,7},{6,0},{7,1},{8,10},{9,11},{10,... | collective-permute-start | bytes 1179656 | tf_op jit(solution)/shard_map/ppermute | solution.py:25
  84.1 7.0 %collective-permute-start.29 = (bf16[128,768]{1,0:T(8,128)(2,1)S(1)}, bf16[128,768]{1,0:T(8,128)(2,1)S(1)}, u32[]{:S(2)}, u32[]{:S(2)}) collective-permute-start(bf16[128,768]{1,0:T(8,128)(2,1)S(1)} %add_convert_fusion.5), channel_id=1, source_target_pairs={{0,1},{1,16},{2,3},{3,18},{4,5},{5,20},{6,7},{7,22},{8,25},{9,8},{... | collective-permute-start | bytes 589832 | tf_op jit(solution)/shard_map/ppermute | solution.py:307
  86.7 6.8 %collective-permute-start.26 = (bf16[128,768]{1,0:T(8,128)(2,1)S(1)}, bf16[128,768]{1,0:T(8,128)(2,1)S(1)}, u32[]{:S(2)}, u32[]{:S(2)}) collective-permute-start(bf16[128,768]{1,0:T(8,128)(2,1)S(1)} %add_convert_fusion.6), channel_id=1, source_target_pairs={{0,1},{1,0},{2,3},{3,2},{4,5},{5,4},{6,7},{7,6},{8,9},{9,8},{10,11... | collective-permute-start | bytes 589832 | tf_op jit(solution)/shard_map/ppermute | solution.py:25
  91.1 6.9 %collective-permute-start.30 = (bf16[128,768]{1,0:T(8,128)(2,1)S(1)}, bf16[128,768]{1,0:T(8,128)(2,1)S(1)}, u32[]{:S(2)}, u32[]{:S(2)}) collective-permute-start(bf16[128,768]{1,0:T(8,128)(2,1)S(1)} %collective-permute-done.29), channel_id=1, source_target_pairs={{0,1},{1,16},{2,3},{3,18},{4,5},{5,20},{6,7},{7,22},{8,25},{9,8},{... | collective-permute-start | bytes 589832 | tf_op jit(solution)/shard_map/ppermute | solution.py:307
  (1 other events, 20.9 us)

commit v10 on v7

--- a/solution.py
+++ b/solution.py
@@ -103,9 +103,11 @@
 
 
 def near_kernel(scale_ref, offset_ref, place_ref, *refs):
-    texts, videos = refs[:8], refs[8:-3]
+    (t0, tp, a1m, a1p, tm, tq), videos = refs[:6], refs[6:-3]
     weights, text, video = refs[-3:]
-    put(text, texts)
+    half = PAIR // 2
+    a2m, b1m, a2p, b1p = tm[:half, :], tm[half:, :], tq[:half, :], tq[half:, :]
+    put(text, [t0, tp, a1m, b1m, a1p, b1p, a2m, a2p])
     put(video, videos)
     core = place_ref[0]
     tile = video.shape[0] // 2
@@ -230,14 +232,13 @@
     v1, tp, a1m, a1p = lax.optimization_barrier((v1, tp, a1m, a1p))
     v01 = jnp.concatenate([v0, v1])
     vm, vp = move(v01, x=1), move(v01, x=-1)
-    a2m, a2p = move(a1m, z=1), move(a1p, z=-1)
-    b1m, b1p = move(tp, z=1), move(tp, z=-1)
-    vm, vp, b1m, b1p, a2m, a2p = lax.optimization_barrier((vm, vp, b1m, b1p, a2m, a2p))
-    b2 = move_by_y_hi(jnp.where(y_hi == 1, b1p, b1m))
+    tm, tq = jnp.concatenate([a1m, tp]), jnp.concatenate([a1p, tp])
+    vm, vp, tm, tq = lax.optimization_barrier((vm, vp, move(tm, z=1), move(tq, z=-1)))
+    b2 = move_by_y_hi(jnp.where(y_hi == 1, tq[rows:], tm[rows:]))
     v2 = move_by_core(jnp.where(core == 1, vp, vm), 1)
     own = [v01, vm, vp]
     videos = own + [move(block, core=1) for block in own]
-    texts = [t0, tp, a1m, b1m, a1p, b1p, a2m, a2p]
+    texts = [t0, tp, a1m, a1p, tm, tq]
 
     near_rows, far_rows = 6 * PAIR, 2 * PAIR
     near, text, near_video = call(

time: 95.1 us -> 95.2 us (level)
  the two profiles are of different devices: /device:TPU:8 before, /device:TPU:2 now
where the time goes in v10:
time: 95.2 us; the launch traced here: 93.4 us
  waiting for transfers between devices  39 us (41%)
  starting transfers between devices  28.3 us (30%)
  Pallas kernels  19.2 us (20%)
  other arithmetic  4.69 us (5%)
  between operations  2.07 us (2%)
    ppermute x24, waiting for transfers between devices, move(): return lax.ppermute(block, AXES, pairs)  32.8 us
    ppermute x24, starting transfers between devices, move(): return lax.ppermute(block, AXES, pairs)  25.3 us
    pallas_call x3, Pallas kernels, call(): pl.pallas_call(kernel, out_shape=outs, in_specs=[SMEM] * len(scalars) + [...  16 us
    convert_element_type x6, other arithmetic, add(): return total.astype(jnp.bfloat16)  4.5 us
    ppermute x1, waiting for transfers between devices, move_by_y_hi(): return lax.ppermute(block, AXES, pairs)  3.45 us
    ppermute x2, starting transfers between devices, move_by_core(): return lax.ppermute(block, AXES, pairs)  2.96 us
    ppermute x2, waiting for transfers between devices, move_by_core(): return lax.ppermute(block, AXES, pairs)  2.79 us
    pallas_call x2, Pallas kernels, back_rows(): pl.pallas_call(back_kernel, out_shape=jax.ShapeDtypeStruct(embedding.shap...  2.05 us
  transfers between devices with their start and end apart: 27, of which 16 were waited for; matrix products, arithmetic and copies ran while one was open for 5% of the time, Pallas kernels for 11%

profile of v10, /device:TPU:2, one launch (start us, length us, event | category | flops | bytes accessed | tf_op | source)
XLA Modules:
  0.0 93.4 jit_solution(4149943926539979274)
XLA Ops:
  0.6 1.2 %unit_low.1 = (bf16[128,768]{1,0:T(8,128)(2,1)S(1)}, bf16[128,768]{1,0:T(8,128)(2,1)S(1)}) custom-call(bf16[128,768]{1,0:T(8,128)(2,1)} %embedding_ref.2, bf16[128,768]{1,0:T(8,128)(2,1)} %embedding_ref.3), custom_call_target="tpu_custom_call" | custom-call | tf_op jit(solution)/shard_map/unit_low/pallas_call | solution.py:48
  1.8 1.7 %collective-permute-start = (bf16[128,768]{1,0:T(8,128)(2,1)S(1)}, bf16[128,768]{1,0:T(8,128)(2,1)S(1)}, u32[]{:S(2)}, u32[]{:S(2)}) collective-permute-start(bf16[128,768]{1,0:T(8,128)(2,1)S(1)} %get-tuple-element.43), channel_id=1, source_target_pairs={{0,1},{1,0},{2,3},{3,2},{4,5},{5,4},{6,7},{7,6},{8,9},{9,8},{10,11... | collective-permute-start | bytes 589832 | tf_op jit(solution)/shard_map/ppermute | solution.py:25
  3.5 5.9 %collective-permute-start.3 = (bf16[128,768]{1,0:T(8,128)(2,1)S(1)}, bf16[128,768]{1,0:T(8,128)(2,1)S(1)}, u32[]{:S(2)}, u32[]{:S(2)}) collective-permute-start(bf16[128,768]{1,0:T(8,128)(2,1)S(1)} %get-tuple-element.44.refs_0_), channel_id=1, source_target_pairs={{0,224},{1,225},{2,226},{3,227},{4,228},{5,229},{6,230},{7,231},{8... | collective-permute-start | bytes 589832 | tf_op jit(solution)/shard_map/ppermute | solution.py:25
  9.3 2.9 %collective-permute-start.1 = (bf16[128,768]{1,0:T(8,128)(2,1)S(1)}, bf16[128,768]{1,0:T(8,128)(2,1)S(1)}, u32[]{:S(2)}, u32[]{:S(2)}) collective-permute-start(bf16[128,768]{1,0:T(8,128)(2,1)S(1)} %get-tuple-element.44.refs_0_), channel_id=1, source_target_pairs={{0,16},{1,17},{2,18},{3,19},{4,20},{5,21},{6,22},{7,23},{8,24},{9,... | collective-permute-start | bytes 589832 | tf_op jit(solution)/shard_map/ppermute | solution.py:25
  13.2 3.4 %collective-permute-done.2.refs_2_ = bf16[128,768]{1,0:T(8,128)(2,1)S(1)} collective-permute-done((bf16[128,768]{1,0:T(8,128)(2,1)S(1)}, bf16[128,768]{1,0:T(8,128)(2,1)S(1)}, u32[]{:S(2)}, u32[]{:S(2)}) %collective-permute-start.2) | collective-permute-done | bytes 196640 | tf_op jit(solution)/shard_map/ppermute | solution.py:25
  17.6 1.5 %collective-permute-start.4 = (bf16[256,768]{1,0:T(8,128)(2,1)S(1)}, bf16[256,768]{1,0:T(8,128)(2,1)S(1)}, u32[]{:S(2)}, u32[]{:S(2)}) collective-permute-start(bf16[256,768]{1,0:T(8,128)(2,1)S(1)} %constant_dynamic-update-slice_fusion.refs_6_), channel_id=1, source_target_pairs={{0,2},{1,3},{2,4},{3,5},{4,6},{5,7},{6,0},{7,1},{8,10},{9,11},{10,... | collective-permute-start | bytes 1179656 | tf_op jit(solution)/shard_map/ppermute | solution.py:25
  19.1 4.2 %collective-permute-start.7 = (bf16[256,768]{1,0:T(8,128)(2,1)S(1)}, bf16[256,768]{1,0:T(8,128)(2,1)S(1)}, u32[]{:S(2)}, u32[]{:S(2)}) collective-permute-start(bf16[256,768]{1,0:T(8,128)(2,1)S(1)} %get-tuple-element.86), channel_id=1, source_target_pairs={{0,224},{1,225},{2,226},{3,227},{4,228},{5,229},{6,230},{7,231},{8... | collective-permute-start | bytes 1179656 | tf_op jit(solution)/shard_map/ppermute | solution.py:25
  24.7 1.7 %collective-permute-done.5.refs_8_ = bf16[256,768]{1,0:T(8,128)(2,1)S(1)} collective-permute-done((bf16[256,768]{1,0:T(8,128)(2,1)S(1)}, bf16[256,768]{1,0:T(8,128)(2,1)S(1)}, u32[]{:S(2)}, u32[]{:S(2)}) %collective-permute-start.5) | collective-permute-done | bytes 393248 | tf_op jit(solution)/shard_map/ppermute | solution.py:25
  26.4 1.3 %collective-permute-done.4.refs_7_ = bf16[256,768]{1,0:T(8,128)(2,1)S(1)} collective-permute-done((bf16[256,768]{1,0:T(8,128)(2,1)S(1)}, bf16[256,768]{1,0:T(8,128)(2,1)S(1)}, u32[]{:S(2)}, u32[]{:S(2)}) %collective-permute-start.4) | collective-permute-done | bytes 393248 | tf_op jit(solution)/shard_map/ppermute | solution.py:25
  27.7 2.6 %collective-permute-done.7.refs_5_ = bf16[256,768]{1,0:T(8,128)(2,1)S(1)} collective-permute-done((bf16[256,768]{1,0:T(8,128)(2,1)S(1)}, bf16[256,768]{1,0:T(8,128)(2,1)S(1)}, u32[]{:S(2)}, u32[]{:S(2)}) %collective-permute-start.7) | collective-permute-done | bytes 393248 | tf_op jit(solution)/shard_map/ppermute | solution.py:25
  30.3 3.4 %collective-permute-done.6.refs_4_ = bf16[256,768]{1,0:T(8,128)(2,1)S(1)} collective-permute-done((bf16[256,768]{1,0:T(8,128)(2,1)S(1)}, bf16[256,768]{1,0:T(8,128)(2,1)S(1)}, u32[]{:S(2)}, u32[]{:S(2)}) %collective-permute-start.6) | collective-permute-done | bytes 393248 | tf_op jit(solution)/shard_map/ppermute | solution.py:25
  34.2 1.6 %collective-permute-start.8 = (bf16[256,768]{1,0:T(8,128)(2,1)S(1)}, bf16[256,768]{1,0:T(8,128)(2,1)S(1)}, u32[]{:S(2)}, u32[]{:S(2)}) collective-permute-start(bf16[256,768]{1,0:T(8,128)(2,1)S(1)} %broadcast_select_fusion), channel_id=1, source_target_pairs={{0,2},{1,3},{2,4},{3,5},{4,6},{5,7},{6,0},{7,1},{8,14},{9,15},{10,... | collective-permute-start | bytes 1179656 | tf_op jit(solution)/shard_map/ppermute | solution.py:306
  36.0 4.3 %near_weights.1 = (bf16[1536,1024]{1,0:T(8,128)(2,1)S(1)}, bf16[1024,768]{1,0:T(8,128)(2,1)S(1)}, bf16[1536,768]{1,0:T(8,128)(2,1)S(1)}) custom-call(f32[1]{0:T(128)S(6)} %copy.7.scale_ref, f32[1]{0:T(128)S(6)} %copy.8.offset_ref, s32[2]{0:T(128)S(1)} %pad_add_fusion.place_ref, bf16[128,768]{1,0:T(8,128)(2,1)S(1)} %get-tuple-element.44.refs_0_, ...), custom_call_target="tpu_custom_call" | custom-call | flops 2415919104 | tf_op jit(solution)/shard_map/near_weights/pallas_call | solution.py:211
  40.3 3.5 %collective-permute-done.9.last = bf16[128,768]{1,0:T(8,128)(2,1)S(1)} collective-permute-done((bf16[128,768]{1,0:T(8,128)(2,1)S(1)}, bf16[128,768]{1,0:T(8,128)(2,1)S(1)}, u32[]{:S(2)}, u32[]{:S(2)}) %collective-permute-start.9) | collective-permute-done | bytes 196640 | tf_op jit(solution)/shard_map/ppermute | solution.py:316
  43.7 1.7 %collective-permute-done.13.refs_1_ = bf16[256,768]{1,0:T(8,128)(2,1)S(1)} collective-permute-done((bf16[256,768]{1,0:T(8,128)(2,1)S(1)}, bf16[256,768]{1,0:T(8,128)(2,1)S(1)}, u32[]{:S(2)}, u32[]{:S(2)}) %collective-permute-start.13) | collective-permute-done | bytes 393248 | tf_op jit(solution)/shard_map/ppermute | solution.py:25
  45.4 7.0 %far_weights_and_sums.1 = (bf16[1536,128]{1,0:T(8,128)(2,1)S(1)}, bf16[512,1152]{1,0:T(8,128)(2,1)S(1)}, bf16[512,768]{1,0:T(8,128)(2,1)S(1)}, bf16[256,768]{1,0...) custom-call(f32[1]{0:T(128)S(6)} %copy.7.scale_ref, ...), custom_call_target="tpu_custom_call" | custom-call | flops 5033164800 | tf_op jit(solution)/shard_map/far_weights_and_sums/pallas_call | solution.py:211
  52.6 2.0 %collective-permute-start.15 = (bf16[256,768]{1,0:T(8,128)(2,1)}, bf16[256,768]{1,0:T(8,128)(2,1)}, u32[]{:S(2)}, u32[]{:S(2)}) collective-permute-start(bf16[256,768]{1,0:T(8,128)(2,1)} %get-tuple-element.60), channel_id=1, source_target_pairs={{0,32},{1,33},{2,34},{3,35},{4,36},{5,37},{6,38},{7,39},{8,40},{9,... | collective-permute-start | bytes 1179656 | tf_op jit(solution)/shard_map/ppermute | solution.py:25
  54.6 4.7 %own_video_and_near_text_sums.1 = (bf16[256,768]{1,0:T(8,128)(2,1)S(1)}, bf16[256,768]{1,0:T(8,128)(2,1)S(1)}, bf16[256,768]{1,0:T(8,128)(2,1)S(1)}, bf16[256,76...) custom-call(bf16[1536,1024]{1,0:T(8,128)(2,1)S(1)} %get-tuple-elemen, ...), custom_call_target="tpu_custom_call" | custom-call | flops 4026531840 | tf_op jit(solution)/shard_map/own_video_and_near_text_sums/pallas_call | solution.py:211
  60.2 1.4 %collective-permute-start.17 = (bf16[256,768]{1,0:T(8,128)(2,1)}, bf16[256,768]{1,0:T(8,128)(2,1)}, u32[]{:S(2)}, u32[]{:S(2)}) collective-permute-start(bf16[256,768]{1,0:T(8,128)(2,1)} %add_convert_fusion.4), channel_id=1, source_target_pairs={{0,6},{1,7},{2,0},{3,1},{4,2},{5,3},{6,4},{7,5},{8,10},{9,11},{10,... | collective-permute-start | bytes 1179656 | tf_op jit(solution)/shard_map/ppermute | solution.py:306
  62.1 2.2 %collective-permute-done.14 = bf16[256,768]{1,0:T(8,128)(2,1)} collective-permute-done((bf16[256,768]{1,0:T(8,128)(2,1)}, bf16[256,768]{1,0:T(8,128)(2,1)}, u32[]{:S(2)}, u32[]{:S(2)}) %collective-permute-start.14) | collective-permute-done | bytes 393248 | tf_op jit(solution)/shard_map/ppermute | solution.py:25
  64.3 1.2 %collective-permute-done.15 = bf16[256,768]{1,0:T(8,128)(2,1)} collective-permute-done((bf16[256,768]{1,0:T(8,128)(2,1)}, bf16[256,768]{1,0:T(8,128)(2,1)}, u32[]{:S(2)}, u32[]{:S(2)}) %collective-permute-start.15) | collective-permute-done | bytes 393248 | tf_op jit(solution)/shard_map/ppermute | solution.py:25
  65.5 2.8 %collective-permute-done.17 = bf16[256,768]{1,0:T(8,128)(2,1)} collective-permute-done((bf16[256,768]{1,0:T(8,128)(2,1)}, bf16[256,768]{1,0:T(8,128)(2,1)}, u32[]{:S(2)}, u32[]{:S(2)}) %collective-permute-start.17) | collective-permute-done | bytes 393248 | tf_op jit(solution)/shard_map/ppermute | solution.py:306
  68.3 1.1 %add_convert_fusion = bf16[256,768]{1,0:T(8,128)(2,1)S(1)} fusion(bf16[256,768]{1,0:T(8,128)(2,1)} %collective-permute-done.14, bf16[256,768]{1,0:T(8,128)(2,1)S(1)} %get-tuple-element.82), kind=kLoop, calls=%fused_computation | loop fusion | flops 786432 | bytes 1179648 | tf_op jit(solution)/shard_map/convert_element_type | solution.py:32
  69.4 1.7 %collective-permute-start.25 = (bf16[256,768]{1,0:T(8,128)(2,1)S(1)}, bf16[256,768]{1,0:T(8,128)(2,1)S(1)}, u32[]{:S(2)}, u32[]{:S(2)}) collective-permute-start(bf16[256,768]{1,0:T(8,128)(2,1)S(1)} %add_convert_fusion), channel_id=1, source_target_pairs={{0,224},{1,225},{2,226},{3,227},{4,228},{5,229},{6,230},{7,231},{8... | collective-permute-start | bytes 1179656 | tf_op jit(solution)/shard_map/ppermute | solution.py:25
  71.1 1.1 %add_convert_fusion.1 = bf16[256,768]{1,0:T(8,128)(2,1)S(1)} fusion(bf16[256,768]{1,0:T(8,128)(2,1)} %collective-permute-done.15, bf16[256,768]{1,0:T(8,128)(2,1)S(1)} %get-tuple-element.80), kind=kLoop, calls=%fused_computation.1 | loop fusion | flops 786432 | bytes 1179648 | tf_op jit(solution)/shard_map/convert_element_type | solution.py:32
  72.6 1.3 %add_convert_fusion.2 = (bf16[256,768]{1,0:T(8,128)(2,1)S(1)}, bf16[256,768]{1,0:T(8,128)(2,1)S(1)}) fusion(bf16[256,768]{1,0:T(8,128)(2,1)S(1)} %collective-permute-done.21, bf16[256,768]{1,0:T(8,128)(2,1)S(1)} %get-tuple-element.77, bf16[256,768]{1,0:T(8,128)(2,1)} %collective-permute-done.17, pred[]{:T(512)S(6)} %eq.15, pred[]{:T(512)S(6)} %eq.13, ...), kind=kLoop, calls=%fused_computation.2 | loop fusion | flops 2752512 | bytes 2752514 | tf_op jit(solution)/shard_map/convert_element_type | solution.py:32
  74.0 1.6 %collective-permute-start.22 = (bf16[256,768]{1,0:T(8,128)(2,1)S(1)}, bf16[256,768]{1,0:T(8,128)(2,1)S(1)}, u32[]{:S(2)}, u32[]{:S(2)}) collective-permute-start(bf16[256,768]{1,0:T(8,128)(2,1)S(1)} %get-tuple-element.84), channel_id=1, source_target_pairs={{0,6},{1,7},{2,0},{3,1},{4,2},{5,3},{6,4},{7,5},{8,14},{9,15},{10,... | collective-permute-start | bytes 1179656 | tf_op jit(solution)/shard_map/ppermute | solution.py:25
  76.1 3.3 %collective-permute-done.25.refs_2_ = bf16[256,768]{1,0:T(8,128)(2,1)S(1)} collective-permute-done((bf16[256,768]{1,0:T(8,128)(2,1)S(1)}, bf16[256,768]{1,0:T(8,128)(2,1)S(1)}, u32[]{:S(2)}, u32[]{:S(2)}) %collective-permute-start.25) | collective-permute-done | bytes 393248 | tf_op jit(solution)/shard_map/ppermute | solution.py:25
  79.4 3.7 %collective-permute-done.24.refs_1_ = bf16[256,768]{1,0:T(8,128)(2,1)S(1)} collective-permute-done((bf16[256,768]{1,0:T(8,128)(2,1)S(1)}, bf16[256,768]{1,0:T(8,128)(2,1)S(1)}, u32[]{:S(2)}, u32[]{:S(2)}) %collective-permute-start.24) | collective-permute-done | bytes 393248 | tf_op jit(solution)/shard_map/ppermute | solution.py:25
  84.0 1.7 %collective-permute-done.20.refs_2_ = bf16[256,768]{1,0:T(8,128)(2,1)S(1)} collective-permute-done((bf16[256,768]{1,0:T(8,128)(2,1)S(1)}, bf16[256,768]{1,0:T(8,128)(2,1)S(1)}, u32[]{:S(2)}, u32[]{:S(2)}) %collective-permute-start.20) | collective-permute-done | bytes 393248 | tf_op jit(solution)/shard_map/ppermute | solution.py:25
  86.0 5.3 %collective-permute-done.26.refs_3_ = bf16[128,768]{1,0:T(8,128)(2,1)S(1)} collective-permute-done((bf16[128,768]{1,0:T(8,128)(2,1)S(1)}, bf16[128,768]{1,0:T(8,128)(2,1)S(1)}, u32[]{:S(2)}, u32[]{:S(2)}) %collective-permute-start.26) | collective-permute-done | bytes 196640 | tf_op jit(solution)/shard_map/ppermute | solution.py:25
  92.4 1.0 %back_rows.2 = f32[128,768]{1,0:T(8,128)} custom-call(f32[1]{0:T(128)S(6)} %copy.7.scale_ref, bf16[128,768]{1,0:T(8,128)(2,1)S(1)} %copy-done.1, bf16[256,768]{1,0:T(8,128)(2,1)S(1)} %get-tuple-element.72.refs_0_, bf16[256,768]{1,0:T(8,128)(2,1)S(1)} %collective-permute-done.18.refs_1_, bf16[256,768]{1,0:T(8,128)(2,1)S(1)} %collective-permute-done.20.refs_2_, ...), custom_call_target="tpu_custom_call" | custom-call | tf_op jit(solution)/shard_map/back_rows/pallas_call | solution.py:65
  (44 shorter events, 7.5 us)
Async XLA Ops:
  1.8 10.4 %collective-permute-start = (bf16[128,768]{1,0:T(8,128)(2,1)S(1)}, bf16[128,768]{1,0:T(8,128)(2,1)S(1)}, u32[]{:S(2)}, u32[]{:S(2)}) collective-permute-start(bf16[128,768]{1,0:T(8,128)(2,1)S(1)} %get-tuple-element.43), channel_id=1, source_target_pairs={{0,1},{1,0},{2,3},{3,2},{4,5},{5,4},{6,7},{7,6},{8,9},{9,8},{10,11... | collective-permute-start | bytes 589832 | tf_op jit(solution)/shard_map/ppermute | solution.py:25
  3.5 9.7 %collective-permute-start.3 = (bf16[128,768]{1,0:T(8,128)(2,1)S(1)}, bf16[128,768]{1,0:T(8,128)(2,1)S(1)}, u32[]{:S(2)}, u32[]{:S(2)}) collective-permute-start(bf16[128,768]{1,0:T(8,128)(2,1)S(1)} %get-tuple-element.44.refs_0_), channel_id=1, source_target_pairs={{0,224},{1,225},{2,226},{3,227},{4,228},{5,229},{6,230},{7,231},{8... | collective-permute-start | bytes 589832 | tf_op jit(solution)/shard_map/ppermute | solution.py:25
  9.3 7.3 %collective-permute-start.2 = (bf16[128,768]{1,0:T(8,128)(2,1)S(1)}, bf16[128,768]{1,0:T(8,128)(2,1)S(1)}, u32[]{:S(2)}, u32[]{:S(2)}) collective-permute-start(bf16[128,768]{1,0:T(8,128)(2,1)S(1)} %get-tuple-element.44.refs_0_), channel_id=1, source_target_pairs={{0,32},{1,33},{2,34},{3,35},{4,36},{5,37},{6,38},{7,39},{8,40},{9,... | collective-permute-start | bytes 589832 | tf_op jit(solution)/shard_map/ppermute | solution.py:25
  9.3 7.6 %collective-permute-start.1 = (bf16[128,768]{1,0:T(8,128)(2,1)S(1)}, bf16[128,768]{1,0:T(8,128)(2,1)S(1)}, u32[]{:S(2)}, u32[]{:S(2)}) collective-permute-start(bf16[128,768]{1,0:T(8,128)(2,1)S(1)} %get-tuple-element.44.refs_0_), channel_id=1, source_target_pairs={{0,16},{1,17},{2,18},{3,19},{4,20},{5,21},{6,22},{7,23},{8,24},{9,... | collective-permute-start | bytes 589832 | tf_op jit(solution)/shard_map/ppermute | solution.py:25
  16.9 9.4 %collective-permute-start.5 = (bf16[256,768]{1,0:T(8,128)(2,1)S(1)}, bf16[256,768]{1,0:T(8,128)(2,1)S(1)}, u32[]{:S(2)}, u32[]{:S(2)}) collective-permute-start(bf16[256,768]{1,0:T(8,128)(2,1)S(1)} %constant_dynamic-update-slice_fusion.refs_6_), channel_id=1, source_target_pairs={{0,6},{1,7},{2,0},{3,1},{4,2},{5,3},{6,4},{7,5},{8,14},{9,15},{10,... | collective-permute-start | bytes 1179656 | tf_op jit(solution)/shard_map/ppermute | solution.py:25
  17.6 10.1 %collective-permute-start.4 = (bf16[256,768]{1,0:T(8,128)(2,1)S(1)}, bf16[256,768]{1,0:T(8,128)(2,1)S(1)}, u32[]{:S(2)}, u32[]{:S(2)}) collective-permute-start(bf16[256,768]{1,0:T(8,128)(2,1)S(1)} %constant_dynamic-update-slice_fusion.refs_6_), channel_id=1, source_target_pairs={{0,2},{1,3},{2,4},{3,5},{4,6},{5,7},{6,0},{7,1},{8,10},{9,11},{10,... | collective-permute-start | bytes 1179656 | tf_op jit(solution)/shard_map/ppermute | solution.py:25
  19.1 11.2 %collective-permute-start.7 = (bf16[256,768]{1,0:T(8,128)(2,1)S(1)}, bf16[256,768]{1,0:T(8,128)(2,1)S(1)}, u32[]{:S(2)}, u32[]{:S(2)}) collective-permute-start(bf16[256,768]{1,0:T(8,128)(2,1)S(1)} %get-tuple-element.86), channel_id=1, source_target_pairs={{0,224},{1,225},{2,226},{3,227},{4,228},{5,229},{6,230},{7,231},{8... | collective-permute-start | bytes 1179656 | tf_op jit(solution)/shard_map/ppermute | solution.py:25
  23.3 10.4 %collective-permute-start.6 = (bf16[256,768]{1,0:T(8,128)(2,1)S(1)}, bf16[256,768]{1,0:T(8,128)(2,1)S(1)}, u32[]{:S(2)}, u32[]{:S(2)}) collective-permute-start(bf16[256,768]{1,0:T(8,128)(2,1)S(1)} %get-tuple-element.87), channel_id=1, source_target_pairs={{0,32},{1,33},{2,34},{3,35},{4,36},{5,37},{6,38},{7,39},{8,40},{9,... | collective-permute-start | bytes 1179656 | tf_op jit(solution)/shard_map/ppermute | solution.py:25
  24.7 11.2 %collective-permute-start.10 = (bf16[256,768]{1,0:T(8,128)(2,1)S(1)}, bf16[256,768]{1,0:T(8,128)(2,1)S(1)}, u32[]{:S(2)}, u32[]{:S(2)}) collective-permute-start(bf16[256,768]{1,0:T(8,128)(2,1)S(1)} %constant_dynamic-update-slice_fusion.refs_6_), channel_id=1, source_target_pairs={{0,8},{1,9},{2,10},{3,11},{4,12},{5,13},{6,14},{7,15},{8,0},{9,1},... | collective-permute-start | bytes 1179656 | tf_op jit(solution)/shard_map/ppermute | solution.py:25
  33.7 2.3 %collective-permute-start.12 = (bf16[256,768]{1,0:T(8,128)(2,1)S(1)}, bf16[256,768]{1,0:T(8,128)(2,1)S(1)}, u32[]{:S(2)}, u32[]{:S(2)}) collective-permute-start(bf16[256,768]{1,0:T(8,128)(2,1)S(1)} %collective-permute-done.5.refs_8_), channel_id=1, source_target_pairs={{0,8},{1,9},{2,10},{3,11},{4,12},{5,13},{6,14},{7,15},{8,0},{9,1},... | collective-permute-start | bytes 1179656 | tf_op jit(solution)/shard_map/ppermute | solution.py:25
  33.7 2.3 %collective-permute-start.11 = (bf16[256,768]{1,0:T(8,128)(2,1)S(1)}, bf16[256,768]{1,0:T(8,128)(2,1)S(1)}, u32[]{:S(2)}, u32[]{:S(2)}) collective-permute-start(bf16[256,768]{1,0:T(8,128)(2,1)S(1)} %collective-permute-done.4.refs_7_), channel_id=1, source_target_pairs={{0,8},{1,9},{2,10},{3,11},{4,12},{5,13},{6,14},{7,15},{8,0},{9,1},... | collective-permute-start | bytes 1179656 | tf_op jit(solution)/shard_map/ppermute | solution.py:25
  34.2 9.5 %collective-permute-start.8 = (bf16[256,768]{1,0:T(8,128)(2,1)S(1)}, bf16[256,768]{1,0:T(8,128)(2,1)S(1)}, u32[]{:S(2)}, u32[]{:S(2)}) collective-permute-start(bf16[256,768]{1,0:T(8,128)(2,1)S(1)} %broadcast_select_fusion), channel_id=1, source_target_pairs={{0,2},{1,3},{2,4},{3,5},{4,6},{5,7},{6,0},{7,1},{8,14},{9,15},{10,... | collective-permute-start | bytes 1179656 | tf_op jit(solution)/shard_map/ppermute | solution.py:306
  35.8 7.9 %collective-permute-start.9 = (bf16[128,768]{1,0:T(8,128)(2,1)S(1)}, bf16[128,768]{1,0:T(8,128)(2,1)S(1)}, u32[]{:S(2)}, u32[]{:S(2)}) collective-permute-start(bf16[128,768]{1,0:T(8,128)(2,1)S(1)} %slice_select_fusion), channel_id=1, source_target_pairs={{0,32},{1,33},{2,34},{3,35},{4,36},{5,37},{6,38},{7,39},{8,40},{9,... | collective-permute-start | bytes 589832 | tf_op jit(solution)/shard_map/ppermute | solution.py:316
  43.7 1.7 %collective-permute-start.13 = (bf16[256,768]{1,0:T(8,128)(2,1)S(1)}, bf16[256,768]{1,0:T(8,128)(2,1)S(1)}, u32[]{:S(2)}, u32[]{:S(2)}) collective-permute-start(bf16[256,768]{1,0:T(8,128)(2,1)S(1)} %collective-permute-done.8.refs_0_), channel_id=1, source_target_pairs={{0,8},{1,9},{2,10},{3,11},{4,12},{5,13},{6,14},{7,15},{8,0},{9,1},... | collective-permute-start | bytes 1179656 | tf_op jit(solution)/shard_map/ppermute | solution.py:25
  52.4 6.9 %collective-permute-start.16 = (bf16[256,768]{1,0:T(8,128)(2,1)S(1)}, bf16[256,768]{1,0:T(8,128)(2,1)S(1)}, u32[]{:S(2)}, u32[]{:S(2)}) collective-permute-start(bf16[256,768]{1,0:T(8,128)(2,1)S(1)} %get-tuple-element.65), channel_id=1, source_target_pairs={{0,8},{1,9},{2,10},{3,11},{4,12},{5,13},{6,14},{7,15},{8,0},{9,1},... | collective-permute-start | bytes 1179656 | tf_op jit(solution)/shard_map/ppermute | solution.py:25
  52.5 11.7 %collective-permute-start.14 = (bf16[256,768]{1,0:T(8,128)(2,1)}, bf16[256,768]{1,0:T(8,128)(2,1)}, u32[]{:S(2)}, u32[]{:S(2)}) collective-permute-start(bf16[256,768]{1,0:T(8,128)(2,1)} %get-tuple-element.59), channel_id=1, source_target_pairs={{0,224},{1,225},{2,226},{3,227},{4,228},{5,229},{6,230},{7,231},{8... | collective-permute-start | bytes 1179656 | tf_op jit(solution)/shard_map/ppermute | solution.py:25
  52.6 12.9 %collective-permute-start.15 = (bf16[256,768]{1,0:T(8,128)(2,1)}, bf16[256,768]{1,0:T(8,128)(2,1)}, u32[]{:S(2)}, u32[]{:S(2)}) collective-permute-start(bf16[256,768]{1,0:T(8,128)(2,1)} %get-tuple-element.60), channel_id=1, source_target_pairs={{0,32},{1,33},{2,34},{3,35},{4,36},{5,37},{6,38},{7,39},{8,40},{9,... | collective-permute-start | bytes 1179656 | tf_op jit(solution)/shard_map/ppermute | solution.py:25
  60.2 8.1 %collective-permute-start.17 = (bf16[256,768]{1,0:T(8,128)(2,1)}, bf16[256,768]{1,0:T(8,128)(2,1)}, u32[]{:S(2)}, u32[]{:S(2)}) collective-permute-start(bf16[256,768]{1,0:T(8,128)(2,1)} %add_convert_fusion.4), channel_id=1, source_target_pairs={{0,6},{1,7},{2,0},{3,1},{4,2},{5,3},{6,4},{7,5},{8,10},{9,11},{10,... | collective-permute-start | bytes 1179656 | tf_op jit(solution)/shard_map/ppermute | solution.py:306
  61.6 22.4 %collective-permute-start.18 = (bf16[256,768]{1,0:T(8,128)(2,1)S(1)}, bf16[256,768]{1,0:T(8,128)(2,1)S(1)}, u32[]{:S(2)}, u32[]{:S(2)}) collective-permute-start(bf16[256,768]{1,0:T(8,128)(2,1)S(1)} %get-tuple-element.73), channel_id=1, source_target_pairs={{0,8},{1,9},{2,10},{3,11},{4,12},{5,13},{6,14},{7,15},{8,0},{9,1},... | collective-permute-start | bytes 1179656 | tf_op jit(solution)/shard_map/ppermute | solution.py:25
  61.6 11.1 %collective-permute-start.19 = (bf16[256,768]{1,0:T(8,128)(2,1)S(1)}, bf16[256,768]{1,0:T(8,128)(2,1)S(1)}, u32[]{:S(2)}, u32[]{:S(2)}) collective-permute-start(bf16[256,768]{1,0:T(8,128)(2,1)S(1)} %get-tuple-element.75), channel_id=1, source_target_pairs={{0,8},{1,9},{2,10},{3,11},{4,12},{5,13},{6,14},{7,15},{8,0},{9,1},... | collective-permute-start | bytes 1179656 | tf_op jit(solution)/shard_map/ppermute | solution.py:25
  64.3 8.4 %collective-permute-start.21 = (bf16[256,768]{1,0:T(8,128)(2,1)S(1)}, bf16[256,768]{1,0:T(8,128)(2,1)S(1)}, u32[]{:S(2)}, u32[]{:S(2)}) collective-permute-start(bf16[256,768]{1,0:T(8,128)(2,1)S(1)} %get-tuple-element.78), channel_id=1, source_target_pairs={{0,8},{1,9},{2,10},{3,11},{4,12},{5,13},{6,14},{7,15},{8,0},{9,1},... | collective-permute-start | bytes 1179656 | tf_op jit(solution)/shard_map/ppermute | solution.py:25
  69.4 10.0 %collective-permute-start.25 = (bf16[256,768]{1,0:T(8,128)(2,1)S(1)}, bf16[256,768]{1,0:T(8,128)(2,1)S(1)}, u32[]{:S(2)}, u32[]{:S(2)}) collective-permute-start(bf16[256,768]{1,0:T(8,128)(2,1)S(1)} %add_convert_fusion), channel_id=1, source_target_pairs={{0,224},{1,225},{2,226},{3,227},{4,228},{5,229},{6,230},{7,231},{8... | collective-permute-start | bytes 1179656 | tf_op jit(solution)/shard_map/ppermute | solution.py:25
  72.2 19.2 %copy-start = (bf16[128,768]{1,0:T(8,128)(2,1)S(1)}, bf16[128,768]{1,0:T(8,128)(2,1)}, u32[]{:S(2)}) copy-start(bf16[128,768]{1,0:T(8,128)(2,1)} %embedding_ref.3) | copy-start | bytes 589828
  72.2 10.9 %collective-permute-start.24 = (bf16[256,768]{1,0:T(8,128)(2,1)S(1)}, bf16[256,768]{1,0:T(8,128)(2,1)S(1)}, u32[]{:S(2)}, u32[]{:S(2)}) collective-permute-start(bf16[256,768]{1,0:T(8,128)(2,1)S(1)} %add_convert_fusion.1), channel_id=1, source_target_pairs={{0,32},{1,33},{2,34},{3,35},{4,36},{5,37},{6,38},{7,39},{8,40},{9,... | collective-permute-start | bytes 1179656 | tf_op jit(solution)/shard_map/ppermute | solution.py:25
  74.0 18.4 %copy-start.1 = (bf16[128,768]{1,0:T(8,128)(2,1)S(1)}, bf16[128,768]{1,0:T(8,128)(2,1)}, u32[]{:S(2)}) copy-start(bf16[128,768]{1,0:T(8,128)(2,1)} %embedding_ref.2) | copy-start | bytes 589828
  74.0 10.0 %collective-permute-start.22 = (bf16[256,768]{1,0:T(8,128)(2,1)S(1)}, bf16[256,768]{1,0:T(8,128)(2,1)S(1)}, u32[]{:S(2)}, u32[]{:S(2)}) collective-permute-start(bf16[256,768]{1,0:T(8,128)(2,1)S(1)} %get-tuple-element.84), channel_id=1, source_target_pairs={{0,6},{1,7},{2,0},{3,1},{4,2},{5,3},{6,4},{7,5},{8,14},{9,15},{10,... | collective-permute-start | bytes 1179656 | tf_op jit(solution)/shard_map/ppermute | solution.py:25
  75.6 10.1 %collective-permute-start.20 = (bf16[256,768]{1,0:T(8,128)(2,1)S(1)}, bf16[256,768]{1,0:T(8,128)(2,1)S(1)}, u32[]{:S(2)}, u32[]{:S(2)}) collective-permute-start(bf16[256,768]{1,0:T(8,128)(2,1)S(1)} %get-tuple-element.85), channel_id=1, source_target_pairs={{0,2},{1,3},{2,4},{3,5},{4,6},{5,7},{6,0},{7,1},{8,10},{9,11},{10,... | collective-permute-start | bytes 1179656 | tf_op jit(solution)/shard_map/ppermute | solution.py:25
  83.2 8.2 %collective-permute-start.26 = (bf16[128,768]{1,0:T(8,128)(2,1)S(1)}, bf16[128,768]{1,0:T(8,128)(2,1)S(1)}, u32[]{:S(2)}, u32[]{:S(2)}) collective-permute-start(bf16[128,768]{1,0:T(8,128)(2,1)S(1)} %add_convert_fusion.5), channel_id=1, source_target_pairs={{0,16},{1,17},{2,18},{3,19},{4,20},{5,21},{6,22},{7,23},{8,24},{9,... | collective-permute-start | bytes 589832 | tf_op jit(solution)/shard_map/ppermute | solution.py:25
  85.8 6.6 %collective-permute-start.23 = (bf16[128,768]{1,0:T(8,128)(2,1)S(1)}, bf16[128,768]{1,0:T(8,128)(2,1)S(1)}, u32[]{:S(2)}, u32[]{:S(2)}) collective-permute-start(bf16[128,768]{1,0:T(8,128)(2,1)S(1)} %add_convert_fusion.6), channel_id=1, source_target_pairs={{0,1},{1,0},{2,3},{3,2},{4,5},{5,4},{6,7},{7,6},{8,9},{9,8},{10,11... | collective-permute-start | bytes 589832 | tf_op jit(solution)/shard_map/ppermute | solution.py:25
